TPU v7x, 32 devices: a whole 2x2x4 slice. The times are simulated.
32 devices in a mesh: group: 2 (over x), inst: 8 (over z, y), tp: 2 (over core).
Axes of the slice: x: 2, y: 2, z: 4, core: 2. Of those that a mesh axis runs over, the one named last changes fastest.
Arguments:
- hidden_new: bfloat16 [2, 384, 5120], P(None, ('group', 'inst'), 'tp'), parts along dimension 1, may hold values from -6 to 6
- queries: bfloat16 [2, 384, 4096], P(None, ('group', 'inst'), 'tp'), parts along dimension 1
- kv_cache: bfloat16 [384, 2, 144, 512], P(('group', 'inst'), None, None, 'tp'), parts along dimension 0
- lengths: int32 [384], P(('group', 'inst')), parts along dimension 0, may hold values from 8 to 142
- destination: int32 [384], P(('group', 'inst')), parts along dimension 0, may hold values from 0 to 191, as said below
- key_weight: bfloat16 [5120, 512], P('tp'), may hold values from -0.078125 to 0.078125
- value_weight: bfloat16 [5120, 512], P('tp'), may hold values from -0.078125 to 0.078125
- key_gain: bfloat16 [128], replicated, may hold values from 0.099609375 to 1.8984375
Outputs:
- attended_out: bfloat16 [2, 384, 4096], P(None, ('group', 'inst'), 'tp'), parts along dimension 1
- moved_cache: bfloat16 [384, 2, 144, 512], P(('group', 'inst'), None, None, 'tp'), parts along dimension 0
There are 2 independent parts, one for each index of `group`. A program takes and returns all parts, laid end to end along the dimension named above; an argument that names none is the same for every part. Nothing has to cross between parts.
Inputs may be any that keep to these rules, and one draw needn't show every extreme that they name: `destination`: A permutation of the 192 slots (slot = instance * 24 + position on the instance). A request that stays on its instance keeps its slot; an instance sends at most one request to any other instance and receives at most one from it.
All inputs are finite; a program needn't handle non-finite values.
Results may differ from a plain program's by a relative error of at most 0.0051.
Values may be sent and summed in bfloat16 or wider, within the bound.
No kernel may reach another device: no remote copies, remote signals or barrier semaphores. Data moves between devices by JAX's collectives and lax.ppermute only.
A program may use at most 128 MiB of HBM per device.

v0:
```python
import math

import jax
import jax.numpy as jnp
from jax import lax
from jax.sharding import PartitionSpec as P

HD = 128


ROPE_BASE = 1000000.0
NORM_EPS = 1e-06


def place_keys(projected, gain_vector, positions):
    row_count, step_count, lane_width = projected.shape
    head_count = lane_width // HD
    pieces = projected.reshape(row_count, step_count, head_count, HD)
    pieces = pieces * lax.rsqrt(jnp.mean(pieces * pieces, axis=-1, keepdims=True) + NORM_EPS)
    pieces = pieces * gain_vector.astype(jnp.float32)
    half_dim = HD // 2
    inverse = jnp.exp(-math.log(ROPE_BASE) * 2.0 * jnp.arange(half_dim, dtype=jnp.float32) / HD)
    angles = positions.astype(jnp.float32)[:, :, None, None] * inverse
    cosine = jnp.cos(angles)
    sine_part = jnp.sin(angles)
    front = pieces[..., :half_dim]
    back = pieces[..., half_dim:]
    turned = jnp.concatenate(
        [front * cosine - back * sine_part, back * cosine + front * sine_part], axis=-1
    )
    return turned.reshape(row_count, step_count, lane_width).astype(jnp.bfloat16)


def attend(queries, kv_rows, lengths, new_keys, new_values):
    row_count, step_count, query_width = queries.shape
    capacity = kv_rows.shape[2]
    lane_width = kv_rows.shape[3]
    head_count = lane_width // HD
    group_size = query_width // lane_width
    grouped = queries.reshape(row_count, step_count, head_count, group_size, HD)
    cached_keys = kv_rows[:, 0].reshape(row_count, capacity, head_count, HD)
    cached_values = kv_rows[:, 1].reshape(row_count, capacity, head_count, HD)
    fresh_keys = new_keys.reshape(row_count, step_count, head_count, HD)
    fresh_values = new_values.reshape(row_count, step_count, head_count, HD)
    factor = 1.0 / math.sqrt(HD)
    cache_scores = (
        jnp.einsum("rskgd,rckd->rskgc", grouped, cached_keys, preferred_element_type=jnp.float32)
        * factor
    )
    fresh_scores = (
        jnp.einsum("rskgd,rtkd->rskgt", grouped, fresh_keys, preferred_element_type=jnp.float32)
        * factor
    )
    live = (
        jnp.arange(capacity, dtype=jnp.int32)[None, None, None, None, :]
        < lengths[:, None, None, None, None]
    )
    cache_scores = jnp.where(live, cache_scores, -jnp.inf)
    causal = jnp.arange(step_count)[None, :] <= jnp.arange(step_count)[:, None]
    fresh_scores = jnp.where(causal[None, :, None, None, :], fresh_scores, -jnp.inf)
    peak_score = jnp.maximum(jnp.max(cache_scores, axis=-1), jnp.max(fresh_scores, axis=-1))[
        ..., None
    ]
    cache_weights = jnp.exp(cache_scores - peak_score)
    fresh_weights = jnp.exp(fresh_scores - peak_score)
    normaliser = jnp.sum(cache_weights, axis=-1, keepdims=True) + jnp.sum(
        fresh_weights, axis=-1, keepdims=True
    )
    cache_weights = (cache_weights / normaliser).astype(jnp.bfloat16)
    fresh_weights = (fresh_weights / normaliser).astype(jnp.bfloat16)
    mixture = jnp.einsum(
        "rskgc,rckd->rskgd", cache_weights, cached_values, preferred_element_type=jnp.float32
    )
    mixture = mixture + jnp.einsum(
        "rskgt,rtkd->rskgd", fresh_weights, fresh_values, preferred_element_type=jnp.float32
    )
    return mixture.reshape(row_count, step_count, query_width).astype(jnp.bfloat16)


def append(kv_rows, lengths, new_keys, new_values):
    capacity = kv_rows.shape[2]
    step_count = new_keys.shape[1]
    position = jnp.arange(capacity, dtype=jnp.int32)[None, :, None]
    live = position < lengths[:, None, None]
    stored_keys = jnp.where(live, kv_rows[:, 0], jnp.zeros((), jnp.bfloat16))
    stored_values = jnp.where(live, kv_rows[:, 1], jnp.zeros((), jnp.bfloat16))
    for step_index in range(step_count):
        landing = position == (lengths + step_index)[:, None, None]
        stored_keys = jnp.where(landing, new_keys[:, step_index][:, None, :], stored_keys)
        stored_values = jnp.where(landing, new_values[:, step_index][:, None, :], stored_values)
    return jnp.stack([stored_keys, stored_values], axis=1)


def outgoing_rows(payload, picked_row, has_peer):
    gathered_rows = jnp.take(payload, picked_row, axis=0)
    peer_mask = has_peer.reshape((-1,) + (1,) * (payload.ndim - 1))
    return jnp.where(peer_mask, gathered_rows, jnp.zeros((), payload.dtype))


def arrange_index(stays, slot_of, arrived_slot, row_count):
    targets = jnp.arange(row_count, dtype=jnp.int32)[:, None]
    local_ids = jnp.arange(row_count, dtype=jnp.int32)[None, :]
    remote_ids = row_count + jnp.arange(arrived_slot.shape[0], dtype=jnp.int32)[None, :]
    local_part = jnp.sum(
        jnp.where(stays[None, :] & (slot_of[None, :] == targets), local_ids, 0), axis=1
    )
    remote_part = jnp.sum(jnp.where(arrived_slot[None, :] == targets, remote_ids, 0), axis=1)
    return local_part + remote_part


def local(hidden_new, queries, kv_cache, lengths, destination, key_weight, value_weight, key_gain):
    step_count = queries.shape[0]
    row_count = lengths.shape[0]
    peer_count = lax.axis_size("inst")
    my_index = lax.axis_index("inst")
    hidden_flat = hidden_new.reshape(step_count * row_count, hidden_new.shape[2])
    key_part = jnp.dot(hidden_flat, key_weight, preferred_element_type=jnp.float32).reshape(
        step_count, row_count, -1
    )
    value_part = jnp.dot(hidden_flat, value_weight, preferred_element_type=jnp.float32).reshape(
        step_count, row_count, -1
    )
    key_sum, value_sum = (
        lax.psum_scatter(key_part, "tp", scatter_dimension=2, tiled=True),
        lax.psum_scatter(value_part, "tp", scatter_dimension=2, tiled=True),
    )
    positions = lengths[:, None] + jnp.arange(step_count, dtype=jnp.int32)[None, :]
    new_keys = place_keys(jnp.swapaxes(key_sum, 0, 1), key_gain, positions)
    new_values = jnp.swapaxes(value_sum, 0, 1).astype(jnp.bfloat16)
    fresh_rows = jnp.stack([new_keys, new_values], axis=1)
    query_rows = jnp.swapaxes(queries, 0, 1)
    target = destination // row_count
    slot_of = destination % row_count
    peer_ids = jnp.arange(peer_count, dtype=jnp.int32)
    outgoing = (target[None, :] == peer_ids[:, None]) & (target[None, :] != my_index)
    has_peer = jnp.any(outgoing, axis=1)
    picked_row = jnp.sum(
        jnp.where(outgoing, jnp.arange(row_count, dtype=jnp.int32)[None, :], 0), axis=1
    )
    sent_slot = jnp.where(has_peer, jnp.sum(jnp.where(outgoing, slot_of[None, :], 0), axis=1), -1)
    sent_length = jnp.sum(jnp.where(outgoing, lengths[None, :], 0), axis=1)
    stays = target == my_index
    got_cache, got_fresh, got_queries, got_slot, got_length = (
        lax.all_to_all(
            outgoing_rows(kv_cache, picked_row, has_peer),
            "inst",
            split_axis=0,
            concat_axis=0,
            tiled=True,
        ),
        lax.all_to_all(
            outgoing_rows(fresh_rows, picked_row, has_peer),
            "inst",
            split_axis=0,
            concat_axis=0,
            tiled=True,
        ),
        lax.all_to_all(
            outgoing_rows(query_rows, picked_row, has_peer),
            "inst",
            split_axis=0,
            concat_axis=0,
            tiled=True,
        ),
        lax.all_to_all(sent_slot, "inst", split_axis=0, concat_axis=0, tiled=True),
        lax.all_to_all(sent_length, "inst", split_axis=0, concat_axis=0, tiled=True),
    )
    source = arrange_index(stays, slot_of, got_slot, row_count)
    cache_here = jnp.take(jnp.concatenate([kv_cache, got_cache], axis=0), source, axis=0)
    fresh_here = jnp.take(jnp.concatenate([fresh_rows, got_fresh], axis=0), source, axis=0)
    length_here = jnp.take(jnp.concatenate([lengths, got_length], axis=0), source, axis=0)
    query_here = jnp.take(jnp.concatenate([query_rows, got_queries], axis=0), source, axis=0)
    attended_rows = attend(query_here, cache_here, length_here, fresh_here[:, 0], fresh_here[:, 1])
    moved_cache = append(cache_here, length_here, fresh_here[:, 0], fresh_here[:, 1])
    return (jnp.swapaxes(attended_rows, 0, 1), moved_cache)


def solution(mesh):
    return jax.shard_map(
        local,
        mesh=mesh,
        in_specs=(
            P(None, ("group", "inst"), "tp"),
            P(None, ("group", "inst"), "tp"),
            P(("group", "inst"), None, None, "tp"),
            P(("group", "inst")),
            P(("group", "inst")),
            P("tp", None),
            P("tp", None),
            P(),
        ),
        out_specs=(P(None, ("group", "inst"), "tp"), P(("group", "inst"), None, None, "tp")),
        check_vma=False,
    )
```

profile of v0, /device:TPU:0, one launch (start us, length us, event | category | flops | bytes accessed | tf_op | source)
XLA Modules:
  0.0 140.4 jit_solution(13952156415587023958)
XLA Ops:
  10.3 7.3 %all-to-all-start = ((s32[8,1,1]{2,1,0:T(1,128)}), s32[8,1,1]{2,1,0:T(1,128)S(1)}, u32[]{:S(2)}, u32[]{:S(2)}) async-start(s32[8,1,1]{2,1,0:T(1,128)} %copy.49), calls=%async_computation | async-start | bytes 8192 | tf_op jit(solution)/shard_map/all_to_all | solution.py:165
  17.6 2.2 %fusion.2 = f32[2,24,512]{2,1,0:T(8,128)} fusion(bf16[2,24,2560]{2,1,0:T(8,128)(2,1)} %param.8, bf16[2560,512]{1,0:T(8,128)(2,1)S(1)} %copy-done), kind=kOutput, calls=%fused_computation.12 | convolution fusion | flops 125829120 | bytes 2965504 | tf_op jit(solution)/shard_map/dot_general | solution.py:117
  19.9 3.0 %fusion = f32[2,24,512]{2,1,0:T(8,128)} fusion(bf16[2,24,2560]{2,1,0:T(8,128)(2,1)S(1)} %copy-done.1, bf16[2560,512]{1,0:T(8,128)(2,1)} %param.14), kind=kOutput, calls=%fused_computation.10 | convolution fusion | flops 125829120 | bytes 2965504 | tf_op jit(solution)/shard_map/dot_general | solution.py:120
  24.0 3.6 %gather_fusion = bf16[8,2,144,256]{3,2,1,0:T(8,128)(2,1)} fusion(bf16[24,2,144,256]{3,2,1,0:T(8,128)(2,1)} %param.10, s32[1024]{0:T(1024)S(1)} %pad_clamp_fusion.1), kind=kCustom, calls=%fused_computation | custom fusion | bytes 2359328 | tf_op jit(solution)/shard_map/jit(_take)/gather | solution.py:95
  28.3 2.5 %select_select_fusion.2 = bf16[8,2,144,256]{3,2,1,0:T(8,128)(2,1)} fusion(bf16[8,2,144,256]{3,2,1,0:T(8,128)(2,1)} %gather_fusion, pred[8]{0:T(512)(128)(4,1)S(1)} %compare_and_fusion, pred[8]{0:T(512)(128)(4,1)S(1)} %fusion.41), kind=kLoop, calls=%fused_computation.24 | loop fusion | flops 1179648 | bytes 2359312 | tf_op jit(solution)/shard_map/jit(_where)/select_n | solution.py:97
  31.8 6.0 %all-to-all-start.2 = ((s32[8,1,1]{2,1,0:T(1,128)}), s32[8,1,1]{2,1,0:T(1,128)S(1)}, u32[]{:S(2)}, u32[]{:S(2)}) async-start(s32[8,1,1]{2,1,0:T(1,128)} %copy.50), calls=%async_computation.2 | async-start | bytes 8192 | tf_op jit(solution)/shard_map/all_to_all | solution.py:166
  39.5 1.5 %reduce-scatter.5.cloned.1.call-done = f32[2,24,256]{2,1,0:T(8,128)} async-done(((f32[2,24,512]{2,1,0:T(8,128)}), f32[2,24,256]{2,1,0:T(8,128)}) %reduce-scatter.5.cloned.1.call-update) | async-done | bytes 49168 | tf_op jit(solution)/shard_map/reduce_scatter | solution.py:125
  42.4 1.8 %all-to-all-done.2 = s32[8,1,1]{2,1,0:T(1,128)S(1)} async-done(((s32[8,1,1]{2,1,0:T(1,128)}), s32[8,1,1]{2,1,0:T(1,128)S(1)}, u32[]{:S(2)}, u32[]{:S(2)}) %all-to-all-start.2) | async-done | bytes 64 | tf_op jit(solution)/shard_map/all_to_all | solution.py:166
  44.2 4.0 %all-to-all-start.3 = ((bf16[8,2,2048]{2,1,0:T(2,128)(2,1)}), bf16[8,2,2048]{2,1,0:T(2,128)(2,1)S(1)}, u32[]{:S(2)}, u32[]{:S(2)}) async-start(bf16[8,2,2048]{2,1,0:T(2,128)(2,1)} %broadcast_select_fusion.2), calls=%async_computation.3 | async-start | bytes 131072 | tf_op jit(solution)/shard_map/all_to_all | solution.py:158
  48.9 6.2 %all-to-all-done.3 = bf16[8,2,2048]{2,1,0:T(2,128)(2,1)S(1)} async-done(((bf16[8,2,2048]{2,1,0:T(2,128)(2,1)}), bf16[8,2,2048]{2,1,0:T(2,128)(2,1)S(1)}, u32[]{:S(2)}, u32[]{:S(2)}) %all-to-all-start.3) | async-done | bytes 65568 | tf_op jit(solution)/shard_map/all_to_all | solution.py:158
  55.1 3.3 %all-to-all-start.4 = ((bf16[8,2,2,256]{3,2,1,0:T(2,128)(2,1)}), bf16[8,2,2,256]{3,2,1,0:T(2,128)(2,1)S(1)}, u32[]{:S(2)}, u32[]{:S(2)}) async-start(bf16[8,2,2,256]{3,2,1,0:T(2,128)(2,1)} %broadcast_select_fusion.5), calls=%async_computation.6 | async-start | bytes 32768 | tf_op jit(solution)/shard_map/all_to_all | solution.py:151
  58.7 6.3 %all-to-all-done.4 = bf16[8,2,2,256]{3,2,1,0:T(2,128)(2,1)S(1)} async-done(((bf16[8,2,2,256]{3,2,1,0:T(2,128)(2,1)}), bf16[8,2,2,256]{3,2,1,0:T(2,128)(2,1)S(1)}, u32[]{:S(2)}, u32[]{:S(2)}) %all-to-all-start.4) | async-done | bytes 16416 | tf_op jit(solution)/shard_map/all_to_all | solution.py:151
  65.0 4.3 %all-to-all-start.1 = ((bf16[8,2,144,256]{3,2,1,0:T(8,128)(2,1)}), bf16[8,2,144,256]{3,2,1,0:T(8,128)(2,1)}, u32[]{:S(2)}, u32[]{:S(2)}) async-start(bf16[8,2,144,256]{3,2,1,0:T(8,128)(2,1)} %select_select_fusion.2), calls=%async_computation.1 | async-start | bytes 2359296 | tf_op jit(solution)/shard_map/all_to_all | solution.py:144
  72.7 1.7 %fusion.49 = (f32[24,2,2,8]{3,1,2,0:T(2,128)S(1)}, f32[24,2,2,8,2]{3,4,1,2,0:T(2,128)}) fusion(bf16[24,2,2,8,128]{4,3,2,1,0:T(8,128)(2,1)S(1)} %gather.35, pred[24]{0:T(512)(128)(4,1)S(1)} %get-tuple-element.7, bf16[24,2,2,256]{3,2,1,0:T(2,128)(2,1)S(1)} %broadcast_select_fusion.3, pred[2,2]{1,0:T(4,128)(4,1)S(1)} %iota_compare_fusion.6), kind=kOutput, calls=%fused_computation.111 | convolution fusion | flops 495360 | bytes 231424 | tf_op jit(solution)/shard_map/rskgd,rtkd->rskgt/dot_general | solution.py:51
  74.4 21.8 %all-to-all-done.1 = bf16[8,2,144,256]{3,2,1,0:T(8,128)(2,1)} async-done(((bf16[8,2,144,256]{3,2,1,0:T(8,128)(2,1)}), bf16[8,2,144,256]{3,2,1,0:T(8,128)(2,1)}, u32[]{:S(2)}, u32[]{:S(2)}) %all-to-all-start.1) | async-done | bytes 1179680 | tf_op jit(solution)/shard_map/all_to_all | solution.py:144
  96.2 4.9 %pad_maximum_fusion = bf16[32,2,144,256]{3,2,1,0:T(8,128)(2,1)} fusion(bf16[8,2,144,256]{3,2,1,0:T(8,128)(2,1)} %all-to-all-done.1, bf16[24,2,144,256]{3,2,1,0:T(8,128)(2,1)} %param.10), kind=kLoop, calls=%fused_computation.7 | loop fusion | flops 2359296 | bytes 9437184 | tf_op jit(solution)/shard_map/concatenate | solution.py:169
  101.1 5.0 %gather_fusion.1 = bf16[24,2,144,256]{3,2,1,0:T(8,128)(2,1)} fusion(bf16[32,2,144,256]{3,2,1,0:T(8,128)(2,1)} %pad_maximum_fusion, s32[1024]{0:T(1024)S(1)} %pad_clamp_fusion), kind=kCustom, calls=%fused_computation.1 | custom fusion | bytes 7077984 | tf_op jit(solution)/shard_map/jit(_take)/gather | solution.py:169
  106.1 2.4 %broadcast_select_fusion = bf16[24,2,144,256]{3,2,1,0:T(8,128)(2,1)S(1)} fusion(bf16[24,2,144,256]{3,2,1,0:T(8,128)(2,1)} %gather_fusion.1, pred[24]{0:T(512)(128)(4,1)S(1)} %get-tuple-element.7), kind=kLoop, calls=%fused_computation.9 | loop fusion | flops 1769472 | bytes 7077912 | tf_op jit(solution)/shard_map/jit(_take)/select_n | solution.py:169
  108.5 4.6 %select_select_fusion.1 = (bf16[24,1,144,256]{3,2,1,0:T(8,128)(2,1)}, bf16[24,1,144,256]{3,2,1,0:T(8,128)(2,1)}, bf16[24,1,144,256]{3,2,1,0:T(8,128)(2,1)}, bf16[24,1,144,256]{3,2,1,0:T(8,128)(2,1)}) fusion(pred[24,144]{1,0:T(8,128)(4,1)S(1)} %get-tuple-element.25, pred[24,144]{1,0:T(8,128)(4,1)S(1)} %get-tuple-element.24, ...), kind=kLoop, calls=%fused_computation.19 | loop fusion | flops 5308416 | bytes 10676352 | tf_op jit(solution)/shard_map/jit(_where)/select_n | solution.py:89
  113.1 4.5 %reshape_squeeze.13 = bf16[24,144,2,128]{3,2,1,0:T(2,128)(2,1)} reshape(bf16[24,1,144,256]{3,2,1,0:T(8,128)(2,1)} %get-tuple-element.12) | data formatting | bytes 3538944 | tf_op jit(solution)/shard_map/reshape;squeeze | solution.py:41
  117.6 2.7 %fusion.48 = (f32[24,2,2,8]{3,1,2,0:T(2,128)S(1)}, f32[24,2,2,8,144]{4,3,1,2,0:T(8,128)S(1)}) fusion(bf16[24,2,2,8,128]{4,3,2,1,0:T(8,128)(2,1)} %copy-done.3, pred[24]{0:T(512)(128)(4,1)S(1)} %get-tuple-element.7, bf16[24,144,2,128,1]{3,2,1,0,4:T(2,128)(2,1)} %bitcast.82, pred[24,144]{1,0:T(8,128)(4,1)S(1)} %get-tuple-element.25), kind=kOutput, calls=%fused_computation.110 | convolution fusion | flops 28740864 | bytes 2415000 | tf_op jit(solution)/shard_map/rskgd,rckd->rskgc/dot_general | solution.py:47
  122.0 4.5 %reshape_squeeze.12 = bf16[24,144,2,128]{3,2,1,0:T(2,128)(2,1)} reshape(bf16[24,1,144,256]{3,2,1,0:T(8,128)(2,1)} %get-tuple-element.13) | data formatting | bytes 3538944 | tf_op jit(solution)/shard_map/reshape;squeeze | solution.py:42
  126.5 2.2 %fusion.23 = bf16[24,2,2,8,128]{4,3,1,2,0:T(8,128)(2,1)S(1)} fusion(f32[24,2,128,2,8]{2,4,3,1,0:T(8,128)} %fusion.32, bf16[24,144,2,128,1]{3,2,1,0,4:T(2,128)(2,1)} %bitcast.83, f32[24,2,2,8,144]{4,3,1,2,0:T(8,128)S(1)} %get-tuple-element.27, f32[24,2,2,8]{3,1,2,0:T(2,128)S(1)} %add.160, f32[24,2,2,8]{3,1,2,0:T(2,128)S(1)} %max.7), kind=kOutput, calls=%fused_computation.26 | convolution fusion | flops 28839936 | bytes 2807808 | tf_op jit(solution)/shard_map/rskgc,rckd->rskgd/dot_general | solution.py:71
  129.4 4.1 %pad_maximum_fusion.1 = bf16[24,2,144,256]{3,2,1,0:T(8,128)(2,1)} fusion(bf16[24,1,144,256]{3,2,1,0:T(8,128)(2,1)} %get-tuple-element.11, bf16[24,1,144,256]{3,2,1,0:T(8,128)(2,1)} %get-tuple-element.10), kind=kLoop, calls=%fused_computation.8 | loop fusion | flops 1769472 | bytes 7077888 | tf_op jit(solution)/shard_map/stack | solution.py:91
  (84 shorter events, 15.8 us)
Async XLA Ops:
  7.2 10.5 %copy-start = (bf16[2560,512]{1,0:T(8,128)(2,1)S(1)}, bf16[2560,512]{1,0:T(8,128)(2,1)}, u32[]{:S(2)}) copy-start(bf16[2560,512]{1,0:T(8,128)(2,1)} %param.13) | copy-start | bytes 7864324
  10.3 21.5 %all-to-all-start = ((s32[8,1,1]{2,1,0:T(1,128)}), s32[8,1,1]{2,1,0:T(1,128)S(1)}, u32[]{:S(2)}, u32[]{:S(2)}) async-start(s32[8,1,1]{2,1,0:T(1,128)} %copy.49), calls=%async_computation | async-start | bytes 8192 | tf_op jit(solution)/shard_map/all_to_all | solution.py:165
  17.6 2.3 %copy-start.1 = (bf16[2,24,2560]{2,1,0:T(8,128)(2,1)S(1)}, bf16[2,24,2560]{2,1,0:T(8,128)(2,1)}, u32[]{:S(2)}) copy-start(bf16[2,24,2560]{2,1,0:T(8,128)(2,1)} %param.8) | copy-start | bytes 737284
  17.6 20.5 %reduce-scatter.3.cloned.1.call-start = ((), (), s32[]{:S(2)}) async-start(), calls=%async_computation.7 | async-start | bytes 147456 | tf_op jit(solution)/shard_map/reduce_scatter | solution.py:124
  19.8 3.1 %copy-start.5 = (s32[24]{0:T(128)S(1)}, s32[24]{0:T(128)}, u32[]{:S(2)}) copy-start(s32[24]{0:T(128)} %param.11) | copy-start | bytes 292
  19.9 4.0 %copy-start.2 = (bf16[2,24,2048]{2,1,0:T(8,128)(2,1)S(1)}, bf16[2,24,2048]{2,1,0:T(8,128)(2,1)}, u32[]{:S(2)}) copy-start(bf16[2,24,2048]{2,1,0:T(8,128)(2,1)} %param.9) | copy-start | bytes 589828
  19.9 21.1 %reduce-scatter.5.cloned.1.call-start = ((), (), s32[]{:S(2)}) async-start(), calls=%async_computation.8 | async-start | bytes 147456 | tf_op jit(solution)/shard_map/reduce_scatter | solution.py:125
  27.7 4.1 %copy-start.6 = (bf16[128]{0:T(256)(128)(2,1)S(1)}, bf16[128]{0:T(256)(128)(2,1)}, u32[]{:S(2)}) copy-start(bf16[128]{0:T(256)(128)(2,1)} %param.15) | copy-start | bytes 772
  31.8 12.4 %all-to-all-start.2 = ((s32[8,1,1]{2,1,0:T(1,128)}), s32[8,1,1]{2,1,0:T(1,128)S(1)}, u32[]{:S(2)}, u32[]{:S(2)}) async-start(s32[8,1,1]{2,1,0:T(1,128)} %copy.50), calls=%async_computation.2 | async-start | bytes 8192 | tf_op jit(solution)/shard_map/all_to_all | solution.py:166
  44.2 10.9 %all-to-all-start.3 = ((bf16[8,2,2048]{2,1,0:T(2,128)(2,1)}), bf16[8,2,2048]{2,1,0:T(2,128)(2,1)S(1)}, u32[]{:S(2)}, u32[]{:S(2)}) async-start(bf16[8,2,2048]{2,1,0:T(2,128)(2,1)} %broadcast_select_fusion.2), calls=%async_computation.3 | async-start | bytes 131072 | tf_op jit(solution)/shard_map/all_to_all | solution.py:158
  55.1 9.9 %all-to-all-start.4 = ((bf16[8,2,2,256]{3,2,1,0:T(2,128)(2,1)}), bf16[8,2,2,256]{3,2,1,0:T(2,128)(2,1)S(1)}, u32[]{:S(2)}, u32[]{:S(2)}) async-start(bf16[8,2,2,256]{3,2,1,0:T(2,128)(2,1)} %broadcast_select_fusion.5), calls=%async_computation.6 | async-start | bytes 32768 | tf_op jit(solution)/shard_map/all_to_all | solution.py:151
  65.0 31.2 %all-to-all-start.1 = ((bf16[8,2,144,256]{3,2,1,0:T(8,128)(2,1)}), bf16[8,2,144,256]{3,2,1,0:T(8,128)(2,1)}, u32[]{:S(2)}, u32[]{:S(2)}) async-start(bf16[8,2,144,256]{3,2,1,0:T(8,128)(2,1)} %select_select_fusion.2), calls=%async_computation.1 | async-start | bytes 2359296 | tf_op jit(solution)/shard_map/all_to_all | solution.py:144
  71.6 29.4 %copy-start.3 = (bf16[24,2,2,8,128]{4,3,2,1,0:T(8,128)(2,1)}, bf16[24,2,2,8,128]{4,3,2,1,0:T(8,128)(2,1)S(1)}, u32[]{:S(2)}) copy-start(bf16[24,2,2,8,128]{4,3,2,1,0:T(8,128)(2,1)S(1)} %gather.35) | copy-start | bytes 589828
  117.6 2.7 %copy-start.4 = (f32[24,2,2,8,2]{3,4,1,2,0:T(2,128)S(1)}, f32[24,2,2,8,2]{3,4,1,2,0:T(2,128)}, u32[]{:S(2)}) copy-start(f32[24,2,2,8,2]{3,4,1,2,0:T(2,128)} %get-tuple-element.29) | copy-start | bytes 18436
Sparse Core Ops, SparseCore 0:
  20.6 8.8 reduce-scatter.2
  32.3 8.6 reduce-scatter.4
where the time goes:
time: 141 us; the launch traced here: 140 us
  waiting for transfers between devices  37.6 us (27%)
  other arithmetic  26 us (18%)
  starting transfers between devices  24.9 us (18%)
  local copies, waits for them, and re-layouts  24.8 us (18%)
  between operations  14.4 us (10%)
  matrix products  12.7 us (9%)
    all_to_all x1, waiting for transfers between devices, local(): lax.all_to_all(outgoing_rows(kv_cache, picked_row, has_peer), 'inst', spl...  21.8 us
    all_to_all x1, starting transfers between devices, local(): lax.all_to_all(sent_slot, 'inst', split_axis=0, concat_axis=0, tiled=True)  7.28 us
    all_to_all x1, waiting for transfers between devices, local(): lax.all_to_all(outgoing_rows(fresh_rows, picked_row, has_peer), 'inst', s...  6.26 us
    all_to_all x1, waiting for transfers between devices, local(): lax.all_to_all(outgoing_rows(query_rows, picked_row, has_peer), 'inst', s...  6.2 us
    all_to_all x1, starting transfers between devices, local(): lax.all_to_all(sent_length, 'inst', split_axis=0, concat_axis=0, tiled=True)  5.97 us
    gather x1, local copies, waits for them, and re-layouts, local(): jnp.take(jnp.concatenate([kv_cache, got_cache], axis=0), source, axis=0)  5.02 us
    gather x3, local copies, waits for them, and re-layouts, outgoing_rows(): gathered_rows = jnp.take(payload, picked_row, axis=0)  4.91 us
    concatenate x1, other arithmetic, local(): jnp.concatenate([kv_cache, got_cache], axis=0)  4.89 us
  transfers between devices with their start and end apart: 7, of which 5 were waited for; matrix products, arithmetic and copies ran while one was open for 16% of the time, Pallas kernels for 0%

commit v1 on v0

v1 whole, which is shorter than its diff:
```python
import functools
import math

import jax
import jax.numpy as jnp
from jax import lax
from jax.experimental import pallas as pl
from jax.experimental.pallas import tpu as pltpu
from jax.sharding import PartitionSpec as P

HD = 128
ROPE_BASE = 1000000.0
NORM_EPS = 1e-06
VMEM_LIMIT = 48 * 1024 * 1024


def peer_after(index, shift, count):
    if count & (count - 1) == 0:
        return index ^ shift
    return (index + shift) % count


def peer_before(index, shift, count):
    if count & (count - 1) == 0:
        return index ^ shift
    return (index + count - shift) % count


def pack_kernel(count, dest_ref, kv_ref, *refs):
    outs, pick_ref, sems = refs[: count - 1], refs[count - 1], refs[count]
    rows = dest_ref.shape[0]
    me = lax.axis_index("inst")
    for peer in range(count):
        pick_ref[peer] = 0

    def note(row, carry):
        pick_ref[dest_ref[row] // rows] = row
        return carry

    lax.fori_loop(0, rows, note, 0)
    copies = []
    for shift in range(1, count):
        row = pick_ref[peer_after(me, shift, count)]
        copy = pltpu.make_async_copy(kv_ref.at[row], outs[shift - 1], sems.at[shift - 1])
        copy.start()
        copies.append(copy)
    for copy in copies:
        copy.wait()


def pack(kv_cache, destination, count):
    block = jax.ShapeDtypeStruct(kv_cache.shape[1:], kv_cache.dtype)
    smem = pl.BlockSpec(memory_space=pltpu.SMEM)
    hbm = pl.BlockSpec(memory_space=pl.ANY)
    outs = pl.pallas_call(
        functools.partial(pack_kernel, count),
        out_shape=[block] * (count - 1) + [jax.ShapeDtypeStruct((count,), jnp.int32)],
        in_specs=[smem, hbm],
        out_specs=[hbm] * (count - 1) + [smem],
        scratch_shapes=[pltpu.SemaphoreType.DMA((count - 1,))],
        name="pack",
    )(destination, kv_cache)
    return outs[:-1], outs[-1]


def project_kernel(hidden_ref, key_ref, value_ref, own_ref, other_ref, total):
    step = pl.program_id(0)
    width = key_ref.shape[1]

    @pl.when(step == 0)
    def _():
        total[...] = jnp.zeros_like(total)

    steps, rows, depth = hidden_ref.shape
    hidden = hidden_ref[...].reshape(steps * rows, depth)
    total[:, :width] += jnp.dot(hidden, key_ref[...], preferred_element_type=jnp.float32)
    total[:, width:] += jnp.dot(hidden, value_ref[...], preferred_element_type=jnp.float32)

    @pl.when(step == pl.num_programs(0) - 1)
    def _():
        half = width // 2
        me = lax.axis_index("tp")
        for ref, core in ((own_ref, me), (other_ref, 1 - me)):
            at = pl.multiple_of(core * half, half)
            ref[:, :half] = total[:, pl.ds(at, half)]
            ref[:, half:] = total[:, pl.ds(pl.multiple_of(width + at, half), half)]


def project(hidden_new, key_weight, value_weight):
    steps, rows, depth = hidden_new.shape
    width = key_weight.shape[1]
    part = depth // 5
    shape = jax.ShapeDtypeStruct((steps * rows, width), jnp.float32)
    whole = pl.BlockSpec((steps * rows, width), lambda i: (0, 0))
    return pl.pallas_call(
        project_kernel,
        grid=(depth // part,),
        out_shape=[shape, shape],
        in_specs=[
            pl.BlockSpec((steps, rows, part), lambda i: (0, 0, i)),
            pl.BlockSpec((part, width), lambda i: (i, 0)),
            pl.BlockSpec((part, width), lambda i: (i, 0)),
        ],
        out_specs=[whole, whole],
        scratch_shapes=[pltpu.VMEM((steps * rows, 2 * width), jnp.float32)],
        compiler_params=pltpu.CompilerParams(vmem_limit_bytes=VMEM_LIMIT),
        cost_estimate=pl.CostEstimate(
            flops=4 * steps * rows * depth * width,
            bytes_accessed=4 * depth * width,
            transcendentals=0,
        ),
        name="project",
    )(hidden_new, key_weight, value_weight)


def attend_kernel(
    count,
    block,
    length_ref,
    pick_ref,
    own_ref,
    got_ref,
    gain_ref,
    cos_ref,
    sin_ref,
    query_ref,
    kv_ref,
    moved_ref,
    mixed_ref,
    *refs,
):
    small_refs, (fresh, query_rows, mixed) = refs[: count - 1], refs[count - 1 :]
    part = pl.program_id(0)
    steps, rows, query_width = query_ref.shape
    capacity, lanes = kv_ref.shape[2:]
    heads = lanes // HD
    group = query_width // lanes
    per_head = steps * group
    per_row = heads * per_head

    def place(step, head, member):
        return head * per_head + step * group + member

    def spot(head, member):
        return slice((head * group + member) * HD, (head * group + member + 1) * HD)

    @pl.when(part == 0)
    def _():
        raw = own_ref[...] + got_ref[...]
        gain = gain_ref[...].astype(jnp.float32)
        for head in range(heads):
            at = slice(head * HD, (head + 1) * HD)
            piece = raw[:, at]
            mean = jnp.mean(piece * piece, axis=-1, keepdims=True)
            piece = piece * lax.rsqrt(mean + NORM_EPS) * gain
            swapped = jnp.concatenate([piece[:, HD // 2 :], piece[:, : HD // 2]], axis=1)
            turned = piece * cos_ref[...] + swapped * sin_ref[...]
            fresh[0, :, at] = turned.astype(jnp.bfloat16).astype(jnp.float32)
        fresh[1] = raw[:, lanes:].astype(jnp.bfloat16).astype(jnp.float32)
        for step in range(steps):
            for head in range(heads):
                for member in range(group):
                    query_rows[pl.ds(place(step, head, member), rows, stride=per_row), :] = (
                        query_ref[step, :, spot(head, member)].astype(jnp.float32)
                    )

    position = lax.broadcasted_iota(jnp.int32, (capacity, lanes), 0)
    lane_head = lax.broadcasted_iota(jnp.int32, (per_row, lanes), 1) // HD
    row_head = lax.broadcasted_iota(jnp.int32, (per_row, lanes), 0) // per_head
    column = lax.broadcasted_iota(jnp.int32, (per_row, capacity), 1)
    row_step = (lax.broadcasted_iota(jnp.int32, (per_row, capacity), 0) % per_head) // group
    factor = 1.0 / math.sqrt(HD)
    scores = []
    for item in range(block):
        row = part * block + item
        length = length_ref[row]
        for which in range(2):
            stored = jnp.where(position < length, kv_ref[item, which].astype(jnp.float32), 0.0)
            for step in range(steps):
                new = fresh[which, pl.ds(step * rows + row, 1), :]
                stored = jnp.where(position == length + step, new, stored)
            moved_ref[item, which] = stored.astype(jnp.bfloat16)
        query = query_rows[pl.ds(pl.multiple_of(row * per_row, per_row), per_row), :]
        query = jnp.where(lane_head == row_head, jnp.concatenate([query] * heads, axis=1), 0.0)
        score = lax.dot_general(
            query.astype(jnp.bfloat16),
            moved_ref[item, 0],
            (((1,), (1,)), ((), ())),
            preferred_element_type=jnp.float32,
        )
        scores.append(jnp.where(column <= length + row_step, score * factor, -jnp.inf))
    weights = []
    for score in scores:
        raised = jnp.exp(score - jnp.max(score, axis=-1, keepdims=True))
        normaliser = jnp.sum(raised, axis=-1, keepdims=True)
        weights.append((raised / normaliser).astype(jnp.bfloat16))
    for item in range(block):
        row = part * block + item
        result = jnp.dot(weights[item], moved_ref[item, 1], preferred_element_type=jnp.float32)
        for head in range(heads):
            mixed[pl.ds(pl.multiple_of(row * per_row + head * per_head, per_head), per_head), :] = (
                result[head * per_head : (head + 1) * per_head, head * HD : (head + 1) * HD]
            )

    @pl.when(part == pl.num_programs(0) - 1)
    def _():
        mixed_ref[...] = mixed[...].astype(jnp.bfloat16)
        me = lax.axis_index("inst")
        for shift in range(1, count):
            row = pick_ref[peer_after(me, shift, count)]
            small = small_refs[shift - 1]
            small[:per_row, :] = mixed[
                pl.ds(pl.multiple_of(row * per_row, per_row), per_row), :
            ].astype(jnp.bfloat16)
            news = []
            for which in range(2):
                for step in range(steps):
                    new = fresh[which, pl.ds(step * rows + row, 1), :]
                    news += [new[:, h * HD : (h + 1) * HD] for h in range(heads)]
            fill = small.shape[0] - per_row - len(news)
            news.append(jnp.zeros((fill, HD), jnp.float32))
            small[per_row:, :] = jnp.concatenate(news, axis=0).astype(jnp.bfloat16)


def attend(kv_cache, queries, own, got, gain, cosine, sine, lengths, pick, count):
    steps, rows, query_width = queries.shape
    capacity, lanes = kv_cache.shape[2:]
    heads = lanes // HD
    per_row = steps * query_width // HD
    block = 4
    small_rows = -(-(per_row + 2 * steps * heads) // 16) * 16
    small = jax.ShapeDtypeStruct((small_rows, HD), jnp.bfloat16)
    smem = pl.BlockSpec(memory_space=pltpu.SMEM)
    vmem = pl.BlockSpec(memory_space=pltpu.VMEM)
    cache_block = pl.BlockSpec((block, 2, capacity, lanes), lambda i: (i, 0, 0, 0))
    outs = pl.pallas_call(
        functools.partial(attend_kernel, count, block),
        grid=(rows // block,),
        out_shape=[
            jax.ShapeDtypeStruct(kv_cache.shape, kv_cache.dtype),
            jax.ShapeDtypeStruct((rows * per_row, HD), jnp.bfloat16),
        ]
        + [small] * (count - 1),
        in_specs=[smem, smem, vmem, vmem, vmem, vmem, vmem, vmem, cache_block],
        out_specs=[cache_block, vmem] + [vmem] * (count - 1),
        scratch_shapes=[
            pltpu.VMEM((2, steps * rows, lanes), jnp.float32),
            pltpu.VMEM((rows * per_row, HD), jnp.float32),
            pltpu.VMEM((rows * per_row, HD), jnp.float32),
        ],
        compiler_params=pltpu.CompilerParams(vmem_limit_bytes=VMEM_LIMIT),
        cost_estimate=pl.CostEstimate(
            flops=4 * rows * per_row * capacity * lanes,
            bytes_accessed=4 * kv_cache.size,
            transcendentals=rows * per_row * capacity,
        ),
        name="attend",
    )(lengths, pick, own, got, gain, cosine, sine, queries, kv_cache)
    return outs[0], outs[1], outs[2:]


def settle_kernel(count, shape, group, facts_ref, mixed_ref, *refs):
    small_refs = refs[: count - 1]
    out_ref, slot_ref, length_ref, mixed = refs[count - 1 :]
    steps, rows, query_width = shape
    per_row = steps * query_width // HD
    me = lax.axis_index("inst")
    mixed[...] = mixed_ref[...].astype(jnp.float32)
    slot_ref[0] = -1
    length_ref[0] = 0
    for shift in range(1, count):
        peer = peer_before(me, shift, count)
        slot_ref[shift] = -1
        length_ref[shift] = 0

        def look(row, carry):
            slot = facts_ref[peer, 0, row] - me * rows

            @pl.when((slot >= 0) & (slot < rows))
            def _():
                slot_ref[shift] = slot
                length_ref[shift] = facts_ref[peer, 1, row]

            return carry

        lax.fori_loop(0, rows, look, 0)
        slot = slot_ref[shift]

        @pl.when(slot >= 0)
        def _():
            mixed[pl.ds(pl.multiple_of(slot * per_row, per_row), per_row), :] = small_refs[
                shift - 1
            ][:per_row, :].astype(jnp.float32)

    for step in range(steps):
        for chunk in range(query_width // HD):
            head, member = chunk // group, chunk % group
            at = head * steps * group + step * group + member
            out_ref[step, :, chunk * HD : (chunk + 1) * HD] = mixed[
                pl.ds(at, rows, stride=per_row), :
            ].astype(jnp.bfloat16)


def settle(facts, mixed, smalls, shape, group, count):
    steps, rows, query_width = shape
    smem = pl.BlockSpec(memory_space=pltpu.SMEM)
    vmem = pl.BlockSpec(memory_space=pltpu.VMEM)
    scalars = jax.ShapeDtypeStruct((count,), jnp.int32)
    return pl.pallas_call(
        functools.partial(settle_kernel, count, shape, group),
        out_shape=[jax.ShapeDtypeStruct(shape, jnp.bfloat16), scalars, scalars],
        in_specs=[smem, vmem] + [vmem] * (count - 1),
        out_specs=[vmem, smem, smem],
        scratch_shapes=[pltpu.VMEM(mixed.shape, jnp.float32)],
        compiler_params=pltpu.CompilerParams(vmem_limit_bytes=VMEM_LIMIT),
        name="settle",
    )(facts, mixed, *smalls)


def land_kernel(count, steps, slot_ref, length_ref, *refs):
    cache_refs = refs[: count - 1]
    small_refs = refs[count - 1 : 2 * (count - 1)]
    _, out_ref, buffer, in_sems, out_sems = refs[2 * (count - 1) :]
    capacity, lanes = buffer.shape[2:]
    heads = lanes // HD
    position = lax.broadcasted_iota(jnp.int32, (capacity, lanes), 0)

    def fetch(shift):
        return pltpu.make_async_copy(
            cache_refs[shift - 1], buffer.at[shift - 1], in_sems.at[shift - 1]
        )

    def store(shift):
        slot = jnp.maximum(slot_ref[shift], 0)
        return pltpu.make_async_copy(
            buffer.at[shift - 1], out_ref.at[slot], out_sems.at[shift - 1]
        )

    for shift in range(1, count):
        fetch(shift).start()
    for shift in range(1, count):
        fetch(shift).wait()

        @pl.when(slot_ref[shift] >= 0)
        def _():
            length = length_ref[shift]
            small = small_refs[shift - 1]
            news = small[small.shape[0] - 16 :, :].astype(jnp.float32)
            for which in range(2):
                stored = buffer[shift - 1, which].astype(jnp.float32)
                stored = jnp.where(position < length, stored, 0.0)
                for step in range(steps):
                    at = (which * steps + step) * heads
                    new = jnp.concatenate([news[at + h : at + h + 1] for h in range(heads)], axis=1)
                    stored = jnp.where(position == length + step, new, stored)
                buffer[shift - 1, which] = stored.astype(jnp.bfloat16)
            store(shift).start()

    for shift in range(1, count):

        @pl.when(slot_ref[shift] >= 0)
        def _():
            store(shift).wait()


def land(slots, lengths, caches, smalls, moved, steps, count):
    smem = pl.BlockSpec(memory_space=pltpu.SMEM)
    vmem = pl.BlockSpec(memory_space=pltpu.VMEM)
    hbm = pl.BlockSpec(memory_space=pl.ANY)
    return pl.pallas_call(
        functools.partial(land_kernel, count, steps),
        out_shape=jax.ShapeDtypeStruct(moved.shape, moved.dtype),
        in_specs=[smem, smem] + [hbm] * (count - 1) + [vmem] * (count - 1) + [hbm],
        out_specs=hbm,
        scratch_shapes=[
            pltpu.VMEM((count - 1,) + moved.shape[1:], moved.dtype),
            pltpu.SemaphoreType.DMA((count - 1,)),
            pltpu.SemaphoreType.DMA((count - 1,)),
        ],
        input_output_aliases={2 + 2 * (count - 1): 0},
        compiler_params=pltpu.CompilerParams(vmem_limit_bytes=VMEM_LIMIT),
        name="land",
    )(slots, lengths, *caches, *smalls, moved)


def rotation(lengths, steps):
    half = HD // 2
    inverse = jnp.exp(-math.log(ROPE_BASE) * 2.0 * jnp.arange(half, dtype=jnp.float32) / HD)
    positions = (lengths[None, :] + jnp.arange(steps, dtype=jnp.int32)[:, None]).reshape(-1)
    angles = positions.astype(jnp.float32)[:, None] * inverse
    cosine, sine = jnp.cos(angles), jnp.sin(angles)
    return jnp.concatenate([cosine, cosine], axis=1), jnp.concatenate([-sine, sine], axis=1)


def local(hidden_new, queries, kv_cache, lengths, destination, key_weight, value_weight, key_gain):
    steps = queries.shape[0]
    group = queries.shape[2] // kv_cache.shape[3]
    count = lax.axis_size("inst")

    def exchange(block, shift):
        pairs = [(i, peer_after(i, shift, count)) for i in range(count)]
        return lax.ppermute(block, "inst", pairs)

    blocks, pick = pack(kv_cache, destination, count)
    order = range(count - 1, 0, -1)
    arriving = {shift: exchange(blocks[shift - 1], shift) for shift in order}
    facts = lax.all_gather(jnp.stack([destination, lengths]), "inst")
    own, other = project(hidden_new, key_weight, value_weight)
    got = lax.ppermute(other, "tp", [(0, 1), (1, 0)])
    cosine, sine = rotation(lengths, steps)
    moved, mixed, smalls = attend(
        kv_cache, queries, own, got, key_gain[None, :], cosine, sine, lengths, pick, count
    )
    small_arriving = {shift: exchange(smalls[shift - 1], shift) for shift in order}
    small_list = [small_arriving[shift] for shift in range(1, count)]
    attended, slots, arrived_lengths = settle(
        facts, mixed, small_list, queries.shape, group, count
    )
    moved = land(
        slots,
        arrived_lengths,
        [arriving[shift] for shift in range(1, count)],
        small_list,
        moved,
        steps,
        count,
    )
    return attended, moved


def solution(mesh):
    return jax.shard_map(
        local,
        mesh=mesh,
        in_specs=(
            P(None, ("group", "inst"), "tp"),
            P(None, ("group", "inst"), "tp"),
            P(("group", "inst"), None, None, "tp"),
            P(("group", "inst")),
            P(("group", "inst")),
            P("tp", None),
            P("tp", None),
            P(),
        ),
        out_specs=(P(None, ("group", "inst"), "tp"), P(("group", "inst"), None, None, "tp")),
        check_vma=False,
    )
```

time: 141 us -> 112 us (0.79)
  the two profiles are of different devices: /device:TPU:0 before, /device:TPU:8 now
where the time goes in v1:
time: 112 us
  Pallas kernels  49.6 us (44%)
  blocking collectives  27.3 us (24%)
  starting transfers between devices  22.2 us (20%)
  local copies, waits for them, and re-layouts  9.01 us (8%)
  other arithmetic  1.56 us (1%)
    pallas_call x1, Pallas kernels, pack(): pl.pallas_call(functools.partial(pack_kernel, count), out_shape=[block] *...  34.2 us
    all_gather x1, blocking collectives, local(): facts = lax.all_gather(jnp.stack([destination, lengths]), 'inst')  27.3 us
    ppermute x14, starting transfers between devices, exchange(): return lax.ppermute(block, 'inst', pairs)  22.2 us
    unnamed x32, local copies, waits for them, and re-layouts  7.69 us
    pallas_call x1, Pallas kernels, attend(): pl.pallas_call(functools.partial(attend_kernel, count, block), grid=(rows...  6.52 us
    pallas_call x1, Pallas kernels, settle(): pl.pallas_call(functools.partial(settle_kernel, count, shape, group), out...  3.77 us
    pallas_call x1, Pallas kernels, land(): pl.pallas_call(functools.partial(land_kernel, count, steps), out_shape=ja...  2.86 us
  transfers between devices with their start and end apart: 15, of which 2 were waited for; matrix products, arithmetic and copies ran while one was open for 3% of the time, Pallas kernels for 40%

profile of v1, /device:TPU:8, one launch (start us, length us, event | category | flops | bytes accessed | tf_op | source)
XLA Modules:
  0.0 111.5 jit_solution(17132653881979960725)
XLA Ops:
  0.7 1.9 %copy-done.1 = bf16[2560,512]{1,0:T(8,128)(2,1)S(1)} copy-done((bf16[2560,512]{1,0:T(8,128)(2,1)S(1)}, bf16[2560,512]{1,0:T(8,128)(2,1)}, u32[]{:S(2)}) %copy-start.1) | copy-done | bytes 2621464
  2.5 1.7 %copy-done.2 = bf16[2560,512]{1,0:T(8,128)(2,1)S(1)} copy-done((bf16[2560,512]{1,0:T(8,128)(2,1)S(1)}, bf16[2560,512]{1,0:T(8,128)(2,1)}, u32[]{:S(2)}) %copy-start.2) | copy-done | bytes 2621464
  4.3 0.9 copy-done.3
  5.2 2.2 %project.1 = (f32[48,512]{1,0:T(8,128)S(1)}, f32[48,512]{1,0:T(8,128)}) custom-call(bf16[2,24,2560]{2,1,0:T(8,128)(2,1)S(1)} %copy-done.3, bf16[2560,512]{1,0:T(8,128)(2,1)S(1)} %copy-done.1, bf16[2560,512]{1,0:T(8,128)(2,1)S(1)} %copy-done.2), custom_call_target="tpu_custom_call" | custom-call | flops 251658240 | bytes 5242880 | tf_op jit(solution)/shard_map/project/pallas_call | solution.py:95
  8.1 34.2 %pack.1 = (bf16[2,144,256]{2,1,0:T(8,128)(2,1)}, bf16[2,144,256]{2,1,0:T(8,128)(2,1)}, bf16[2,144,256]{2,1,0:T(8,128)(2,1)}, bf16[2,144,256]{2,1,0:T(8,128)(2,1)...) custom-call(s32[24]{0:T(128)} %dest_ref.1, ...), custom_call_target="tpu_custom_call" | custom-call | tf_op jit(solution)/shard_map/pack/pallas_call | solution.py:55
  42.3 1.6 %collective-permute-start.8 = (bf16[2,144,256]{2,1,0:T(8,128)(2,1)}, bf16[2,144,256]{2,1,0:T(8,128)(2,1)}, u32[]{:S(2)}, u32[]{:S(2)}) collective-permute-start(bf16[2,144,256]{2,1,0:T(8,128)(2,1)} %get-tuple-element.38), channel_id=1, source_target_pairs={{0,2},{2,0},{4,6},{6,4},{8,10},{10,8},{12,14},{14,12},{1,3},{3,1},... | collective-permute-start | bytes 442376 | tf_op jit(solution)/shard_map/ppermute | solution.py:402
  45.0 1.3 %convert_element_type.11 = f32[48]{0:T(128)} reshape(f32[2,24]{1,0:T(2,128)} %add_convert_fusion) | data formatting | bytes 384 | tf_op jit(solution)/shard_map/convert_element_type | solution.py:390
  46.3 0.9 fusion
  47.3 0.9 copy-done.4
  48.2 0.9 copy-done.6
  49.8 6.5 %attend.1 = (bf16[24,2,144,256]{3,2,1,0:T(8,128)(2,1)}, bf16[768,128]{1,0:T(8,128)(2,1)S(1)}, bf16[48,128]{1,0:T(8,128)(2,1)S(1)}, bf16[48,128]{1,0:T(8,128)(2,1...) custom-call(s32[24]{0:T(128)S(1)} %copy-done.7, ...), custom_call_target="tpu_custom_call" | custom-call | flops 113246208 | bytes 7077888 | tf_op jit(solution)/shard_map/attend/pallas_call | solution.py:236
  56.4 2.0 %collective-permute-start.2 = (bf16[48,128]{1,0:T(8,128)(2,1)S(1)}, bf16[48,128]{1,0:T(8,128)(2,1)S(1)}, u32[]{:S(2)}, u32[]{:S(2)}) collective-permute-start(bf16[48,128]{1,0:T(8,128)(2,1)S(1)} %get-tuple-element.29), channel_id=1, source_target_pairs={{0,4},{2,6},{4,0},{6,2},{8,12},{10,14},{12,8},{14,10},{1,5},{3,7},... | collective-permute-start | bytes 36872 | tf_op jit(solution)/shard_map/ppermute | solution.py:402
  58.4 1.4 %collective-permute-start.3 = (bf16[48,128]{1,0:T(8,128)(2,1)S(1)}, bf16[48,128]{1,0:T(8,128)(2,1)S(1)}, u32[]{:S(2)}, u32[]{:S(2)}) collective-permute-start(bf16[48,128]{1,0:T(8,128)(2,1)S(1)} %get-tuple-element.30), channel_id=1, source_target_pairs={{0,6},{2,4},{4,2},{6,0},{8,14},{10,12},{12,10},{14,8},{1,7},{3,5},... | collective-permute-start | bytes 36872 | tf_op jit(solution)/shard_map/ppermute | solution.py:402
  60.0 2.6 %collective-permute-start.4 = (bf16[48,128]{1,0:T(8,128)(2,1)S(1)}, bf16[48,128]{1,0:T(8,128)(2,1)S(1)}, u32[]{:S(2)}, u32[]{:S(2)}) collective-permute-start(bf16[48,128]{1,0:T(8,128)(2,1)S(1)} %get-tuple-element.31), channel_id=1, source_target_pairs={{0,8},{2,10},{4,12},{6,14},{8,0},{10,2},{12,4},{14,6},{1,9},{3,11}... | collective-permute-start | bytes 36872 | tf_op jit(solution)/shard_map/ppermute | solution.py:402
  62.6 1.5 %collective-permute-start.5 = (bf16[48,128]{1,0:T(8,128)(2,1)S(1)}, bf16[48,128]{1,0:T(8,128)(2,1)S(1)}, u32[]{:S(2)}, u32[]{:S(2)}) collective-permute-start(bf16[48,128]{1,0:T(8,128)(2,1)S(1)} %get-tuple-element.32), channel_id=1, source_target_pairs={{0,10},{2,8},{4,14},{6,12},{8,2},{10,0},{12,6},{14,4},{1,11},{3,9}... | collective-permute-start | bytes 36872 | tf_op jit(solution)/shard_map/ppermute | solution.py:402
  64.0 1.5 %collective-permute-start.6 = (bf16[48,128]{1,0:T(8,128)(2,1)S(1)}, bf16[48,128]{1,0:T(8,128)(2,1)S(1)}, u32[]{:S(2)}, u32[]{:S(2)}) collective-permute-start(bf16[48,128]{1,0:T(8,128)(2,1)S(1)} %get-tuple-element.33), channel_id=1, source_target_pairs={{0,12},{2,14},{4,8},{6,10},{8,4},{10,6},{12,0},{14,2},{1,13},{3,15... | collective-permute-start | bytes 36872 | tf_op jit(solution)/shard_map/ppermute | solution.py:402
  65.6 1.7 %collective-permute-start.7 = (bf16[48,128]{1,0:T(8,128)(2,1)S(1)}, bf16[48,128]{1,0:T(8,128)(2,1)S(1)}, u32[]{:S(2)}, u32[]{:S(2)}) collective-permute-start(bf16[48,128]{1,0:T(8,128)(2,1)S(1)} %get-tuple-element.34), channel_id=1, source_target_pairs={{0,14},{2,12},{4,10},{6,8},{8,6},{10,4},{12,2},{14,0},{1,15},{3,13... | collective-permute-start | bytes 36872 | tf_op jit(solution)/shard_map/ppermute | solution.py:402
  68.1 2.3 %collective-permute-start.10 = (bf16[2,144,256]{2,1,0:T(8,128)(2,1)S(1)}, bf16[2,144,256]{2,1,0:T(8,128)(2,1)S(1)}, u32[]{:S(2)}, u32[]{:S(2)}) collective-permute-start(bf16[2,144,256]{2,1,0:T(8,128)(2,1)S(1)} %copy-done.15), channel_id=1, source_target_pairs={{0,6},{2,4},{4,2},{6,0},{8,14},{10,12},{12,10},{14,8},{1,7},{3,5},... | collective-permute-start | bytes 442376 | tf_op jit(solution)/shard_map/ppermute | solution.py:402
  71.2 3.3 %collective-permute-start.12 = (bf16[2,144,256]{2,1,0:T(8,128)(2,1)S(1)}, bf16[2,144,256]{2,1,0:T(8,128)(2,1)S(1)}, u32[]{:S(2)}, u32[]{:S(2)}) collective-permute-start(bf16[2,144,256]{2,1,0:T(8,128)(2,1)S(1)} %copy-done.13), channel_id=1, source_target_pairs={{0,10},{2,8},{4,14},{6,12},{8,2},{10,0},{12,6},{14,4},{1,11},{3,9}... | collective-permute-start | bytes 442376 | tf_op jit(solution)/shard_map/ppermute | solution.py:402
  74.5 1.5 %collective-permute-start.13 = (bf16[2,144,256]{2,1,0:T(8,128)(2,1)S(1)}, bf16[2,144,256]{2,1,0:T(8,128)(2,1)S(1)}, u32[]{:S(2)}, u32[]{:S(2)}) collective-permute-start(bf16[2,144,256]{2,1,0:T(8,128)(2,1)S(1)} %copy-done.12), channel_id=1, source_target_pairs={{0,12},{2,14},{4,8},{6,10},{8,4},{10,6},{12,0},{14,2},{1,13},{3,15... | collective-permute-start | bytes 442376 | tf_op jit(solution)/shard_map/ppermute | solution.py:402
  76.0 1.5 %collective-permute-start.14 = (bf16[2,144,256]{2,1,0:T(8,128)(2,1)S(1)}, bf16[2,144,256]{2,1,0:T(8,128)(2,1)S(1)}, u32[]{:S(2)}, u32[]{:S(2)}) collective-permute-start(bf16[2,144,256]{2,1,0:T(8,128)(2,1)S(1)} %copy-done.11), channel_id=1, source_target_pairs={{0,14},{2,12},{4,10},{6,8},{8,6},{10,4},{12,2},{14,0},{1,15},{3,13... | collective-permute-start | bytes 442376 | tf_op jit(solution)/shard_map/ppermute | solution.py:402
  77.5 27.3 %all-gather.1.facts_ref = s32[8,2,24]{2,1,0:T(2,128)S(1)} all-gather(s32[1,2,24]{2,1,0:T(2,128)S(1)} %add_bitcast_fusion), channel_id=2, replica_groups=mesh['group'=2,'inst'=8,'tp'=2] {'inst'}, dimensions={0}, use_global_device_ids=true | all-gather | bytes 1728 | tf_op jit(solution)/shard_map/all_gather | solution.py:407
  104.8 3.8 %settle.1 = (bf16[2,24,2048]{2,1,0:T(8,128)(2,1)}, s32[8]{0:T(128)S(1)}, s32[8]{0:T(128)S(1)}) custom-call(s32[8,2,24]{2,1,0:T(2,128)S(1)} %all-gather.1.facts_ref, bf16[768,128]{1,0:T(8,128)(2,1)S(1)} %get-tuple-element.27.mixed_ref, bf16[48,128]{1,0:T(8,128)(2,1)S(1)} %collective-permute-done.1.refs_0_.refs_7_, ...), custom_call_target="tpu_custom_call" | custom-call | tf_op jit(solution)/shard_map/settle/pallas_call | solution.py:309
  108.7 2.9 %land.1 = bf16[24,2,144,256]{3,2,1,0:T(8,128)(2,1)} custom-call(s32[8]{0:T(128)S(1)} %get-tuple-element.36.slot_ref, s32[8]{0:T(128)S(1)} %get-tuple-element.37.length_ref, bf16[2,144,256]{2,1,0:T(8,128)(2,1)} %collective-permute-done.8.refs_0_, bf16[2,144,256]{2,1,0:T(8,128)(2,1)} %collective-permute-done.9.refs_1_, ...), custom_call_target="tpu_custom_call", output_to_operand_aliasing={{}: (16, {})} | custom-call | tf_op jit(solution)/shard_map/land/pallas_call | solution.py:370
  (50 shorter events, 4.4 us)
Async XLA Ops:
  0.6 46.6 %copy-start = (bf16[24,2,144,256]{3,2,1,0:T(8,128)(2,1)S(1)}, bf16[24,2,144,256]{3,2,1,0:T(8,128)(2,1)}, u32[]{:S(2)}) copy-start(bf16[24,2,144,256]{3,2,1,0:T(8,128)(2,1)} %kv_ref.3) | copy-start | bytes 10616836
  5.2 39.2 %copy-start.7 = (s32[24]{0:T(128)S(1)}, s32[24]{0:T(128)}, u32[]{:S(2)}) copy-start(s32[24]{0:T(128)} %length_ref.1) | copy-start | bytes 292
  5.2 42.1 %copy-start.8 = (bf16[128]{0:T(256)(128)(2,1)S(1)}, bf16[128]{0:T(256)(128)(2,1)}, u32[]{:S(2)}) copy-start(bf16[128]{0:T(256)(128)(2,1)} %param.15) | copy-start | bytes 772
  8.1 69.4 %copy-start.10 = (s32[24]{0:T(128)S(1)}, s32[24]{0:T(128)}, u32[]{:S(2)}) copy-start(s32[24]{0:T(128)} %dest_ref.1) | copy-start | bytes 292
  8.1 39.2 %collective-permute-start = (f32[48,512]{1,0:T(8,128)}, f32[48,512]{1,0:T(8,128)}, u32[]{:S(2)}, u32[]{:S(2)}) collective-permute-start(f32[48,512]{1,0:T(8,128)} %get-tuple-element.26), channel_id=1, source_target_pairs={{0,1},{1,0},{2,3},{3,2},{4,5},{5,4},{6,7},{7,6},{8,9},{9,8},{10,11... | collective-permute-start | bytes 294920 | tf_op jit(solution)/shard_map/ppermute | solution.py:409
  42.3 32.2 %collective-permute-start.8 = (bf16[2,144,256]{2,1,0:T(8,128)(2,1)}, bf16[2,144,256]{2,1,0:T(8,128)(2,1)}, u32[]{:S(2)}, u32[]{:S(2)}) collective-permute-start(bf16[2,144,256]{2,1,0:T(8,128)(2,1)} %get-tuple-element.38), channel_id=1, source_target_pairs={{0,2},{2,0},{4,6},{6,4},{8,10},{10,8},{12,14},{14,12},{1,3},{3,1},... | collective-permute-start | bytes 442376 | tf_op jit(solution)/shard_map/ppermute | solution.py:402
  43.9 32.1 %collective-permute-start.9 = (bf16[2,144,256]{2,1,0:T(8,128)(2,1)}, bf16[2,144,256]{2,1,0:T(8,128)(2,1)}, u32[]{:S(2)}, u32[]{:S(2)}) collective-permute-start(bf16[2,144,256]{2,1,0:T(8,128)(2,1)} %get-tuple-element.39), channel_id=1, source_target_pairs={{0,4},{2,6},{4,0},{6,2},{8,12},{10,14},{12,8},{14,10},{1,5},{3,7},... | collective-permute-start | bytes 442376 | tf_op jit(solution)/shard_map/ppermute | solution.py:402
  46.3 29.7 %copy-start.11 = (bf16[2,144,256]{2,1,0:T(8,128)(2,1)S(1)}, bf16[2,144,256]{2,1,0:T(8,128)(2,1)}, u32[]{:S(2)}) copy-start(bf16[2,144,256]{2,1,0:T(8,128)(2,1)} %get-tuple-element.44) | copy-start | bytes 442372
  49.8 18.3 %copy-start.15 = (bf16[2,144,256]{2,1,0:T(8,128)(2,1)S(1)}, bf16[2,144,256]{2,1,0:T(8,128)(2,1)}, u32[]{:S(2)}) copy-start(bf16[2,144,256]{2,1,0:T(8,128)(2,1)} %get-tuple-element.40) | copy-start | bytes 442372
  49.8 20.6 %copy-start.14 = (bf16[2,144,256]{2,1,0:T(8,128)(2,1)S(1)}, bf16[2,144,256]{2,1,0:T(8,128)(2,1)}, u32[]{:S(2)}) copy-start(bf16[2,144,256]{2,1,0:T(8,128)(2,1)} %get-tuple-element.41) | copy-start | bytes 442372
  49.8 21.4 %copy-start.13 = (bf16[2,144,256]{2,1,0:T(8,128)(2,1)S(1)}, bf16[2,144,256]{2,1,0:T(8,128)(2,1)}, u32[]{:S(2)}) copy-start(bf16[2,144,256]{2,1,0:T(8,128)(2,1)} %get-tuple-element.42) | copy-start | bytes 442372
  49.8 24.8 %copy-start.12 = (bf16[2,144,256]{2,1,0:T(8,128)(2,1)S(1)}, bf16[2,144,256]{2,1,0:T(8,128)(2,1)}, u32[]{:S(2)}) copy-start(bf16[2,144,256]{2,1,0:T(8,128)(2,1)} %get-tuple-element.43) | copy-start | bytes 442372
  56.3 3.7 %collective-permute-start.1 = (bf16[48,128]{1,0:T(8,128)(2,1)S(1)}, bf16[48,128]{1,0:T(8,128)(2,1)S(1)}, u32[]{:S(2)}, u32[]{:S(2)}) collective-permute-start(bf16[48,128]{1,0:T(8,128)(2,1)S(1)} %get-tuple-element.28), channel_id=1, source_target_pairs={{0,2},{2,0},{4,6},{6,4},{8,10},{10,8},{12,14},{14,12},{1,3},{3,1},... | collective-permute-start | bytes 36872 | tf_op jit(solution)/shard_map/ppermute | solution.py:402
  56.4 6.2 %collective-permute-start.2 = (bf16[48,128]{1,0:T(8,128)(2,1)S(1)}, bf16[48,128]{1,0:T(8,128)(2,1)S(1)}, u32[]{:S(2)}, u32[]{:S(2)}) collective-permute-start(bf16[48,128]{1,0:T(8,128)(2,1)S(1)} %get-tuple-element.29), channel_id=1, source_target_pairs={{0,4},{2,6},{4,0},{6,2},{8,12},{10,14},{12,8},{14,10},{1,5},{3,7},... | collective-permute-start | bytes 36872 | tf_op jit(solution)/shard_map/ppermute | solution.py:402
  58.4 5.7 %collective-permute-start.3 = (bf16[48,128]{1,0:T(8,128)(2,1)S(1)}, bf16[48,128]{1,0:T(8,128)(2,1)S(1)}, u32[]{:S(2)}, u32[]{:S(2)}) collective-permute-start(bf16[48,128]{1,0:T(8,128)(2,1)S(1)} %get-tuple-element.30), channel_id=1, source_target_pairs={{0,6},{2,4},{4,2},{6,0},{8,14},{10,12},{12,10},{14,8},{1,7},{3,5},... | collective-permute-start | bytes 36872 | tf_op jit(solution)/shard_map/ppermute | solution.py:402
  60.0 5.6 %collective-permute-start.4 = (bf16[48,128]{1,0:T(8,128)(2,1)S(1)}, bf16[48,128]{1,0:T(8,128)(2,1)S(1)}, u32[]{:S(2)}, u32[]{:S(2)}) collective-permute-start(bf16[48,128]{1,0:T(8,128)(2,1)S(1)} %get-tuple-element.31), channel_id=1, source_target_pairs={{0,8},{2,10},{4,12},{6,14},{8,0},{10,2},{12,4},{14,6},{1,9},{3,11}... | collective-permute-start | bytes 36872 | tf_op jit(solution)/shard_map/ppermute | solution.py:402
  62.6 5.5 %collective-permute-start.5 = (bf16[48,128]{1,0:T(8,128)(2,1)S(1)}, bf16[48,128]{1,0:T(8,128)(2,1)S(1)}, u32[]{:S(2)}, u32[]{:S(2)}) collective-permute-start(bf16[48,128]{1,0:T(8,128)(2,1)S(1)} %get-tuple-element.32), channel_id=1, source_target_pairs={{0,10},{2,8},{4,14},{6,12},{8,2},{10,0},{12,6},{14,4},{1,11},{3,9}... | collective-permute-start | bytes 36872 | tf_op jit(solution)/shard_map/ppermute | solution.py:402
  64.0 6.3 %collective-permute-start.6 = (bf16[48,128]{1,0:T(8,128)(2,1)S(1)}, bf16[48,128]{1,0:T(8,128)(2,1)S(1)}, u32[]{:S(2)}, u32[]{:S(2)}) collective-permute-start(bf16[48,128]{1,0:T(8,128)(2,1)S(1)} %get-tuple-element.33), channel_id=1, source_target_pairs={{0,12},{2,14},{4,8},{6,10},{8,4},{10,6},{12,0},{14,2},{1,13},{3,15... | collective-permute-start | bytes 36872 | tf_op jit(solution)/shard_map/ppermute | solution.py:402
  65.6 5.6 %collective-permute-start.7 = (bf16[48,128]{1,0:T(8,128)(2,1)S(1)}, bf16[48,128]{1,0:T(8,128)(2,1)S(1)}, u32[]{:S(2)}, u32[]{:S(2)}) collective-permute-start(bf16[48,128]{1,0:T(8,128)(2,1)S(1)} %get-tuple-element.34), channel_id=1, source_target_pairs={{0,14},{2,12},{4,10},{6,8},{8,6},{10,4},{12,2},{14,0},{1,15},{3,13... | collective-permute-start | bytes 36872 | tf_op jit(solution)/shard_map/ppermute | solution.py:402
  68.1 40.6 %collective-permute-start.10 = (bf16[2,144,256]{2,1,0:T(8,128)(2,1)S(1)}, bf16[2,144,256]{2,1,0:T(8,128)(2,1)S(1)}, u32[]{:S(2)}, u32[]{:S(2)}) collective-permute-start(bf16[2,144,256]{2,1,0:T(8,128)(2,1)S(1)} %copy-done.15), channel_id=1, source_target_pairs={{0,6},{2,4},{4,2},{6,0},{8,14},{10,12},{12,10},{14,8},{1,7},{3,5},... | collective-permute-start | bytes 442376 | tf_op jit(solution)/shard_map/ppermute | solution.py:402
  70.3 38.3 %collective-permute-start.11 = (bf16[2,144,256]{2,1,0:T(8,128)(2,1)S(1)}, bf16[2,144,256]{2,1,0:T(8,128)(2,1)S(1)}, u32[]{:S(2)}, u32[]{:S(2)}) collective-permute-start(bf16[2,144,256]{2,1,0:T(8,128)(2,1)S(1)} %copy-done.14), channel_id=1, source_target_pairs={{0,8},{2,10},{4,12},{6,14},{8,0},{10,2},{12,4},{14,6},{1,9},{3,11}... | collective-permute-start | bytes 442376 | tf_op jit(solution)/shard_map/ppermute | solution.py:402
  71.2 37.5 %collective-permute-start.12 = (bf16[2,144,256]{2,1,0:T(8,128)(2,1)S(1)}, bf16[2,144,256]{2,1,0:T(8,128)(2,1)S(1)}, u32[]{:S(2)}, u32[]{:S(2)}) collective-permute-start(bf16[2,144,256]{2,1,0:T(8,128)(2,1)S(1)} %copy-done.13), channel_id=1, source_target_pairs={{0,10},{2,8},{4,14},{6,12},{8,2},{10,0},{12,6},{14,4},{1,11},{3,9}... | collective-permute-start | bytes 442376 | tf_op jit(solution)/shard_map/ppermute | solution.py:402
  74.5 34.1 %collective-permute-start.13 = (bf16[2,144,256]{2,1,0:T(8,128)(2,1)S(1)}, bf16[2,144,256]{2,1,0:T(8,128)(2,1)S(1)}, u32[]{:S(2)}, u32[]{:S(2)}) collective-permute-start(bf16[2,144,256]{2,1,0:T(8,128)(2,1)S(1)} %copy-done.12), channel_id=1, source_target_pairs={{0,12},{2,14},{4,8},{6,10},{8,4},{10,6},{12,0},{14,2},{1,13},{3,15... | collective-permute-start | bytes 442376 | tf_op jit(solution)/shard_map/ppermute | solution.py:402
  76.0 32.7 %collective-permute-start.14 = (bf16[2,144,256]{2,1,0:T(8,128)(2,1)S(1)}, bf16[2,144,256]{2,1,0:T(8,128)(2,1)S(1)}, u32[]{:S(2)}, u32[]{:S(2)}) collective-permute-start(bf16[2,144,256]{2,1,0:T(8,128)(2,1)S(1)} %copy-done.11), channel_id=1, source_target_pairs={{0,14},{2,12},{4,10},{6,8},{8,6},{10,4},{12,2},{14,0},{1,15},{3,13... | collective-permute-start | bytes 442376 | tf_op jit(solution)/shard_map/ppermute | solution.py:402
  (7 other events, 7.7 us)

commit v2 on v1

v2 whole, which is shorter than its diff:
```python
import functools
import math

import jax
import jax.numpy as jnp
from jax import lax
from jax.experimental import pallas as pl
from jax.experimental.pallas import tpu as pltpu
from jax.sharding import PartitionSpec as P

HD = 128
ROPE_BASE = 1000000.0
NORM_EPS = 1e-06
VMEM_LIMIT = 40 * 1024 * 1024
FACTS = 16
WINDOW = 32


def peer_to(index, shift, count, paired=None):
    if count & (count - 1) == 0:
        return index ^ (shift if paired is None else paired)
    return (index + shift) % count


def near_size(count):
    return 4 if count % 4 == 0 and count & (count - 1) == 0 else 1


def peer_of(me, piece, near, to):
    count = lax.axis_size("inst")
    if piece < near:
        return me // near * near + piece
    return peer_to(me, piece, count) if to else peer_to(me, count - piece, count, piece)


def pack_kernel(count, near, dest_ref, length_ref, kv_ref, near_ref, *refs):
    far_refs, pick_ref, sems = refs[: count - near], refs[count - near], refs[count - near + 1]
    rows = dest_ref.shape[0]
    capacity = kv_ref.shape[2]
    lanes = kv_ref.shape[3]
    me = lax.axis_index("inst")
    for peer in range(count):
        pick_ref[peer] = 0

    def note(row, carry):
        pick_ref[dest_ref[row] // rows] = row
        return carry

    lax.fori_loop(0, rows, note, 0)
    order = list(range(near, count)) + list(range(near))
    copies = []
    for piece in order:
        row = pick_ref[peer_of(me, piece, near, True)]
        block = near_ref.at[piece] if piece < near else far_refs[piece - near]
        for which in range(2):
            copy = pltpu.make_async_copy(
                kv_ref.at[row, which],
                block.at[pl.ds(which * capacity, capacity)],
                sems.at[piece, which],
            )
            copy.start()
            copies.append(copy)
    for piece in order:
        peer = peer_of(me, piece, near, True)
        row = pick_ref[peer]
        slot = jnp.where(dest_ref[row] // rows == peer, dest_ref[row] % rows, -1)
        block = near_ref.at[piece] if piece < near else far_refs[piece - near]
        line = lax.broadcasted_iota(jnp.int32, (FACTS, lanes), 0)
        facts = jnp.where(line == 0, slot, length_ref[row])
        block[2 * capacity :, :] = facts.astype(jnp.float32).astype(jnp.bfloat16)
    for copy in copies:
        copy.wait()


def pack(kv_cache, destination, lengths, count, near):
    height = 2 * kv_cache.shape[2] + FACTS
    width = kv_cache.shape[3]
    far = jax.ShapeDtypeStruct((height, width), kv_cache.dtype)
    smem = pl.BlockSpec(memory_space=pltpu.SMEM)
    vmem = pl.BlockSpec(memory_space=pltpu.VMEM)
    outs = pl.pallas_call(
        functools.partial(pack_kernel, count, near),
        out_shape=[jax.ShapeDtypeStruct((near, height, width), kv_cache.dtype)]
        + [far] * (count - near)
        + [jax.ShapeDtypeStruct((count,), jnp.int32)],
        in_specs=[smem, smem, pl.BlockSpec(memory_space=pltpu.HBM)],
        out_specs=[vmem] * (count - near + 1) + [smem],
        scratch_shapes=[pltpu.SemaphoreType.DMA((count, 2))],
        compiler_params=pltpu.CompilerParams(vmem_limit_bytes=VMEM_LIMIT),
        name="pack",
    )(destination, lengths, kv_cache)
    return outs[0], outs[1:-1], outs[-1]


def project_kernel(_, hidden_ref, key_ref, value_ref, own_ref, other_ref, total):
    step = pl.program_id(0)
    width = key_ref.shape[1]

    @pl.when(step == 0)
    def _():
        total[...] = jnp.zeros_like(total)

    steps, rows, depth = hidden_ref.shape
    hidden = hidden_ref[...].reshape(steps * rows, depth)
    total[:, :width] += jnp.dot(hidden, key_ref[...], preferred_element_type=jnp.float32)
    total[:, width:] += jnp.dot(hidden, value_ref[...], preferred_element_type=jnp.float32)

    @pl.when(step == pl.num_programs(0) - 1)
    def _():
        half = width // 2
        me = lax.axis_index("tp")
        for ref, core in ((own_ref, me), (other_ref, 1 - me)):
            at = pl.multiple_of(core * half, half)
            ref[:, :half] = total[:, pl.ds(at, half)]
            ref[:, half:] = total[:, pl.ds(pl.multiple_of(width + at, half), half)]


def project(hidden_new, key_weight, value_weight, pick):
    steps, rows, depth = hidden_new.shape
    width = key_weight.shape[1]
    part = depth // 5
    shape = jax.ShapeDtypeStruct((steps * rows, width), jnp.float32)
    whole = pl.BlockSpec((steps * rows, width), lambda i: (0, 0))
    return pl.pallas_call(
        project_kernel,
        grid=(depth // part,),
        out_shape=[shape, shape],
        in_specs=[
            pl.BlockSpec(memory_space=pltpu.SMEM),
            pl.BlockSpec((steps, rows, part), lambda i: (0, 0, i)),
            pl.BlockSpec((part, width), lambda i: (i, 0)),
            pl.BlockSpec((part, width), lambda i: (i, 0)),
        ],
        out_specs=[whole, whole],
        scratch_shapes=[pltpu.VMEM((steps * rows, 2 * width), jnp.float32)],
        compiler_params=pltpu.CompilerParams(vmem_limit_bytes=VMEM_LIMIT),
        cost_estimate=pl.CostEstimate(
            flops=4 * steps * rows * depth * width,
            bytes_accessed=4 * depth * width,
            transcendentals=0,
        ),
        name="project",
    )(pick, hidden_new, key_weight, value_weight)


def attend_kernel(
    count,
    block,
    length_ref,
    pick_ref,
    own_ref,
    got_ref,
    gain_ref,
    cos_ref,
    sin_ref,
    query_ref,
    kv_ref,
    moved_ref,
    mixed_ref,
    small_ref,
    fresh,
    query_rows,
    mixed,
):
    part = pl.program_id(0)
    steps, rows, query_width = query_ref.shape
    capacity, lanes = kv_ref.shape[2:]
    heads = lanes // HD
    group = query_width // lanes
    per_head = steps * group
    per_row = heads * per_head

    def place(step, head, member):
        return head * per_head + step * group + member

    def spot(head, member):
        return slice((head * group + member) * HD, (head * group + member + 1) * HD)

    @pl.when(part == 0)
    def _():
        raw = own_ref[...] + got_ref[...]
        gain = gain_ref[...].astype(jnp.float32)
        for head in range(heads):
            at = slice(head * HD, (head + 1) * HD)
            piece = raw[:, at]
            mean = jnp.mean(piece * piece, axis=-1, keepdims=True)
            piece = piece * lax.rsqrt(mean + NORM_EPS) * gain
            swapped = jnp.concatenate([piece[:, HD // 2 :], piece[:, : HD // 2]], axis=1)
            turned = piece * cos_ref[...] + swapped * sin_ref[...]
            fresh[0, :, at] = turned.astype(jnp.bfloat16).astype(jnp.float32)
        fresh[1] = raw[:, lanes:].astype(jnp.bfloat16).astype(jnp.float32)
        for step in range(steps):
            for head in range(heads):
                for member in range(group):
                    query_rows[pl.ds(place(step, head, member), rows, stride=per_row), :] = (
                        query_ref[step, :, spot(head, member)].astype(jnp.float32)
                    )

    position = lax.broadcasted_iota(jnp.int32, (capacity, HD), 0)
    lane_head = lax.broadcasted_iota(jnp.int32, (per_row, lanes), 1) // HD
    row_head = lax.broadcasted_iota(jnp.int32, (per_row, lanes), 0) // per_head
    column = lax.broadcasted_iota(jnp.int32, (per_row, capacity), 1)
    row_step = (lax.broadcasted_iota(jnp.int32, (per_row, capacity), 0) % per_head) // group
    factor = 1.0 / math.sqrt(HD)
    scores = []
    for item in range(block):
        row = part * block + item
        length = length_ref[row]
        kept = position < length
        landing = [position == length + step for step in range(steps)]
        for which in range(2):
            news = [fresh[which, pl.ds(step * rows + row, 1), :] for step in range(steps)]
            for head in range(heads):
                at = slice(head * HD, (head + 1) * HD)
                stored = jnp.where(kept, kv_ref[item, which, :, at].astype(jnp.float32), 0.0)
                for step in range(steps):
                    stored = jnp.where(landing[step], news[step][:, at], stored)
                moved_ref[item, which, :, at] = stored.astype(jnp.bfloat16)
        query = query_rows[pl.ds(pl.multiple_of(row * per_row, per_row), per_row), :]
        query = jnp.where(lane_head == row_head, jnp.concatenate([query] * heads, axis=1), 0.0)
        score = lax.dot_general(
            query.astype(jnp.bfloat16),
            moved_ref[item, 0],
            (((1,), (1,)), ((), ())),
            preferred_element_type=jnp.float32,
        )
        scores.append(jnp.where(column <= length + row_step, score * factor, -jnp.inf))
    weights = []
    for score in scores:
        raised = jnp.exp(score - jnp.max(score, axis=-1, keepdims=True))
        normaliser = jnp.sum(raised, axis=-1, keepdims=True)
        weights.append((raised / normaliser).astype(jnp.bfloat16))
    for item in range(block):
        row = part * block + item
        result = jnp.dot(weights[item], moved_ref[item, 1], preferred_element_type=jnp.float32)
        for head in range(heads):
            mixed[pl.ds(pl.multiple_of(row * per_row + head * per_head, per_head), per_head), :] = (
                result[head * per_head : (head + 1) * per_head, head * HD : (head + 1) * HD]
            )

    @pl.when(part == pl.num_programs(0) - 1)
    def _():
        mixed_ref[...] = mixed[...].astype(jnp.bfloat16)
        for peer in range(count):
            row = pick_ref[peer]
            small_ref[peer, :per_row, :] = mixed[
                pl.ds(pl.multiple_of(row * per_row, per_row), per_row), :
            ].astype(jnp.bfloat16)
            news = []
            for which in range(2):
                for step in range(steps):
                    new = fresh[which, pl.ds(step * rows + row, 1), :]
                    news += [new[:, h * HD : (h + 1) * HD] for h in range(heads)]
            fill = small_ref.shape[1] - per_row - len(news)
            news.append(jnp.zeros((fill, HD), jnp.float32))
            small_ref[peer, per_row:, :] = jnp.concatenate(news, axis=0).astype(jnp.bfloat16)


def attend(kv_cache, queries, own, got, gain, cosine, sine, lengths, pick, count):
    steps, rows, query_width = queries.shape
    capacity, lanes = kv_cache.shape[2:]
    heads = lanes // HD
    per_row = steps * query_width // HD
    block = 8
    small_rows = -(-(per_row + 2 * steps * heads) // 16) * 16
    small = jax.ShapeDtypeStruct((count, small_rows, HD), jnp.bfloat16)
    smem = pl.BlockSpec(memory_space=pltpu.SMEM)
    vmem = pl.BlockSpec(memory_space=pltpu.VMEM)
    cache_block = pl.BlockSpec((block, 2, capacity, lanes), lambda i: (i, 0, 0, 0))
    return pl.pallas_call(
        functools.partial(attend_kernel, count, block),
        grid=(rows // block,),
        out_shape=[
            jax.ShapeDtypeStruct(kv_cache.shape, kv_cache.dtype),
            jax.ShapeDtypeStruct((rows * per_row, HD), jnp.bfloat16),
            small,
        ],
        in_specs=[smem, smem, vmem, vmem, vmem, vmem, vmem, vmem, cache_block],
        out_specs=[cache_block, vmem, vmem],
        scratch_shapes=[
            pltpu.VMEM((2, steps * rows, lanes), jnp.float32),
            pltpu.VMEM((rows * per_row, HD), jnp.float32),
            pltpu.VMEM((rows * per_row, HD), jnp.float32),
        ],
        compiler_params=pltpu.CompilerParams(vmem_limit_bytes=VMEM_LIMIT),
        cost_estimate=pl.CostEstimate(
            flops=4 * rows * per_row * capacity * lanes,
            bytes_accessed=4 * kv_cache.size,
            transcendentals=rows * per_row * capacity,
        ),
        name="attend",
    )(lengths, pick, own, got, gain, cosine, sine, queries, kv_cache)


def window_start(length, capacity):
    return pl.multiple_of(jnp.minimum(length // 16 * 16, capacity - WINDOW), 16)


def land_kernel(count, near, near_ref, *refs):
    far_refs = refs[: count - near]
    _, out_ref, slot_ref, length_ref, window_ref, buffer, sems = refs[count - near :]
    capacity, lanes = buffer.shape[2:]
    position = lax.broadcasted_iota(jnp.int32, (capacity, HD), 0)
    me = lax.axis_index("inst")

    def store(piece):
        slot = jnp.maximum(slot_ref[piece], 0)
        return pltpu.make_async_copy(buffer.at[piece], out_ref.at[slot], sems.at[piece])

    blocks = [near_ref.at[piece] for piece in range(near)] + list(far_refs)
    for piece, block in enumerate(blocks):
        facts = block[2 * capacity :, :HD].astype(jnp.float32)
        slot = jnp.max(facts[0:1]).astype(jnp.int32)
        length = jnp.max(facts[1:2]).astype(jnp.int32)
        if piece < near:
            slot = jnp.where(me % near == piece, -1, slot)
        slot_ref[piece] = slot
        length_ref[piece] = length
    for piece, block in enumerate(blocks):

        @pl.when(slot_ref[piece] >= 0)
        def _():
            length = length_ref[piece]
            kept = position < length
            for which in range(2):
                for at in range(0, lanes, HD):
                    stored = block[which * capacity : (which + 1) * capacity, at : at + HD]
                    stored = jnp.where(kept, stored.astype(jnp.float32), 0.0)
                    buffer[piece, which, :, at : at + HD] = stored.astype(jnp.bfloat16)
            store(piece).start()
            start = window_start(length, capacity)
            window_ref[piece] = buffer[piece, :, pl.ds(start, WINDOW), :]

    for piece in range(count):

        @pl.when(slot_ref[piece] >= 0)
        def _():
            store(piece).wait()


def land(near_got, far_got, moved, count, near):
    smem = pl.BlockSpec(memory_space=pltpu.SMEM)
    vmem = pl.BlockSpec(memory_space=pltpu.VMEM)
    hbm = pl.BlockSpec(memory_space=pl.ANY)
    scalars = jax.ShapeDtypeStruct((count,), jnp.int32)
    lanes = moved.shape[3]
    return pl.pallas_call(
        functools.partial(land_kernel, count, near),
        out_shape=[
            jax.ShapeDtypeStruct(moved.shape, moved.dtype),
            scalars,
            scalars,
            jax.ShapeDtypeStruct((count, 2, WINDOW, lanes), moved.dtype),
        ],
        in_specs=[vmem] * (count - near + 1) + [hbm],
        out_specs=[hbm, smem, smem, vmem],
        scratch_shapes=[
            pltpu.VMEM((count,) + moved.shape[1:], moved.dtype),
            pltpu.SemaphoreType.DMA((count,)),
        ],
        input_output_aliases={count - near + 1: 0},
        compiler_params=pltpu.CompilerParams(vmem_limit_bytes=VMEM_LIMIT),
        name="land",
    )(near_got, *far_got, moved)


def settle_kernel(
    count,
    near,
    group,
    slot_ref,
    length_ref,
    mixed_ref,
    small_ref,
    window_ref,
    _,
    out_ref,
    moved_ref,
    mixed,
    windows,
    sems,
):
    steps, rows, query_width = out_ref.shape
    per_row = steps * query_width // HD
    capacity, lanes = moved_ref.shape[2:]
    heads = lanes // HD
    me = lax.axis_index("inst")
    position = lax.broadcasted_iota(jnp.int32, (WINDOW, lanes), 0)

    def store(piece):
        slot = jnp.maximum(slot_ref[piece], 0)
        start = window_start(length_ref[piece], capacity)
        return pltpu.make_async_copy(
            windows.at[piece], moved_ref.at[slot, :, pl.ds(start, WINDOW), :], sems.at[piece]
        )

    mixed[...] = mixed_ref[...].astype(jnp.float32)
    for piece in range(count):

        @pl.when(slot_ref[piece] >= 0)
        def _():
            slot, length = slot_ref[piece], length_ref[piece]
            peer = peer_of(me, piece, near, False)
            news = small_ref[peer, per_row:, :].astype(jnp.float32)
            ahead = length - window_start(length, capacity)
            for which in range(2):
                stored = window_ref[piece, which].astype(jnp.float32)
                for step in range(steps):
                    at = (which * steps + step) * heads
                    new = jnp.concatenate([news[at + h : at + h + 1] for h in range(heads)], axis=1)
                    stored = jnp.where(position == ahead + step, new, stored)
                windows[piece, which] = stored.astype(jnp.bfloat16)
            store(piece).start()
            mixed[pl.ds(pl.multiple_of(slot * per_row, per_row), per_row), :] = small_ref[
                peer, :per_row, :
            ].astype(jnp.float32)

    for step in range(steps):
        for chunk in range(query_width // HD):
            head, member = chunk // group, chunk % group
            at = head * steps * group + step * group + member
            out_ref[step, :, chunk * HD : (chunk + 1) * HD] = mixed[
                pl.ds(at, rows, stride=per_row), :
            ].astype(jnp.bfloat16)

    for piece in range(count):

        @pl.when(slot_ref[piece] >= 0)
        def _():
            store(piece).wait()


def settle(slots, lengths, mixed, small, windows, moved, shape, group, count, near):
    smem = pl.BlockSpec(memory_space=pltpu.SMEM)
    vmem = pl.BlockSpec(memory_space=pltpu.VMEM)
    hbm = pl.BlockSpec(memory_space=pl.ANY)
    return pl.pallas_call(
        functools.partial(settle_kernel, count, near, group),
        out_shape=[
            jax.ShapeDtypeStruct(shape, jnp.bfloat16),
            jax.ShapeDtypeStruct(moved.shape, moved.dtype),
        ],
        in_specs=[smem, smem, vmem, vmem, vmem, hbm],
        out_specs=[vmem, hbm],
        scratch_shapes=[
            pltpu.VMEM(mixed.shape, jnp.float32),
            pltpu.VMEM(windows.shape, windows.dtype),
            pltpu.SemaphoreType.DMA((count,)),
        ],
        input_output_aliases={5: 1},
        compiler_params=pltpu.CompilerParams(vmem_limit_bytes=VMEM_LIMIT),
        name="settle",
    )(slots, lengths, mixed, small, windows, moved)


def rotation(lengths, steps):
    half = HD // 2
    inverse = jnp.exp(-math.log(ROPE_BASE) * 2.0 * jnp.arange(half, dtype=jnp.float32) / HD)
    positions = (lengths[None, :] + jnp.arange(steps, dtype=jnp.int32)[:, None]).reshape(-1)
    angles = positions.astype(jnp.float32)[:, None] * inverse
    cosine, sine = jnp.cos(angles), jnp.sin(angles)
    return jnp.concatenate([cosine, cosine], axis=1), jnp.concatenate([-sine, sine], axis=1)


def local(hidden_new, queries, kv_cache, lengths, destination, key_weight, value_weight, key_gain):
    steps = queries.shape[0]
    group = queries.shape[2] // kv_cache.shape[3]
    count = lax.axis_size("inst")
    near = near_size(count)

    near_blocks, far_blocks, pick = pack(kv_cache, destination, lengths, count, near)
    far_got = []
    for piece, block in enumerate(far_blocks, near):
        pairs = [(i, int(peer_to(i, piece, count))) for i in range(count)]
        far_got.append(lax.ppermute(block, "inst", pairs))
    near_got = near_blocks
    if near > 1:
        teams = [list(range(i, i + near)) for i in range(0, count, near)]
        near_got = lax.all_to_all(
            near_blocks, "inst", 0, 0, axis_index_groups=teams, tiled=True
        )
    own, other = project(hidden_new, key_weight, value_weight, pick)
    got = lax.ppermute(other, "tp", [(0, 1), (1, 0)])
    cosine, sine = rotation(lengths, steps)
    moved, mixed, small = attend(
        kv_cache, queries, own, got, key_gain[None, :], cosine, sine, lengths, pick, count
    )
    small_got = lax.all_to_all(small, "inst", 0, 0, tiled=True)
    moved, slots, arrived, windows = land(near_got, far_got, moved, count, near)
    return tuple(
        settle(
            slots, arrived, mixed, small_got, windows, moved, queries.shape, group, count, near
        )
    )


def solution(mesh):
    return jax.shard_map(
        local,
        mesh=mesh,
        in_specs=(
            P(None, ("group", "inst"), "tp"),
            P(None, ("group", "inst"), "tp"),
            P(("group", "inst"), None, None, "tp"),
            P(("group", "inst")),
            P(("group", "inst")),
            P("tp", None),
            P("tp", None),
            P(),
        ),
        out_specs=(P(None, ("group", "inst"), "tp"), P(("group", "inst"), None, None, "tp")),
        check_vma=False,
    )
```

time: 112 us -> 78.1 us (0.70)
  Pallas kernels: 49.6 us -> 16.9 us
  blocking collectives: 27.3 us -> 0 us
  waiting for transfers between devices: 1.09 us -> 26.3 us
  local copies, waits for them, and re-layouts: 9.01 us -> 15.8 us
  starting transfers between devices: 22.2 us -> 17 us
    pallas_call x3, Pallas kernels: 40.8 us -> 8.42 us  [the longest x1 3.41 us: pack(): pl.pallas_call(functools.partial(pack_kernel, count, near), out_shape=[ja...]
    all_gather x1 -> x0, blocking collectives: 27.3 us -> none  [local(): facts = lax.all_gather(jnp.stack([destination, lengths]), 'inst')]
    ppermute x14 -> x4, waiting for transfers between devices: 1.08 us -> 26.3 us  [local(): far_got.append(lax.ppermute(block, 'inst', pairs))]
    ppermute x14 -> x4, starting transfers between devices: 22.2 us -> 5.85 us  [local(): far_got.append(lax.ppermute(block, 'inst', pairs))]
    all_to_all x0 -> x2, starting transfers between devices: none -> 11.2 us  [the longest x1 6.67 us: local(): small_got = lax.all_to_all(small, 'inst', 0, 0, tiled=True)]
    unnamed x32 -> x40, local copies, waits for them, and re-layouts: 7.69 us -> 15 us
  transfers between devices with their start and end apart: 15 -> 7, of which waited for: 2 -> 4; matrix products, arithmetic and copies ran while one was open for 3% -> 2% of each run, Pallas kernels for 40% -> 15%
where the time goes in v2:
time: 78.1 us; the launch traced here: 77.6 us
  waiting for transfers between devices  26.3 us (34%)
  starting transfers between devices  17 us (22%)
  Pallas kernels  16.9 us (22%)
  local copies, waits for them, and re-layouts  15.8 us (20%)
  other arithmetic  0.84 us (1%)
    ppermute x4, waiting for transfers between devices, local(): far_got.append(lax.ppermute(block, 'inst', pairs))  26.3 us
    unnamed x40, local copies, waits for them, and re-layouts  15 us
    all_to_all x1, starting transfers between devices, local(): small_got = lax.all_to_all(small, 'inst', 0, 0, tiled=True)  6.67 us
    ppermute x4, starting transfers between devices, local(): far_got.append(lax.ppermute(block, 'inst', pairs))  5.85 us
    pallas_call x1, Pallas kernels, attend(): pl.pallas_call(functools.partial(attend_kernel, count, block), grid=(rows...  5.66 us
    all_to_all x1, starting transfers between devices, local(): lax.all_to_all(near_blocks, 'inst', 0, 0, axis_index_groups=teams, tiled=...  4.51 us
    pallas_call x1, Pallas kernels, pack(): pl.pallas_call(functools.partial(pack_kernel, count, near), out_shape=[ja...  3.41 us
    pallas_call x1, Pallas kernels, land(): pl.pallas_call(functools.partial(land_kernel, count, near), out_shape=[ja...  2.9 us
  transfers between devices with their start and end apart: 7, of which 4 were waited for; matrix products, arithmetic and copies ran while one was open for 2% of the time, Pallas kernels for 15%

profile of v2, /device:TPU:8, one launch (start us, length us, event | category | flops | bytes accessed | tf_op | source)
XLA Modules:
  0.0 77.6 jit_solution(4260301415681019487)
XLA Ops:
  0.6 2.0 %copy-done = bf16[24,2,144,256]{3,2,1,0:T(8,128)(2,1)S(1)} copy-done((bf16[24,2,144,256]{3,2,1,0:T(8,128)(2,1)S(1)}, bf16[24,2,144,256]{3,2,1,0:T(8,128)(2,1)}, u32[]{:S(2)}) %copy-start) | copy-done | bytes 3538968
  4.0 3.4 %pack.1 = (bf16[4,304,256]{2,1,0:T(8,128)(2,1)S(1)}, bf16[304,256]{1,0:T(8,128)(2,1)S(1)}, bf16[304,256]{1,0:T(8,128)(2,1)S(1)}, bf16[304,256]{1,0:T(8,128)(2,1)...) custom-call(s32[24]{0:T(128)S(1)} %copy-done.14, s32[24]{0:T(128)S(1)} %copy-done.12, bf16[24,2,144,256]{3,2,1,0:T(8,128)(2,1)S(1)} %copy-done), custom_call_target="tpu_custom_call" | custom-call | tf_op jit(solution)/shard_map/pack/pallas_call | solution.py:81
  7.4 0.9 %copy-done.4 = bf16[4,304,256]{2,1,0:T(8,128)(2,1)} copy-done((bf16[4,304,256]{2,1,0:T(8,128)(2,1)}, bf16[4,304,256]{2,1,0:T(8,128)(2,1)S(1)}, u32[]{:S(2)}) %copy-start.4) | copy-done | bytes 622616
  9.6 0.7 copy-done.18
  10.9 4.5 %all-to-all-start = ((bf16[4,304,256]{2,1,0:T(8,128)(2,1)}), bf16[4,304,256]{2,1,0:T(8,128)(2,1)}, u32[]{:S(2)}, u32[]{:S(2)}) async-start(bf16[4,304,256]{2,1,0:T(8,128)(2,1)} %copy-done.4), calls=%async_computation | async-start | bytes 1245184 | tf_op jit(solution)/shard_map/all_to_all | solution.py:479
  15.4 1.7 %copy-done.2 = bf16[2560,512]{1,0:T(8,128)(2,1)S(1)} copy-done((bf16[2560,512]{1,0:T(8,128)(2,1)S(1)}, bf16[2560,512]{1,0:T(8,128)(2,1)}, u32[]{:S(2)}) %copy-start.2) | copy-done | bytes 2621464
  17.1 1.7 %copy-done.3 = bf16[2560,512]{1,0:T(8,128)(2,1)S(1)} copy-done((bf16[2560,512]{1,0:T(8,128)(2,1)S(1)}, bf16[2560,512]{1,0:T(8,128)(2,1)}, u32[]{:S(2)}) %copy-start.3) | copy-done | bytes 2621464
  18.9 0.9 %copy-done.5 = bf16[2,24,2560]{2,1,0:T(8,128)(2,1)S(1)} copy-done((bf16[2,24,2560]{2,1,0:T(8,128)(2,1)S(1)}, bf16[2,24,2560]{2,1,0:T(8,128)(2,1)}, u32[]{:S(2)}) %copy-start.5) | copy-done | bytes 245784
  19.8 2.8 %project.1 = (f32[48,512]{1,0:T(8,128)S(1)}, f32[48,512]{1,0:T(8,128)}) custom-call(s32[8]{0:T(128)S(1)} %get-tuple-element.22._.pick_ref, bf16[2,24,2560]{2,1,0:T(8,128)(2,1)S(1)} %copy-done.5, bf16[2560,512]{1,0:T(8,128)(2,1)S(1)} %copy-done.2, bf16[2560,512]{1,0:T(8,128)(2,1)S(1)} %copy-done.3), custom_call_target="tpu_custom_call" | custom-call | flops 251658240 | bytes 5242880 | tf_op jit(solution)/shard_map/project/pallas_call | solution.py:124
  23.9 0.7 convert_element_type.11
  24.9 0.9 %copy-done.6 = bf16[2,24,2048]{2,1,0:T(8,128)(2,1)S(1)} copy-done((bf16[2,24,2048]{2,1,0:T(8,128)(2,1)S(1)}, bf16[2,24,2048]{2,1,0:T(8,128)(2,1)}, u32[]{:S(2)}) %copy-start.6) | copy-done | bytes 196632
  25.8 0.9 %copy-done.11 = f32[48,512]{1,0:T(8,128)S(1)} copy-done((f32[48,512]{1,0:T(8,128)S(1)}, f32[48,512]{1,0:T(8,128)}, u32[]{:S(2)}) %copy-start.11) | copy-done | bytes 98328
  26.7 5.7 %attend.1 = (bf16[24,2,144,256]{3,2,1,0:T(8,128)(2,1)}, bf16[768,128]{1,0:T(8,128)(2,1)S(1)}, bf16[8,48,128]{2,1,0:T(8,128)(2,1)S(1)}) custom-call(s32[24]{0:T(128)S(1)} %copy-done.13, s32[8]{0:T(128)S(1)} %get-tuple-element.22._.pick_ref, f32[48,512]{1,0:T(8,128)S(1)} %copy-done.11, f32[48,512]{1,0:T(8,128)} %collective-permute-done.4.got_ref, ...), custom_call_target="tpu_custom_call" | custom-call | flops 113246208 | bytes 7077888 | tf_op jit(solution)/shard_map/attend/pallas_call | solution.py:270
  32.4 0.7 copy-done.7
  33.7 6.7 %all-to-all-start.1 = ((bf16[8,48,128]{2,1,0:T(8,128)(2,1)}), bf16[8,48,128]{2,1,0:T(8,128)(2,1)S(1)}, u32[]{:S(2)}, u32[]{:S(2)}) async-start(bf16[8,48,128]{2,1,0:T(8,128)(2,1)} %copy-done.9), calls=%async_computation.1 | async-start | bytes 196608 | tf_op jit(solution)/shard_map/all_to_all | solution.py:488
  40.4 2.4 %collective-permute-start = (bf16[304,256]{1,0:T(8,128)(2,1)}, bf16[304,256]{1,0:T(8,128)(2,1)S(1)}, u32[]{:S(2)}, u32[]{:S(2)}) collective-permute-start(bf16[304,256]{1,0:T(8,128)(2,1)} %copy-done.19), channel_id=1, source_target_pairs={{0,8},{2,10},{4,12},{6,14},{8,0},{10,2},{12,4},{14,6},{1,9},{3,11}... | collective-permute-start | bytes 466952 | tf_op jit(solution)/shard_map/ppermute | solution.py:475
  42.8 1.5 %collective-permute-start.1 = (bf16[304,256]{1,0:T(8,128)(2,1)}, bf16[304,256]{1,0:T(8,128)(2,1)S(1)}, u32[]{:S(2)}, u32[]{:S(2)}) collective-permute-start(bf16[304,256]{1,0:T(8,128)(2,1)} %copy-done.18), channel_id=1, source_target_pairs={{0,10},{2,8},{4,14},{6,12},{8,2},{10,0},{12,6},{14,4},{1,11},{3,9}... | collective-permute-start | bytes 466952 | tf_op jit(solution)/shard_map/ppermute | solution.py:475
  44.2 1.5 %collective-permute-start.2 = (bf16[304,256]{1,0:T(8,128)(2,1)}, bf16[304,256]{1,0:T(8,128)(2,1)S(1)}, u32[]{:S(2)}, u32[]{:S(2)}) collective-permute-start(bf16[304,256]{1,0:T(8,128)(2,1)} %copy-done.17), channel_id=1, source_target_pairs={{0,12},{2,14},{4,8},{6,10},{8,4},{10,6},{12,0},{14,2},{1,13},{3,15... | collective-permute-start | bytes 466952 | tf_op jit(solution)/shard_map/ppermute | solution.py:475
  46.2 13.6 %collective-permute-done.refs_0_ = bf16[304,256]{1,0:T(8,128)(2,1)S(1)} collective-permute-done((bf16[304,256]{1,0:T(8,128)(2,1)}, bf16[304,256]{1,0:T(8,128)(2,1)S(1)}, u32[]{:S(2)}, u32[]{:S(2)}) %collective-permute-start) | collective-permute-done | bytes 155680 | tf_op jit(solution)/shard_map/ppermute | solution.py:475
  59.9 3.3 %collective-permute-done.1.refs_1_ = bf16[304,256]{1,0:T(8,128)(2,1)S(1)} collective-permute-done((bf16[304,256]{1,0:T(8,128)(2,1)}, bf16[304,256]{1,0:T(8,128)(2,1)S(1)}, u32[]{:S(2)}, u32[]{:S(2)}) %collective-permute-start.1) | collective-permute-done | bytes 155680 | tf_op jit(solution)/shard_map/ppermute | solution.py:475
  63.2 5.8 %collective-permute-done.2.refs_2_ = bf16[304,256]{1,0:T(8,128)(2,1)S(1)} collective-permute-done((bf16[304,256]{1,0:T(8,128)(2,1)}, bf16[304,256]{1,0:T(8,128)(2,1)S(1)}, u32[]{:S(2)}, u32[]{:S(2)}) %collective-permute-start.2) | collective-permute-done | bytes 155680 | tf_op jit(solution)/shard_map/ppermute | solution.py:475
  69.0 3.5 %collective-permute-done.3.refs_3_ = bf16[304,256]{1,0:T(8,128)(2,1)S(1)} collective-permute-done((bf16[304,256]{1,0:T(8,128)(2,1)}, bf16[304,256]{1,0:T(8,128)(2,1)S(1)}, u32[]{:S(2)}, u32[]{:S(2)}) %collective-permute-start.3) | collective-permute-done | bytes 155680 | tf_op jit(solution)/shard_map/ppermute | solution.py:475
  72.5 2.9 %land.1 = (bf16[24,2,144,256]{3,2,1,0:T(8,128)(2,1)}, s32[8]{0:T(128)S(1)}, s32[8]{0:T(128)S(1)}, bf16[8,2,32,256]{3,2,1,0:T(8,128)(2,1)S(1)}) custom-call(bf16[4,304,256]{2,1,0:T(8,128)(2,1)} %all-to-all-done.near_ref, bf16[304,256]{1,0:T(8,128)(2,1)S(1)} %collective-permute-done.refs_0_, ...), custom_call_target="tpu_custom_call", output_to_operand_aliasing={{0}: (5, {})} | custom-call | tf_op jit(solution)/shard_map/land/pallas_call | solution.py:347
  75.5 2.1 %settle.1 = (bf16[2,24,2048]{2,1,0:T(8,128)(2,1)}, bf16[24,2,144,256]{3,2,1,0:T(8,128)(2,1)}) custom-call(s32[8]{0:T(128)S(1)} %get-tuple-element.26.slot_ref, s32[8]{0:T(128)S(1)} %get-tuple-element.27.length_ref, bf16[768,128]{1,0:T(8,128)(2,1)S(1)} %copy-done.8, ...), custom_call_target="tpu_custom_call", output_to_operand_aliasing={{1}: (5, {})} | custom-call | tf_op jit(solution)/shard_map/settle/pallas_call | solution.py:437
  (40 shorter events, 6.0 us)
Async XLA Ops:
  0.6 2.0 %copy-start = (bf16[24,2,144,256]{3,2,1,0:T(8,128)(2,1)S(1)}, bf16[24,2,144,256]{3,2,1,0:T(8,128)(2,1)}, u32[]{:S(2)}) copy-start(bf16[24,2,144,256]{3,2,1,0:T(8,128)(2,1)} %kv_ref.3) | copy-start | bytes 10616836
  2.6 0.7 copy-start.12
  3.3 0.7 copy-start.14
  3.9 19.3 %copy-start.13 = (s32[24]{0:T(128)S(1)}, s32[24]{0:T(128)}, u32[]{:S(2)}) copy-start(s32[24]{0:T(128)} %length_ref.3) | copy-start | bytes 292
  3.9 21.0 %copy-start.15 = (bf16[128]{0:T(256)(128)(2,1)S(1)}, bf16[128]{0:T(256)(128)(2,1)}, u32[]{:S(2)}) copy-start(bf16[128]{0:T(256)(128)(2,1)} %param.15) | copy-start | bytes 772
  7.4 0.9 %copy-start.4 = (bf16[4,304,256]{2,1,0:T(8,128)(2,1)}, bf16[4,304,256]{2,1,0:T(8,128)(2,1)S(1)}, u32[]{:S(2)}) copy-start(bf16[4,304,256]{2,1,0:T(8,128)(2,1)S(1)} %get-tuple-element.17) | copy-start | bytes 1867780
  8.2 0.7 copy-start.16
  9.6 0.7 copy-start.18
  10.2 0.7 copy-start.19
  10.9 14.0 %copy-start.1 = (bf16[24,2,144,256]{3,2,1,0:T(8,128)(2,1)S(1)}, bf16[24,2,144,256]{3,2,1,0:T(8,128)(2,1)}, u32[]{:S(2)}) copy-start(bf16[24,2,144,256]{3,2,1,0:T(8,128)(2,1)} %kv_ref.3) | copy-start | bytes 10616836
  10.9 22.8 %all-to-all-start = ((bf16[4,304,256]{2,1,0:T(8,128)(2,1)}), bf16[4,304,256]{2,1,0:T(8,128)(2,1)}, u32[]{:S(2)}, u32[]{:S(2)}) async-start(bf16[4,304,256]{2,1,0:T(8,128)(2,1)} %copy-done.4), calls=%async_computation | async-start | bytes 1245184 | tf_op jit(solution)/shard_map/all_to_all | solution.py:479
  15.4 1.7 %copy-start.2 = (bf16[2560,512]{1,0:T(8,128)(2,1)S(1)}, bf16[2560,512]{1,0:T(8,128)(2,1)}, u32[]{:S(2)}) copy-start(bf16[2560,512]{1,0:T(8,128)(2,1)} %key_ref.1) | copy-start | bytes 7864324
  17.1 1.7 %copy-start.3 = (bf16[2560,512]{1,0:T(8,128)(2,1)S(1)}, bf16[2560,512]{1,0:T(8,128)(2,1)}, u32[]{:S(2)}) copy-start(bf16[2560,512]{1,0:T(8,128)(2,1)} %value_ref.1) | copy-start | bytes 7864324
  18.9 0.9 %copy-start.5 = (bf16[2,24,2560]{2,1,0:T(8,128)(2,1)S(1)}, bf16[2,24,2560]{2,1,0:T(8,128)(2,1)}, u32[]{:S(2)}) copy-start(bf16[2,24,2560]{2,1,0:T(8,128)(2,1)} %hidden_ref.1) | copy-start | bytes 737284
  23.3 1.6 %collective-permute-start.4 = (f32[48,512]{1,0:T(8,128)}, f32[48,512]{1,0:T(8,128)}, u32[]{:S(2)}, u32[]{:S(2)}) collective-permute-start(f32[48,512]{1,0:T(8,128)} %get-tuple-element.24), channel_id=1, source_target_pairs={{0,1},{1,0},{2,3},{3,2},{4,5},{5,4},{6,7},{7,6},{8,9},{9,8},{10,11... | collective-permute-start | bytes 294920 | tf_op jit(solution)/shard_map/ppermute | solution.py:483
  24.9 0.9 %copy-start.6 = (bf16[2,24,2048]{2,1,0:T(8,128)(2,1)S(1)}, bf16[2,24,2048]{2,1,0:T(8,128)(2,1)}, u32[]{:S(2)}) copy-start(bf16[2,24,2048]{2,1,0:T(8,128)(2,1)} %query_ref.1) | copy-start | bytes 589828
  25.8 0.9 %copy-start.11 = (f32[48,512]{1,0:T(8,128)S(1)}, f32[48,512]{1,0:T(8,128)}, u32[]{:S(2)}) copy-start(f32[48,512]{1,0:T(8,128)} %copy-done.10) | copy-start | bytes 294916
  32.4 0.7 copy-start.7
  33.7 41.7 %copy-start.8 = (bf16[768,128]{1,0:T(8,128)(2,1)S(1)}, bf16[768,128]{1,0:T(8,128)(2,1)}, u32[]{:S(2)}) copy-start(bf16[768,128]{1,0:T(8,128)(2,1)} %copy-done.7) | copy-start | bytes 589828
  33.7 41.7 %all-to-all-start.1 = ((bf16[8,48,128]{2,1,0:T(8,128)(2,1)}), bf16[8,48,128]{2,1,0:T(8,128)(2,1)S(1)}, u32[]{:S(2)}, u32[]{:S(2)}) async-start(bf16[8,48,128]{2,1,0:T(8,128)(2,1)} %copy-done.9), calls=%async_computation.1 | async-start | bytes 196608 | tf_op jit(solution)/shard_map/all_to_all | solution.py:488
  40.4 19.5 %collective-permute-start = (bf16[304,256]{1,0:T(8,128)(2,1)}, bf16[304,256]{1,0:T(8,128)(2,1)S(1)}, u32[]{:S(2)}, u32[]{:S(2)}) collective-permute-start(bf16[304,256]{1,0:T(8,128)(2,1)} %copy-done.19), channel_id=1, source_target_pairs={{0,8},{2,10},{4,12},{6,14},{8,0},{10,2},{12,4},{14,6},{1,9},{3,11}... | collective-permute-start | bytes 466952 | tf_op jit(solution)/shard_map/ppermute | solution.py:475
  42.8 20.5 %collective-permute-start.1 = (bf16[304,256]{1,0:T(8,128)(2,1)}, bf16[304,256]{1,0:T(8,128)(2,1)S(1)}, u32[]{:S(2)}, u32[]{:S(2)}) collective-permute-start(bf16[304,256]{1,0:T(8,128)(2,1)} %copy-done.18), channel_id=1, source_target_pairs={{0,10},{2,8},{4,14},{6,12},{8,2},{10,0},{12,6},{14,4},{1,11},{3,9}... | collective-permute-start | bytes 466952 | tf_op jit(solution)/shard_map/ppermute | solution.py:475
  44.2 24.8 %collective-permute-start.2 = (bf16[304,256]{1,0:T(8,128)(2,1)}, bf16[304,256]{1,0:T(8,128)(2,1)S(1)}, u32[]{:S(2)}, u32[]{:S(2)}) collective-permute-start(bf16[304,256]{1,0:T(8,128)(2,1)} %copy-done.17), channel_id=1, source_target_pairs={{0,12},{2,14},{4,8},{6,10},{8,4},{10,6},{12,0},{14,2},{1,13},{3,15... | collective-permute-start | bytes 466952 | tf_op jit(solution)/shard_map/ppermute | solution.py:475
  45.7 26.9 %collective-permute-start.3 = (bf16[304,256]{1,0:T(8,128)(2,1)}, bf16[304,256]{1,0:T(8,128)(2,1)S(1)}, u32[]{:S(2)}, u32[]{:S(2)}) collective-permute-start(bf16[304,256]{1,0:T(8,128)(2,1)} %copy-done.16), channel_id=1, source_target_pairs={{0,14},{2,12},{4,10},{6,8},{8,6},{10,4},{12,2},{14,0},{1,15},{3,13... | collective-permute-start | bytes 466952 | tf_op jit(solution)/shard_map/ppermute | solution.py:475
  (3 other events, 1.9 us)

commit v3 on v2

--- a/solution.py
+++ b/solution.py
@@ -11,8 +11,11 @@
 HD = 128
 ROPE_BASE = 1000000.0
 NORM_EPS = 1e-06
-VMEM_LIMIT = 40 * 1024 * 1024
+VMEM_LIMIT = 62 * 1024 * 1024
+SMALL_LIMIT = 40 * 1024 * 1024
 FACTS = 16
+LIGHT = pl.CostEstimate(flops=1, bytes_accessed=1, transcendentals=0)
+HEAVY = pl.CostEstimate(flops=1 << 36, bytes_accessed=1 << 28, transcendentals=0)
 WINDOW = 32
 
 
@@ -34,10 +37,10 @@
 
 
 def pack_kernel(count, near, dest_ref, length_ref, kv_ref, near_ref, *refs):
-    far_refs, pick_ref, sems = refs[: count - near], refs[count - near], refs[count - near + 1]
+    far_refs = refs[: count - near]
+    pick_ref, buffer, in_sems, out_sems = refs[count - near :]
     rows = dest_ref.shape[0]
-    capacity = kv_ref.shape[2]
-    lanes = kv_ref.shape[3]
+    capacity, lanes = kv_ref.shape[2:]
     me = lax.axis_index("inst")
     for peer in range(count):
         pick_ref[peer] = 0
@@ -48,28 +51,36 @@
 
     lax.fori_loop(0, rows, note, 0)
     order = list(range(near, count)) + list(range(near))
-    copies = []
+    fetches, stores = {}, {}
     for piece in order:
         row = pick_ref[peer_of(me, piece, near, True)]
-        block = near_ref.at[piece] if piece < near else far_refs[piece - near]
-        for which in range(2):
-            copy = pltpu.make_async_copy(
+        fetches[piece] = [
+            pltpu.make_async_copy(
                 kv_ref.at[row, which],
-                block.at[pl.ds(which * capacity, capacity)],
-                sems.at[piece, which],
+                buffer.at[piece, pl.ds(which * capacity, capacity)],
+                in_sems.at[piece, which],
             )
+            for which in range(2)
+        ]
+        for copy in fetches[piece]:
             copy.start()
-            copies.append(copy)
+    line = lax.broadcasted_iota(jnp.int32, (FACTS, lanes), 0)
     for piece in order:
         peer = peer_of(me, piece, near, True)
         row = pick_ref[peer]
         slot = jnp.where(dest_ref[row] // rows == peer, dest_ref[row] % rows, -1)
-        block = near_ref.at[piece] if piece < near else far_refs[piece - near]
-        line = lax.broadcasted_iota(jnp.int32, (FACTS, lanes), 0)
         facts = jnp.where(line == 0, slot, length_ref[row])
-        block[2 * capacity :, :] = facts.astype(jnp.float32).astype(jnp.bfloat16)
-    for copy in copies:
-        copy.wait()
+        buffer[piece, 2 * capacity :, :] = facts.astype(jnp.float32).astype(jnp.bfloat16)
+        for copy in fetches[piece]:
+            copy.wait()
+        stores[piece] = pltpu.make_async_copy(
+            buffer.at[piece],
+            near_ref.at[piece] if piece < near else far_refs[piece - near],
+            out_sems.at[piece],
+        )
+        stores[piece].start()
+    for piece in order:
+        stores[piece].wait()
 
 
 def pack(kv_cache, destination, lengths, count, near):
@@ -77,22 +88,28 @@
     width = kv_cache.shape[3]
     far = jax.ShapeDtypeStruct((height, width), kv_cache.dtype)
     smem = pl.BlockSpec(memory_space=pltpu.SMEM)
-    vmem = pl.BlockSpec(memory_space=pltpu.VMEM)
+    hbm = pl.BlockSpec(memory_space=pl.ANY)
     outs = pl.pallas_call(
         functools.partial(pack_kernel, count, near),
         out_shape=[jax.ShapeDtypeStruct((near, height, width), kv_cache.dtype)]
         + [far] * (count - near)
         + [jax.ShapeDtypeStruct((count,), jnp.int32)],
-        in_specs=[smem, smem, pl.BlockSpec(memory_space=pltpu.HBM)],
-        out_specs=[vmem] * (count - near + 1) + [smem],
-        scratch_shapes=[pltpu.SemaphoreType.DMA((count, 2))],
+        in_specs=[smem, smem, hbm],
+        out_specs=[hbm] * (count - near + 1) + [smem],
+        scratch_shapes=[
+            pltpu.VMEM((count, height, width), kv_cache.dtype),
+            pltpu.SemaphoreType.DMA((count, 2)),
+            pltpu.SemaphoreType.DMA((count,)),
+        ],
         compiler_params=pltpu.CompilerParams(vmem_limit_bytes=VMEM_LIMIT),
+        cost_estimate=LIGHT,
         name="pack",
     )(destination, lengths, kv_cache)
     return outs[0], outs[1:-1], outs[-1]
 
 
-def project_kernel(_, hidden_ref, key_ref, value_ref, own_ref, other_ref, total):
+def project_kernel(_, hidden_ref, key_ref, value_ref, own_ref, other_ref, near_ref, total):
+    del near_ref
     step = pl.program_id(0)
     width = key_ref.shape[1]
 
@@ -115,7 +132,7 @@
             ref[:, half:] = total[:, pl.ds(pl.multiple_of(width + at, half), half)]
 
 
-def project(hidden_new, key_weight, value_weight, pick):
+def project(hidden_new, key_weight, value_weight, near_blocks):
     steps, rows, depth = hidden_new.shape
     width = key_weight.shape[1]
     part = depth // 5
@@ -124,23 +141,34 @@
     return pl.pallas_call(
         project_kernel,
         grid=(depth // part,),
-        out_shape=[shape, shape],
+        out_shape=[shape, shape, jax.ShapeDtypeStruct(near_blocks.shape, near_blocks.dtype)],
         in_specs=[
-            pl.BlockSpec(memory_space=pltpu.SMEM),
+            pl.BlockSpec(memory_space=pl.ANY),
             pl.BlockSpec((steps, rows, part), lambda i: (0, 0, i)),
             pl.BlockSpec((part, width), lambda i: (i, 0)),
             pl.BlockSpec((part, width), lambda i: (i, 0)),
         ],
-        out_specs=[whole, whole],
+        out_specs=[whole, whole, pl.BlockSpec(memory_space=pl.ANY)],
         scratch_shapes=[pltpu.VMEM((steps * rows, 2 * width), jnp.float32)],
         compiler_params=pltpu.CompilerParams(vmem_limit_bytes=VMEM_LIMIT),
-        cost_estimate=pl.CostEstimate(
-            flops=4 * steps * rows * depth * width,
-            bytes_accessed=4 * depth * width,
-            transcendentals=0,
-        ),
+        input_output_aliases={0: 2},
+        cost_estimate=LIGHT,
         name="project",
-    )(pick, hidden_new, key_weight, value_weight)
+    )(near_blocks, hidden_new, key_weight, value_weight)
+
+
+def rotation(length_ref, steps, rows):
+    half = HD // 2
+    line = lax.broadcasted_iota(jnp.int32, (steps * rows, HD), 0)
+    lane = lax.broadcasted_iota(jnp.int32, (steps * rows, HD), 1)
+    position = jnp.zeros((steps * rows, HD), jnp.int32)
+    for step in range(steps):
+        for row in range(rows):
+            position = jnp.where(line == step * rows + row, length_ref[row] + step, position)
+    order = (lane % half).astype(jnp.float32)
+    angle = position.astype(jnp.float32) * jnp.exp(-math.log(ROPE_BASE) * 2.0 * order / HD)
+    sine = jnp.sin(angle)
+    return jnp.cos(angle), jnp.where(lane < half, -sine, sine)
 
 
 def attend_kernel(
@@ -151,8 +179,6 @@
     own_ref,
     got_ref,
     gain_ref,
-    cos_ref,
-    sin_ref,
     query_ref,
     kv_ref,
     moved_ref,
@@ -179,6 +205,7 @@
     @pl.when(part == 0)
     def _():
         raw = own_ref[...] + got_ref[...]
+        cosine, sine = rotation(length_ref, steps, rows)
         gain = gain_ref[...].astype(jnp.float32)
         for head in range(heads):
             at = slice(head * HD, (head + 1) * HD)
@@ -186,7 +213,7 @@
             mean = jnp.mean(piece * piece, axis=-1, keepdims=True)
             piece = piece * lax.rsqrt(mean + NORM_EPS) * gain
             swapped = jnp.concatenate([piece[:, HD // 2 :], piece[:, : HD // 2]], axis=1)
-            turned = piece * cos_ref[...] + swapped * sin_ref[...]
+            turned = piece * cosine + swapped * sine
             fresh[0, :, at] = turned.astype(jnp.bfloat16).astype(jnp.float32)
         fresh[1] = raw[:, lanes:].astype(jnp.bfloat16).astype(jnp.float32)
         for step in range(steps):
@@ -256,7 +283,7 @@
             small_ref[peer, per_row:, :] = jnp.concatenate(news, axis=0).astype(jnp.bfloat16)
 
 
-def attend(kv_cache, queries, own, got, gain, cosine, sine, lengths, pick, count):
+def attend(kv_cache, queries, own, got, gain, lengths, pick, count):
     steps, rows, query_width = queries.shape
     capacity, lanes = kv_cache.shape[2:]
     heads = lanes // HD
@@ -275,7 +302,7 @@
             jax.ShapeDtypeStruct((rows * per_row, HD), jnp.bfloat16),
             small,
         ],
-        in_specs=[smem, smem, vmem, vmem, vmem, vmem, vmem, vmem, cache_block],
+        in_specs=[smem, smem, vmem, vmem, vmem, vmem, cache_block],
         out_specs=[cache_block, vmem, vmem],
         scratch_shapes=[
             pltpu.VMEM((2, steps * rows, lanes), jnp.float32),
@@ -283,13 +310,9 @@
             pltpu.VMEM((rows * per_row, HD), jnp.float32),
         ],
         compiler_params=pltpu.CompilerParams(vmem_limit_bytes=VMEM_LIMIT),
-        cost_estimate=pl.CostEstimate(
-            flops=4 * rows * per_row * capacity * lanes,
-            bytes_accessed=4 * kv_cache.size,
-            transcendentals=rows * per_row * capacity,
-        ),
+        cost_estimate=LIGHT,
         name="attend",
-    )(lengths, pick, own, got, gain, cosine, sine, queries, kv_cache)
+    )(lengths, pick, own, got, gain, queries, kv_cache)
 
 
 def window_start(length, capacity):
@@ -359,7 +382,8 @@
             pltpu.SemaphoreType.DMA((count,)),
         ],
         input_output_aliases={count - near + 1: 0},
-        compiler_params=pltpu.CompilerParams(vmem_limit_bytes=VMEM_LIMIT),
+        compiler_params=pltpu.CompilerParams(vmem_limit_bytes=SMALL_LIMIT),
+        cost_estimate=HEAVY,
         name="land",
     )(near_got, *far_got, moved)
 
@@ -448,22 +472,13 @@
             pltpu.SemaphoreType.DMA((count,)),
         ],
         input_output_aliases={5: 1},
-        compiler_params=pltpu.CompilerParams(vmem_limit_bytes=VMEM_LIMIT),
+        compiler_params=pltpu.CompilerParams(vmem_limit_bytes=SMALL_LIMIT),
+        cost_estimate=LIGHT,
         name="settle",
     )(slots, lengths, mixed, small, windows, moved)
 
 
-def rotation(lengths, steps):
-    half = HD // 2
-    inverse = jnp.exp(-math.log(ROPE_BASE) * 2.0 * jnp.arange(half, dtype=jnp.float32) / HD)
-    positions = (lengths[None, :] + jnp.arange(steps, dtype=jnp.int32)[:, None]).reshape(-1)
-    angles = positions.astype(jnp.float32)[:, None] * inverse
-    cosine, sine = jnp.cos(angles), jnp.sin(angles)
-    return jnp.concatenate([cosine, cosine], axis=1), jnp.concatenate([-sine, sine], axis=1)
-
-
 def local(hidden_new, queries, kv_cache, lengths, destination, key_weight, value_weight, key_gain):
-    steps = queries.shape[0]
     group = queries.shape[2] // kv_cache.shape[3]
     count = lax.axis_size("inst")
     near = near_size(count)
@@ -473,17 +488,16 @@
     for piece, block in enumerate(far_blocks, near):
         pairs = [(i, int(peer_to(i, piece, count))) for i in range(count)]
         far_got.append(lax.ppermute(block, "inst", pairs))
+    own, other, near_blocks = project(hidden_new, key_weight, value_weight, near_blocks)
     near_got = near_blocks
     if near > 1:
         teams = [list(range(i, i + near)) for i in range(0, count, near)]
         near_got = lax.all_to_all(
             near_blocks, "inst", 0, 0, axis_index_groups=teams, tiled=True
         )
-    own, other = project(hidden_new, key_weight, value_weight, pick)
     got = lax.ppermute(other, "tp", [(0, 1), (1, 0)])
-    cosine, sine = rotation(lengths, steps)
     moved, mixed, small = attend(
-        kv_cache, queries, own, got, key_gain[None, :], cosine, sine, lengths, pick, count
+        kv_cache, queries, own, got, key_gain[None, :], lengths, pick, count
     )
     small_got = lax.all_to_all(small, "inst", 0, 0, tiled=True)
     moved, slots, arrived, windows = land(near_got, far_got, moved, count, near)

time: 78.1 us -> 50.8 us (0.65)
  the two profiles are of different devices: /device:TPU:8 before, /device:TPU:0 now
where the time goes in v3:
time: 50.8 us; the launch traced here: 50 us
  Pallas kernels  20.1 us (40%)
  starting transfers between devices  19.1 us (38%)
  waiting for transfers between devices  9.4 us (19%)
  between operations  0.7 us (1%)
  local copies, waits for them, and re-layouts  0.67 us (1%)
    ppermute x4, starting transfers between devices, local(): far_got.append(lax.ppermute(block, 'inst', pairs))  7.94 us
    pallas_call x1, Pallas kernels, attend(): pl.pallas_call(functools.partial(attend_kernel, count, block), grid=(rows...  6.86 us
    all_to_all x1, starting transfers between devices, local(): small_got = lax.all_to_all(small, 'inst', 0, 0, tiled=True)  5.94 us
    pallas_call x1, Pallas kernels, project(): pl.pallas_call(project_kernel, grid=(depth // part,), out_shape=[shape, s...  5.38 us
    all_to_all x1, starting transfers between devices, local(): lax.all_to_all(near_blocks, 'inst', 0, 0, axis_index_groups=teams, tiled=...  5.25 us
    all_to_all x1, waiting for transfers between devices, local(): small_got = lax.all_to_all(small, 'inst', 0, 0, tiled=True)  5.14 us
    pallas_call x1, Pallas kernels, pack(): pl.pallas_call(functools.partial(pack_kernel, count, near), out_shape=[ja...  3.9 us
    ppermute x4, waiting for transfers between devices, local(): far_got.append(lax.ppermute(block, 'inst', pairs))  2.75 us
  transfers between devices with their start and end apart: 7, of which 3 were waited for; matrix products, arithmetic and copies ran while one was open for 0% of the time, Pallas kernels for 17%

profile of v3, /device:TPU:0, one launch (start us, length us, event | category | flops | bytes accessed | tf_op | source)
XLA Modules:
  0.0 50.0 jit_solution(7553125435201230178)
XLA Ops:
  0.6 3.9 %pack.1 = (bf16[4,304,256]{2,1,0:T(8,128)(2,1)}, bf16[304,256]{1,0:T(8,128)(2,1)}, bf16[304,256]{1,0:T(8,128)(2,1)}, bf16[304,256]{1,0:T(8,128)(2,1)}, bf16[304,256]{1,0:T(8,128)(2,1)}, /*index=5*/s32[8]{0:T(128)}) custom-call(s32[24]{0:T(128)} %dest_ref.1, s32[24]{0:T(128)} %length_ref.3, bf16[24,2,144,256]{3,2,1,0:T(8,128)(2,1)} %kv_ref.3), custom_call_target="tpu_custom_call" | custom-call | flops 1 | bytes 1 | tf_op jit(solution)/shard_map/pack/pallas_call | solution.py:92
  4.5 0.0 copy-start.5
  4.6 0.0 copy-start.4
  4.6 0.0 copy-start.3
  4.6 0.0 copy-start.2
  4.6 5.4 %project.1 = (f32[48,512]{1,0:T(8,128)}, f32[48,512]{1,0:T(8,128)}, bf16[4,304,256]{2,1,0:T(8,128)(2,1)}) custom-call(bf16[4,304,256]{2,1,0:T(8,128)(2,1)} %get-tuple-element.18._, bf16[2,24,2560]{2,1,0:T(8,128)(2,1)} %hidden_ref.1, bf16[2560,512]{1,0:T(8,128)(2,1)} %key_ref.1, bf16[2560,512]{1,0:T(8,128)(2,1)} %value_ref.1), custom_call_target="tpu_custom_call", output_to_operand_aliasing={{2}: (0, {})} | custom-call | flops 1 | bytes 1 | tf_op jit(solution)/shard_map/project/pallas_call | solution.py:141
  10.0 5.2 %all-to-all-start = ((bf16[4,304,256]{2,1,0:T(8,128)(2,1)}), bf16[4,304,256]{2,1,0:T(8,128)(2,1)S(1)}, u32[]{:S(2)}, u32[]{:S(2)}) async-start(bf16[4,304,256]{2,1,0:T(8,128)(2,1)} %get-tuple-element.19), calls=%async_computation | async-start | bytes 1245184 | tf_op jit(solution)/shard_map/all_to_all | solution.py:495
  15.2 2.6 %collective-permute-start = (bf16[304,256]{1,0:T(8,128)(2,1)S(1)}, bf16[304,256]{1,0:T(8,128)(2,1)S(1)}, u32[]{:S(2)}, u32[]{:S(2)}) collective-permute-start(bf16[304,256]{1,0:T(8,128)(2,1)S(1)} %copy-done.5), channel_id=1, source_target_pairs={{0,8},{2,10},{4,12},{6,14},{8,0},{10,2},{12,4},{14,6},{1,9},{3,11}... | collective-permute-start | bytes 466952 | tf_op jit(solution)/shard_map/ppermute | solution.py:490
  17.8 1.8 %collective-permute-start.1 = (bf16[304,256]{1,0:T(8,128)(2,1)S(1)}, bf16[304,256]{1,0:T(8,128)(2,1)S(1)}, u32[]{:S(2)}, u32[]{:S(2)}) collective-permute-start(bf16[304,256]{1,0:T(8,128)(2,1)S(1)} %copy-done.4), channel_id=1, source_target_pairs={{0,10},{2,8},{4,14},{6,12},{8,2},{10,0},{12,6},{14,4},{1,11},{3,9}... | collective-permute-start | bytes 466952 | tf_op jit(solution)/shard_map/ppermute | solution.py:490
  19.6 3.5 %collective-permute-start.2 = (bf16[304,256]{1,0:T(8,128)(2,1)S(1)}, bf16[304,256]{1,0:T(8,128)(2,1)S(1)}, u32[]{:S(2)}, u32[]{:S(2)}) collective-permute-start(bf16[304,256]{1,0:T(8,128)(2,1)S(1)} %copy-done.3), channel_id=1, source_target_pairs={{0,12},{2,14},{4,8},{6,10},{8,4},{10,6},{12,0},{14,2},{1,13},{3,15... | collective-permute-start | bytes 466952 | tf_op jit(solution)/shard_map/ppermute | solution.py:490
  23.1 0.1 collective-permute-start.3
  23.2 0.0 collective-permute-start.4
  23.2 1.5 %collective-permute-done.4.got_ref = f32[48,512]{1,0:T(8,128)S(1)} collective-permute-done((f32[48,512]{1,0:T(8,128)}, f32[48,512]{1,0:T(8,128)S(1)}, u32[]{:S(2)}, u32[]{:S(2)}) %collective-permute-start.4) | collective-permute-done | bytes 98336 | tf_op jit(solution)/shard_map/ppermute | solution.py:498
  24.7 0.6 %copy-done.1 = f32[48,512]{1,0:T(8,128)} copy-done((f32[48,512]{1,0:T(8,128)}, f32[48,512]{1,0:T(8,128)S(1)}, u32[]{:S(2)}) %copy-start.1) | copy-done | bytes 98328
  25.3 6.9 %attend.1 = (bf16[24,2,144,256]{3,2,1,0:T(8,128)(2,1)}, bf16[768,128]{1,0:T(8,128)(2,1)}, bf16[8,48,128]{2,1,0:T(8,128)(2,1)}) custom-call(s32[24]{0:T(128)} %length_ref.3, s32[8]{0:T(128)} %get-tuple-element.24.pick_ref, f32[48,512]{1,0:T(8,128)} %get-tuple-element.25.own_ref, f32[48,512]{1,0:T(8,128)} %copy-done.1, bf16[1,128]{1,0:T(2,128)(2,1)} %bitcast.1, ...), custom_call_target="tpu_custom_call" | custom-call | flops 1 | bytes 1 | tf_op jit(solution)/shard_map/attend/pallas_call | solution.py:297
  32.2 0.0 all-to-all-done.near_ref
  32.2 5.9 %all-to-all-start.1 = ((bf16[8,48,128]{2,1,0:T(8,128)(2,1)}), bf16[8,48,128]{2,1,0:T(8,128)(2,1)S(1)}, u32[]{:S(2)}, u32[]{:S(2)}) async-start(bf16[8,48,128]{2,1,0:T(8,128)(2,1)} %get-tuple-element.31), calls=%async_computation.1 | async-start | bytes 196608 | tf_op jit(solution)/shard_map/all_to_all | solution.py:502
  38.1 0.0 collective-permute-done.refs_0_
  38.2 2.7 %collective-permute-done.1.refs_1_ = bf16[304,256]{1,0:T(8,128)(2,1)S(1)} collective-permute-done((bf16[304,256]{1,0:T(8,128)(2,1)S(1)}, bf16[304,256]{1,0:T(8,128)(2,1)S(1)}, u32[]{:S(2)}, u32[]{:S(2)}) %collective-permute-start.1) | collective-permute-done | bytes 155680 | tf_op jit(solution)/shard_map/ppermute | solution.py:490
  40.9 0.0 collective-permute-done.2.refs_2_
  40.9 0.0 collective-permute-done.3.refs_3_
  40.9 1.8 %land.1 = (bf16[24,2,144,256]{3,2,1,0:T(8,128)(2,1)}, s32[8]{0:T(128)S(1)}, s32[8]{0:T(128)S(1)}, bf16[8,2,32,256]{3,2,1,0:T(8,128)(2,1)S(1)}) custom-call(bf16[4,304,256]{2,1,0:T(8,128)(2,1)S(1)} %all-to-all-done.near_ref, bf16[304,256]{1,0:T(8,128)(2,1)S(1)} %collective-permute-done.refs_0_, ...), custom_call_target="tpu_custom_call", output_to_operand_aliasing={{0}: (5, {})} | custom-call | flops 68719476736 | bytes 268435456 | tf_op jit(solution)/shard_map/land/pallas_call | solution.py:370
  42.7 5.1 %all-to-all-done.1.small_ref = bf16[8,48,128]{2,1,0:T(8,128)(2,1)S(1)} async-done(((bf16[8,48,128]{2,1,0:T(8,128)(2,1)}), bf16[8,48,128]{2,1,0:T(8,128)(2,1)S(1)}, u32[]{:S(2)}, u32[]{:S(2)}) %all-to-all-start.1) | async-done | bytes 98336 | tf_op jit(solution)/shard_map/all_to_all | solution.py:502
  47.9 2.1 %settle.1 = (bf16[2,24,2048]{2,1,0:T(8,128)(2,1)}, bf16[24,2,144,256]{3,2,1,0:T(8,128)(2,1)}) custom-call(s32[8]{0:T(128)S(1)} %get-tuple-element.28.slot_ref, s32[8]{0:T(128)S(1)} %get-tuple-element.29.length_ref, bf16[768,128]{1,0:T(8,128)(2,1)S(1)} %copy-done, bf16[8,48,128]{2,1,0:T(8,128)(2,1)S(1)} %all-to-all-done.1.small_ref, ...), custom_call_target="tpu_custom_call", output_to_operand_aliasing={{1}: (5, {})} | custom-call | flops 1 | bytes 1 | tf_op jit(solution)/shard_map/settle/pallas_call | solution.py:461
  (7 shorter events, 0.0 us)
Async XLA Ops:
  4.5 10.7 %copy-start.5 = (bf16[304,256]{1,0:T(8,128)(2,1)S(1)}, bf16[304,256]{1,0:T(8,128)(2,1)}, u32[]{:S(2)}) copy-start(bf16[304,256]{1,0:T(8,128)(2,1)} %get-tuple-element.20) | copy-start | bytes 466948
  4.6 13.3 %copy-start.4 = (bf16[304,256]{1,0:T(8,128)(2,1)S(1)}, bf16[304,256]{1,0:T(8,128)(2,1)}, u32[]{:S(2)}) copy-start(bf16[304,256]{1,0:T(8,128)(2,1)} %get-tuple-element.21) | copy-start | bytes 466948
  4.6 15.0 %copy-start.3 = (bf16[304,256]{1,0:T(8,128)(2,1)S(1)}, bf16[304,256]{1,0:T(8,128)(2,1)}, u32[]{:S(2)}) copy-start(bf16[304,256]{1,0:T(8,128)(2,1)} %get-tuple-element.22) | copy-start | bytes 466948
  4.6 18.5 %copy-start.2 = (bf16[304,256]{1,0:T(8,128)(2,1)S(1)}, bf16[304,256]{1,0:T(8,128)(2,1)}, u32[]{:S(2)}) copy-start(bf16[304,256]{1,0:T(8,128)(2,1)} %get-tuple-element.23) | copy-start | bytes 466948
  10.0 22.2 %all-to-all-start = ((bf16[4,304,256]{2,1,0:T(8,128)(2,1)}), bf16[4,304,256]{2,1,0:T(8,128)(2,1)S(1)}, u32[]{:S(2)}, u32[]{:S(2)}) async-start(bf16[4,304,256]{2,1,0:T(8,128)(2,1)} %get-tuple-element.19), calls=%async_computation | async-start | bytes 1245184 | tf_op jit(solution)/shard_map/all_to_all | solution.py:495
  15.2 22.9 %collective-permute-start = (bf16[304,256]{1,0:T(8,128)(2,1)S(1)}, bf16[304,256]{1,0:T(8,128)(2,1)S(1)}, u32[]{:S(2)}, u32[]{:S(2)}) collective-permute-start(bf16[304,256]{1,0:T(8,128)(2,1)S(1)} %copy-done.5), channel_id=1, source_target_pairs={{0,8},{2,10},{4,12},{6,14},{8,0},{10,2},{12,4},{14,6},{1,9},{3,11}... | collective-permute-start | bytes 466952 | tf_op jit(solution)/shard_map/ppermute | solution.py:490
  17.8 23.1 %collective-permute-start.1 = (bf16[304,256]{1,0:T(8,128)(2,1)S(1)}, bf16[304,256]{1,0:T(8,128)(2,1)S(1)}, u32[]{:S(2)}, u32[]{:S(2)}) collective-permute-start(bf16[304,256]{1,0:T(8,128)(2,1)S(1)} %copy-done.4), channel_id=1, source_target_pairs={{0,10},{2,8},{4,14},{6,12},{8,2},{10,0},{12,6},{14,4},{1,11},{3,9}... | collective-permute-start | bytes 466952 | tf_op jit(solution)/shard_map/ppermute | solution.py:490
  19.6 21.3 %collective-permute-start.2 = (bf16[304,256]{1,0:T(8,128)(2,1)S(1)}, bf16[304,256]{1,0:T(8,128)(2,1)S(1)}, u32[]{:S(2)}, u32[]{:S(2)}) collective-permute-start(bf16[304,256]{1,0:T(8,128)(2,1)S(1)} %copy-done.3), channel_id=1, source_target_pairs={{0,12},{2,14},{4,8},{6,10},{8,4},{10,6},{12,0},{14,2},{1,13},{3,15... | collective-permute-start | bytes 466952 | tf_op jit(solution)/shard_map/ppermute | solution.py:490
  23.1 17.8 %collective-permute-start.3 = (bf16[304,256]{1,0:T(8,128)(2,1)S(1)}, bf16[304,256]{1,0:T(8,128)(2,1)S(1)}, u32[]{:S(2)}, u32[]{:S(2)}) collective-permute-start(bf16[304,256]{1,0:T(8,128)(2,1)S(1)} %copy-done.2), channel_id=1, source_target_pairs={{0,14},{2,12},{4,10},{6,8},{8,6},{10,4},{12,2},{14,0},{1,15},{3,13... | collective-permute-start | bytes 466952 | tf_op jit(solution)/shard_map/ppermute | solution.py:490
  23.2 1.5 %collective-permute-start.4 = (f32[48,512]{1,0:T(8,128)}, f32[48,512]{1,0:T(8,128)S(1)}, u32[]{:S(2)}, u32[]{:S(2)}) collective-permute-start(f32[48,512]{1,0:T(8,128)} %get-tuple-element.26), channel_id=1, source_target_pairs={{0,1},{1,0},{2,3},{3,2},{4,5},{5,4},{6,7},{7,6},{8,9},{9,8},{10,11... | collective-permute-start | bytes 294920 | tf_op jit(solution)/shard_map/ppermute | solution.py:498
  24.7 0.6 %copy-start.1 = (f32[48,512]{1,0:T(8,128)}, f32[48,512]{1,0:T(8,128)S(1)}, u32[]{:S(2)}) copy-start(f32[48,512]{1,0:T(8,128)S(1)} %collective-permute-done.4.got_ref) | copy-start | bytes 294916
  32.2 15.7 %all-to-all-start.1 = ((bf16[8,48,128]{2,1,0:T(8,128)(2,1)}), bf16[8,48,128]{2,1,0:T(8,128)(2,1)S(1)}, u32[]{:S(2)}, u32[]{:S(2)}) async-start(bf16[8,48,128]{2,1,0:T(8,128)(2,1)} %get-tuple-element.31), calls=%async_computation.1 | async-start | bytes 196608 | tf_op jit(solution)/shard_map/all_to_all | solution.py:502
  40.9 7.0 %copy-start = (bf16[768,128]{1,0:T(8,128)(2,1)S(1)}, bf16[768,128]{1,0:T(8,128)(2,1)}, u32[]{:S(2)}) copy-start(bf16[768,128]{1,0:T(8,128)(2,1)} %get-tuple-element.30.mixed_ref) | copy-start | bytes 589828

commit v4 on v3

v4 whole, which is shorter than its diff:
```python
import functools
import math

import jax
import jax.numpy as jnp
from jax import lax
from jax.experimental import pallas as pl
from jax.experimental.pallas import tpu as pltpu
from jax.sharding import PartitionSpec as P

HD = 128
ROPE_BASE = 1000000.0
NORM_EPS = 1e-06
VMEM_LIMIT = 62 * 1024 * 1024
PACK_LIMIT = 59 * 1024 * 1024
SMALL_LIMIT = 40 * 1024 * 1024
LIGHT = pl.CostEstimate(flops=1, bytes_accessed=1, transcendentals=0)
HEAVY = pl.CostEstimate(flops=1 << 36, bytes_accessed=1 << 28, transcendentals=0)
TILE = 16
WINDOW = 32


def quotient(value, divisor, bound):
    factor = -(-(1 << 16) // divisor)
    if bound * factor < 1 << 31 and all(
        (x * factor) >> 16 == x // divisor for x in range(bound)
    ):
        return (value * factor) >> 16
    return value // divisor


def peer_to(index, shift, count, paired=None):
    if count & (count - 1) == 0:
        return index ^ (shift if paired is None else paired)
    return (index + shift) % count


def near_size(count):
    return 4 if count % 4 == 0 and count & (count - 1) == 0 else 1


def peer_of(me, piece, near, to):
    count = lax.axis_size("inst")
    if piece < near:
        return me // near * near + piece
    return peer_to(me, piece, count) if to else peer_to(me, count - piece, count, piece)


def pack_kernel(count, near, dest_ref, length_ref, kv_ref, near_ref, *refs):
    far_refs = refs[: count - near]
    pick_ref, sems = refs[count - near :]
    rows = dest_ref.shape[0]
    capacity, lanes = kv_ref.shape[2:]
    me = lax.axis_index("inst")
    for peer in range(count):
        pick_ref[peer] = 0
    for row in range(rows):
        pick_ref[quotient(dest_ref[row], rows, rows * count)] = row
    order = list(range(near)) + list(range(near, count))
    blocks = [near_ref.at[piece] for piece in range(near)] + list(far_refs)
    copies = {}
    for piece in order:
        row = pick_ref[peer_of(me, piece, near, True)]
        copies[piece] = pltpu.make_async_copy(kv_ref.at[row], blocks[piece], sems.at[piece])
        copies[piece].start()
    tile = (TILE, lanes)
    last = lax.broadcasted_iota(jnp.int32, tile, 0) == TILE - 1
    first_lanes = lax.broadcasted_iota(jnp.int32, tile, 1) < HD
    for piece in order:
        peer = peer_of(me, piece, near, True)
        row = pick_ref[peer]
        slot = dest_ref[row] - peer * rows
        slot = jnp.where((slot >= 0) & (slot < rows), slot, -1)
        facts = jnp.where(first_lanes, slot, length_ref[row]).astype(jnp.float32)
        copies[piece].wait()
        end = blocks[piece][0, capacity - TILE :, :].astype(jnp.float32)
        blocks[piece][0, capacity - TILE :, :] = jnp.where(last, facts, end).astype(jnp.bfloat16)


def pack(kv_cache, destination, lengths, count, near):
    shape = kv_cache.shape[1:]
    smem = pl.BlockSpec(memory_space=pltpu.SMEM)
    vmem = pl.BlockSpec(memory_space=pltpu.VMEM)
    outs = pl.pallas_call(
        functools.partial(pack_kernel, count, near),
        out_shape=[jax.ShapeDtypeStruct((near,) + shape, kv_cache.dtype)]
        + [jax.ShapeDtypeStruct(shape, kv_cache.dtype)] * (count - near)
        + [jax.ShapeDtypeStruct((count,), jnp.int32)],
        in_specs=[smem, smem, pl.BlockSpec(memory_space=pl.ANY)],
        out_specs=[vmem] * (count - near + 1) + [smem],
        scratch_shapes=[pltpu.SemaphoreType.DMA((count,))],
        compiler_params=pltpu.CompilerParams(vmem_limit_bytes=PACK_LIMIT),
        cost_estimate=LIGHT,
        name="pack",
    )(destination, lengths, kv_cache)
    return outs[0], outs[1:-1], outs[-1]


def project_kernel(chunks, hidden_ref, key_ref, value_ref, own_ref, other_ref, held, total, sems):
    steps, rows, depth = hidden_ref.shape
    width = key_ref.shape[1]
    part = depth // chunks
    copies = []
    for chunk in range(chunks):
        span = pl.ds(chunk * part, part)
        for which, ref in enumerate((key_ref, value_ref)):
            copies.append(
                pltpu.make_async_copy(
                    ref.at[span], held.at[which, span], sems.at[chunk, which]
                )
            )
            copies[-1].start()
    hidden = hidden_ref[...].reshape(steps * rows, depth)
    sums = [None, None]
    for chunk in range(chunks):
        for which in range(2):
            copies[2 * chunk + which].wait()
            product = jnp.dot(
                hidden[:, chunk * part : (chunk + 1) * part],
                held[which, chunk * part : (chunk + 1) * part, :],
                preferred_element_type=jnp.float32,
            )
            sums[which] = product if chunk == 0 else sums[which] + product
    total[:, :width] = sums[0]
    total[:, width:] = sums[1]
    half = width // 2
    me = lax.axis_index("tp")
    for ref, core in ((own_ref, me), (other_ref, 1 - me)):
        at = pl.multiple_of(core * half, half)
        ref[:, :half] = total[:, pl.ds(at, half)]
        ref[:, half:] = total[:, pl.ds(pl.multiple_of(width + at, half), half)]


def project(hidden_new, key_weight, value_weight):
    steps, rows, depth = hidden_new.shape
    width = key_weight.shape[1]
    chunks = 5
    shape = jax.ShapeDtypeStruct((steps * rows, width), jnp.float32)
    vmem = pl.BlockSpec(memory_space=pltpu.VMEM)
    hbm = pl.BlockSpec(memory_space=pl.ANY)
    return pl.pallas_call(
        functools.partial(project_kernel, chunks),
        out_shape=[shape, shape],
        in_specs=[vmem, hbm, hbm],
        out_specs=[vmem, vmem],
        scratch_shapes=[
            pltpu.VMEM((2, depth, width), key_weight.dtype),
            pltpu.VMEM((steps * rows, 2 * width), jnp.float32),
            pltpu.SemaphoreType.DMA((chunks, 2)),
        ],
        compiler_params=pltpu.CompilerParams(vmem_limit_bytes=VMEM_LIMIT),
        cost_estimate=LIGHT,
        name="project",
    )(hidden_new, key_weight, value_weight)


def rotation(length_ref, steps, rows):
    half = HD // 2
    line = lax.broadcasted_iota(jnp.int32, (steps * rows, HD), 0)
    lane = lax.broadcasted_iota(jnp.int32, (steps * rows, HD), 1)
    position = jnp.zeros((steps * rows, HD), jnp.int32)
    for step in range(steps):
        for row in range(rows):
            position = jnp.where(line == step * rows + row, length_ref[row] + step, position)
    order = (lane % half).astype(jnp.float32)
    angle = position.astype(jnp.float32) * jnp.exp(-math.log(ROPE_BASE) * 2.0 * order / HD)
    sine = jnp.sin(angle)
    return jnp.cos(angle), jnp.where(lane < half, -sine, sine)


def attend_kernel(
    count,
    block,
    length_ref,
    dest_ref,
    pick_ref,
    own_ref,
    got_ref,
    gain_ref,
    query_ref,
    kv_ref,
    _,
    moved_ref,
    mixed_ref,
    small_ref,
    late_ref,
    fresh,
    query_rows,
    query_columns,
    mixed,
):
    del late_ref
    part = pl.program_id(0)
    steps, rows, query_width = query_ref.shape
    capacity, lanes = kv_ref.shape[2:]
    heads = lanes // HD
    group = query_width // lanes
    per_head = steps * group
    per_row = heads * per_head
    team = HD // per_row

    @pl.when(part == 0)
    def _():
        raw = own_ref[...] + got_ref[...]
        cosine, sine = rotation(length_ref, steps, rows)
        gain = gain_ref[...].astype(jnp.float32)
        for head in range(heads):
            at = slice(head * HD, (head + 1) * HD)
            piece = raw[:, at]
            mean = jnp.mean(piece * piece, axis=-1, keepdims=True)
            piece = piece * lax.rsqrt(mean + NORM_EPS) * gain
            swapped = jnp.concatenate([piece[:, HD // 2 :], piece[:, : HD // 2]], axis=1)
            turned = piece * cosine + swapped * sine
            fresh[0, :, at] = turned.astype(jnp.bfloat16).astype(jnp.float32)
        fresh[1] = raw[:, lanes:].astype(jnp.bfloat16).astype(jnp.float32)
        for step in range(steps):
            for chunk in range(query_width // HD):
                head, member = chunk // group, chunk % group
                at = head * per_head + step * group + member
                query_rows[pl.ds(at, rows, stride=per_row), :] = query_ref[
                    step, :, chunk * HD : (chunk + 1) * HD
                ].astype(jnp.float32)
        for index in range(rows // team):
            query_columns[index] = query_rows[index * HD : (index + 1) * HD, :].T

    position = lax.broadcasted_iota(jnp.int32, (capacity, HD), 0)
    column = lax.broadcasted_iota(jnp.int32, (capacity, HD), 1)
    column_item = column // per_row
    column_step = (column % per_head) // group
    column_head = lax.broadcasted_iota(jnp.int32, (HD, HD), 1) % per_row // per_head
    factor = 1.0 / math.sqrt(HD)
    teams = range(block // team)
    scores = []
    for index in teams:
        queries = query_columns[part * (block // team) + index]
        queries = jnp.concatenate(
            [jnp.where(column_head == head, queries, 0.0) for head in range(heads)], axis=0
        ).astype(jnp.bfloat16)
        score, limit = None, None
        for member in range(team):
            item = index * team + member
            row = part * block + item
            length = length_ref[row]
            kept = position < length
            landing = [position == length + step for step in range(steps)]
            for which in range(2):
                news = [fresh[which, pl.ds(step * rows + row, 1), :] for step in range(steps)]
                for head in range(heads):
                    at = slice(head * HD, (head + 1) * HD)
                    stored = jnp.where(kept, kv_ref[item, which, :, at].astype(jnp.float32), 0.0)
                    for step in range(steps):
                        stored = jnp.where(landing[step], news[step][:, at], stored)
                    moved_ref[item, which, :, at] = stored.astype(jnp.bfloat16)
            one = jnp.dot(moved_ref[item, 0], queries, preferred_element_type=jnp.float32)
            score = one if member == 0 else jnp.where(column_item == member, one, score)
            limit = length if member == 0 else jnp.where(column_item == member, length, limit)
        scores.append(jnp.where(position <= limit + column_step, score * factor, -jnp.inf))
    weights = []
    for score in scores:
        raised = jnp.exp(score - jnp.max(score, axis=0, keepdims=True))
        normaliser = jnp.sum(raised, axis=0, keepdims=True)
        weights.append((raised / normaliser).T.astype(jnp.bfloat16))
    for index in teams:
        for member in range(team):
            item = index * team + member
            row = part * block + item
            result = jnp.dot(
                weights[index][member * per_row : (member + 1) * per_row],
                moved_ref[item, 1],
                preferred_element_type=jnp.float32,
            )
            for head in range(heads):
                at = pl.multiple_of(row * per_row + head * per_head, per_head)
                mixed[pl.ds(at, per_head), :] = result[
                    head * per_head : (head + 1) * per_head, head * HD : (head + 1) * HD
                ]

    @pl.when(part == pl.num_programs(0) - 1)
    def _():
        mixed_ref[...] = mixed[...].astype(jnp.bfloat16)
        for peer in range(count):
            row = pick_ref[peer]
            small_ref[peer, :per_row, :] = mixed[
                pl.ds(pl.multiple_of(row * per_row, per_row), per_row), :
            ].astype(jnp.bfloat16)
            news = []
            for which in range(2):
                for step in range(steps):
                    new = fresh[which, pl.ds(step * rows + row, 1), :]
                    news += [new[:, h * HD : (h + 1) * HD] for h in range(heads)]
            slot = dest_ref[row] - peer * rows
            slot = jnp.where((slot >= 0) & (slot < rows), slot, -1).astype(jnp.float32)
            fill = small_ref.shape[1] - per_row - len(news)
            news.append(jnp.full((fill, HD), slot))
            small_ref[peer, per_row:, :] = jnp.concatenate(news, axis=0).astype(jnp.bfloat16)


def attend(
    kv_cache, queries, own, got, gain, lengths, destination, pick, late, count
):
    steps, rows, query_width = queries.shape
    capacity, lanes = kv_cache.shape[2:]
    heads = lanes // HD
    per_row = steps * query_width // HD
    block = 8
    small_rows = per_row + -(-(2 * steps * heads + 1) // TILE) * TILE
    small = jax.ShapeDtypeStruct((count, small_rows, HD), jnp.bfloat16)
    smem = pl.BlockSpec(memory_space=pltpu.SMEM)
    vmem = pl.BlockSpec(memory_space=pltpu.VMEM)
    hbm = pl.BlockSpec(memory_space=pl.ANY)
    cache_block = pl.BlockSpec((block, 2, capacity, lanes), lambda i: (i, 0, 0, 0))
    return pl.pallas_call(
        functools.partial(attend_kernel, count, block),
        grid=(rows // block,),
        out_shape=[
            jax.ShapeDtypeStruct(kv_cache.shape, kv_cache.dtype),
            jax.ShapeDtypeStruct((rows * per_row, HD), jnp.bfloat16),
            small,
            jax.ShapeDtypeStruct(late.shape, late.dtype),
        ],
        in_specs=[smem, smem, smem, vmem, vmem, vmem, vmem, cache_block, hbm],
        out_specs=[cache_block, vmem, vmem, hbm],
        scratch_shapes=[
            pltpu.VMEM((2, steps * rows, lanes), jnp.float32),
            pltpu.VMEM((rows * per_row, HD), jnp.float32),
            pltpu.VMEM((rows * per_row // HD, HD, HD), jnp.float32),
            pltpu.VMEM((rows * per_row, HD), jnp.float32),
        ],
        input_output_aliases={8: 3},
        compiler_params=pltpu.CompilerParams(vmem_limit_bytes=VMEM_LIMIT),
        cost_estimate=LIGHT,
        name="attend",
    )(lengths, destination, pick, own, got, gain, queries, kv_cache, late)


def read_facts(block):
    capacity = block.shape[1]
    facts = block[0, capacity - TILE :, :].astype(jnp.float32)[TILE - 1 :]
    return (
        jnp.max(facts[:, :HD]).astype(jnp.int32),
        jnp.max(facts[:, HD : 2 * HD]).astype(jnp.int32),
    )


def window_start(length, capacity):
    return pl.multiple_of(jnp.minimum(length // TILE * TILE, capacity - WINDOW), TILE)


def clean(block, length, out):
    capacity, lanes = block.shape[1:]
    kept = lax.broadcasted_iota(jnp.int32, (capacity, HD), 0) < length
    for which in range(2):
        for at in range(0, lanes, HD):
            stored = block[which, :, at : at + HD].astype(jnp.float32)
            out[which, :, at : at + HD] = jnp.where(kept, stored, 0.0).astype(jnp.bfloat16)


def insert(window, news, ahead, steps, out):
    height, lanes = window.shape[1:]
    heads = lanes // HD
    position = lax.broadcasted_iota(jnp.int32, (height, lanes), 0)
    for which in range(2):
        stored = window[which].astype(jnp.float32)
        for step in range(steps):
            at = (which * steps + step) * heads
            new = jnp.concatenate([news[at + h : at + h + 1] for h in range(heads)], axis=1)
            stored = jnp.where(position == ahead + step, new, stored)
        out[which] = stored.astype(jnp.bfloat16)


def land_kernel(near, near_ref, *refs):
    far_refs = refs[:-7]
    _, out_ref, slot_ref, length_ref, window_ref, buffer, sems = refs[-7:]
    capacity = buffer.shape[2]
    me = lax.axis_index("inst")
    blocks = [near_ref.at[piece] for piece in range(near)] + list(far_refs)

    def store(piece):
        slot = jnp.maximum(slot_ref[piece], 0)
        return pltpu.make_async_copy(buffer.at[piece], out_ref.at[slot], sems.at[piece])

    for piece, block in enumerate(blocks):
        slot, length = read_facts(block)
        if piece < near:
            slot = jnp.where(me % near == piece, -1, slot)
        slot_ref[piece] = slot
        length_ref[piece] = length
    for piece, block in enumerate(blocks):

        @pl.when(slot_ref[piece] >= 0)
        def _():
            length = length_ref[piece]
            clean(block, length, buffer.at[piece])
            store(piece).start()
            start = window_start(length, capacity)
            window_ref[piece] = buffer[piece, :, pl.ds(start, WINDOW), :]

    for piece in range(len(blocks)):

        @pl.when(slot_ref[piece] >= 0)
        def _():
            store(piece).wait()


def land(near_got, far_got, moved):
    near = near_got.shape[0]
    pieces = near + len(far_got)
    smem = pl.BlockSpec(memory_space=pltpu.SMEM)
    vmem = pl.BlockSpec(memory_space=pltpu.VMEM)
    hbm = pl.BlockSpec(memory_space=pl.ANY)
    scalars = jax.ShapeDtypeStruct((pieces,), jnp.int32)
    return pl.pallas_call(
        functools.partial(land_kernel, near),
        out_shape=[
            jax.ShapeDtypeStruct(moved.shape, moved.dtype),
            scalars,
            scalars,
            jax.ShapeDtypeStruct((pieces, 2, WINDOW, moved.shape[3]), moved.dtype),
        ],
        in_specs=[vmem] * (1 + len(far_got)) + [hbm],
        out_specs=[hbm, smem, smem, vmem],
        scratch_shapes=[
            pltpu.VMEM((pieces,) + moved.shape[1:], moved.dtype),
            pltpu.SemaphoreType.DMA((pieces,)),
        ],
        input_output_aliases={1 + len(far_got): 0},
        compiler_params=pltpu.CompilerParams(vmem_limit_bytes=SMALL_LIMIT),
        cost_estimate=HEAVY,
        name="land",
    )(near_got, *far_got, moved)


def settle_kernel(
    count,
    near,
    group,
    slot_ref,
    length_ref,
    mixed_ref,
    small_ref,
    window_ref,
    _,
    out_ref,
    moved_ref,
    mixed,
    windows,
    sems,
):
    steps, rows, query_width = out_ref.shape
    per_row = steps * query_width // HD
    capacity, lanes = moved_ref.shape[2:]
    heads = lanes // HD
    me = lax.axis_index("inst")
    pieces = slot_ref.shape[0]

    def store(piece):
        slot = jnp.maximum(slot_ref[piece], 0)
        start = window_start(length_ref[piece], capacity)
        return pltpu.make_async_copy(
            windows.at[piece], moved_ref.at[slot, :, pl.ds(start, WINDOW), :], sems.at[piece]
        )

    def take(slot, peer):
        mixed[pl.ds(pl.multiple_of(slot * per_row, per_row), per_row), :] = small_ref[
            peer, :per_row, :
        ].astype(jnp.float32)

    for piece in range(pieces):

        @pl.when(slot_ref[piece] >= 0)
        def _():
            length = length_ref[piece]
            peer = peer_of(me, piece, near, False)
            news = small_ref[peer, per_row:, :].astype(jnp.float32)
            ahead = length - window_start(length, capacity)
            insert(window_ref.at[piece], news, ahead, steps, windows.at[piece])
            store(piece).start()

    mixed[...] = mixed_ref[...].astype(jnp.float32)
    for piece in range(count):
        peer = peer_of(me, piece, near, False)
        if piece < pieces:
            slot = slot_ref[piece]
        else:
            line = 2 * steps * heads
            facts = small_ref[peer, per_row:, :].astype(jnp.float32)[line : line + 1]
            slot = jnp.max(facts).astype(jnp.int32)
        pl.when(slot >= 0)(functools.partial(take, slot, peer))
    for step in range(steps):
        for chunk in range(query_width // HD):
            head, member = chunk // group, chunk % group
            at = head * steps * group + step * group + member
            out_ref[step, :, chunk * HD : (chunk + 1) * HD] = mixed[
                pl.ds(at, rows, stride=per_row), :
            ].astype(jnp.bfloat16)

    for piece in range(pieces):

        @pl.when(slot_ref[piece] >= 0)
        def _():
            store(piece).wait()


def settle(slots, lengths, mixed, small, windows, moved, shape, group, count, near):
    smem = pl.BlockSpec(memory_space=pltpu.SMEM)
    vmem = pl.BlockSpec(memory_space=pltpu.VMEM)
    hbm = pl.BlockSpec(memory_space=pl.ANY)
    return pl.pallas_call(
        functools.partial(settle_kernel, count, near, group),
        out_shape=[
            jax.ShapeDtypeStruct(shape, jnp.bfloat16),
            jax.ShapeDtypeStruct(moved.shape, moved.dtype),
        ],
        in_specs=[smem, smem, vmem, vmem, vmem, hbm],
        out_specs=[vmem, hbm],
        scratch_shapes=[
            pltpu.VMEM(mixed.shape, jnp.float32),
            pltpu.VMEM(windows.shape, windows.dtype),
            pltpu.SemaphoreType.DMA((slots.shape[0],)),
        ],
        input_output_aliases={5: 1},
        compiler_params=pltpu.CompilerParams(vmem_limit_bytes=SMALL_LIMIT),
        cost_estimate=LIGHT,
        name="settle",
    )(slots, lengths, mixed, small, windows, moved)


def finish_kernel(count, near, steps, late_ref, small_ref, _, out_ref, buffer, sem):
    capacity, lanes = buffer.shape[1:]
    news_rows = 2 * steps * (lanes // HD)
    slot, length = read_facts(late_ref)
    peer = peer_of(lax.axis_index("inst"), count - 1, near, False)

    @pl.when(slot >= 0)
    def _():
        clean(late_ref, length, buffer)
        start = window_start(length, capacity)
        window = buffer.at[:, pl.ds(start, WINDOW), :]
        height = small_ref.shape[1]
        tail = height - -(-(news_rows + 1) // TILE) * TILE
        news = small_ref[peer, tail:, :].astype(jnp.float32)
        insert(window, news, length - start, steps, window)
        copy = pltpu.make_async_copy(buffer, out_ref.at[slot], sem)
        copy.start()
        copy.wait()


def finish(late_got, small, moved, steps, count, near):
    vmem = pl.BlockSpec(memory_space=pltpu.VMEM)
    hbm = pl.BlockSpec(memory_space=pl.ANY)
    return pl.pallas_call(
        functools.partial(finish_kernel, count, near, steps),
        out_shape=jax.ShapeDtypeStruct(moved.shape, moved.dtype),
        in_specs=[vmem, vmem, hbm],
        out_specs=hbm,
        scratch_shapes=[
            pltpu.VMEM(late_got.shape, late_got.dtype),
            pltpu.SemaphoreType.DMA,
        ],
        input_output_aliases={2: 0},
        compiler_params=pltpu.CompilerParams(vmem_limit_bytes=SMALL_LIMIT),
        cost_estimate=LIGHT,
        name="finish",
    )(late_got, small, moved)


def local(hidden_new, queries, kv_cache, lengths, destination, key_weight, value_weight, key_gain):
    steps = queries.shape[0]
    group = queries.shape[2] // kv_cache.shape[3]
    count = lax.axis_size("inst")
    near = near_size(count)

    def send(block, piece):
        pairs = [(i, peer_to(i, piece, count)) for i in range(count)]
        return lax.ppermute(block, "inst", pairs)

    near_blocks, far_blocks, pick = pack(kv_cache, destination, lengths, count, near)
    near_got = near_blocks
    if near > 1:
        teams = [list(range(i, i + near)) for i in range(0, count, near)]
        near_got = lax.all_to_all(near_blocks, "inst", 0, 0, axis_index_groups=teams, tiled=True)
    far_got = [send(block, piece) for piece, block in enumerate(far_blocks[:-1], near)]
    own, other = project(hidden_new, key_weight, value_weight)
    got = lax.ppermute(other, "tp", [(0, 1), (1, 0)])
    moved, mixed, small, late = attend(
        kv_cache,
        queries,
        own,
        got,
        key_gain[None, :],
        lengths,
        destination,
        pick,
        far_blocks[-1],
        count,
    )
    late_got = send(late, count - 1)
    small_got = lax.all_to_all(small, "inst", 0, 0, tiled=True)
    moved, slots, arrived, windows = land(near_got, far_got, moved)
    attended, moved = settle(
        slots, arrived, mixed, small_got, windows, moved, queries.shape, group, count, near
    )
    return attended, finish(late_got, small_got, moved, steps, count, near)


def solution(mesh):
    return jax.shard_map(
        local,
        mesh=mesh,
        in_specs=(
            P(None, ("group", "inst"), "tp"),
            P(None, ("group", "inst"), "tp"),
            P(("group", "inst"), None, None, "tp"),
            P(("group", "inst")),
            P(("group", "inst")),
            P("tp", None),
            P("tp", None),
            P(),
        ),
        out_specs=(P(None, ("group", "inst"), "tp"), P(("group", "inst"), None, None, "tp")),
        check_vma=False,
    )
```

time: 50.8 us -> 46.9 us (0.923)
  waiting for transfers between devices: 9.4 us -> 6.82 us
  Pallas kernels: 20.1 us -> 19.1 us
    ppermute x4, waiting for transfers between devices: 2.75 us -> 0.01 us  [send(): return lax.ppermute(block, 'inst', pairs)]
    pallas_call x1, Pallas kernels: 3.9 us -> 3.17 us  [pack(): pl.pallas_call(functools.partial(pack_kernel, count, near), out_shape=[ja...]
    pallas_call x2 -> x3, Pallas kernels: 7.21 us -> 7.05 us  [the longest x1 4.44 us: project(): pl.pallas_call(functools.partial(project_kernel, chunks), out_shape=[shap...]
  transfers between devices with their start and end apart: 7 -> 7, of which waited for: 3 -> 2; matrix products, arithmetic and copies ran while one was open for 0% -> 0% of each run, Pallas kernels for 17% -> 32%
where the time goes in v4:
time: 46.9 us; the launch traced here: 46.5 us
  starting transfers between devices  19.2 us (41%)
  Pallas kernels  19.1 us (41%)
  waiting for transfers between devices  6.82 us (15%)
  between operations  0.72 us (2%)
  local copies, waits for them, and re-layouts  0.64 us (1%)
    ppermute x4, starting transfers between devices, send(): return lax.ppermute(block, 'inst', pairs)  7.93 us
    pallas_call x1, Pallas kernels, attend(): pl.pallas_call(functools.partial(attend_kernel, count, block), grid=(rows...  6.78 us
    all_to_all x1, starting transfers between devices, local(): small_got = lax.all_to_all(small, 'inst', 0, 0, tiled=True)  5.98 us
    all_to_all x1, waiting for transfers between devices, local(): small_got = lax.all_to_all(small, 'inst', 0, 0, tiled=True)  5.31 us
    all_to_all x1, starting transfers between devices, local(): lax.all_to_all(near_blocks, 'inst', 0, 0, axis_index_groups=teams, tiled=...  5.26 us
    pallas_call x1, Pallas kernels, project(): pl.pallas_call(functools.partial(project_kernel, chunks), out_shape=[shap...  4.44 us
    pallas_call x1, Pallas kernels, pack(): pl.pallas_call(functools.partial(pack_kernel, count, near), out_shape=[ja...  3.17 us
    pallas_call x1, Pallas kernels, settle(): pl.pallas_call(functools.partial(settle_kernel, count, near, group), out_...  2.06 us
  transfers between devices with their start and end apart: 7, of which 2 were waited for; matrix products, arithmetic and copies ran while one was open for 0% of the time, Pallas kernels for 32%

profile of v4, /device:TPU:0, one launch (start us, length us, event | category | flops | bytes accessed | tf_op | source)
XLA Modules:
  0.0 46.5 jit_solution(9897798533529545892)
XLA Ops:
  0.6 3.2 %pack.1 = (bf16[4,2,144,256]{3,2,1,0:T(8,128)(2,1)}, bf16[2,144,256]{2,1,0:T(8,128)(2,1)}, bf16[2,144,256]{2,1,0:T(8,128)(2,1)}, bf16[2,144,256]{2,1,0:T(8,128)(...) custom-call(s32[24]{0:T(128)} %dest_ref.3, s32[24]{0:T(128)} %length_ref.3, bf16[24,2,144,256]{3,2,1,0:T(8,128)(2,1)} %kv_ref.3), custom_call_target="tpu_custom_call" | custom-call | flops 1 | bytes 1 | tf_op jit(solution)/shard_map/pack/pallas_call | solution.py:84
  3.8 5.3 %all-to-all-start = ((bf16[4,2,144,256]{3,2,1,0:T(8,128)(2,1)}), bf16[4,2,144,256]{3,2,1,0:T(8,128)(2,1)S(1)}, u32[]{:S(2)}, u32[]{:S(2)}) async-start(bf16[4,2,144,256]{3,2,1,0:T(8,128)(2,1)} %get-tuple-element.20), calls=%async_computation | async-start | bytes 1179648 | tf_op jit(solution)/shard_map/all_to_all | solution.py:581
  9.1 2.6 %collective-permute-start = (bf16[2,144,256]{2,1,0:T(8,128)(2,1)}, bf16[2,144,256]{2,1,0:T(8,128)(2,1)S(1)}, u32[]{:S(2)}, u32[]{:S(2)}) collective-permute-start(bf16[2,144,256]{2,1,0:T(8,128)(2,1)} %get-tuple-element.21), channel_id=1, source_target_pairs={{0,8},{2,10},{4,12},{6,14},{8,0},{10,2},{12,4},{14,6},{1,9},{3,11}... | collective-permute-start | bytes 442376 | tf_op jit(solution)/shard_map/ppermute | solution.py:575
  11.7 1.8 %collective-permute-start.1 = (bf16[2,144,256]{2,1,0:T(8,128)(2,1)}, bf16[2,144,256]{2,1,0:T(8,128)(2,1)S(1)}, u32[]{:S(2)}, u32[]{:S(2)}) collective-permute-start(bf16[2,144,256]{2,1,0:T(8,128)(2,1)} %get-tuple-element.22), channel_id=1, source_target_pairs={{0,10},{2,8},{4,14},{6,12},{8,2},{10,0},{12,6},{14,4},{1,11},{3,9}... | collective-permute-start | bytes 442376 | tf_op jit(solution)/shard_map/ppermute | solution.py:575
  13.5 3.5 %collective-permute-start.2 = (bf16[2,144,256]{2,1,0:T(8,128)(2,1)}, bf16[2,144,256]{2,1,0:T(8,128)(2,1)S(1)}, u32[]{:S(2)}, u32[]{:S(2)}) collective-permute-start(bf16[2,144,256]{2,1,0:T(8,128)(2,1)} %get-tuple-element.23), channel_id=1, source_target_pairs={{0,12},{2,14},{4,8},{6,10},{8,4},{10,6},{12,0},{14,2},{1,13},{3,15... | collective-permute-start | bytes 442376 | tf_op jit(solution)/shard_map/ppermute | solution.py:575
  16.9 4.4 %project.1 = (f32[48,512]{1,0:T(8,128)}, f32[48,512]{1,0:T(8,128)}) custom-call(bf16[2,24,2560]{2,1,0:T(8,128)(2,1)} %hidden_ref.1, bf16[2560,512]{1,0:T(8,128)(2,1)} %key_ref.1, bf16[2560,512]{1,0:T(8,128)(2,1)} %value_ref.1), custom_call_target="tpu_custom_call" | custom-call | flops 1 | bytes 1 | tf_op jit(solution)/shard_map/project/pallas_call | solution.py:141
  21.4 0.1 collective-permute-start.3
  21.5 1.5 %collective-permute-done.3.got_ref = f32[48,512]{1,0:T(8,128)S(1)} collective-permute-done((f32[48,512]{1,0:T(8,128)}, f32[48,512]{1,0:T(8,128)S(1)}, u32[]{:S(2)}, u32[]{:S(2)}) %collective-permute-start.3) | collective-permute-done | bytes 98336 | tf_op jit(solution)/shard_map/ppermute | solution.py:584
  23.0 0.0 copy-start.1
  23.0 0.6 %copy-done.1 = f32[48,512]{1,0:T(8,128)} copy-done((f32[48,512]{1,0:T(8,128)}, f32[48,512]{1,0:T(8,128)S(1)}, u32[]{:S(2)}) %copy-start.1) | copy-done | bytes 98328
  23.6 6.8 %attend.1 = (bf16[24,2,144,256]{3,2,1,0:T(8,128)(2,1)}, bf16[768,128]{1,0:T(8,128)(2,1)}, bf16[8,48,128]{2,1,0:T(8,128)(2,1)}, bf16[2,144,256]{2,1,0:T(8,128)(2,1)}) custom-call(s32[24]{0:T(128)} %length_ref.3, s32[24]{0:T(128)} %dest_ref.3, s32[8]{0:T(128)} %get-tuple-element.24.pick_ref, ...), custom_call_target="tpu_custom_call", output_to_operand_aliasing={{3}: (8, {})} | custom-call | flops 1 | bytes 1 | tf_op jit(solution)/shard_map/attend/pallas_call | solution.py:312
  30.4 0.1 collective-permute-start.4
  30.5 0.0 all-to-all-done.near_ref
  30.5 6.0 %all-to-all-start.1 = ((bf16[8,48,128]{2,1,0:T(8,128)(2,1)}), bf16[8,48,128]{2,1,0:T(8,128)(2,1)S(1)}, u32[]{:S(2)}, u32[]{:S(2)}) async-start(bf16[8,48,128]{2,1,0:T(8,128)(2,1)} %get-tuple-element.32), calls=%async_computation.1 | async-start | bytes 196608 | tf_op jit(solution)/shard_map/all_to_all | solution.py:598
  36.4 0.0 collective-permute-done.refs_0_
  36.4 0.0 collective-permute-done.1.refs_1_
  36.5 0.0 collective-permute-done.2.refs_2_
  36.5 0.0 copy-start
  36.5 1.8 %land.1 = (bf16[24,2,144,256]{3,2,1,0:T(8,128)(2,1)}, s32[7]{0:T(128)S(1)}, s32[7]{0:T(128)S(1)}, bf16[7,2,32,256]{3,2,1,0:T(8,128)(2,1)S(1)}) custom-call(bf16[4,2,144,256]{3,2,1,0:T(8,128)(2,1)S(1)} %all-to-all-done.near_ref, bf16[2,144,256]{2,1,0:T(8,128)(2,1)S(1)} %collective-permute-done.refs_0_, ...), custom_call_target="tpu_custom_call", output_to_operand_aliasing={{0}: (4, {})} | custom-call | flops 68719476736 | bytes 268435456 | tf_op jit(solution)/shard_map/land/pallas_call | solution.py:412
  38.3 5.3 %all-to-all-done.1.small_ref = bf16[8,48,128]{2,1,0:T(8,128)(2,1)S(1)} async-done(((bf16[8,48,128]{2,1,0:T(8,128)(2,1)}), bf16[8,48,128]{2,1,0:T(8,128)(2,1)S(1)}, u32[]{:S(2)}, u32[]{:S(2)}) %all-to-all-start.1) | async-done | bytes 98336 | tf_op jit(solution)/shard_map/all_to_all | solution.py:598
  43.6 0.0 copy-done
  43.6 2.1 %settle.1 = (bf16[2,24,2048]{2,1,0:T(8,128)(2,1)}, bf16[24,2,144,256]{3,2,1,0:T(8,128)(2,1)}) custom-call(s32[7]{0:T(128)S(1)} %get-tuple-element.29.slot_ref, s32[7]{0:T(128)S(1)} %get-tuple-element.30.length_ref, bf16[768,128]{1,0:T(8,128)(2,1)S(1)} %copy-done, bf16[8,48,128]{2,1,0:T(8,128)(2,1)S(1)} %all-to-all-done.1.small_ref, ...), custom_call_target="tpu_custom_call", output_to_operand_aliasing={{1}: (5, {})} | custom-call | flops 1 | bytes 1 | tf_op jit(solution)/shard_map/settle/pallas_call | solution.py:508
  45.6 0.0 collective-permute-done.4.late_ref
  45.6 0.8 %finish.1 = bf16[24,2,144,256]{3,2,1,0:T(8,128)(2,1)} custom-call(bf16[2,144,256]{2,1,0:T(8,128)(2,1)S(1)} %collective-permute-done.4.late_ref, bf16[8,48,128]{2,1,0:T(8,128)(2,1)S(1)} %all-to-all-done.1.small_ref, bf16[24,2,144,256]{3,2,1,0:T(8,128)(2,1)} %get-tuple-element.37._), custom_call_target="tpu_custom_call", output_to_operand_aliasing={{}: (2, {})} | custom-call | flops 1 | bytes 1 | tf_op jit(solution)/shard_map/finish/pallas_call | solution.py:551
Async XLA Ops:
  3.8 26.6 %all-to-all-start = ((bf16[4,2,144,256]{3,2,1,0:T(8,128)(2,1)}), bf16[4,2,144,256]{3,2,1,0:T(8,128)(2,1)S(1)}, u32[]{:S(2)}, u32[]{:S(2)}) async-start(bf16[4,2,144,256]{3,2,1,0:T(8,128)(2,1)} %get-tuple-element.20), calls=%async_computation | async-start | bytes 1179648 | tf_op jit(solution)/shard_map/all_to_all | solution.py:581
  9.1 27.4 %collective-permute-start = (bf16[2,144,256]{2,1,0:T(8,128)(2,1)}, bf16[2,144,256]{2,1,0:T(8,128)(2,1)S(1)}, u32[]{:S(2)}, u32[]{:S(2)}) collective-permute-start(bf16[2,144,256]{2,1,0:T(8,128)(2,1)} %get-tuple-element.21), channel_id=1, source_target_pairs={{0,8},{2,10},{4,12},{6,14},{8,0},{10,2},{12,4},{14,6},{1,9},{3,11}... | collective-permute-start | bytes 442376 | tf_op jit(solution)/shard_map/ppermute | solution.py:575
  11.7 24.8 %collective-permute-start.1 = (bf16[2,144,256]{2,1,0:T(8,128)(2,1)}, bf16[2,144,256]{2,1,0:T(8,128)(2,1)S(1)}, u32[]{:S(2)}, u32[]{:S(2)}) collective-permute-start(bf16[2,144,256]{2,1,0:T(8,128)(2,1)} %get-tuple-element.22), channel_id=1, source_target_pairs={{0,10},{2,8},{4,14},{6,12},{8,2},{10,0},{12,6},{14,4},{1,11},{3,9}... | collective-permute-start | bytes 442376 | tf_op jit(solution)/shard_map/ppermute | solution.py:575
  13.5 23.0 %collective-permute-start.2 = (bf16[2,144,256]{2,1,0:T(8,128)(2,1)}, bf16[2,144,256]{2,1,0:T(8,128)(2,1)S(1)}, u32[]{:S(2)}, u32[]{:S(2)}) collective-permute-start(bf16[2,144,256]{2,1,0:T(8,128)(2,1)} %get-tuple-element.23), channel_id=1, source_target_pairs={{0,12},{2,14},{4,8},{6,10},{8,4},{10,6},{12,0},{14,2},{1,13},{3,15... | collective-permute-start | bytes 442376 | tf_op jit(solution)/shard_map/ppermute | solution.py:575
  21.4 1.6 %collective-permute-start.3 = (f32[48,512]{1,0:T(8,128)}, f32[48,512]{1,0:T(8,128)S(1)}, u32[]{:S(2)}, u32[]{:S(2)}) collective-permute-start(f32[48,512]{1,0:T(8,128)} %get-tuple-element.26), channel_id=1, source_target_pairs={{0,1},{1,0},{2,3},{3,2},{4,5},{5,4},{6,7},{7,6},{8,9},{9,8},{10,11... | collective-permute-start | bytes 294920 | tf_op jit(solution)/shard_map/ppermute | solution.py:584
  23.0 0.6 %copy-start.1 = (f32[48,512]{1,0:T(8,128)}, f32[48,512]{1,0:T(8,128)S(1)}, u32[]{:S(2)}) copy-start(f32[48,512]{1,0:T(8,128)S(1)} %collective-permute-done.3.got_ref) | copy-start | bytes 294916
  30.4 15.3 %collective-permute-start.4 = (bf16[2,144,256]{2,1,0:T(8,128)(2,1)}, bf16[2,144,256]{2,1,0:T(8,128)(2,1)S(1)}, u32[]{:S(2)}, u32[]{:S(2)}) collective-permute-start(bf16[2,144,256]{2,1,0:T(8,128)(2,1)} %get-tuple-element.36), channel_id=1, source_target_pairs={{0,14},{2,12},{4,10},{6,8},{8,6},{10,4},{12,2},{14,0},{1,15},{3,13... | collective-permute-start | bytes 442376 | tf_op jit(solution)/shard_map/ppermute | solution.py:575
  30.5 13.1 %all-to-all-start.1 = ((bf16[8,48,128]{2,1,0:T(8,128)(2,1)}), bf16[8,48,128]{2,1,0:T(8,128)(2,1)S(1)}, u32[]{:S(2)}, u32[]{:S(2)}) async-start(bf16[8,48,128]{2,1,0:T(8,128)(2,1)} %get-tuple-element.32), calls=%async_computation.1 | async-start | bytes 196608 | tf_op jit(solution)/shard_map/all_to_all | solution.py:598
  36.5 7.1 %copy-start = (bf16[768,128]{1,0:T(8,128)(2,1)S(1)}, bf16[768,128]{1,0:T(8,128)(2,1)}, u32[]{:S(2)}) copy-start(bf16[768,128]{1,0:T(8,128)(2,1)} %get-tuple-element.31.mixed_ref) | copy-start | bytes 589828

commit v5 on v4

--- a/solution.py
+++ b/solution.py
@@ -12,7 +12,7 @@
 ROPE_BASE = 1000000.0
 NORM_EPS = 1e-06
 VMEM_LIMIT = 62 * 1024 * 1024
-PACK_LIMIT = 59 * 1024 * 1024
+ATTEND_LIMIT = 56 * 1024 * 1024
 SMALL_LIMIT = 40 * 1024 * 1024
 LIGHT = pl.CostEstimate(flops=1, bytes_accessed=1, transcendentals=0)
 HEAVY = pl.CostEstimate(flops=1 << 36, bytes_accessed=1 << 28, transcendentals=0)
@@ -29,92 +29,75 @@
     return value // divisor
 
 
-def peer_to(index, shift, count, paired=None):
-    if count & (count - 1) == 0:
-        return index ^ (shift if paired is None else paired)
-    return (index + shift) % count
-
-
-def near_size(count):
-    return 4 if count % 4 == 0 and count & (count - 1) == 0 else 1
-
-
-def peer_of(me, piece, near, to):
-    count = lax.axis_size("inst")
-    if piece < near:
-        return me // near * near + piece
-    return peer_to(me, piece, count) if to else peer_to(me, count - piece, count, piece)
-
-
-def pack_kernel(count, near, dest_ref, length_ref, kv_ref, near_ref, *refs):
-    far_refs = refs[: count - near]
-    pick_ref, sems = refs[count - near :]
+def peer_to(index, shift, count):
+    return index ^ shift if count & (count - 1) == 0 else (index + shift) % count
+
+
+def peer_from(index, shift, count):
+    return index ^ shift if count & (count - 1) == 0 else (index + count - shift) % count
+
+
+def prepare_kernel(
+    count, chunks, dest_ref, length_ref, hidden_ref, kv_ref, key_ref, value_ref, *refs
+):
+    block_refs = refs[: count - 1]
+    pick_ref, own_ref, other_ref, blocks, held, total = refs[count - 1 : count + 5]
+    in_sems, out_sems, weight_sems = refs[count + 5 :]
     rows = dest_ref.shape[0]
     capacity, lanes = kv_ref.shape[2:]
     me = lax.axis_index("inst")
+    shifts = range(1, count)
+
     for peer in range(count):
         pick_ref[peer] = 0
     for row in range(rows):
         pick_ref[quotient(dest_ref[row], rows, rows * count)] = row
-    order = list(range(near)) + list(range(near, count))
-    blocks = [near_ref.at[piece] for piece in range(near)] + list(far_refs)
-    copies = {}
-    for piece in order:
-        row = pick_ref[peer_of(me, piece, near, True)]
-        copies[piece] = pltpu.make_async_copy(kv_ref.at[row], blocks[piece], sems.at[piece])
-        copies[piece].start()
+    fetches, stores = {}, {}
+    for shift in shifts:
+        row = pick_ref[peer_to(me, shift, count)]
+        fetches[shift] = pltpu.make_async_copy(
+            kv_ref.at[row], blocks.at[shift - 1], in_sems.at[shift - 1]
+        )
+        fetches[shift].start()
+
+    steps, _, depth = hidden_ref.shape
+    width = key_ref.shape[1]
+    part = depth // chunks
+    weights = []
+    for chunk in range(chunks):
+        span = pl.ds(chunk * part, part)
+        for which, ref in enumerate((key_ref, value_ref)):
+            weights.append(
+                pltpu.make_async_copy(
+                    ref.at[span], held.at[which, span], weight_sems.at[chunk, which]
+                )
+            )
+            weights[-1].start()
+
     tile = (TILE, lanes)
     last = lax.broadcasted_iota(jnp.int32, tile, 0) == TILE - 1
     first_lanes = lax.broadcasted_iota(jnp.int32, tile, 1) < HD
-    for piece in order:
-        peer = peer_of(me, piece, near, True)
+    for shift in shifts:
+        peer = peer_to(me, shift, count)
         row = pick_ref[peer]
         slot = dest_ref[row] - peer * rows
         slot = jnp.where((slot >= 0) & (slot < rows), slot, -1)
         facts = jnp.where(first_lanes, slot, length_ref[row]).astype(jnp.float32)
-        copies[piece].wait()
-        end = blocks[piece][0, capacity - TILE :, :].astype(jnp.float32)
-        blocks[piece][0, capacity - TILE :, :] = jnp.where(last, facts, end).astype(jnp.bfloat16)
-
-
-def pack(kv_cache, destination, lengths, count, near):
-    shape = kv_cache.shape[1:]
-    smem = pl.BlockSpec(memory_space=pltpu.SMEM)
-    vmem = pl.BlockSpec(memory_space=pltpu.VMEM)
-    outs = pl.pallas_call(
-        functools.partial(pack_kernel, count, near),
-        out_shape=[jax.ShapeDtypeStruct((near,) + shape, kv_cache.dtype)]
-        + [jax.ShapeDtypeStruct(shape, kv_cache.dtype)] * (count - near)
-        + [jax.ShapeDtypeStruct((count,), jnp.int32)],
-        in_specs=[smem, smem, pl.BlockSpec(memory_space=pl.ANY)],
-        out_specs=[vmem] * (count - near + 1) + [smem],
-        scratch_shapes=[pltpu.SemaphoreType.DMA((count,))],
-        compiler_params=pltpu.CompilerParams(vmem_limit_bytes=PACK_LIMIT),
-        cost_estimate=LIGHT,
-        name="pack",
-    )(destination, lengths, kv_cache)
-    return outs[0], outs[1:-1], outs[-1]
-
-
-def project_kernel(chunks, hidden_ref, key_ref, value_ref, own_ref, other_ref, held, total, sems):
-    steps, rows, depth = hidden_ref.shape
-    width = key_ref.shape[1]
-    part = depth // chunks
-    copies = []
-    for chunk in range(chunks):
-        span = pl.ds(chunk * part, part)
-        for which, ref in enumerate((key_ref, value_ref)):
-            copies.append(
-                pltpu.make_async_copy(
-                    ref.at[span], held.at[which, span], sems.at[chunk, which]
-                )
-            )
-            copies[-1].start()
+        fetches[shift].wait()
+        end = blocks[shift - 1, 0, capacity - TILE :, :].astype(jnp.float32)
+        blocks[shift - 1, 0, capacity - TILE :, :] = jnp.where(last, facts, end).astype(
+            jnp.bfloat16
+        )
+        stores[shift] = pltpu.make_async_copy(
+            blocks.at[shift - 1], block_refs[shift - 1], out_sems.at[shift - 1]
+        )
+        stores[shift].start()
+
     hidden = hidden_ref[...].reshape(steps * rows, depth)
     sums = [None, None]
     for chunk in range(chunks):
         for which in range(2):
-            copies[2 * chunk + which].wait()
+            weights[2 * chunk + which].wait()
             product = jnp.dot(
                 hidden[:, chunk * part : (chunk + 1) * part],
                 held[which, chunk * part : (chunk + 1) * part, :],
@@ -124,34 +107,43 @@
     total[:, :width] = sums[0]
     total[:, width:] = sums[1]
     half = width // 2
-    me = lax.axis_index("tp")
-    for ref, core in ((own_ref, me), (other_ref, 1 - me)):
-        at = pl.multiple_of(core * half, half)
+    core = lax.axis_index("tp")
+    for ref, place in ((own_ref, core), (other_ref, 1 - core)):
+        at = pl.multiple_of(place * half, half)
         ref[:, :half] = total[:, pl.ds(at, half)]
         ref[:, half:] = total[:, pl.ds(pl.multiple_of(width + at, half), half)]
-
-
-def project(hidden_new, key_weight, value_weight):
+    for shift in shifts:
+        stores[shift].wait()
+
+
+def prepare(destination, lengths, hidden_new, kv_cache, key_weight, value_weight, count):
     steps, rows, depth = hidden_new.shape
     width = key_weight.shape[1]
     chunks = 5
-    shape = jax.ShapeDtypeStruct((steps * rows, width), jnp.float32)
+    shape = kv_cache.shape[1:]
+    part = jax.ShapeDtypeStruct((steps * rows, width), jnp.float32)
+    smem = pl.BlockSpec(memory_space=pltpu.SMEM)
     vmem = pl.BlockSpec(memory_space=pltpu.VMEM)
     hbm = pl.BlockSpec(memory_space=pl.ANY)
-    return pl.pallas_call(
-        functools.partial(project_kernel, chunks),
-        out_shape=[shape, shape],
-        in_specs=[vmem, hbm, hbm],
-        out_specs=[vmem, vmem],
+    outs = pl.pallas_call(
+        functools.partial(prepare_kernel, count, chunks),
+        out_shape=[jax.ShapeDtypeStruct(shape, kv_cache.dtype)] * (count - 1)
+        + [jax.ShapeDtypeStruct((count,), jnp.int32), part, part],
+        in_specs=[smem, smem, vmem, hbm, hbm, hbm],
+        out_specs=[hbm] * (count - 1) + [smem, vmem, vmem],
         scratch_shapes=[
+            pltpu.VMEM((count - 1,) + shape, kv_cache.dtype),
             pltpu.VMEM((2, depth, width), key_weight.dtype),
             pltpu.VMEM((steps * rows, 2 * width), jnp.float32),
+            pltpu.SemaphoreType.DMA((count - 1,)),
+            pltpu.SemaphoreType.DMA((count - 1,)),
             pltpu.SemaphoreType.DMA((chunks, 2)),
         ],
         compiler_params=pltpu.CompilerParams(vmem_limit_bytes=VMEM_LIMIT),
         cost_estimate=LIGHT,
-        name="project",
-    )(hidden_new, key_weight, value_weight)
+        name="prepare",
+    )(destination, lengths, hidden_new, kv_cache, key_weight, value_weight)
+    return outs[: count - 1], *outs[count - 1 :]
 
 
 def rotation(length_ref, steps, rows):
@@ -179,17 +171,11 @@
     gain_ref,
     query_ref,
     kv_ref,
-    _,
-    moved_ref,
-    mixed_ref,
-    small_ref,
-    late_ref,
-    fresh,
-    query_rows,
-    query_columns,
-    mixed,
+    *refs,
 ):
-    del late_ref
+    late = (len(refs) - 7) // 2
+    moved_ref, mixed_ref, small_ref = refs[late : late + 3]
+    fresh, query_rows, query_columns, mixed = refs[-4:]
     part = pl.program_id(0)
     steps, rows, query_width = query_ref.shape
     capacity, lanes = kv_ref.shape[2:]
@@ -298,6 +284,7 @@
 def attend(
     kv_cache, queries, own, got, gain, lengths, destination, pick, late, count
 ):
+    late_shapes = [jax.ShapeDtypeStruct(x.shape, x.dtype) for x in late]
     steps, rows, query_width = queries.shape
     capacity, lanes = kv_cache.shape[2:]
     heads = lanes // HD
@@ -309,28 +296,29 @@
     vmem = pl.BlockSpec(memory_space=pltpu.VMEM)
     hbm = pl.BlockSpec(memory_space=pl.ANY)
     cache_block = pl.BlockSpec((block, 2, capacity, lanes), lambda i: (i, 0, 0, 0))
-    return pl.pallas_call(
+    outs = pl.pallas_call(
         functools.partial(attend_kernel, count, block),
         grid=(rows // block,),
         out_shape=[
             jax.ShapeDtypeStruct(kv_cache.shape, kv_cache.dtype),
             jax.ShapeDtypeStruct((rows * per_row, HD), jnp.bfloat16),
             small,
-            jax.ShapeDtypeStruct(late.shape, late.dtype),
-        ],
-        in_specs=[smem, smem, smem, vmem, vmem, vmem, vmem, cache_block, hbm],
-        out_specs=[cache_block, vmem, vmem, hbm],
+        ]
+        + late_shapes,
+        in_specs=[smem, smem, smem, vmem, vmem, vmem, vmem, cache_block] + [hbm] * len(late),
+        out_specs=[cache_block, vmem, vmem] + [hbm] * len(late),
         scratch_shapes=[
             pltpu.VMEM((2, steps * rows, lanes), jnp.float32),
             pltpu.VMEM((rows * per_row, HD), jnp.float32),
             pltpu.VMEM((rows * per_row // HD, HD, HD), jnp.float32),
             pltpu.VMEM((rows * per_row, HD), jnp.float32),
         ],
-        input_output_aliases={8: 3},
-        compiler_params=pltpu.CompilerParams(vmem_limit_bytes=VMEM_LIMIT),
+        input_output_aliases={8 + i: 3 + i for i in range(len(late))},
+        compiler_params=pltpu.CompilerParams(vmem_limit_bytes=ATTEND_LIMIT),
         cost_estimate=LIGHT,
         name="attend",
-    )(lengths, destination, pick, own, got, gain, queries, kv_cache, late)
+    )(lengths, destination, pick, own, got, gain, queries, kv_cache, *late)
+    return outs[0], outs[1], outs[2], outs[3:]
 
 
 def read_facts(block):
@@ -368,23 +356,17 @@
         out[which] = stored.astype(jnp.bfloat16)
 
 
-def land_kernel(near, near_ref, *refs):
-    far_refs = refs[:-7]
-    _, out_ref, slot_ref, length_ref, window_ref, buffer, sems = refs[-7:]
+def land_kernel(pieces, *refs):
+    blocks = refs[:pieces]
+    _, out_ref, slot_ref, length_ref, window_ref, buffer, sems = refs[pieces:]
     capacity = buffer.shape[2]
-    me = lax.axis_index("inst")
-    blocks = [near_ref.at[piece] for piece in range(near)] + list(far_refs)
 
     def store(piece):
         slot = jnp.maximum(slot_ref[piece], 0)
         return pltpu.make_async_copy(buffer.at[piece], out_ref.at[slot], sems.at[piece])
 
     for piece, block in enumerate(blocks):
-        slot, length = read_facts(block)
-        if piece < near:
-            slot = jnp.where(me % near == piece, -1, slot)
-        slot_ref[piece] = slot
-        length_ref[piece] = length
+        slot_ref[piece], length_ref[piece] = read_facts(block)
     for piece, block in enumerate(blocks):
 
         @pl.when(slot_ref[piece] >= 0)
@@ -395,44 +377,43 @@
             start = window_start(length, capacity)
             window_ref[piece] = buffer[piece, :, pl.ds(start, WINDOW), :]
 
-    for piece in range(len(blocks)):
+    for piece in range(pieces):
 
         @pl.when(slot_ref[piece] >= 0)
         def _():
             store(piece).wait()
 
 
-def land(near_got, far_got, moved):
-    near = near_got.shape[0]
-    pieces = near + len(far_got)
+def land(got, moved):
+    pieces = len(got)
     smem = pl.BlockSpec(memory_space=pltpu.SMEM)
     vmem = pl.BlockSpec(memory_space=pltpu.VMEM)
     hbm = pl.BlockSpec(memory_space=pl.ANY)
     scalars = jax.ShapeDtypeStruct((pieces,), jnp.int32)
     return pl.pallas_call(
-        functools.partial(land_kernel, near),
+        functools.partial(land_kernel, pieces),
         out_shape=[
             jax.ShapeDtypeStruct(moved.shape, moved.dtype),
             scalars,
             scalars,
             jax.ShapeDtypeStruct((pieces, 2, WINDOW, moved.shape[3]), moved.dtype),
         ],
-        in_specs=[vmem] * (1 + len(far_got)) + [hbm],
+        in_specs=[vmem] * pieces + [hbm],
         out_specs=[hbm, smem, smem, vmem],
         scratch_shapes=[
             pltpu.VMEM((pieces,) + moved.shape[1:], moved.dtype),
             pltpu.SemaphoreType.DMA((pieces,)),
         ],
-        input_output_aliases={1 + len(far_got): 0},
+        input_output_aliases={pieces: 0},
         compiler_params=pltpu.CompilerParams(vmem_limit_bytes=SMALL_LIMIT),
         cost_estimate=HEAVY,
         name="land",
-    )(near_got, *far_got, moved)
+    )(*got, moved)
 
 
 def settle_kernel(
     count,
-    near,
+    early,
     group,
     slot_ref,
     length_ref,
@@ -451,7 +432,7 @@
     capacity, lanes = moved_ref.shape[2:]
     heads = lanes // HD
     me = lax.axis_index("inst")
-    pieces = slot_ref.shape[0]
+    pieces = len(early)
 
     def store(piece):
         slot = jnp.maximum(slot_ref[piece], 0)
@@ -470,17 +451,17 @@
         @pl.when(slot_ref[piece] >= 0)
         def _():
             length = length_ref[piece]
-            peer = peer_of(me, piece, near, False)
+            peer = peer_from(me, early[piece], count)
             news = small_ref[peer, per_row:, :].astype(jnp.float32)
             ahead = length - window_start(length, capacity)
             insert(window_ref.at[piece], news, ahead, steps, windows.at[piece])
             store(piece).start()
 
     mixed[...] = mixed_ref[...].astype(jnp.float32)
-    for piece in range(count):
-        peer = peer_of(me, piece, near, False)
-        if piece < pieces:
-            slot = slot_ref[piece]
+    for shift in range(1, count):
+        peer = peer_from(me, shift, count)
+        if shift in early:
+            slot = slot_ref[early.index(shift)]
         else:
             line = 2 * steps * heads
             facts = small_ref[peer, per_row:, :].astype(jnp.float32)[line : line + 1]
@@ -501,12 +482,12 @@
             store(piece).wait()
 
 
-def settle(slots, lengths, mixed, small, windows, moved, shape, group, count, near):
+def settle(slots, lengths, mixed, small, windows, moved, shape, group, count, early):
     smem = pl.BlockSpec(memory_space=pltpu.SMEM)
     vmem = pl.BlockSpec(memory_space=pltpu.VMEM)
     hbm = pl.BlockSpec(memory_space=pl.ANY)
     return pl.pallas_call(
-        functools.partial(settle_kernel, count, near, group),
+        functools.partial(settle_kernel, count, early, group),
         out_shape=[
             jax.ShapeDtypeStruct(shape, jnp.bfloat16),
             jax.ShapeDtypeStruct(moved.shape, moved.dtype),
@@ -525,64 +506,75 @@
     )(slots, lengths, mixed, small, windows, moved)
 
 
-def finish_kernel(count, near, steps, late_ref, small_ref, _, out_ref, buffer, sem):
-    capacity, lanes = buffer.shape[1:]
-    news_rows = 2 * steps * (lanes // HD)
-    slot, length = read_facts(late_ref)
-    peer = peer_of(lax.axis_index("inst"), count - 1, near, False)
-
-    @pl.when(slot >= 0)
-    def _():
-        clean(late_ref, length, buffer)
-        start = window_start(length, capacity)
-        window = buffer.at[:, pl.ds(start, WINDOW), :]
-        height = small_ref.shape[1]
-        tail = height - -(-(news_rows + 1) // TILE) * TILE
-        news = small_ref[peer, tail:, :].astype(jnp.float32)
-        insert(window, news, length - start, steps, window)
-        copy = pltpu.make_async_copy(buffer, out_ref.at[slot], sem)
-        copy.start()
-        copy.wait()
-
-
-def finish(late_got, small, moved, steps, count, near):
+def finish_kernel(count, late, steps, *refs):
+    blocks = refs[: len(late)]
+    small_ref, _, out_ref, buffer, sems, slot_ref = refs[len(late) :]
+    capacity, lanes = buffer.shape[2:]
+    height = small_ref.shape[1]
+    tail = height - -(-(2 * steps * (lanes // HD) + 1) // TILE) * TILE
+    me = lax.axis_index("inst")
+
+    def store(piece):
+        slot = jnp.maximum(slot_ref[piece], 0)
+        return pltpu.make_async_copy(buffer.at[piece], out_ref.at[slot], sems.at[piece])
+
+    facts = [read_facts(block) for block in blocks]
+    for piece, (slot, length) in enumerate(facts):
+        slot_ref[piece] = slot
+
+        @pl.when(slot >= 0)
+        def _():
+            clean(blocks[piece], length, buffer.at[piece])
+            start = window_start(length, capacity)
+            window = buffer.at[piece, :, pl.ds(start, WINDOW), :]
+            news = small_ref[peer_from(me, late[piece], count), tail:, :].astype(jnp.float32)
+            insert(window, news, length - start, steps, window)
+            store(piece).start()
+
+    for piece in range(len(late)):
+
+        @pl.when(slot_ref[piece] >= 0)
+        def _():
+            store(piece).wait()
+
+
+def finish(got, small, moved, steps, count, late):
     vmem = pl.BlockSpec(memory_space=pltpu.VMEM)
     hbm = pl.BlockSpec(memory_space=pl.ANY)
     return pl.pallas_call(
-        functools.partial(finish_kernel, count, near, steps),
+        functools.partial(finish_kernel, count, late, steps),
         out_shape=jax.ShapeDtypeStruct(moved.shape, moved.dtype),
-        in_specs=[vmem, vmem, hbm],
+        in_specs=[vmem] * len(got) + [vmem, hbm],
         out_specs=hbm,
         scratch_shapes=[
-            pltpu.VMEM(late_got.shape, late_got.dtype),
-            pltpu.SemaphoreType.DMA,
+            pltpu.VMEM((len(got),) + moved.shape[1:], moved.dtype),
+            pltpu.SemaphoreType.DMA((len(got),)),
+            pltpu.SMEM((len(got),), jnp.int32),
         ],
-        input_output_aliases={2: 0},
+        input_output_aliases={len(got) + 1: 0},
         compiler_params=pltpu.CompilerParams(vmem_limit_bytes=SMALL_LIMIT),
         cost_estimate=LIGHT,
         name="finish",
-    )(late_got, small, moved)
+    )(*got, small, moved)
 
 
 def local(hidden_new, queries, kv_cache, lengths, destination, key_weight, value_weight, key_gain):
     steps = queries.shape[0]
     group = queries.shape[2] // kv_cache.shape[3]
     count = lax.axis_size("inst")
-    near = near_size(count)
-
-    def send(block, piece):
-        pairs = [(i, peer_to(i, piece, count)) for i in range(count)]
+    early = list(range(max(count // 2, 1), count - 1))
+    late = [count - 1] + list(range(1, max(count // 2, 1)))
+
+    def send(block, shift):
+        pairs = [(i, peer_to(i, shift, count)) for i in range(count)]
         return lax.ppermute(block, "inst", pairs)
 
-    near_blocks, far_blocks, pick = pack(kv_cache, destination, lengths, count, near)
-    near_got = near_blocks
-    if near > 1:
-        teams = [list(range(i, i + near)) for i in range(0, count, near)]
-        near_got = lax.all_to_all(near_blocks, "inst", 0, 0, axis_index_groups=teams, tiled=True)
-    far_got = [send(block, piece) for piece, block in enumerate(far_blocks[:-1], near)]
-    own, other = project(hidden_new, key_weight, value_weight)
+    blocks, pick, own, other = prepare(
+        destination, lengths, hidden_new, kv_cache, key_weight, value_weight, count
+    )
+    early_got = [send(blocks[shift - 1], shift) for shift in early]
     got = lax.ppermute(other, "tp", [(0, 1), (1, 0)])
-    moved, mixed, small, late = attend(
+    moved, mixed, small, late_blocks = attend(
         kv_cache,
         queries,
         own,
@@ -591,16 +583,16 @@
         lengths,
         destination,
         pick,
-        far_blocks[-1],
+        [blocks[shift - 1] for shift in late],
         count,
     )
-    late_got = send(late, count - 1)
+    late_got = [send(block, shift) for block, shift in zip(late_blocks, late)]
     small_got = lax.all_to_all(small, "inst", 0, 0, tiled=True)
-    moved, slots, arrived, windows = land(near_got, far_got, moved)
+    moved, slots, arrived, windows = land(early_got, moved)
     attended, moved = settle(
-        slots, arrived, mixed, small_got, windows, moved, queries.shape, group, count, near
+        slots, arrived, mixed, small_got, windows, moved, queries.shape, group, count, early
     )
-    return attended, finish(late_got, small_got, moved, steps, count, near)
+    return attended, finish(late_got, small_got, moved, steps, count, late)
 
 
 def solution(mesh):

time: 46.9 us -> 46.1 us (0.983)
  Pallas kernels: 19.1 us -> 17.5 us
  starting transfers between devices: 19.2 us -> 20.5 us
    ppermute x4 -> x7, starting transfers between devices: 7.93 us -> 17.1 us  [send(): return lax.ppermute(block, 'inst', pairs)]
    all_to_all x1, waiting for transfers between devices: 5.31 us -> 0.01 us  [local(): small_got = lax.all_to_all(small, 'inst', 0, 0, tiled=True)]
    all_to_all x1 -> x0, starting transfers between devices: 5.26 us -> none  [local(): lax.all_to_all(near_blocks, 'inst', 0, 0, axis_index_groups=teams, tiled=...]
    ppermute x4 -> x7, waiting for transfers between devices: 0.01 us -> 4.91 us  [send(): return lax.ppermute(block, 'inst', pairs)]
    all_to_all x1, starting transfers between devices: 5.98 us -> 3.36 us  [local(): small_got = lax.all_to_all(small, 'inst', 0, 0, tiled=True)]
    pallas_call x5 -> x4, Pallas kernels: 12.3 us -> 10.8 us  [the longest x1 6.05 us: prepare(): pl.pallas_call(functools.partial(prepare_kernel, count, chunks), out_shap...]
  transfers between devices with their start and end apart: 7 -> 9, of which waited for: 2 -> 3; matrix products, arithmetic and copies ran while one was open for 0% -> 0% of each run, Pallas kernels for 32% -> 23%
where the time goes in v5:
time: 46.1 us; the launch traced here: 45.8 us
  starting transfers between devices  20.5 us (44%)
  Pallas kernels  17.5 us (38%)
  waiting for transfers between devices  6.43 us (14%)
  between operations  0.7 us (2%)
  local copies, waits for them, and re-layouts  0.64 us (1%)
    ppermute x7, starting transfers between devices, send(): return lax.ppermute(block, 'inst', pairs)  17.1 us
    pallas_call x1, Pallas kernels, attend(): pl.pallas_call(functools.partial(attend_kernel, count, block), grid=(rows...  6.79 us
    pallas_call x1, Pallas kernels, prepare(): pl.pallas_call(functools.partial(prepare_kernel, count, chunks), out_shap...  6.05 us
    ppermute x7, waiting for transfers between devices, send(): return lax.ppermute(block, 'inst', pairs)  4.91 us
    all_to_all x1, starting transfers between devices, local(): small_got = lax.all_to_all(small, 'inst', 0, 0, tiled=True)  3.36 us
    pallas_call x1, Pallas kernels, settle(): pl.pallas_call(functools.partial(settle_kernel, count, early, group), out...  2.11 us
    pallas_call x1, Pallas kernels, land(): pl.pallas_call(functools.partial(land_kernel, pieces), out_shape=[jax.Sha...  1.56 us
    ppermute x1, waiting for transfers between devices, local(): got = lax.ppermute(other, 'tp', [(0, 1), (1, 0)])  1.51 us
  transfers between devices with their start and end apart: 9, of which 3 were waited for; matrix products, arithmetic and copies ran while one was open for 0% of the time, Pallas kernels for 23%

profile of v5, /device:TPU:0, one launch (start us, length us, event | category | flops | bytes accessed | tf_op | source)
XLA Modules:
  0.0 45.8 jit_solution(7601159850457078265)
XLA Ops:
  0.6 6.0 %prepare.1 = (bf16[2,144,256]{2,1,0:T(8,128)(2,1)}, bf16[2,144,256]{2,1,0:T(8,128)(2,1)}, bf16[2,144,256]{2,1,0:T(8,128)(2,1)}, bf16[2,144,256]{2,1,0:T(8,128)(2...) custom-call(s32[24]{0:T(128)} %dest_ref.3, ...), custom_call_target="tpu_custom_call" | custom-call | flops 1 | bytes 1 | tf_op jit(solution)/shard_map/prepare/pallas_call | solution.py:128
  6.7 4.1 %collective-permute-start = (bf16[2,144,256]{2,1,0:T(8,128)(2,1)}, bf16[2,144,256]{2,1,0:T(8,128)(2,1)S(1)}, u32[]{:S(2)}, u32[]{:S(2)}) collective-permute-start(bf16[2,144,256]{2,1,0:T(8,128)(2,1)} %get-tuple-element.25), channel_id=1, source_target_pairs={{0,8},{2,10},{4,12},{6,14},{8,0},{10,2},{12,4},{14,6},{1,9},{3,11}... | collective-permute-start | bytes 442376 | tf_op jit(solution)/shard_map/ppermute | solution.py:570
  10.8 1.3 %collective-permute-start.1 = (bf16[2,144,256]{2,1,0:T(8,128)(2,1)}, bf16[2,144,256]{2,1,0:T(8,128)(2,1)S(1)}, u32[]{:S(2)}, u32[]{:S(2)}) collective-permute-start(bf16[2,144,256]{2,1,0:T(8,128)(2,1)} %get-tuple-element.26), channel_id=1, source_target_pairs={{0,10},{2,8},{4,14},{6,12},{8,2},{10,0},{12,6},{14,4},{1,11},{3,9}... | collective-permute-start | bytes 442376 | tf_op jit(solution)/shard_map/ppermute | solution.py:570
  12.1 3.6 %collective-permute-start.2 = (bf16[2,144,256]{2,1,0:T(8,128)(2,1)}, bf16[2,144,256]{2,1,0:T(8,128)(2,1)S(1)}, u32[]{:S(2)}, u32[]{:S(2)}) collective-permute-start(bf16[2,144,256]{2,1,0:T(8,128)(2,1)} %get-tuple-element.27), channel_id=1, source_target_pairs={{0,12},{2,14},{4,8},{6,10},{8,4},{10,6},{12,0},{14,2},{1,13},{3,15... | collective-permute-start | bytes 442376 | tf_op jit(solution)/shard_map/ppermute | solution.py:570
  15.7 0.0 collective-permute-start.3
  15.7 1.5 %collective-permute-done.3.got_ref = f32[48,512]{1,0:T(8,128)S(1)} collective-permute-done((f32[48,512]{1,0:T(8,128)}, f32[48,512]{1,0:T(8,128)S(1)}, u32[]{:S(2)}, u32[]{:S(2)}) %collective-permute-start.3) | collective-permute-done | bytes 98336 | tf_op jit(solution)/shard_map/ppermute | solution.py:576
  17.2 0.6 %copy-done.1 = f32[48,512]{1,0:T(8,128)} copy-done((f32[48,512]{1,0:T(8,128)}, f32[48,512]{1,0:T(8,128)S(1)}, u32[]{:S(2)}) %copy-start.1) | copy-done | bytes 98328
  17.8 6.8 %attend.1 = (bf16[24,2,144,256]{3,2,1,0:T(8,128)(2,1)}, bf16[768,128]{1,0:T(8,128)(2,1)}, bf16[8,48,128]{2,1,0:T(8,128)(2,1)}, bf16[2,144,256]{2,1,0:T(8,128)(2,...) custom-call(s32[24]{0:T(128)} %length_ref.3, ...), custom_call_target="tpu_custom_call", output_to_operand_aliasing={{3}: (8, {}), {4}: (9, {}), {5}: (10, {}), {6}: (11, {})} | custom-call | flops 1 | bytes 1 | tf_op jit(solution)/shard_map/attend/pallas_call | solution.py:299
  24.6 3.4 %all-to-all-start = ((bf16[8,48,128]{2,1,0:T(8,128)(2,1)}), bf16[8,48,128]{2,1,0:T(8,128)(2,1)S(1)}, u32[]{:S(2)}, u32[]{:S(2)}) async-start(bf16[8,48,128]{2,1,0:T(8,128)(2,1)} %get-tuple-element.39), calls=%async_computation | async-start | bytes 196608 | tf_op jit(solution)/shard_map/all_to_all | solution.py:590
  28.0 4.7 %collective-permute-start.4 = (bf16[2,144,256]{2,1,0:T(8,128)(2,1)}, bf16[2,144,256]{2,1,0:T(8,128)(2,1)S(1)}, u32[]{:S(2)}, u32[]{:S(2)}) collective-permute-start(bf16[2,144,256]{2,1,0:T(8,128)(2,1)} %get-tuple-element.43), channel_id=1, source_target_pairs={{0,14},{2,12},{4,10},{6,8},{8,6},{10,4},{12,2},{14,0},{1,15},{3,13... | collective-permute-start | bytes 442376 | tf_op jit(solution)/shard_map/ppermute | solution.py:570
  32.7 0.6 %collective-permute-start.5 = (bf16[2,144,256]{2,1,0:T(8,128)(2,1)}, bf16[2,144,256]{2,1,0:T(8,128)(2,1)S(1)}, u32[]{:S(2)}, u32[]{:S(2)}) collective-permute-start(bf16[2,144,256]{2,1,0:T(8,128)(2,1)} %get-tuple-element.44), channel_id=1, source_target_pairs={{0,2},{2,0},{4,6},{6,4},{8,10},{10,8},{12,14},{14,12},{1,3},{3,1},... | collective-permute-start | bytes 442376 | tf_op jit(solution)/shard_map/ppermute | solution.py:570
  33.2 0.0 collective-permute-done.refs_0_
  33.2 0.0 collective-permute-start.6
  33.2 0.0 collective-permute-done.1.refs_1_
  33.2 2.9 %collective-permute-start.7 = (bf16[2,144,256]{2,1,0:T(8,128)(2,1)}, bf16[2,144,256]{2,1,0:T(8,128)(2,1)S(1)}, u32[]{:S(2)}, u32[]{:S(2)}) collective-permute-start(bf16[2,144,256]{2,1,0:T(8,128)(2,1)} %get-tuple-element.46), channel_id=1, source_target_pairs={{0,6},{2,4},{4,2},{6,0},{8,14},{10,12},{12,10},{14,8},{1,7},{3,5},... | collective-permute-start | bytes 442376 | tf_op jit(solution)/shard_map/ppermute | solution.py:570
  36.1 0.0 collective-permute-done.2.refs_2_
  36.2 1.6 %land.1 = (bf16[24,2,144,256]{3,2,1,0:T(8,128)(2,1)}, s32[3]{0:T(128)S(1)}, s32[3]{0:T(128)S(1)}, bf16[3,2,32,256]{3,2,1,0:T(8,128)(2,1)S(1)}) custom-call(bf16[2,144,256]{2,1,0:T(8,128)(2,1)S(1)} %collective-permute-done.refs_0_, bf16[2,144,256]{2,1,0:T(8,128)(2,1)S(1)} %collective-permute-done.1.refs_1_, ...), custom_call_target="tpu_custom_call", output_to_operand_aliasing={{0}: (3, {})} | custom-call | flops 68719476736 | bytes 268435456 | tf_op jit(solution)/shard_map/land/pallas_call | solution.py:393
  37.7 0.0 all-to-all-done.small_ref.refs_4_
  37.7 2.1 %settle.1 = (bf16[2,24,2048]{2,1,0:T(8,128)(2,1)}, bf16[24,2,144,256]{3,2,1,0:T(8,128)(2,1)}) custom-call(s32[3]{0:T(128)S(1)} %get-tuple-element.36.slot_ref, s32[3]{0:T(128)S(1)} %get-tuple-element.37.length_ref, bf16[768,128]{1,0:T(8,128)(2,1)S(1)} %copy-done, ...), custom_call_target="tpu_custom_call", output_to_operand_aliasing={{1}: (5, {})} | custom-call | flops 1 | bytes 1 | tf_op jit(solution)/shard_map/settle/pallas_call | solution.py:489
  39.9 0.0 collective-permute-done.4.refs_0_
  39.9 1.3 %collective-permute-done.5.refs_1_ = bf16[2,144,256]{2,1,0:T(8,128)(2,1)S(1)} collective-permute-done((bf16[2,144,256]{2,1,0:T(8,128)(2,1)}, bf16[2,144,256]{2,1,0:T(8,128)(2,1)S(1)}, u32[]{:S(2)}, u32[]{:S(2)}) %collective-permute-start.5) | collective-permute-done | bytes 147488 | tf_op jit(solution)/shard_map/ppermute | solution.py:570
  41.2 0.0 collective-permute-done.6.refs_2_
  41.2 3.6 %collective-permute-done.7.refs_3_ = bf16[2,144,256]{2,1,0:T(8,128)(2,1)S(1)} collective-permute-done((bf16[2,144,256]{2,1,0:T(8,128)(2,1)}, bf16[2,144,256]{2,1,0:T(8,128)(2,1)S(1)}, u32[]{:S(2)}, u32[]{:S(2)}) %collective-permute-start.7) | collective-permute-done | bytes 147488 | tf_op jit(solution)/shard_map/ppermute | solution.py:570
  44.8 1.0 %finish.1 = bf16[24,2,144,256]{3,2,1,0:T(8,128)(2,1)} custom-call(bf16[2,144,256]{2,1,0:T(8,128)(2,1)S(1)} %collective-permute-done.4.refs_0_, bf16[2,144,256]{2,1,0:T(8,128)(2,1)S(1)} %collective-permute-done.5.refs_1_, bf16[2,144,256]{2,1,0:T(8,128)(2,1)S(1)} %collective-permute-done.6.refs_2_, ...), custom_call_target="tpu_custom_call", output_to_operand_aliasing={{}: (5, {})} | custom-call | flops 1 | bytes 1 | tf_op jit(solution)/shard_map/finish/pallas_call | solution.py:544
  (3 shorter events, 0.0 us)
Async XLA Ops:
  6.7 26.5 %collective-permute-start = (bf16[2,144,256]{2,1,0:T(8,128)(2,1)}, bf16[2,144,256]{2,1,0:T(8,128)(2,1)S(1)}, u32[]{:S(2)}, u32[]{:S(2)}) collective-permute-start(bf16[2,144,256]{2,1,0:T(8,128)(2,1)} %get-tuple-element.25), channel_id=1, source_target_pairs={{0,8},{2,10},{4,12},{6,14},{8,0},{10,2},{12,4},{14,6},{1,9},{3,11}... | collective-permute-start | bytes 442376 | tf_op jit(solution)/shard_map/ppermute | solution.py:570
  10.8 22.4 %collective-permute-start.1 = (bf16[2,144,256]{2,1,0:T(8,128)(2,1)}, bf16[2,144,256]{2,1,0:T(8,128)(2,1)S(1)}, u32[]{:S(2)}, u32[]{:S(2)}) collective-permute-start(bf16[2,144,256]{2,1,0:T(8,128)(2,1)} %get-tuple-element.26), channel_id=1, source_target_pairs={{0,10},{2,8},{4,14},{6,12},{8,2},{10,0},{12,6},{14,4},{1,11},{3,9}... | collective-permute-start | bytes 442376 | tf_op jit(solution)/shard_map/ppermute | solution.py:570
  12.1 24.1 %collective-permute-start.2 = (bf16[2,144,256]{2,1,0:T(8,128)(2,1)}, bf16[2,144,256]{2,1,0:T(8,128)(2,1)S(1)}, u32[]{:S(2)}, u32[]{:S(2)}) collective-permute-start(bf16[2,144,256]{2,1,0:T(8,128)(2,1)} %get-tuple-element.27), channel_id=1, source_target_pairs={{0,12},{2,14},{4,8},{6,10},{8,4},{10,6},{12,0},{14,2},{1,13},{3,15... | collective-permute-start | bytes 442376 | tf_op jit(solution)/shard_map/ppermute | solution.py:570
  15.7 1.5 %collective-permute-start.3 = (f32[48,512]{1,0:T(8,128)}, f32[48,512]{1,0:T(8,128)S(1)}, u32[]{:S(2)}, u32[]{:S(2)}) collective-permute-start(f32[48,512]{1,0:T(8,128)} %get-tuple-element.30), channel_id=1, source_target_pairs={{0,1},{1,0},{2,3},{3,2},{4,5},{5,4},{6,7},{7,6},{8,9},{9,8},{10,11... | collective-permute-start | bytes 294920 | tf_op jit(solution)/shard_map/ppermute | solution.py:576
  17.2 0.6 %copy-start.1 = (f32[48,512]{1,0:T(8,128)}, f32[48,512]{1,0:T(8,128)S(1)}, u32[]{:S(2)}) copy-start(f32[48,512]{1,0:T(8,128)S(1)} %collective-permute-done.3.got_ref) | copy-start | bytes 294916
  24.6 13.1 %all-to-all-start = ((bf16[8,48,128]{2,1,0:T(8,128)(2,1)}), bf16[8,48,128]{2,1,0:T(8,128)(2,1)S(1)}, u32[]{:S(2)}, u32[]{:S(2)}) async-start(bf16[8,48,128]{2,1,0:T(8,128)(2,1)} %get-tuple-element.39), calls=%async_computation | async-start | bytes 196608 | tf_op jit(solution)/shard_map/all_to_all | solution.py:590
  28.0 11.9 %collective-permute-start.4 = (bf16[2,144,256]{2,1,0:T(8,128)(2,1)}, bf16[2,144,256]{2,1,0:T(8,128)(2,1)S(1)}, u32[]{:S(2)}, u32[]{:S(2)}) collective-permute-start(bf16[2,144,256]{2,1,0:T(8,128)(2,1)} %get-tuple-element.43), channel_id=1, source_target_pairs={{0,14},{2,12},{4,10},{6,8},{8,6},{10,4},{12,2},{14,0},{1,15},{3,13... | collective-permute-start | bytes 442376 | tf_op jit(solution)/shard_map/ppermute | solution.py:570
  32.7 8.5 %collective-permute-start.5 = (bf16[2,144,256]{2,1,0:T(8,128)(2,1)}, bf16[2,144,256]{2,1,0:T(8,128)(2,1)S(1)}, u32[]{:S(2)}, u32[]{:S(2)}) collective-permute-start(bf16[2,144,256]{2,1,0:T(8,128)(2,1)} %get-tuple-element.44), channel_id=1, source_target_pairs={{0,2},{2,0},{4,6},{6,4},{8,10},{10,8},{12,14},{14,12},{1,3},{3,1},... | collective-permute-start | bytes 442376 | tf_op jit(solution)/shard_map/ppermute | solution.py:570
  33.2 7.9 %collective-permute-start.6 = (bf16[2,144,256]{2,1,0:T(8,128)(2,1)}, bf16[2,144,256]{2,1,0:T(8,128)(2,1)S(1)}, u32[]{:S(2)}, u32[]{:S(2)}) collective-permute-start(bf16[2,144,256]{2,1,0:T(8,128)(2,1)} %get-tuple-element.45), channel_id=1, source_target_pairs={{0,4},{2,6},{4,0},{6,2},{8,12},{10,14},{12,8},{14,10},{1,5},{3,7},... | collective-permute-start | bytes 442376 | tf_op jit(solution)/shard_map/ppermute | solution.py:570
  33.2 11.6 %collective-permute-start.7 = (bf16[2,144,256]{2,1,0:T(8,128)(2,1)}, bf16[2,144,256]{2,1,0:T(8,128)(2,1)S(1)}, u32[]{:S(2)}, u32[]{:S(2)}) collective-permute-start(bf16[2,144,256]{2,1,0:T(8,128)(2,1)} %get-tuple-element.46), channel_id=1, source_target_pairs={{0,6},{2,4},{4,2},{6,0},{8,14},{10,12},{12,10},{14,8},{1,7},{3,5},... | collective-permute-start | bytes 442376 | tf_op jit(solution)/shard_map/ppermute | solution.py:570
  36.2 1.6 %copy-start = (bf16[768,128]{1,0:T(8,128)(2,1)S(1)}, bf16[768,128]{1,0:T(8,128)(2,1)}, u32[]{:S(2)}) copy-start(bf16[768,128]{1,0:T(8,128)(2,1)} %get-tuple-element.38.mixed_ref) | copy-start | bytes 589828

commit v6 on v5

--- a/solution.py
+++ b/solution.py
@@ -41,25 +41,15 @@
     count, chunks, dest_ref, length_ref, hidden_ref, kv_ref, key_ref, value_ref, *refs
 ):
     block_refs = refs[: count - 1]
-    pick_ref, own_ref, other_ref, blocks, held, total = refs[count - 1 : count + 5]
-    in_sems, out_sems, weight_sems = refs[count + 5 :]
+    pick_ref, own_ref, other_ref, blocks, hidden_held, held, total = refs[count - 1 : count + 6]
+    in_sems, out_sems, hidden_sem, weight_sems = refs[count + 6 :]
     rows = dest_ref.shape[0]
     capacity, lanes = kv_ref.shape[2:]
     me = lax.axis_index("inst")
     shifts = range(1, count)
 
-    for peer in range(count):
-        pick_ref[peer] = 0
-    for row in range(rows):
-        pick_ref[quotient(dest_ref[row], rows, rows * count)] = row
-    fetches, stores = {}, {}
-    for shift in shifts:
-        row = pick_ref[peer_to(me, shift, count)]
-        fetches[shift] = pltpu.make_async_copy(
-            kv_ref.at[row], blocks.at[shift - 1], in_sems.at[shift - 1]
-        )
-        fetches[shift].start()
-
+    hidden_copy = pltpu.make_async_copy(hidden_ref, hidden_held, hidden_sem)
+    hidden_copy.start()
     steps, _, depth = hidden_ref.shape
     width = key_ref.shape[1]
     part = depth // chunks
@@ -73,6 +63,18 @@
                 )
             )
             weights[-1].start()
+
+    for peer in range(count):
+        pick_ref[peer] = 0
+    for row in range(rows):
+        pick_ref[quotient(dest_ref[row], rows, rows * count)] = row
+    fetches, stores = {}, {}
+    for shift in shifts:
+        row = pick_ref[peer_to(me, shift, count)]
+        fetches[shift] = pltpu.make_async_copy(
+            kv_ref.at[row], blocks.at[shift - 1], in_sems.at[shift - 1]
+        )
+        fetches[shift].start()
 
     tile = (TILE, lanes)
     last = lax.broadcasted_iota(jnp.int32, tile, 0) == TILE - 1
@@ -93,7 +95,8 @@
         )
         stores[shift].start()
 
-    hidden = hidden_ref[...].reshape(steps * rows, depth)
+    hidden_copy.wait()
+    hidden = hidden_held[...].reshape(steps * rows, depth)
     sums = [None, None]
     for chunk in range(chunks):
         for which in range(2):
@@ -129,14 +132,16 @@
         functools.partial(prepare_kernel, count, chunks),
         out_shape=[jax.ShapeDtypeStruct(shape, kv_cache.dtype)] * (count - 1)
         + [jax.ShapeDtypeStruct((count,), jnp.int32), part, part],
-        in_specs=[smem, smem, vmem, hbm, hbm, hbm],
+        in_specs=[smem, smem, hbm, hbm, hbm, hbm],
         out_specs=[hbm] * (count - 1) + [smem, vmem, vmem],
         scratch_shapes=[
             pltpu.VMEM((count - 1,) + shape, kv_cache.dtype),
+            pltpu.VMEM(hidden_new.shape, hidden_new.dtype),
             pltpu.VMEM((2, depth, width), key_weight.dtype),
             pltpu.VMEM((steps * rows, 2 * width), jnp.float32),
             pltpu.SemaphoreType.DMA((count - 1,)),
             pltpu.SemaphoreType.DMA((count - 1,)),
+            pltpu.SemaphoreType.DMA,
             pltpu.SemaphoreType.DMA((chunks, 2)),
         ],
         compiler_params=pltpu.CompilerParams(vmem_limit_bytes=VMEM_LIMIT),
@@ -173,10 +178,10 @@
     kv_ref,
     *refs,
 ):
-    late = (len(refs) - 7) // 2
+    late = (len(refs) - 14) // 2
     moved_ref, mixed_ref, small_ref = refs[late : late + 3]
-    fresh, query_rows, query_columns, mixed = refs[-4:]
-    part = pl.program_id(0)
+    fresh, query_held, query_rows, query_columns, mixed, sums, held = refs[-11:-4]
+    sum_sems, query_sem, in_sems, out_sems = refs[-4:]
     steps, rows, query_width = query_ref.shape
     capacity, lanes = kv_ref.shape[2:]
     heads = lanes // HD
@@ -185,29 +190,55 @@
     per_row = heads * per_head
     team = HD // per_row
 
-    @pl.when(part == 0)
-    def _():
-        raw = own_ref[...] + got_ref[...]
-        cosine, sine = rotation(length_ref, steps, rows)
-        gain = gain_ref[...].astype(jnp.float32)
-        for head in range(heads):
-            at = slice(head * HD, (head + 1) * HD)
-            piece = raw[:, at]
-            mean = jnp.mean(piece * piece, axis=-1, keepdims=True)
-            piece = piece * lax.rsqrt(mean + NORM_EPS) * gain
-            swapped = jnp.concatenate([piece[:, HD // 2 :], piece[:, : HD // 2]], axis=1)
-            turned = piece * cosine + swapped * sine
-            fresh[0, :, at] = turned.astype(jnp.bfloat16).astype(jnp.float32)
-        fresh[1] = raw[:, lanes:].astype(jnp.bfloat16).astype(jnp.float32)
-        for step in range(steps):
-            for chunk in range(query_width // HD):
-                head, member = chunk // group, chunk % group
-                at = head * per_head + step * group + member
-                query_rows[pl.ds(at, rows, stride=per_row), :] = query_ref[
-                    step, :, chunk * HD : (chunk + 1) * HD
-                ].astype(jnp.float32)
-        for index in range(rows // team):
-            query_columns[index] = query_rows[index * HD : (index + 1) * HD, :].T
+    query_copy = pltpu.make_async_copy(query_ref, query_held, query_sem)
+    query_copy.start()
+    sum_copies = [
+        pltpu.make_async_copy(ref, sums.at[index], sum_sems.at[index])
+        for index, ref in enumerate((own_ref, got_ref))
+    ]
+    for copy in sum_copies:
+        copy.start()
+
+    def span(index):
+        return pl.ds(index * team, team)
+
+    def fetch(index):
+        return pltpu.make_async_copy(
+            kv_ref.at[span(index)], held.at[span(index)], in_sems.at[index]
+        )
+
+    def store(index):
+        return pltpu.make_async_copy(
+            held.at[span(index)], moved_ref.at[span(index)], out_sems.at[index]
+        )
+
+    for index in range(rows // team):
+        fetch(index).start()
+
+    cosine, sine = rotation(length_ref, steps, rows)
+    query_copy.wait()
+    for step in range(steps):
+        for chunk in range(query_width // HD):
+            head, member = chunk // group, chunk % group
+            at = head * per_head + step * group + member
+            query_rows[pl.ds(at, rows, stride=per_row), :] = query_held[
+                step, :, chunk * HD : (chunk + 1) * HD
+            ].astype(jnp.float32)
+    for index in range(rows // team):
+        query_columns[index] = query_rows[index * HD : (index + 1) * HD, :].T
+    for copy in sum_copies:
+        copy.wait()
+    raw = sums[0] + sums[1]
+    gain = gain_ref[...].astype(jnp.float32)
+    for head in range(heads):
+        at = slice(head * HD, (head + 1) * HD)
+        piece = raw[:, at]
+        mean = jnp.mean(piece * piece, axis=-1, keepdims=True)
+        piece = piece * lax.rsqrt(mean + NORM_EPS) * gain
+        swapped = jnp.concatenate([piece[:, HD // 2 :], piece[:, : HD // 2]], axis=1)
+        turned = piece * cosine + swapped * sine
+        fresh[0, :, at] = turned.astype(jnp.bfloat16).astype(jnp.float32)
+    fresh[1] = raw[:, lanes:].astype(jnp.bfloat16).astype(jnp.float32)
 
     position = lax.broadcasted_iota(jnp.int32, (capacity, HD), 0)
     column = lax.broadcasted_iota(jnp.int32, (capacity, HD), 1)
@@ -216,69 +247,77 @@
     column_head = lax.broadcasted_iota(jnp.int32, (HD, HD), 1) % per_row // per_head
     factor = 1.0 / math.sqrt(HD)
     teams = range(block // team)
-    scores = []
-    for index in teams:
-        queries = query_columns[part * (block // team) + index]
-        queries = jnp.concatenate(
-            [jnp.where(column_head == head, queries, 0.0) for head in range(heads)], axis=0
-        ).astype(jnp.bfloat16)
-        score, limit = None, None
-        for member in range(team):
-            item = index * team + member
-            row = part * block + item
-            length = length_ref[row]
-            kept = position < length
-            landing = [position == length + step for step in range(steps)]
-            for which in range(2):
-                news = [fresh[which, pl.ds(step * rows + row, 1), :] for step in range(steps)]
+
+    def work(part, carry):
+        for index in teams:
+            fetch(part * len(teams) + index).wait()
+        scores = []
+        for index in teams:
+            queries = query_columns[part * len(teams) + index]
+            queries = jnp.concatenate(
+                [jnp.where(column_head == head, queries, 0.0) for head in range(heads)], axis=0
+            ).astype(jnp.bfloat16)
+            score, limit = None, None
+            for member in range(team):
+                row = part * block + index * team + member
+                length = length_ref[row]
+                kept = position < length
+                landing = [position == length + step for step in range(steps)]
+                for which in range(2):
+                    news = [fresh[which, pl.ds(step * rows + row, 1), :] for step in range(steps)]
+                    for head in range(heads):
+                        at = slice(head * HD, (head + 1) * HD)
+                        stored = held[row, which, :, at].astype(jnp.float32)
+                        stored = jnp.where(kept, stored, 0.0)
+                        for step in range(steps):
+                            stored = jnp.where(landing[step], news[step][:, at], stored)
+                        held[row, which, :, at] = stored.astype(jnp.bfloat16)
+                one = jnp.dot(held[row, 0], queries, preferred_element_type=jnp.float32)
+                score = one if member == 0 else jnp.where(column_item == member, one, score)
+                limit = length if member == 0 else jnp.where(column_item == member, length, limit)
+            scores.append(jnp.where(position <= limit + column_step, score * factor, -jnp.inf))
+        weights = []
+        for score in scores:
+            raised = jnp.exp(score - jnp.max(score, axis=0, keepdims=True))
+            normaliser = jnp.sum(raised, axis=0, keepdims=True)
+            weights.append((raised / normaliser).T.astype(jnp.bfloat16))
+        for index in teams:
+            for member in range(team):
+                row = part * block + index * team + member
+                result = jnp.dot(
+                    weights[index][member * per_row : (member + 1) * per_row],
+                    held[row, 1],
+                    preferred_element_type=jnp.float32,
+                )
                 for head in range(heads):
-                    at = slice(head * HD, (head + 1) * HD)
-                    stored = jnp.where(kept, kv_ref[item, which, :, at].astype(jnp.float32), 0.0)
-                    for step in range(steps):
-                        stored = jnp.where(landing[step], news[step][:, at], stored)
-                    moved_ref[item, which, :, at] = stored.astype(jnp.bfloat16)
-            one = jnp.dot(moved_ref[item, 0], queries, preferred_element_type=jnp.float32)
-            score = one if member == 0 else jnp.where(column_item == member, one, score)
-            limit = length if member == 0 else jnp.where(column_item == member, length, limit)
-        scores.append(jnp.where(position <= limit + column_step, score * factor, -jnp.inf))
-    weights = []
-    for score in scores:
-        raised = jnp.exp(score - jnp.max(score, axis=0, keepdims=True))
-        normaliser = jnp.sum(raised, axis=0, keepdims=True)
-        weights.append((raised / normaliser).T.astype(jnp.bfloat16))
-    for index in teams:
-        for member in range(team):
-            item = index * team + member
-            row = part * block + item
-            result = jnp.dot(
-                weights[index][member * per_row : (member + 1) * per_row],
-                moved_ref[item, 1],
-                preferred_element_type=jnp.float32,
-            )
-            for head in range(heads):
-                at = pl.multiple_of(row * per_row + head * per_head, per_head)
-                mixed[pl.ds(at, per_head), :] = result[
-                    head * per_head : (head + 1) * per_head, head * HD : (head + 1) * HD
-                ]
-
-    @pl.when(part == pl.num_programs(0) - 1)
-    def _():
-        mixed_ref[...] = mixed[...].astype(jnp.bfloat16)
-        for peer in range(count):
-            row = pick_ref[peer]
-            small_ref[peer, :per_row, :] = mixed[
-                pl.ds(pl.multiple_of(row * per_row, per_row), per_row), :
-            ].astype(jnp.bfloat16)
-            news = []
-            for which in range(2):
-                for step in range(steps):
-                    new = fresh[which, pl.ds(step * rows + row, 1), :]
-                    news += [new[:, h * HD : (h + 1) * HD] for h in range(heads)]
-            slot = dest_ref[row] - peer * rows
-            slot = jnp.where((slot >= 0) & (slot < rows), slot, -1).astype(jnp.float32)
-            fill = small_ref.shape[1] - per_row - len(news)
-            news.append(jnp.full((fill, HD), slot))
-            small_ref[peer, per_row:, :] = jnp.concatenate(news, axis=0).astype(jnp.bfloat16)
+                    at = pl.multiple_of(row * per_row + head * per_head, per_head)
+                    mixed[pl.ds(at, per_head), :] = result[
+                        head * per_head : (head + 1) * per_head, head * HD : (head + 1) * HD
+                    ]
+        for index in teams:
+            store(part * len(teams) + index).start()
+        return carry
+
+    lax.fori_loop(0, rows // block, work, 0)
+
+    mixed_ref[...] = mixed[...].astype(jnp.bfloat16)
+    for peer in range(count):
+        row = pick_ref[peer]
+        small_ref[peer, :per_row, :] = mixed[
+            pl.ds(pl.multiple_of(row * per_row, per_row), per_row), :
+        ].astype(jnp.bfloat16)
+        news = []
+        for which in range(2):
+            for step in range(steps):
+                new = fresh[which, pl.ds(step * rows + row, 1), :]
+                news += [new[:, h * HD : (h + 1) * HD] for h in range(heads)]
+        slot = dest_ref[row] - peer * rows
+        slot = jnp.where((slot >= 0) & (slot < rows), slot, -1).astype(jnp.float32)
+        fill = small_ref.shape[1] - per_row - len(news)
+        news.append(jnp.full((fill, HD), slot))
+        small_ref[peer, per_row:, :] = jnp.concatenate(news, axis=0).astype(jnp.bfloat16)
+    for index in range(rows // team):
+        store(index).wait()
 
 
 def attend(
@@ -290,32 +329,38 @@
     heads = lanes // HD
     per_row = steps * query_width // HD
     block = 8
+    teams = rows * per_row // HD
     small_rows = per_row + -(-(2 * steps * heads + 1) // TILE) * TILE
     small = jax.ShapeDtypeStruct((count, small_rows, HD), jnp.bfloat16)
     smem = pl.BlockSpec(memory_space=pltpu.SMEM)
     vmem = pl.BlockSpec(memory_space=pltpu.VMEM)
     hbm = pl.BlockSpec(memory_space=pl.ANY)
-    cache_block = pl.BlockSpec((block, 2, capacity, lanes), lambda i: (i, 0, 0, 0))
     outs = pl.pallas_call(
         functools.partial(attend_kernel, count, block),
-        grid=(rows // block,),
         out_shape=[
             jax.ShapeDtypeStruct(kv_cache.shape, kv_cache.dtype),
             jax.ShapeDtypeStruct((rows * per_row, HD), jnp.bfloat16),
             small,
         ]
         + late_shapes,
-        in_specs=[smem, smem, smem, vmem, vmem, vmem, vmem, cache_block] + [hbm] * len(late),
-        out_specs=[cache_block, vmem, vmem] + [hbm] * len(late),
+        in_specs=[smem, smem, smem, hbm, hbm, vmem, hbm, hbm] + [hbm] * len(late),
+        out_specs=[hbm, vmem, vmem] + [hbm] * len(late),
         scratch_shapes=[
             pltpu.VMEM((2, steps * rows, lanes), jnp.float32),
+            pltpu.VMEM(queries.shape, queries.dtype),
             pltpu.VMEM((rows * per_row, HD), jnp.float32),
-            pltpu.VMEM((rows * per_row // HD, HD, HD), jnp.float32),
+            pltpu.VMEM((teams, HD, HD), jnp.float32),
             pltpu.VMEM((rows * per_row, HD), jnp.float32),
+            pltpu.VMEM((2,) + own.shape, own.dtype),
+            pltpu.VMEM(kv_cache.shape, kv_cache.dtype),
+            pltpu.SemaphoreType.DMA((2,)),
+            pltpu.SemaphoreType.DMA,
+            pltpu.SemaphoreType.DMA((teams,)),
+            pltpu.SemaphoreType.DMA((teams,)),
         ],
         input_output_aliases={8 + i: 3 + i for i in range(len(late))},
         compiler_params=pltpu.CompilerParams(vmem_limit_bytes=ATTEND_LIMIT),
-        cost_estimate=LIGHT,
+        cost_estimate=HEAVY,
         name="attend",
     )(lengths, destination, pick, own, got, gain, queries, kv_cache, *late)
     return outs[0], outs[1], outs[2], outs[3:]
@@ -562,8 +607,9 @@
     steps = queries.shape[0]
     group = queries.shape[2] // kv_cache.shape[3]
     count = lax.axis_size("inst")
-    early = list(range(max(count // 2, 1), count - 1))
-    late = [count - 1] + list(range(1, max(count // 2, 1)))
+    half = max(count // 2, 1)
+    early = list(range(half, count - 1)) + [half - 1] * (half > 1)
+    late = [count - 1] + list(range(half - 2, 0, -1))
 
     def send(block, shift):
         pairs = [(i, peer_to(i, shift, count)) for i in range(count)]

time: 46.1 us -> 41.7 us (0.905)
  waiting for transfers between devices: 6.43 us -> 2.9 us
  starting transfers between devices: 20.5 us -> 18.6 us
  Pallas kernels: 17.5 us -> 18.6 us
    ppermute x7, waiting for transfers between devices: 4.91 us -> 1.36 us  [send(): return lax.ppermute(block, 'inst', pairs)]
    ppermute x7, starting transfers between devices: 17.1 us -> 13.9 us  [send(): return lax.ppermute(block, 'inst', pairs)]
    all_to_all x1, waiting for transfers between devices: 0.01 us -> 1.53 us  [local(): small_got = lax.all_to_all(small, 'inst', 0, 0, tiled=True)]
    ppermute x1, waiting for transfers between devices: 1.51 us -> 0.01 us  [local(): got = lax.ppermute(other, 'tp', [(0, 1), (1, 0)])]
    pallas_call x1, Pallas kernels: 6.79 us -> 8.15 us  [attend(): pl.pallas_call(functools.partial(attend_kernel, count, block), out_shape=...]
    all_to_all x1, starting transfers between devices: 3.36 us -> 4.21 us  [local(): small_got = lax.all_to_all(small, 'inst', 0, 0, tiled=True)]
    ppermute x1, starting transfers between devices: 0.01 us -> 0.52 us  [local(): got = lax.ppermute(other, 'tp', [(0, 1), (1, 0)])]
  transfers between devices with their start and end apart: 9 -> 9, of which waited for: 3 -> 4; matrix products, arithmetic and copies ran while one was open for 0% -> 0% of each run, Pallas kernels for 23% -> 29%
where the time goes in v6:
time: 41.7 us; the launch traced here: 41.4 us
  Pallas kernels  18.6 us (45%)
  starting transfers between devices  18.6 us (45%)
  waiting for transfers between devices  2.9 us (7%)
  between operations  0.68 us (2%)
  local copies, waits for them, and re-layouts  0.64 us (2%)
    ppermute x7, starting transfers between devices, send(): return lax.ppermute(block, 'inst', pairs)  13.9 us
    pallas_call x1, Pallas kernels, attend(): pl.pallas_call(functools.partial(attend_kernel, count, block), out_shape=...  8.15 us
    pallas_call x1, Pallas kernels, prepare(): pl.pallas_call(functools.partial(prepare_kernel, count, chunks), out_shap...  5.83 us
    all_to_all x1, starting transfers between devices, local(): small_got = lax.all_to_all(small, 'inst', 0, 0, tiled=True)  4.21 us
    pallas_call x1, Pallas kernels, settle(): pl.pallas_call(functools.partial(settle_kernel, count, early, group), out...  2.03 us
    pallas_call x1, Pallas kernels, land(): pl.pallas_call(functools.partial(land_kernel, pieces), out_shape=[jax.Sha...  1.62 us
    all_to_all x1, waiting for transfers between devices, local(): small_got = lax.all_to_all(small, 'inst', 0, 0, tiled=True)  1.53 us
    ppermute x7, waiting for transfers between devices, send(): return lax.ppermute(block, 'inst', pairs)  1.36 us
  transfers between devices with their start and end apart: 9, of which 4 were waited for; matrix products, arithmetic and copies ran while one was open for 0% of the time, Pallas kernels for 29%

profile of v6, /device:TPU:0, one launch (start us, length us, event | category | flops | bytes accessed | tf_op | source)
XLA Modules:
  0.0 41.4 jit_solution(4613737567066930323)
XLA Ops:
  0.6 5.8 %prepare.1 = (bf16[2,144,256]{2,1,0:T(8,128)(2,1)}, bf16[2,144,256]{2,1,0:T(8,128)(2,1)}, bf16[2,144,256]{2,1,0:T(8,128)(2,1)}, bf16[2,144,256]{2,1,0:T(8,128)(2...) custom-call(s32[24]{0:T(128)} %dest_ref.3, ...), custom_call_target="tpu_custom_call" | custom-call | flops 1 | bytes 1 | tf_op jit(solution)/shard_map/prepare/pallas_call | solution.py:131
  6.5 0.5 %collective-permute-start.4 = (f32[48,512]{1,0:T(8,128)}, f32[48,512]{1,0:T(8,128)S(1)}, u32[]{:S(2)}, u32[]{:S(2)}) collective-permute-start(f32[48,512]{1,0:T(8,128)} %get-tuple-element.30), channel_id=1, source_target_pairs={{0,1},{1,0},{2,3},{3,2},{4,5},{5,4},{6,7},{7,6},{8,9},{9,8},{10,11... | collective-permute-start | bytes 294920 | tf_op jit(solution)/shard_map/ppermute | solution.py:622
  7.0 3.7 %collective-permute-start = (bf16[2,144,256]{2,1,0:T(8,128)(2,1)}, bf16[2,144,256]{2,1,0:T(8,128)(2,1)S(1)}, u32[]{:S(2)}, u32[]{:S(2)}) collective-permute-start(bf16[2,144,256]{2,1,0:T(8,128)(2,1)} %get-tuple-element.24), channel_id=1, source_target_pairs={{0,8},{2,10},{4,12},{6,14},{8,0},{10,2},{12,4},{14,6},{1,9},{3,11}... | collective-permute-start | bytes 442376 | tf_op jit(solution)/shard_map/ppermute | solution.py:616
  10.6 1.3 %collective-permute-start.1 = (bf16[2,144,256]{2,1,0:T(8,128)(2,1)}, bf16[2,144,256]{2,1,0:T(8,128)(2,1)S(1)}, u32[]{:S(2)}, u32[]{:S(2)}) collective-permute-start(bf16[2,144,256]{2,1,0:T(8,128)(2,1)} %get-tuple-element.25), channel_id=1, source_target_pairs={{0,10},{2,8},{4,14},{6,12},{8,2},{10,0},{12,6},{14,4},{1,11},{3,9}... | collective-permute-start | bytes 442376 | tf_op jit(solution)/shard_map/ppermute | solution.py:616
  11.9 3.6 %collective-permute-start.2 = (bf16[2,144,256]{2,1,0:T(8,128)(2,1)}, bf16[2,144,256]{2,1,0:T(8,128)(2,1)S(1)}, u32[]{:S(2)}, u32[]{:S(2)}) collective-permute-start(bf16[2,144,256]{2,1,0:T(8,128)(2,1)} %get-tuple-element.26), channel_id=1, source_target_pairs={{0,12},{2,14},{4,8},{6,10},{8,4},{10,6},{12,0},{14,2},{1,13},{3,15... | collective-permute-start | bytes 442376 | tf_op jit(solution)/shard_map/ppermute | solution.py:616
  15.5 0.0 collective-permute-start.3
  15.5 0.0 collective-permute-done.4.got_ref
  15.5 0.6 %copy-done.1 = f32[48,512]{1,0:T(8,128)} copy-done((f32[48,512]{1,0:T(8,128)}, f32[48,512]{1,0:T(8,128)S(1)}, u32[]{:S(2)}) %copy-start.1) | copy-done | bytes 98328
  16.2 8.2 %attend.1 = (bf16[24,2,144,256]{3,2,1,0:T(8,128)(2,1)}, bf16[768,128]{1,0:T(8,128)(2,1)}, bf16[8,48,128]{2,1,0:T(8,128)(2,1)}, bf16[2,144,256]{2,1,0:T(8,128)(2,...) custom-call(s32[24]{0:T(128)} %length_ref.3, ...), custom_call_target="tpu_custom_call", output_to_operand_aliasing={{3}: (8, {}), {4}: (9, {}), {5}: (10, {})} | custom-call | flops 68719476736 | bytes 268435456 | tf_op jit(solution)/shard_map/attend/pallas_call | solution.py:338
  24.3 4.2 %all-to-all-start = ((bf16[8,48,128]{2,1,0:T(8,128)(2,1)}), bf16[8,48,128]{2,1,0:T(8,128)(2,1)S(1)}, u32[]{:S(2)}, u32[]{:S(2)}) async-start(bf16[8,48,128]{2,1,0:T(8,128)(2,1)} %get-tuple-element.38), calls=%async_computation | async-start | bytes 196608 | tf_op jit(solution)/shard_map/all_to_all | solution.py:636
  28.5 4.7 %collective-permute-start.5 = (bf16[2,144,256]{2,1,0:T(8,128)(2,1)}, bf16[2,144,256]{2,1,0:T(8,128)(2,1)S(1)}, u32[]{:S(2)}, u32[]{:S(2)}) collective-permute-start(bf16[2,144,256]{2,1,0:T(8,128)(2,1)} %get-tuple-element.42), channel_id=1, source_target_pairs={{0,14},{2,12},{4,10},{6,8},{8,6},{10,4},{12,2},{14,0},{1,15},{3,13... | collective-permute-start | bytes 442376 | tf_op jit(solution)/shard_map/ppermute | solution.py:616
  33.3 0.0 collective-permute-done.refs_0_
  33.3 0.0 collective-permute-start.6
  33.3 0.0 collective-permute-done.1.refs_1_
  33.3 0.6 %collective-permute-start.7 = (bf16[2,144,256]{2,1,0:T(8,128)(2,1)}, bf16[2,144,256]{2,1,0:T(8,128)(2,1)S(1)}, u32[]{:S(2)}, u32[]{:S(2)}) collective-permute-start(bf16[2,144,256]{2,1,0:T(8,128)(2,1)} %get-tuple-element.44), channel_id=1, source_target_pairs={{0,2},{2,0},{4,6},{6,4},{8,10},{10,8},{12,14},{14,12},{1,3},{3,1},... | collective-permute-start | bytes 442376 | tf_op jit(solution)/shard_map/ppermute | solution.py:616
  33.9 0.0 collective-permute-done.2.refs_2_
  33.9 0.0 collective-permute-done.3.refs_3_
  33.9 1.6 %land.1 = (bf16[24,2,144,256]{3,2,1,0:T(8,128)(2,1)}, s32[4]{0:T(128)S(1)}, s32[4]{0:T(128)S(1)}, bf16[4,2,32,256]{3,2,1,0:T(8,128)(2,1)S(1)}) custom-call(bf16[2,144,256]{2,1,0:T(8,128)(2,1)S(1)} %collective-permute-done.refs_0_, bf16[2,144,256]{2,1,0:T(8,128)(2,1)S(1)} %collective-permute-done.1.refs_1_, ...), custom_call_target="tpu_custom_call", output_to_operand_aliasing={{0}: (4, {})} | custom-call | flops 68719476736 | bytes 268435456 | tf_op jit(solution)/shard_map/land/pallas_call | solution.py:438
  35.6 1.5 %all-to-all-done.small_ref.refs_3_ = bf16[8,48,128]{2,1,0:T(8,128)(2,1)S(1)} async-done(((bf16[8,48,128]{2,1,0:T(8,128)(2,1)}), bf16[8,48,128]{2,1,0:T(8,128)(2,1)S(1)}, u32[]{:S(2)}, u32[]{:S(2)}) %all-to-all-start) | async-done | bytes 98336 | tf_op jit(solution)/shard_map/all_to_all | solution.py:636
  37.1 2.0 %settle.1 = (bf16[2,24,2048]{2,1,0:T(8,128)(2,1)}, bf16[24,2,144,256]{3,2,1,0:T(8,128)(2,1)}) custom-call(s32[4]{0:T(128)S(1)} %get-tuple-element.35.slot_ref, s32[4]{0:T(128)S(1)} %get-tuple-element.36.length_ref, bf16[768,128]{1,0:T(8,128)(2,1)S(1)} %copy-done, ...), custom_call_target="tpu_custom_call", output_to_operand_aliasing={{1}: (5, {})} | custom-call | flops 1 | bytes 1 | tf_op jit(solution)/shard_map/settle/pallas_call | solution.py:534
  39.1 0.3 collective-permute-done.5.refs_0_
  39.5 0.9 %collective-permute-done.6.refs_1_ = bf16[2,144,256]{2,1,0:T(8,128)(2,1)S(1)} collective-permute-done((bf16[2,144,256]{2,1,0:T(8,128)(2,1)}, bf16[2,144,256]{2,1,0:T(8,128)(2,1)S(1)}, u32[]{:S(2)}, u32[]{:S(2)}) %collective-permute-start.6) | collective-permute-done | bytes 147488 | tf_op jit(solution)/shard_map/ppermute | solution.py:616
  40.4 0.1 collective-permute-done.7.refs_2_
  40.5 1.0 %finish.1 = bf16[24,2,144,256]{3,2,1,0:T(8,128)(2,1)} custom-call(bf16[2,144,256]{2,1,0:T(8,128)(2,1)S(1)} %collective-permute-done.5.refs_0_, bf16[2,144,256]{2,1,0:T(8,128)(2,1)S(1)} %collective-permute-done.6.refs_1_, bf16[2,144,256]{2,1,0:T(8,128)(2,1)S(1)} %collective-permute-done.7.refs_2_, ...), custom_call_target="tpu_custom_call", output_to_operand_aliasing={{}: (4, {})} | custom-call | flops 1 | bytes 1 | tf_op jit(solution)/shard_map/finish/pallas_call | solution.py:589
  (3 shorter events, 0.0 us)
Async XLA Ops:
  6.5 9.1 %collective-permute-start.4 = (f32[48,512]{1,0:T(8,128)}, f32[48,512]{1,0:T(8,128)S(1)}, u32[]{:S(2)}, u32[]{:S(2)}) collective-permute-start(f32[48,512]{1,0:T(8,128)} %get-tuple-element.30), channel_id=1, source_target_pairs={{0,1},{1,0},{2,3},{3,2},{4,5},{5,4},{6,7},{7,6},{8,9},{9,8},{10,11... | collective-permute-start | bytes 294920 | tf_op jit(solution)/shard_map/ppermute | solution.py:622
  7.0 26.3 %collective-permute-start = (bf16[2,144,256]{2,1,0:T(8,128)(2,1)}, bf16[2,144,256]{2,1,0:T(8,128)(2,1)S(1)}, u32[]{:S(2)}, u32[]{:S(2)}) collective-permute-start(bf16[2,144,256]{2,1,0:T(8,128)(2,1)} %get-tuple-element.24), channel_id=1, source_target_pairs={{0,8},{2,10},{4,12},{6,14},{8,0},{10,2},{12,4},{14,6},{1,9},{3,11}... | collective-permute-start | bytes 442376 | tf_op jit(solution)/shard_map/ppermute | solution.py:616
  10.6 22.6 %collective-permute-start.1 = (bf16[2,144,256]{2,1,0:T(8,128)(2,1)}, bf16[2,144,256]{2,1,0:T(8,128)(2,1)S(1)}, u32[]{:S(2)}, u32[]{:S(2)}) collective-permute-start(bf16[2,144,256]{2,1,0:T(8,128)(2,1)} %get-tuple-element.25), channel_id=1, source_target_pairs={{0,10},{2,8},{4,14},{6,12},{8,2},{10,0},{12,6},{14,4},{1,11},{3,9}... | collective-permute-start | bytes 442376 | tf_op jit(solution)/shard_map/ppermute | solution.py:616
  11.9 22.0 %collective-permute-start.2 = (bf16[2,144,256]{2,1,0:T(8,128)(2,1)}, bf16[2,144,256]{2,1,0:T(8,128)(2,1)S(1)}, u32[]{:S(2)}, u32[]{:S(2)}) collective-permute-start(bf16[2,144,256]{2,1,0:T(8,128)(2,1)} %get-tuple-element.26), channel_id=1, source_target_pairs={{0,12},{2,14},{4,8},{6,10},{8,4},{10,6},{12,0},{14,2},{1,13},{3,15... | collective-permute-start | bytes 442376 | tf_op jit(solution)/shard_map/ppermute | solution.py:616
  15.5 18.4 %collective-permute-start.3 = (bf16[2,144,256]{2,1,0:T(8,128)(2,1)}, bf16[2,144,256]{2,1,0:T(8,128)(2,1)S(1)}, u32[]{:S(2)}, u32[]{:S(2)}) collective-permute-start(bf16[2,144,256]{2,1,0:T(8,128)(2,1)} %get-tuple-element.27), channel_id=1, source_target_pairs={{0,6},{2,4},{4,2},{6,0},{8,14},{10,12},{12,10},{14,8},{1,7},{3,5},... | collective-permute-start | bytes 442376 | tf_op jit(solution)/shard_map/ppermute | solution.py:616
  15.5 0.6 %copy-start.1 = (f32[48,512]{1,0:T(8,128)}, f32[48,512]{1,0:T(8,128)S(1)}, u32[]{:S(2)}) copy-start(f32[48,512]{1,0:T(8,128)S(1)} %collective-permute-done.4.got_ref) | copy-start | bytes 294916
  24.3 12.7 %all-to-all-start = ((bf16[8,48,128]{2,1,0:T(8,128)(2,1)}), bf16[8,48,128]{2,1,0:T(8,128)(2,1)S(1)}, u32[]{:S(2)}, u32[]{:S(2)}) async-start(bf16[8,48,128]{2,1,0:T(8,128)(2,1)} %get-tuple-element.38), calls=%async_computation | async-start | bytes 196608 | tf_op jit(solution)/shard_map/all_to_all | solution.py:636
  28.5 10.9 %collective-permute-start.5 = (bf16[2,144,256]{2,1,0:T(8,128)(2,1)}, bf16[2,144,256]{2,1,0:T(8,128)(2,1)S(1)}, u32[]{:S(2)}, u32[]{:S(2)}) collective-permute-start(bf16[2,144,256]{2,1,0:T(8,128)(2,1)} %get-tuple-element.42), channel_id=1, source_target_pairs={{0,14},{2,12},{4,10},{6,8},{8,6},{10,4},{12,2},{14,0},{1,15},{3,13... | collective-permute-start | bytes 442376 | tf_op jit(solution)/shard_map/ppermute | solution.py:616
  33.3 7.1 %collective-permute-start.6 = (bf16[2,144,256]{2,1,0:T(8,128)(2,1)}, bf16[2,144,256]{2,1,0:T(8,128)(2,1)S(1)}, u32[]{:S(2)}, u32[]{:S(2)}) collective-permute-start(bf16[2,144,256]{2,1,0:T(8,128)(2,1)} %get-tuple-element.43), channel_id=1, source_target_pairs={{0,4},{2,6},{4,0},{6,2},{8,12},{10,14},{12,8},{14,10},{1,5},{3,7},... | collective-permute-start | bytes 442376 | tf_op jit(solution)/shard_map/ppermute | solution.py:616
  33.3 7.2 %collective-permute-start.7 = (bf16[2,144,256]{2,1,0:T(8,128)(2,1)}, bf16[2,144,256]{2,1,0:T(8,128)(2,1)S(1)}, u32[]{:S(2)}, u32[]{:S(2)}) collective-permute-start(bf16[2,144,256]{2,1,0:T(8,128)(2,1)} %get-tuple-element.44), channel_id=1, source_target_pairs={{0,2},{2,0},{4,6},{6,4},{8,10},{10,8},{12,14},{14,12},{1,3},{3,1},... | collective-permute-start | bytes 442376 | tf_op jit(solution)/shard_map/ppermute | solution.py:616
  33.9 3.2 %copy-start = (bf16[768,128]{1,0:T(8,128)(2,1)S(1)}, bf16[768,128]{1,0:T(8,128)(2,1)}, u32[]{:S(2)}) copy-start(bf16[768,128]{1,0:T(8,128)(2,1)} %get-tuple-element.37.mixed_ref) | copy-start | bytes 589828

commit v7 on v6

--- a/solution.py
+++ b/solution.py
@@ -37,22 +37,84 @@
     return index ^ shift if count & (count - 1) == 0 else (index + count - shift) % count
 
 
-def prepare_kernel(
-    count, chunks, dest_ref, length_ref, hidden_ref, kv_ref, key_ref, value_ref, *refs
-):
-    block_refs = refs[: count - 1]
-    pick_ref, own_ref, other_ref, blocks, hidden_held, held, total = refs[count - 1 : count + 6]
-    in_sems, out_sems, hidden_sem, weight_sems = refs[count + 6 :]
+def pack_kernel(count, early, dest_ref, length_ref, kv_ref, *refs):
+    block_refs = refs[: len(early)]
+    pick_ref, blocks, in_sems, out_sems = refs[len(early) :]
     rows = dest_ref.shape[0]
     capacity, lanes = kv_ref.shape[2:]
     me = lax.axis_index("inst")
-    shifts = range(1, count)
-
+    for peer in range(count):
+        pick_ref[peer] = 0
+    for row in range(rows):
+        pick_ref[quotient(dest_ref[row], rows, rows * count)] = row
+    fetches, stores = [], []
+    for piece, shift in enumerate(early):
+        row = pick_ref[peer_to(me, shift, count)]
+        fetches.append(
+            pltpu.make_async_copy(kv_ref.at[row], blocks.at[piece], in_sems.at[piece])
+        )
+        fetches[-1].start()
+    tile = (TILE, lanes)
+    last = lax.broadcasted_iota(jnp.int32, tile, 0) == TILE - 1
+    first_lanes = lax.broadcasted_iota(jnp.int32, tile, 1) < HD
+    for piece, shift in enumerate(early):
+        peer = peer_to(me, shift, count)
+        row = pick_ref[peer]
+        slot = dest_ref[row] - peer * rows
+        slot = jnp.where((slot >= 0) & (slot < rows), slot, -1)
+        facts = jnp.where(first_lanes, slot, length_ref[row]).astype(jnp.float32)
+        fetches[piece].wait()
+        end = blocks[piece, 0, capacity - TILE :, :].astype(jnp.float32)
+        blocks[piece, 0, capacity - TILE :, :] = jnp.where(last, facts, end).astype(jnp.bfloat16)
+        stores.append(
+            pltpu.make_async_copy(blocks.at[piece], block_refs[piece], out_sems.at[piece])
+        )
+        stores[-1].start()
+    for copy in stores:
+        copy.wait()
+
+
+def pack(kv_cache, destination, lengths, count, early):
+    shape = kv_cache.shape[1:]
+    smem = pl.BlockSpec(memory_space=pltpu.SMEM)
+    hbm = pl.BlockSpec(memory_space=pl.ANY)
+    outs = pl.pallas_call(
+        functools.partial(pack_kernel, count, early),
+        out_shape=[jax.ShapeDtypeStruct(shape, kv_cache.dtype)] * len(early)
+        + [jax.ShapeDtypeStruct((count,), jnp.int32)],
+        in_specs=[smem, smem, hbm],
+        out_specs=[hbm] * len(early) + [smem],
+        scratch_shapes=[
+            pltpu.VMEM((len(early),) + shape, kv_cache.dtype),
+            pltpu.SemaphoreType.DMA((len(early),)),
+            pltpu.SemaphoreType.DMA((len(early),)),
+        ],
+        compiler_params=pltpu.CompilerParams(vmem_limit_bytes=VMEM_LIMIT),
+        cost_estimate=LIGHT,
+        name="pack",
+    )(destination, lengths, kv_cache)
+    return outs[:-1], outs[-1]
+
+
+def project_kernel(
+    chunks,
+    _,
+    hidden_ref,
+    key_ref,
+    value_ref,
+    own_ref,
+    other_ref,
+    hidden_held,
+    held,
+    total,
+    hidden_sem,
+    weight_sems,
+):
+    steps, rows, depth = hidden_ref.shape
+    width = key_ref.shape[1]
+    part = depth // chunks
     hidden_copy = pltpu.make_async_copy(hidden_ref, hidden_held, hidden_sem)
     hidden_copy.start()
-    steps, _, depth = hidden_ref.shape
-    width = key_ref.shape[1]
-    part = depth // chunks
     weights = []
     for chunk in range(chunks):
         span = pl.ds(chunk * part, part)
@@ -63,38 +125,6 @@
                 )
             )
             weights[-1].start()
-
-    for peer in range(count):
-        pick_ref[peer] = 0
-    for row in range(rows):
-        pick_ref[quotient(dest_ref[row], rows, rows * count)] = row
-    fetches, stores = {}, {}
-    for shift in shifts:
-        row = pick_ref[peer_to(me, shift, count)]
-        fetches[shift] = pltpu.make_async_copy(
-            kv_ref.at[row], blocks.at[shift - 1], in_sems.at[shift - 1]
-        )
-        fetches[shift].start()
-
-    tile = (TILE, lanes)
-    last = lax.broadcasted_iota(jnp.int32, tile, 0) == TILE - 1
-    first_lanes = lax.broadcasted_iota(jnp.int32, tile, 1) < HD
-    for shift in shifts:
-        peer = peer_to(me, shift, count)
-        row = pick_ref[peer]
-        slot = dest_ref[row] - peer * rows
-        slot = jnp.where((slot >= 0) & (slot < rows), slot, -1)
-        facts = jnp.where(first_lanes, slot, length_ref[row]).astype(jnp.float32)
-        fetches[shift].wait()
-        end = blocks[shift - 1, 0, capacity - TILE :, :].astype(jnp.float32)
-        blocks[shift - 1, 0, capacity - TILE :, :] = jnp.where(last, facts, end).astype(
-            jnp.bfloat16
-        )
-        stores[shift] = pltpu.make_async_copy(
-            blocks.at[shift - 1], block_refs[shift - 1], out_sems.at[shift - 1]
-        )
-        stores[shift].start()
-
     hidden_copy.wait()
     hidden = hidden_held[...].reshape(steps * rows, depth)
     sums = [None, None]
@@ -115,40 +145,31 @@
         at = pl.multiple_of(place * half, half)
         ref[:, :half] = total[:, pl.ds(at, half)]
         ref[:, half:] = total[:, pl.ds(pl.multiple_of(width + at, half), half)]
-    for shift in shifts:
-        stores[shift].wait()
-
-
-def prepare(destination, lengths, hidden_new, kv_cache, key_weight, value_weight, count):
+
+
+def project(hidden_new, key_weight, value_weight, pick):
     steps, rows, depth = hidden_new.shape
     width = key_weight.shape[1]
     chunks = 5
-    shape = kv_cache.shape[1:]
     part = jax.ShapeDtypeStruct((steps * rows, width), jnp.float32)
-    smem = pl.BlockSpec(memory_space=pltpu.SMEM)
     vmem = pl.BlockSpec(memory_space=pltpu.VMEM)
     hbm = pl.BlockSpec(memory_space=pl.ANY)
-    outs = pl.pallas_call(
-        functools.partial(prepare_kernel, count, chunks),
-        out_shape=[jax.ShapeDtypeStruct(shape, kv_cache.dtype)] * (count - 1)
-        + [jax.ShapeDtypeStruct((count,), jnp.int32), part, part],
-        in_specs=[smem, smem, hbm, hbm, hbm, hbm],
-        out_specs=[hbm] * (count - 1) + [smem, vmem, vmem],
+    return pl.pallas_call(
+        functools.partial(project_kernel, chunks),
+        out_shape=[part, part],
+        in_specs=[hbm, hbm, hbm, hbm],
+        out_specs=[vmem, vmem],
         scratch_shapes=[
-            pltpu.VMEM((count - 1,) + shape, kv_cache.dtype),
             pltpu.VMEM(hidden_new.shape, hidden_new.dtype),
             pltpu.VMEM((2, depth, width), key_weight.dtype),
             pltpu.VMEM((steps * rows, 2 * width), jnp.float32),
-            pltpu.SemaphoreType.DMA((count - 1,)),
-            pltpu.SemaphoreType.DMA((count - 1,)),
             pltpu.SemaphoreType.DMA,
             pltpu.SemaphoreType.DMA((chunks, 2)),
         ],
         compiler_params=pltpu.CompilerParams(vmem_limit_bytes=VMEM_LIMIT),
         cost_estimate=LIGHT,
-        name="prepare",
-    )(destination, lengths, hidden_new, kv_cache, key_weight, value_weight)
-    return outs[: count - 1], *outs[count - 1 :]
+        name="project",
+    )(pick, hidden_new, key_weight, value_weight)
 
 
 def rotation(length_ref, steps, rows):
@@ -167,6 +188,7 @@
 
 def attend_kernel(
     count,
+    late,
     block,
     length_ref,
     dest_ref,
@@ -178,10 +200,10 @@
     kv_ref,
     *refs,
 ):
-    late = (len(refs) - 14) // 2
-    moved_ref, mixed_ref, small_ref = refs[late : late + 3]
-    fresh, query_held, query_rows, query_columns, mixed, sums, held = refs[-11:-4]
-    sum_sems, query_sem, in_sems, out_sems = refs[-4:]
+    moved_ref, mixed_ref, small_ref = refs[:3]
+    late_refs = refs[3 : 3 + len(late)]
+    fresh, query_held, query_rows, query_columns, mixed, sums, held, appended = refs[-13:-5]
+    sum_sems, query_sem, in_sems, out_sems, late_sems = refs[-5:]
     steps, rows, query_width = query_ref.shape
     capacity, lanes = kv_ref.shape[2:]
     heads = lanes // HD
@@ -209,7 +231,7 @@
 
     def store(index):
         return pltpu.make_async_copy(
-            held.at[span(index)], moved_ref.at[span(index)], out_sems.at[index]
+            appended.at[span(index)], moved_ref.at[span(index)], out_sems.at[index]
         )
 
     for index in range(rows // team):
@@ -248,11 +270,10 @@
     factor = 1.0 / math.sqrt(HD)
     teams = range(block // team)
 
-    def work(part, carry):
+    for part in range(rows // block):
+        scores = []
         for index in teams:
             fetch(part * len(teams) + index).wait()
-        scores = []
-        for index in teams:
             queries = query_columns[part * len(teams) + index]
             queries = jnp.concatenate(
                 [jnp.where(column_head == head, queries, 0.0) for head in range(heads)], axis=0
@@ -264,18 +285,19 @@
                 kept = position < length
                 landing = [position == length + step for step in range(steps)]
                 for which in range(2):
-                    news = [fresh[which, pl.ds(step * rows + row, 1), :] for step in range(steps)]
                     for head in range(heads):
                         at = slice(head * HD, (head + 1) * HD)
                         stored = held[row, which, :, at].astype(jnp.float32)
                         stored = jnp.where(kept, stored, 0.0)
                         for step in range(steps):
-                            stored = jnp.where(landing[step], news[step][:, at], stored)
-                        held[row, which, :, at] = stored.astype(jnp.bfloat16)
-                one = jnp.dot(held[row, 0], queries, preferred_element_type=jnp.float32)
+                            new = fresh[which, step * rows + row : step * rows + row + 1, at]
+                            stored = jnp.where(landing[step], new, stored)
+                        appended[row, which, :, at] = stored.astype(jnp.bfloat16)
+                one = jnp.dot(appended[row, 0], queries, preferred_element_type=jnp.float32)
                 score = one if member == 0 else jnp.where(column_item == member, one, score)
                 limit = length if member == 0 else jnp.where(column_item == member, length, limit)
             scores.append(jnp.where(position <= limit + column_step, score * factor, -jnp.inf))
+            store(part * len(teams) + index).start()
         weights = []
         for score in scores:
             raised = jnp.exp(score - jnp.max(score, axis=0, keepdims=True))
@@ -286,20 +308,23 @@
                 row = part * block + index * team + member
                 result = jnp.dot(
                     weights[index][member * per_row : (member + 1) * per_row],
-                    held[row, 1],
+                    appended[row, 1],
                     preferred_element_type=jnp.float32,
                 )
                 for head in range(heads):
-                    at = pl.multiple_of(row * per_row + head * per_head, per_head)
-                    mixed[pl.ds(at, per_head), :] = result[
+                    at = row * per_row + head * per_head
+                    mixed[at : at + per_head, :] = result[
                         head * per_head : (head + 1) * per_head, head * HD : (head + 1) * HD
                     ]
-        for index in teams:
-            store(part * len(teams) + index).start()
-        return carry
-
-    lax.fori_loop(0, rows // block, work, 0)
-
+
+    me = lax.axis_index("inst")
+    sends = []
+    for piece, shift in enumerate(late):
+        row = pick_ref[peer_to(me, shift, count)]
+        sends.append(
+            pltpu.make_async_copy(appended.at[row], late_refs[piece], late_sems.at[piece])
+        )
+        sends[-1].start()
     mixed_ref[...] = mixed[...].astype(jnp.bfloat16)
     for peer in range(count):
         row = pick_ref[peer]
@@ -318,12 +343,11 @@
         small_ref[peer, per_row:, :] = jnp.concatenate(news, axis=0).astype(jnp.bfloat16)
     for index in range(rows // team):
         store(index).wait()
-
-
-def attend(
-    kv_cache, queries, own, got, gain, lengths, destination, pick, late, count
-):
-    late_shapes = [jax.ShapeDtypeStruct(x.shape, x.dtype) for x in late]
+    for copy in sends:
+        copy.wait()
+
+
+def attend(kv_cache, queries, own, got, gain, lengths, destination, pick, count, late):
     steps, rows, query_width = queries.shape
     capacity, lanes = kv_cache.shape[2:]
     heads = lanes // HD
@@ -336,14 +360,14 @@
     vmem = pl.BlockSpec(memory_space=pltpu.VMEM)
     hbm = pl.BlockSpec(memory_space=pl.ANY)
     outs = pl.pallas_call(
-        functools.partial(attend_kernel, count, block),
+        functools.partial(attend_kernel, count, late, block),
         out_shape=[
             jax.ShapeDtypeStruct(kv_cache.shape, kv_cache.dtype),
             jax.ShapeDtypeStruct((rows * per_row, HD), jnp.bfloat16),
             small,
         ]
-        + late_shapes,
-        in_specs=[smem, smem, smem, hbm, hbm, vmem, hbm, hbm] + [hbm] * len(late),
+        + [jax.ShapeDtypeStruct(kv_cache.shape[1:], kv_cache.dtype)] * len(late),
+        in_specs=[smem, smem, smem, hbm, hbm, vmem, hbm, hbm],
         out_specs=[hbm, vmem, vmem] + [hbm] * len(late),
         scratch_shapes=[
             pltpu.VMEM((2, steps * rows, lanes), jnp.float32),
@@ -353,17 +377,18 @@
             pltpu.VMEM((rows * per_row, HD), jnp.float32),
             pltpu.VMEM((2,) + own.shape, own.dtype),
             pltpu.VMEM(kv_cache.shape, kv_cache.dtype),
+            pltpu.VMEM(kv_cache.shape, kv_cache.dtype),
             pltpu.SemaphoreType.DMA((2,)),
             pltpu.SemaphoreType.DMA,
             pltpu.SemaphoreType.DMA((teams,)),
             pltpu.SemaphoreType.DMA((teams,)),
+            pltpu.SemaphoreType.DMA((len(late),)),
         ],
-        input_output_aliases={8 + i: 3 + i for i in range(len(late))},
         compiler_params=pltpu.CompilerParams(vmem_limit_bytes=ATTEND_LIMIT),
-        cost_estimate=HEAVY,
+        cost_estimate=LIGHT,
         name="attend",
-    )(lengths, destination, pick, own, got, gain, queries, kv_cache, *late)
-    return outs[0], outs[1], outs[2], outs[3:]
+    )(lengths, destination, pick, own, got, gain, queries, kv_cache)
+    return outs
 
 
 def read_facts(block):
@@ -459,6 +484,7 @@
 def settle_kernel(
     count,
     early,
+    late,
     group,
     slot_ref,
     length_ref,
@@ -468,6 +494,7 @@
     _,
     out_ref,
     moved_ref,
+    late_slot_ref,
     mixed,
     windows,
     sems,
@@ -511,6 +538,7 @@
             line = 2 * steps * heads
             facts = small_ref[peer, per_row:, :].astype(jnp.float32)[line : line + 1]
             slot = jnp.max(facts).astype(jnp.int32)
+            late_slot_ref[late.index(shift)] = slot
         pl.when(slot >= 0)(functools.partial(take, slot, peer))
     for step in range(steps):
         for chunk in range(query_width // HD):
@@ -527,18 +555,19 @@
             store(piece).wait()
 
 
-def settle(slots, lengths, mixed, small, windows, moved, shape, group, count, early):
+def settle(slots, lengths, mixed, small, windows, moved, shape, group, count, early, late):
     smem = pl.BlockSpec(memory_space=pltpu.SMEM)
     vmem = pl.BlockSpec(memory_space=pltpu.VMEM)
     hbm = pl.BlockSpec(memory_space=pl.ANY)
     return pl.pallas_call(
-        functools.partial(settle_kernel, count, early, group),
+        functools.partial(settle_kernel, count, early, late, group),
         out_shape=[
             jax.ShapeDtypeStruct(shape, jnp.bfloat16),
             jax.ShapeDtypeStruct(moved.shape, moved.dtype),
+            jax.ShapeDtypeStruct((len(late),), jnp.int32),
         ],
         in_specs=[smem, smem, vmem, vmem, vmem, hbm],
-        out_specs=[vmem, hbm],
+        out_specs=[vmem, hbm, smem],
         scratch_shapes=[
             pltpu.VMEM(mixed.shape, jnp.float32),
             pltpu.VMEM(windows.shape, windows.dtype),
@@ -551,94 +580,63 @@
     )(slots, lengths, mixed, small, windows, moved)
 
 
-def finish_kernel(count, late, steps, *refs):
-    blocks = refs[: len(late)]
-    small_ref, _, out_ref, buffer, sems, slot_ref = refs[len(late) :]
-    capacity, lanes = buffer.shape[2:]
-    height = small_ref.shape[1]
-    tail = height - -(-(2 * steps * (lanes // HD) + 1) // TILE) * TILE
-    me = lax.axis_index("inst")
+def finish_kernel(slot_ref, *refs):
+    pieces = slot_ref.shape[0]
+    blocks = refs[:pieces]
+    _, out_ref, sems = refs[pieces:]
 
     def store(piece):
         slot = jnp.maximum(slot_ref[piece], 0)
-        return pltpu.make_async_copy(buffer.at[piece], out_ref.at[slot], sems.at[piece])
-
-    facts = [read_facts(block) for block in blocks]
-    for piece, (slot, length) in enumerate(facts):
-        slot_ref[piece] = slot
-
-        @pl.when(slot >= 0)
-        def _():
-            clean(blocks[piece], length, buffer.at[piece])
-            start = window_start(length, capacity)
-            window = buffer.at[piece, :, pl.ds(start, WINDOW), :]
-            news = small_ref[peer_from(me, late[piece], count), tail:, :].astype(jnp.float32)
-            insert(window, news, length - start, steps, window)
-            store(piece).start()
-
-    for piece in range(len(late)):
-
-        @pl.when(slot_ref[piece] >= 0)
-        def _():
-            store(piece).wait()
-
-
-def finish(got, small, moved, steps, count, late):
+        return pltpu.make_async_copy(blocks[piece], out_ref.at[slot], sems.at[piece])
+
+    for piece in range(pieces):
+        pl.when(slot_ref[piece] >= 0)(store(piece).start)
+    for piece in range(pieces):
+        pl.when(slot_ref[piece] >= 0)(store(piece).wait)
+
+
+def finish(slots, got, moved):
+    smem = pl.BlockSpec(memory_space=pltpu.SMEM)
     vmem = pl.BlockSpec(memory_space=pltpu.VMEM)
     hbm = pl.BlockSpec(memory_space=pl.ANY)
     return pl.pallas_call(
-        functools.partial(finish_kernel, count, late, steps),
+        finish_kernel,
         out_shape=jax.ShapeDtypeStruct(moved.shape, moved.dtype),
-        in_specs=[vmem] * len(got) + [vmem, hbm],
+        in_specs=[smem] + [vmem] * len(got) + [hbm],
         out_specs=hbm,
-        scratch_shapes=[
-            pltpu.VMEM((len(got),) + moved.shape[1:], moved.dtype),
-            pltpu.SemaphoreType.DMA((len(got),)),
-            pltpu.SMEM((len(got),), jnp.int32),
-        ],
+        scratch_shapes=[pltpu.SemaphoreType.DMA((len(got),))],
         input_output_aliases={len(got) + 1: 0},
         compiler_params=pltpu.CompilerParams(vmem_limit_bytes=SMALL_LIMIT),
         cost_estimate=LIGHT,
         name="finish",
-    )(*got, small, moved)
+    )(slots, *got, moved)
 
 
 def local(hidden_new, queries, kv_cache, lengths, destination, key_weight, value_weight, key_gain):
-    steps = queries.shape[0]
     group = queries.shape[2] // kv_cache.shape[3]
     count = lax.axis_size("inst")
     half = max(count // 2, 1)
-    early = list(range(half, count - 1)) + [half - 1] * (half > 1)
-    late = [count - 1] + list(range(half - 2, 0, -1))
+    early = list(range(half, count))
+    late = list(range(half - 1, 0, -1))
 
     def send(block, shift):
         pairs = [(i, peer_to(i, shift, count)) for i in range(count)]
         return lax.ppermute(block, "inst", pairs)
 
-    blocks, pick, own, other = prepare(
-        destination, lengths, hidden_new, kv_cache, key_weight, value_weight, count
-    )
-    early_got = [send(blocks[shift - 1], shift) for shift in early]
+    blocks, pick = pack(kv_cache, destination, lengths, count, early)
+    early_got = [send(block, shift) for block, shift in zip(blocks, early)]
+    own, other = project(hidden_new, key_weight, value_weight, pick)
     got = lax.ppermute(other, "tp", [(0, 1), (1, 0)])
-    moved, mixed, small, late_blocks = attend(
-        kv_cache,
-        queries,
-        own,
-        got,
-        key_gain[None, :],
-        lengths,
-        destination,
-        pick,
-        [blocks[shift - 1] for shift in late],
-        count,
+    moved, mixed, small, *late_blocks = attend(
+        kv_cache, queries, own, got, key_gain[None, :], lengths, destination, pick, count, late
     )
     late_got = [send(block, shift) for block, shift in zip(late_blocks, late)]
     small_got = lax.all_to_all(small, "inst", 0, 0, tiled=True)
     moved, slots, arrived, windows = land(early_got, moved)
-    attended, moved = settle(
-        slots, arrived, mixed, small_got, windows, moved, queries.shape, group, count, early
+    attended, moved, late_slots = settle(
+        slots, arrived, mixed, small_got, windows, moved, queries.shape, group, count, early, late
     )
-    return attended, finish(late_got, small_got, moved, steps, count, late)
+    return attended, finish(late_slots, late_got, moved)
 
 
 def solution(mesh):

time: 41.7 us -> 46.6 us (1.12)
  waiting for transfers between devices: 2.9 us -> 5.65 us
  Pallas kernels: 18.6 us -> 20.6 us
    pallas_call x4 -> x5, Pallas kernels: 17 us -> 19 us  [the longest x1 8.14 us: attend(): pl.pallas_call(functools.partial(attend_kernel, count, late, block), out_...]
    all_to_all x1, starting transfers between devices: 4.21 us -> 6.01 us  [local(): small_got = lax.all_to_all(small, 'inst', 0, 0, tiled=True)]
    ppermute x1, waiting for transfers between devices: 0.01 us -> 1.5 us  [local(): got = lax.ppermute(other, 'tp', [(0, 1), (1, 0)])]
    ppermute x7, starting transfers between devices: 13.9 us -> 12.6 us  [send(): return lax.ppermute(block, 'inst', pairs)]
    all_to_all x1, waiting for transfers between devices: 1.53 us -> 2.59 us  [local(): small_got = lax.all_to_all(small, 'inst', 0, 0, tiled=True)]
  transfers between devices with their start and end apart: 9 -> 9, of which waited for: 4 -> 3; matrix products, arithmetic and copies ran while one was open for 0% -> 0% of each run, Pallas kernels for 29% -> 35%
where the time goes in v7:
time: 46.6 us; the launch traced here: 46.3 us
  Pallas kernels  20.6 us (44%)
  starting transfers between devices  18.6 us (40%)
  waiting for transfers between devices  5.65 us (12%)
  between operations  0.7 us (2%)
  local copies, waits for them, and re-layouts  0.63 us (1%)
    ppermute x7, starting transfers between devices, send(): return lax.ppermute(block, 'inst', pairs)  12.6 us
    pallas_call x1, Pallas kernels, attend(): pl.pallas_call(functools.partial(attend_kernel, count, late, block), out_...  8.14 us
    all_to_all x1, starting transfers between devices, local(): small_got = lax.all_to_all(small, 'inst', 0, 0, tiled=True)  6.01 us
    pallas_call x1, Pallas kernels, project(): pl.pallas_call(functools.partial(project_kernel, chunks), out_shape=[part...  4.42 us
    pallas_call x1, Pallas kernels, pack(): pl.pallas_call(functools.partial(pack_kernel, count, early), out_shape=[j...  3.09 us
    all_to_all x1, waiting for transfers between devices, local(): small_got = lax.all_to_all(small, 'inst', 0, 0, tiled=True)  2.59 us
    pallas_call x1, Pallas kernels, settle(): pl.pallas_call(functools.partial(settle_kernel, count, early, late, group...  2.04 us
    pallas_call x1, Pallas kernels, land(): pl.pallas_call(functools.partial(land_kernel, pieces), out_shape=[jax.Sha...  1.62 us
  transfers between devices with their start and end apart: 9, of which 3 were waited for; matrix products, arithmetic and copies ran while one was open for 0% of the time, Pallas kernels for 35%

profile of v7, /device:TPU:0, one launch (start us, length us, event | category | flops | bytes accessed | tf_op | source)
XLA Modules:
  0.0 46.3 jit_solution(5880990094801589759)
XLA Ops:
  0.6 3.1 %pack.1 = (bf16[2,144,256]{2,1,0:T(8,128)(2,1)}, bf16[2,144,256]{2,1,0:T(8,128)(2,1)}, bf16[2,144,256]{2,1,0:T(8,128)(2,1)}, bf16[2,144,256]{2,1,0:T(8,128)(2,1)}, s32[8]{0:T(128)}) custom-call(s32[24]{0:T(128)} %dest_ref.3, s32[24]{0:T(128)} %length_ref.3, bf16[24,2,144,256]{3,2,1,0:T(8,128)(2,1)} %kv_ref.3), custom_call_target="tpu_custom_call" | custom-call | flops 1 | bytes 1 | tf_op jit(solution)/shard_map/pack/pallas_call | solution.py:81
  3.7 4.1 %collective-permute-start = (bf16[2,144,256]{2,1,0:T(8,128)(2,1)}, bf16[2,144,256]{2,1,0:T(8,128)(2,1)S(1)}, u32[]{:S(2)}, u32[]{:S(2)}) collective-permute-start(bf16[2,144,256]{2,1,0:T(8,128)(2,1)} %get-tuple-element.22), channel_id=1, source_target_pairs={{0,8},{2,10},{4,12},{6,14},{8,0},{10,2},{12,4},{14,6},{1,9},{3,11}... | collective-permute-start | bytes 442376 | tf_op jit(solution)/shard_map/ppermute | solution.py:624
  7.8 1.3 %collective-permute-start.1 = (bf16[2,144,256]{2,1,0:T(8,128)(2,1)}, bf16[2,144,256]{2,1,0:T(8,128)(2,1)S(1)}, u32[]{:S(2)}, u32[]{:S(2)}) collective-permute-start(bf16[2,144,256]{2,1,0:T(8,128)(2,1)} %get-tuple-element.23), channel_id=1, source_target_pairs={{0,10},{2,8},{4,14},{6,12},{8,2},{10,0},{12,6},{14,4},{1,11},{3,9}... | collective-permute-start | bytes 442376 | tf_op jit(solution)/shard_map/ppermute | solution.py:624
  9.1 3.6 %collective-permute-start.2 = (bf16[2,144,256]{2,1,0:T(8,128)(2,1)}, bf16[2,144,256]{2,1,0:T(8,128)(2,1)S(1)}, u32[]{:S(2)}, u32[]{:S(2)}) collective-permute-start(bf16[2,144,256]{2,1,0:T(8,128)(2,1)} %get-tuple-element.24), channel_id=1, source_target_pairs={{0,12},{2,14},{4,8},{6,10},{8,4},{10,6},{12,0},{14,2},{1,13},{3,15... | collective-permute-start | bytes 442376 | tf_op jit(solution)/shard_map/ppermute | solution.py:624
  12.7 0.0 collective-permute-start.3
  12.7 4.4 %project.1 = (f32[48,512]{1,0:T(8,128)}, f32[48,512]{1,0:T(8,128)}) custom-call(s32[8]{0:T(128)} %get-tuple-element.26._.pick_ref, bf16[2,24,2560]{2,1,0:T(8,128)(2,1)} %hidden_ref.1, bf16[2560,512]{1,0:T(8,128)(2,1)} %key_ref.1, bf16[2560,512]{1,0:T(8,128)(2,1)} %value_ref.1), custom_call_target="tpu_custom_call" | custom-call | flops 1 | bytes 1 | tf_op jit(solution)/shard_map/project/pallas_call | solution.py:157
  17.2 0.1 collective-permute-start.4
  17.2 1.5 %collective-permute-done.4.got_ref = f32[48,512]{1,0:T(8,128)S(1)} collective-permute-done((f32[48,512]{1,0:T(8,128)}, f32[48,512]{1,0:T(8,128)S(1)}, u32[]{:S(2)}, u32[]{:S(2)}) %collective-permute-start.4) | collective-permute-done | bytes 98336 | tf_op jit(solution)/shard_map/ppermute | solution.py:629
  18.7 0.6 %copy-done.1 = f32[48,512]{1,0:T(8,128)} copy-done((f32[48,512]{1,0:T(8,128)}, f32[48,512]{1,0:T(8,128)S(1)}, u32[]{:S(2)}) %copy-start.1) | copy-done | bytes 98328
  19.4 8.1 %attend.1 = (bf16[24,2,144,256]{3,2,1,0:T(8,128)(2,1)}, bf16[768,128]{1,0:T(8,128)(2,1)}, bf16[8,48,128]{2,1,0:T(8,128)(2,1)}, bf16[2,144,256]{2,1,0:T(8,128)(2,...) custom-call(s32[24]{0:T(128)} %length_ref.3, s32[24]{0:T(128)} %dest_ref.3, ...), custom_call_target="tpu_custom_call" | custom-call | flops 1 | bytes 1 | tf_op jit(solution)/shard_map/attend/pallas_call | solution.py:362
  27.5 6.0 %all-to-all-start = ((bf16[8,48,128]{2,1,0:T(8,128)(2,1)}), bf16[8,48,128]{2,1,0:T(8,128)(2,1)S(1)}, u32[]{:S(2)}, u32[]{:S(2)}) async-start(bf16[8,48,128]{2,1,0:T(8,128)(2,1)} %get-tuple-element.33), calls=%async_computation | async-start | bytes 196608 | tf_op jit(solution)/shard_map/all_to_all | solution.py:634
  33.5 2.9 %collective-permute-start.5 = (bf16[2,144,256]{2,1,0:T(8,128)(2,1)}, bf16[2,144,256]{2,1,0:T(8,128)(2,1)S(1)}, u32[]{:S(2)}, u32[]{:S(2)}) collective-permute-start(bf16[2,144,256]{2,1,0:T(8,128)(2,1)} %get-tuple-element.38), channel_id=1, source_target_pairs={{0,6},{2,4},{4,2},{6,0},{8,14},{10,12},{12,10},{14,8},{1,7},{3,5},... | collective-permute-start | bytes 442376 | tf_op jit(solution)/shard_map/ppermute | solution.py:624
  36.4 0.0 collective-permute-done.refs_0_
  36.4 0.6 %collective-permute-start.6 = (bf16[2,144,256]{2,1,0:T(8,128)(2,1)}, bf16[2,144,256]{2,1,0:T(8,128)(2,1)S(1)}, u32[]{:S(2)}, u32[]{:S(2)}) collective-permute-start(bf16[2,144,256]{2,1,0:T(8,128)(2,1)} %get-tuple-element.39), channel_id=1, source_target_pairs={{0,4},{2,6},{4,0},{6,2},{8,12},{10,14},{12,8},{14,10},{1,5},{3,7},... | collective-permute-start | bytes 442376 | tf_op jit(solution)/shard_map/ppermute | solution.py:624
  37.0 0.0 collective-permute-done.1.refs_1_
  37.0 0.1 collective-permute-start.7
  37.1 0.0 collective-permute-done.2.refs_2_
  37.1 0.0 collective-permute-done.3.refs_3_
  37.1 1.6 %land.1 = (bf16[24,2,144,256]{3,2,1,0:T(8,128)(2,1)}, s32[4]{0:T(128)S(1)}, s32[4]{0:T(128)S(1)}, bf16[4,2,32,256]{3,2,1,0:T(8,128)(2,1)S(1)}) custom-call(bf16[2,144,256]{2,1,0:T(8,128)(2,1)S(1)} %collective-permute-done.refs_0_, bf16[2,144,256]{2,1,0:T(8,128)(2,1)S(1)} %collective-permute-done.1.refs_1_, ...), custom_call_target="tpu_custom_call", output_to_operand_aliasing={{0}: (4, {})} | custom-call | flops 68719476736 | bytes 268435456 | tf_op jit(solution)/shard_map/land/pallas_call | solution.py:463
  38.7 2.6 %all-to-all-done.small_ref = bf16[8,48,128]{2,1,0:T(8,128)(2,1)S(1)} async-done(((bf16[8,48,128]{2,1,0:T(8,128)(2,1)}), bf16[8,48,128]{2,1,0:T(8,128)(2,1)S(1)}, u32[]{:S(2)}, u32[]{:S(2)}) %all-to-all-start) | async-done | bytes 98336 | tf_op jit(solution)/shard_map/all_to_all | solution.py:634
  41.3 2.0 %settle.1 = (bf16[2,24,2048]{2,1,0:T(8,128)(2,1)}, bf16[24,2,144,256]{3,2,1,0:T(8,128)(2,1)}, s32[3]{0:T(128)S(1)}) custom-call(s32[4]{0:T(128)S(1)} %get-tuple-element.30.slot_ref, s32[4]{0:T(128)S(1)} %get-tuple-element.31.length_ref, bf16[768,128]{1,0:T(8,128)(2,1)S(1)} %copy-done, ...), custom_call_target="tpu_custom_call", output_to_operand_aliasing={{1}: (5, {})} | custom-call | flops 1 | bytes 1 | tf_op jit(solution)/shard_map/settle/pallas_call | solution.py:562
  43.4 0.0 collective-permute-done.5.refs_0_
  43.4 1.5 %collective-permute-done.6.refs_1_ = bf16[2,144,256]{2,1,0:T(8,128)(2,1)S(1)} collective-permute-done((bf16[2,144,256]{2,1,0:T(8,128)(2,1)}, bf16[2,144,256]{2,1,0:T(8,128)(2,1)S(1)}, u32[]{:S(2)}, u32[]{:S(2)}) %collective-permute-start.6) | collective-permute-done | bytes 147488 | tf_op jit(solution)/shard_map/ppermute | solution.py:624
  44.9 1.3 %finish.1 = bf16[24,2,144,256]{3,2,1,0:T(8,128)(2,1)} custom-call(s32[3]{0:T(128)S(1)} %get-tuple-element.37.slot_ref, bf16[2,144,256]{2,1,0:T(8,128)(2,1)S(1)} %collective-permute-done.5.refs_0_, bf16[2,144,256]{2,1,0:T(8,128)(2,1)S(1)} %collective-permute-done.6.refs_1_, ...), custom_call_target="tpu_custom_call", output_to_operand_aliasing={{}: (4, {})} | custom-call | flops 1 | bytes 1 | tf_op jit(solution)/shard_map/finish/pallas_call | solution.py:602
  (4 shorter events, 0.0 us)
Async XLA Ops:
  3.7 32.7 %collective-permute-start = (bf16[2,144,256]{2,1,0:T(8,128)(2,1)}, bf16[2,144,256]{2,1,0:T(8,128)(2,1)S(1)}, u32[]{:S(2)}, u32[]{:S(2)}) collective-permute-start(bf16[2,144,256]{2,1,0:T(8,128)(2,1)} %get-tuple-element.22), channel_id=1, source_target_pairs={{0,8},{2,10},{4,12},{6,14},{8,0},{10,2},{12,4},{14,6},{1,9},{3,11}... | collective-permute-start | bytes 442376 | tf_op jit(solution)/shard_map/ppermute | solution.py:624
  7.8 29.2 %collective-permute-start.1 = (bf16[2,144,256]{2,1,0:T(8,128)(2,1)}, bf16[2,144,256]{2,1,0:T(8,128)(2,1)S(1)}, u32[]{:S(2)}, u32[]{:S(2)}) collective-permute-start(bf16[2,144,256]{2,1,0:T(8,128)(2,1)} %get-tuple-element.23), channel_id=1, source_target_pairs={{0,10},{2,8},{4,14},{6,12},{8,2},{10,0},{12,6},{14,4},{1,11},{3,9}... | collective-permute-start | bytes 442376 | tf_op jit(solution)/shard_map/ppermute | solution.py:624
  9.1 28.0 %collective-permute-start.2 = (bf16[2,144,256]{2,1,0:T(8,128)(2,1)}, bf16[2,144,256]{2,1,0:T(8,128)(2,1)S(1)}, u32[]{:S(2)}, u32[]{:S(2)}) collective-permute-start(bf16[2,144,256]{2,1,0:T(8,128)(2,1)} %get-tuple-element.24), channel_id=1, source_target_pairs={{0,12},{2,14},{4,8},{6,10},{8,4},{10,6},{12,0},{14,2},{1,13},{3,15... | collective-permute-start | bytes 442376 | tf_op jit(solution)/shard_map/ppermute | solution.py:624
  12.7 24.4 %collective-permute-start.3 = (bf16[2,144,256]{2,1,0:T(8,128)(2,1)}, bf16[2,144,256]{2,1,0:T(8,128)(2,1)S(1)}, u32[]{:S(2)}, u32[]{:S(2)}) collective-permute-start(bf16[2,144,256]{2,1,0:T(8,128)(2,1)} %get-tuple-element.25), channel_id=1, source_target_pairs={{0,14},{2,12},{4,10},{6,8},{8,6},{10,4},{12,2},{14,0},{1,15},{3,13... | collective-permute-start | bytes 442376 | tf_op jit(solution)/shard_map/ppermute | solution.py:624
  17.2 1.6 %collective-permute-start.4 = (f32[48,512]{1,0:T(8,128)}, f32[48,512]{1,0:T(8,128)S(1)}, u32[]{:S(2)}, u32[]{:S(2)}) collective-permute-start(f32[48,512]{1,0:T(8,128)} %get-tuple-element.28), channel_id=1, source_target_pairs={{0,1},{1,0},{2,3},{3,2},{4,5},{5,4},{6,7},{7,6},{8,9},{9,8},{10,11... | collective-permute-start | bytes 294920 | tf_op jit(solution)/shard_map/ppermute | solution.py:629
  18.7 0.6 %copy-start.1 = (f32[48,512]{1,0:T(8,128)}, f32[48,512]{1,0:T(8,128)S(1)}, u32[]{:S(2)}) copy-start(f32[48,512]{1,0:T(8,128)S(1)} %collective-permute-done.4.got_ref) | copy-start | bytes 294916
  27.5 13.8 %all-to-all-start = ((bf16[8,48,128]{2,1,0:T(8,128)(2,1)}), bf16[8,48,128]{2,1,0:T(8,128)(2,1)S(1)}, u32[]{:S(2)}, u32[]{:S(2)}) async-start(bf16[8,48,128]{2,1,0:T(8,128)(2,1)} %get-tuple-element.33), calls=%async_computation | async-start | bytes 196608 | tf_op jit(solution)/shard_map/all_to_all | solution.py:634
  33.5 9.8 %collective-permute-start.5 = (bf16[2,144,256]{2,1,0:T(8,128)(2,1)}, bf16[2,144,256]{2,1,0:T(8,128)(2,1)S(1)}, u32[]{:S(2)}, u32[]{:S(2)}) collective-permute-start(bf16[2,144,256]{2,1,0:T(8,128)(2,1)} %get-tuple-element.38), channel_id=1, source_target_pairs={{0,6},{2,4},{4,2},{6,0},{8,14},{10,12},{12,10},{14,8},{1,7},{3,5},... | collective-permute-start | bytes 442376 | tf_op jit(solution)/shard_map/ppermute | solution.py:624
  36.4 8.5 %collective-permute-start.6 = (bf16[2,144,256]{2,1,0:T(8,128)(2,1)}, bf16[2,144,256]{2,1,0:T(8,128)(2,1)S(1)}, u32[]{:S(2)}, u32[]{:S(2)}) collective-permute-start(bf16[2,144,256]{2,1,0:T(8,128)(2,1)} %get-tuple-element.39), channel_id=1, source_target_pairs={{0,4},{2,6},{4,0},{6,2},{8,12},{10,14},{12,8},{14,10},{1,5},{3,7},... | collective-permute-start | bytes 442376 | tf_op jit(solution)/shard_map/ppermute | solution.py:624
  37.0 7.9 %collective-permute-start.7 = (bf16[2,144,256]{2,1,0:T(8,128)(2,1)}, bf16[2,144,256]{2,1,0:T(8,128)(2,1)S(1)}, u32[]{:S(2)}, u32[]{:S(2)}) collective-permute-start(bf16[2,144,256]{2,1,0:T(8,128)(2,1)} %get-tuple-element.40), channel_id=1, source_target_pairs={{0,2},{2,0},{4,6},{6,4},{8,10},{10,8},{12,14},{14,12},{1,3},{3,1},... | collective-permute-start | bytes 442376 | tf_op jit(solution)/shard_map/ppermute | solution.py:624
  37.1 4.2 %copy-start = (bf16[768,128]{1,0:T(8,128)(2,1)S(1)}, bf16[768,128]{1,0:T(8,128)(2,1)}, u32[]{:S(2)}) copy-start(bf16[768,128]{1,0:T(8,128)(2,1)} %get-tuple-element.32.mixed_ref) | copy-start | bytes 589828

commit v8 on v6

--- a/solution.py
+++ b/solution.py
@@ -50,20 +50,6 @@
 
     hidden_copy = pltpu.make_async_copy(hidden_ref, hidden_held, hidden_sem)
     hidden_copy.start()
-    steps, _, depth = hidden_ref.shape
-    width = key_ref.shape[1]
-    part = depth // chunks
-    weights = []
-    for chunk in range(chunks):
-        span = pl.ds(chunk * part, part)
-        for which, ref in enumerate((key_ref, value_ref)):
-            weights.append(
-                pltpu.make_async_copy(
-                    ref.at[span], held.at[which, span], weight_sems.at[chunk, which]
-                )
-            )
-            weights[-1].start()
-
     for peer in range(count):
         pick_ref[peer] = 0
     for row in range(rows):
@@ -76,6 +62,22 @@
         )
         fetches[shift].start()
 
+    steps, _, depth = hidden_ref.shape
+    width = key_ref.shape[1]
+    part = depth // chunks
+
+    def weight(chunk, which):
+        ref = (key_ref, value_ref)[which]
+        span = pl.ds(chunk * part, part)
+        return pltpu.make_async_copy(
+            ref.at[span], held.at[which, span], weight_sems.at[chunk, which]
+        )
+
+    def weights_start(chunk):
+        for which in range(2):
+            weight(chunk, which).start()
+
+    weights_start(0)
     tile = (TILE, lanes)
     last = lax.broadcasted_iota(jnp.int32, tile, 0) == TILE - 1
     first_lanes = lax.broadcasted_iota(jnp.int32, tile, 1) < HD
@@ -95,12 +97,16 @@
         )
         stores[shift].start()
 
+    weights_start(1)
     hidden_copy.wait()
     hidden = hidden_held[...].reshape(steps * rows, depth)
     sums = [None, None]
     for chunk in range(chunks):
         for which in range(2):
-            weights[2 * chunk + which].wait()
+            weight(chunk, which).wait()
+        if chunk + 2 < chunks:
+            weights_start(chunk + 2)
+        for which in range(2):
             product = jnp.dot(
                 hidden[:, chunk * part : (chunk + 1) * part],
                 held[which, chunk * part : (chunk + 1) * part, :],
@@ -178,9 +184,9 @@
     kv_ref,
     *refs,
 ):
-    late = (len(refs) - 14) // 2
+    late = (len(refs) - 15) // 2
     moved_ref, mixed_ref, small_ref = refs[late : late + 3]
-    fresh, query_held, query_rows, query_columns, mixed, sums, held = refs[-11:-4]
+    fresh, query_held, query_rows, query_columns, mixed, sums, held, appended = refs[-12:-4]
     sum_sems, query_sem, in_sems, out_sems = refs[-4:]
     steps, rows, query_width = query_ref.shape
     capacity, lanes = kv_ref.shape[2:]
@@ -209,10 +215,11 @@
 
     def store(index):
         return pltpu.make_async_copy(
-            held.at[span(index)], moved_ref.at[span(index)], out_sems.at[index]
+            appended.at[span(index)], moved_ref.at[span(index)], out_sems.at[index]
         )
 
-    for index in range(rows // team):
+    teams = range(block // team)
+    for index in teams:
         fetch(index).start()
 
     cosine, sine = rotation(length_ref, steps, rows)
@@ -246,11 +253,13 @@
     column_step = (column % per_head) // group
     column_head = lax.broadcasted_iota(jnp.int32, (HD, HD), 1) % per_row // per_head
     factor = 1.0 / math.sqrt(HD)
-    teams = range(block // team)
-
-    def work(part, carry):
+
+    for part in range(rows // block):
         for index in teams:
             fetch(part * len(teams) + index).wait()
+        if (part + 1) * block < rows:
+            for index in teams:
+                fetch((part + 1) * len(teams) + index).start()
         scores = []
         for index in teams:
             queries = query_columns[part * len(teams) + index]
@@ -264,18 +273,20 @@
                 kept = position < length
                 landing = [position == length + step for step in range(steps)]
                 for which in range(2):
-                    news = [fresh[which, pl.ds(step * rows + row, 1), :] for step in range(steps)]
                     for head in range(heads):
                         at = slice(head * HD, (head + 1) * HD)
                         stored = held[row, which, :, at].astype(jnp.float32)
                         stored = jnp.where(kept, stored, 0.0)
                         for step in range(steps):
-                            stored = jnp.where(landing[step], news[step][:, at], stored)
-                        held[row, which, :, at] = stored.astype(jnp.bfloat16)
-                one = jnp.dot(held[row, 0], queries, preferred_element_type=jnp.float32)
+                            new = fresh[which, step * rows + row : step * rows + row + 1, at]
+                            stored = jnp.where(landing[step], new, stored)
+                        appended[row, which, :, at] = stored.astype(jnp.bfloat16)
+                one = jnp.dot(appended[row, 0], queries, preferred_element_type=jnp.float32)
                 score = one if member == 0 else jnp.where(column_item == member, one, score)
                 limit = length if member == 0 else jnp.where(column_item == member, length, limit)
             scores.append(jnp.where(position <= limit + column_step, score * factor, -jnp.inf))
+        for index in teams:
+            store(part * len(teams) + index).start()
         weights = []
         for score in scores:
             raised = jnp.exp(score - jnp.max(score, axis=0, keepdims=True))
@@ -286,19 +297,14 @@
                 row = part * block + index * team + member
                 result = jnp.dot(
                     weights[index][member * per_row : (member + 1) * per_row],
-                    held[row, 1],
+                    appended[row, 1],
                     preferred_element_type=jnp.float32,
                 )
                 for head in range(heads):
-                    at = pl.multiple_of(row * per_row + head * per_head, per_head)
-                    mixed[pl.ds(at, per_head), :] = result[
+                    at = row * per_row + head * per_head
+                    mixed[at : at + per_head, :] = result[
                         head * per_head : (head + 1) * per_head, head * HD : (head + 1) * HD
                     ]
-        for index in teams:
-            store(part * len(teams) + index).start()
-        return carry
-
-    lax.fori_loop(0, rows // block, work, 0)
 
     mixed_ref[...] = mixed[...].astype(jnp.bfloat16)
     for peer in range(count):
@@ -353,6 +359,7 @@
             pltpu.VMEM((rows * per_row, HD), jnp.float32),
             pltpu.VMEM((2,) + own.shape, own.dtype),
             pltpu.VMEM(kv_cache.shape, kv_cache.dtype),
+            pltpu.VMEM(kv_cache.shape, kv_cache.dtype),
             pltpu.SemaphoreType.DMA((2,)),
             pltpu.SemaphoreType.DMA,
             pltpu.SemaphoreType.DMA((teams,)),

time: 41.7 us -> 42.3 us (1.014)
  Pallas kernels: 18.6 us -> 19.1 us
    pallas_call x1, Pallas kernels: 5.83 us -> 6.54 us  [prepare(): pl.pallas_call(functools.partial(prepare_kernel, count, chunks), out_shap...]
  transfers between devices with their start and end apart: 9 -> 9, of which waited for: 4 -> 4; matrix products, arithmetic and copies ran while one was open for 0% -> 0% of each run, Pallas kernels for 29% -> 28%
where the time goes in v8:
time: 42.3 us; the launch traced here: 41.9 us
  Pallas kernels  19.1 us (45%)
  starting transfers between devices  18.6 us (44%)
  waiting for transfers between devices  2.89 us (7%)
  between operations  0.68 us (2%)
  local copies, waits for them, and re-layouts  0.64 us (2%)
    ppermute x7, starting transfers between devices, send(): return lax.ppermute(block, 'inst', pairs)  13.9 us
    pallas_call x1, Pallas kernels, attend(): pl.pallas_call(functools.partial(attend_kernel, count, block), out_shape=...  7.93 us
    pallas_call x1, Pallas kernels, prepare(): pl.pallas_call(functools.partial(prepare_kernel, count, chunks), out_shap...  6.54 us
    all_to_all x1, starting transfers between devices, local(): small_got = lax.all_to_all(small, 'inst', 0, 0, tiled=True)  4.21 us
    pallas_call x1, Pallas kernels, settle(): pl.pallas_call(functools.partial(settle_kernel, count, early, group), out...  2.03 us
    pallas_call x1, Pallas kernels, land(): pl.pallas_call(functools.partial(land_kernel, pieces), out_shape=[jax.Sha...  1.62 us
    all_to_all x1, waiting for transfers between devices, local(): small_got = lax.all_to_all(small, 'inst', 0, 0, tiled=True)  1.52 us
    ppermute x7, waiting for transfers between devices, send(): return lax.ppermute(block, 'inst', pairs)  1.37 us
  transfers between devices with their start and end apart: 9, of which 4 were waited for; matrix products, arithmetic and copies ran while one was open for 0% of the time, Pallas kernels for 28%

profile of v8, /device:TPU:0, one launch (start us, length us, event | category | flops | bytes accessed | tf_op | source)
XLA Modules:
  0.0 41.9 jit_solution(12610502938977374164)
XLA Ops:
  0.6 6.5 %prepare.1 = (bf16[2,144,256]{2,1,0:T(8,128)(2,1)}, bf16[2,144,256]{2,1,0:T(8,128)(2,1)}, bf16[2,144,256]{2,1,0:T(8,128)(2,1)}, bf16[2,144,256]{2,1,0:T(8,128)(2...) custom-call(s32[24]{0:T(128)} %dest_ref.3, ...), custom_call_target="tpu_custom_call" | custom-call | flops 1 | bytes 1 | tf_op jit(solution)/shard_map/prepare/pallas_call | solution.py:137
  7.2 0.5 %collective-permute-start.4 = (f32[48,512]{1,0:T(8,128)}, f32[48,512]{1,0:T(8,128)S(1)}, u32[]{:S(2)}, u32[]{:S(2)}) collective-permute-start(f32[48,512]{1,0:T(8,128)} %get-tuple-element.30), channel_id=1, source_target_pairs={{0,1},{1,0},{2,3},{3,2},{4,5},{5,4},{6,7},{7,6},{8,9},{9,8},{10,11... | collective-permute-start | bytes 294920 | tf_op jit(solution)/shard_map/ppermute | solution.py:629
  7.7 3.7 %collective-permute-start = (bf16[2,144,256]{2,1,0:T(8,128)(2,1)}, bf16[2,144,256]{2,1,0:T(8,128)(2,1)S(1)}, u32[]{:S(2)}, u32[]{:S(2)}) collective-permute-start(bf16[2,144,256]{2,1,0:T(8,128)(2,1)} %get-tuple-element.24), channel_id=1, source_target_pairs={{0,8},{2,10},{4,12},{6,14},{8,0},{10,2},{12,4},{14,6},{1,9},{3,11}... | collective-permute-start | bytes 442376 | tf_op jit(solution)/shard_map/ppermute | solution.py:623
  11.4 1.3 %collective-permute-start.1 = (bf16[2,144,256]{2,1,0:T(8,128)(2,1)}, bf16[2,144,256]{2,1,0:T(8,128)(2,1)S(1)}, u32[]{:S(2)}, u32[]{:S(2)}) collective-permute-start(bf16[2,144,256]{2,1,0:T(8,128)(2,1)} %get-tuple-element.25), channel_id=1, source_target_pairs={{0,10},{2,8},{4,14},{6,12},{8,2},{10,0},{12,6},{14,4},{1,11},{3,9}... | collective-permute-start | bytes 442376 | tf_op jit(solution)/shard_map/ppermute | solution.py:623
  12.6 3.6 %collective-permute-start.2 = (bf16[2,144,256]{2,1,0:T(8,128)(2,1)}, bf16[2,144,256]{2,1,0:T(8,128)(2,1)S(1)}, u32[]{:S(2)}, u32[]{:S(2)}) collective-permute-start(bf16[2,144,256]{2,1,0:T(8,128)(2,1)} %get-tuple-element.26), channel_id=1, source_target_pairs={{0,12},{2,14},{4,8},{6,10},{8,4},{10,6},{12,0},{14,2},{1,13},{3,15... | collective-permute-start | bytes 442376 | tf_op jit(solution)/shard_map/ppermute | solution.py:623
  16.3 0.0 collective-permute-start.3
  16.3 0.0 collective-permute-done.4.got_ref
  16.3 0.6 %copy-done.1 = f32[48,512]{1,0:T(8,128)} copy-done((f32[48,512]{1,0:T(8,128)}, f32[48,512]{1,0:T(8,128)S(1)}, u32[]{:S(2)}) %copy-start.1) | copy-done | bytes 98328
  16.9 7.9 %attend.1 = (bf16[24,2,144,256]{3,2,1,0:T(8,128)(2,1)}, bf16[768,128]{1,0:T(8,128)(2,1)}, bf16[8,48,128]{2,1,0:T(8,128)(2,1)}, bf16[2,144,256]{2,1,0:T(8,128)(2,...) custom-call(s32[24]{0:T(128)} %length_ref.3, ...), custom_call_target="tpu_custom_call", output_to_operand_aliasing={{3}: (8, {}), {4}: (9, {}), {5}: (10, {})} | custom-call | flops 68719476736 | bytes 268435456 | tf_op jit(solution)/shard_map/attend/pallas_call | solution.py:344
  24.8 4.2 %all-to-all-start = ((bf16[8,48,128]{2,1,0:T(8,128)(2,1)}), bf16[8,48,128]{2,1,0:T(8,128)(2,1)S(1)}, u32[]{:S(2)}, u32[]{:S(2)}) async-start(bf16[8,48,128]{2,1,0:T(8,128)(2,1)} %get-tuple-element.38), calls=%async_computation | async-start | bytes 196608 | tf_op jit(solution)/shard_map/all_to_all | solution.py:643
  29.0 4.7 %collective-permute-start.5 = (bf16[2,144,256]{2,1,0:T(8,128)(2,1)}, bf16[2,144,256]{2,1,0:T(8,128)(2,1)S(1)}, u32[]{:S(2)}, u32[]{:S(2)}) collective-permute-start(bf16[2,144,256]{2,1,0:T(8,128)(2,1)} %get-tuple-element.42), channel_id=1, source_target_pairs={{0,14},{2,12},{4,10},{6,8},{8,6},{10,4},{12,2},{14,0},{1,15},{3,13... | collective-permute-start | bytes 442376 | tf_op jit(solution)/shard_map/ppermute | solution.py:623
  33.8 0.0 collective-permute-done.refs_0_
  33.8 0.0 collective-permute-start.6
  33.8 0.0 collective-permute-done.1.refs_1_
  33.8 0.6 %collective-permute-start.7 = (bf16[2,144,256]{2,1,0:T(8,128)(2,1)}, bf16[2,144,256]{2,1,0:T(8,128)(2,1)S(1)}, u32[]{:S(2)}, u32[]{:S(2)}) collective-permute-start(bf16[2,144,256]{2,1,0:T(8,128)(2,1)} %get-tuple-element.44), channel_id=1, source_target_pairs={{0,2},{2,0},{4,6},{6,4},{8,10},{10,8},{12,14},{14,12},{1,3},{3,1},... | collective-permute-start | bytes 442376 | tf_op jit(solution)/shard_map/ppermute | solution.py:623
  34.4 0.0 collective-permute-done.2.refs_2_
  34.4 0.0 collective-permute-done.3.refs_3_
  34.4 1.6 %land.1 = (bf16[24,2,144,256]{3,2,1,0:T(8,128)(2,1)}, s32[4]{0:T(128)S(1)}, s32[4]{0:T(128)S(1)}, bf16[4,2,32,256]{3,2,1,0:T(8,128)(2,1)S(1)}) custom-call(bf16[2,144,256]{2,1,0:T(8,128)(2,1)S(1)} %collective-permute-done.refs_0_, bf16[2,144,256]{2,1,0:T(8,128)(2,1)S(1)} %collective-permute-done.1.refs_1_, ...), custom_call_target="tpu_custom_call", output_to_operand_aliasing={{0}: (4, {})} | custom-call | flops 68719476736 | bytes 268435456 | tf_op jit(solution)/shard_map/land/pallas_call | solution.py:445
  36.0 1.5 %all-to-all-done.small_ref.refs_3_ = bf16[8,48,128]{2,1,0:T(8,128)(2,1)S(1)} async-done(((bf16[8,48,128]{2,1,0:T(8,128)(2,1)}), bf16[8,48,128]{2,1,0:T(8,128)(2,1)S(1)}, u32[]{:S(2)}, u32[]{:S(2)}) %all-to-all-start) | async-done | bytes 98336 | tf_op jit(solution)/shard_map/all_to_all | solution.py:643
  37.6 2.0 %settle.1 = (bf16[2,24,2048]{2,1,0:T(8,128)(2,1)}, bf16[24,2,144,256]{3,2,1,0:T(8,128)(2,1)}) custom-call(s32[4]{0:T(128)S(1)} %get-tuple-element.35.slot_ref, s32[4]{0:T(128)S(1)} %get-tuple-element.36.length_ref, bf16[768,128]{1,0:T(8,128)(2,1)S(1)} %copy-done, ...), custom_call_target="tpu_custom_call", output_to_operand_aliasing={{1}: (5, {})} | custom-call | flops 1 | bytes 1 | tf_op jit(solution)/shard_map/settle/pallas_call | solution.py:541
  39.6 0.3 collective-permute-done.5.refs_0_
  40.0 0.9 %collective-permute-done.6.refs_1_ = bf16[2,144,256]{2,1,0:T(8,128)(2,1)S(1)} collective-permute-done((bf16[2,144,256]{2,1,0:T(8,128)(2,1)}, bf16[2,144,256]{2,1,0:T(8,128)(2,1)S(1)}, u32[]{:S(2)}, u32[]{:S(2)}) %collective-permute-start.6) | collective-permute-done | bytes 147488 | tf_op jit(solution)/shard_map/ppermute | solution.py:623
  40.8 0.1 collective-permute-done.7.refs_2_
  41.0 1.0 %finish.1 = bf16[24,2,144,256]{3,2,1,0:T(8,128)(2,1)} custom-call(bf16[2,144,256]{2,1,0:T(8,128)(2,1)S(1)} %collective-permute-done.5.refs_0_, bf16[2,144,256]{2,1,0:T(8,128)(2,1)S(1)} %collective-permute-done.6.refs_1_, bf16[2,144,256]{2,1,0:T(8,128)(2,1)S(1)} %collective-permute-done.7.refs_2_, ...), custom_call_target="tpu_custom_call", output_to_operand_aliasing={{}: (4, {})} | custom-call | flops 1 | bytes 1 | tf_op jit(solution)/shard_map/finish/pallas_call | solution.py:596
  (3 shorter events, 0.0 us)
Async XLA Ops:
  7.2 9.1 %collective-permute-start.4 = (f32[48,512]{1,0:T(8,128)}, f32[48,512]{1,0:T(8,128)S(1)}, u32[]{:S(2)}, u32[]{:S(2)}) collective-permute-start(f32[48,512]{1,0:T(8,128)} %get-tuple-element.30), channel_id=1, source_target_pairs={{0,1},{1,0},{2,3},{3,2},{4,5},{5,4},{6,7},{7,6},{8,9},{9,8},{10,11... | collective-permute-start | bytes 294920 | tf_op jit(solution)/shard_map/ppermute | solution.py:629
  7.7 26.1 %collective-permute-start = (bf16[2,144,256]{2,1,0:T(8,128)(2,1)}, bf16[2,144,256]{2,1,0:T(8,128)(2,1)S(1)}, u32[]{:S(2)}, u32[]{:S(2)}) collective-permute-start(bf16[2,144,256]{2,1,0:T(8,128)(2,1)} %get-tuple-element.24), channel_id=1, source_target_pairs={{0,8},{2,10},{4,12},{6,14},{8,0},{10,2},{12,4},{14,6},{1,9},{3,11}... | collective-permute-start | bytes 442376 | tf_op jit(solution)/shard_map/ppermute | solution.py:623
  11.4 22.4 %collective-permute-start.1 = (bf16[2,144,256]{2,1,0:T(8,128)(2,1)}, bf16[2,144,256]{2,1,0:T(8,128)(2,1)S(1)}, u32[]{:S(2)}, u32[]{:S(2)}) collective-permute-start(bf16[2,144,256]{2,1,0:T(8,128)(2,1)} %get-tuple-element.25), channel_id=1, source_target_pairs={{0,10},{2,8},{4,14},{6,12},{8,2},{10,0},{12,6},{14,4},{1,11},{3,9}... | collective-permute-start | bytes 442376 | tf_op jit(solution)/shard_map/ppermute | solution.py:623
  12.6 21.8 %collective-permute-start.2 = (bf16[2,144,256]{2,1,0:T(8,128)(2,1)}, bf16[2,144,256]{2,1,0:T(8,128)(2,1)S(1)}, u32[]{:S(2)}, u32[]{:S(2)}) collective-permute-start(bf16[2,144,256]{2,1,0:T(8,128)(2,1)} %get-tuple-element.26), channel_id=1, source_target_pairs={{0,12},{2,14},{4,8},{6,10},{8,4},{10,6},{12,0},{14,2},{1,13},{3,15... | collective-permute-start | bytes 442376 | tf_op jit(solution)/shard_map/ppermute | solution.py:623
  16.3 18.2 %collective-permute-start.3 = (bf16[2,144,256]{2,1,0:T(8,128)(2,1)}, bf16[2,144,256]{2,1,0:T(8,128)(2,1)S(1)}, u32[]{:S(2)}, u32[]{:S(2)}) collective-permute-start(bf16[2,144,256]{2,1,0:T(8,128)(2,1)} %get-tuple-element.27), channel_id=1, source_target_pairs={{0,6},{2,4},{4,2},{6,0},{8,14},{10,12},{12,10},{14,8},{1,7},{3,5},... | collective-permute-start | bytes 442376 | tf_op jit(solution)/shard_map/ppermute | solution.py:623
  16.3 0.6 %copy-start.1 = (f32[48,512]{1,0:T(8,128)}, f32[48,512]{1,0:T(8,128)S(1)}, u32[]{:S(2)}) copy-start(f32[48,512]{1,0:T(8,128)S(1)} %collective-permute-done.4.got_ref) | copy-start | bytes 294916
  24.8 12.7 %all-to-all-start = ((bf16[8,48,128]{2,1,0:T(8,128)(2,1)}), bf16[8,48,128]{2,1,0:T(8,128)(2,1)S(1)}, u32[]{:S(2)}, u32[]{:S(2)}) async-start(bf16[8,48,128]{2,1,0:T(8,128)(2,1)} %get-tuple-element.38), calls=%async_computation | async-start | bytes 196608 | tf_op jit(solution)/shard_map/all_to_all | solution.py:643
  29.0 10.9 %collective-permute-start.5 = (bf16[2,144,256]{2,1,0:T(8,128)(2,1)}, bf16[2,144,256]{2,1,0:T(8,128)(2,1)S(1)}, u32[]{:S(2)}, u32[]{:S(2)}) collective-permute-start(bf16[2,144,256]{2,1,0:T(8,128)(2,1)} %get-tuple-element.42), channel_id=1, source_target_pairs={{0,14},{2,12},{4,10},{6,8},{8,6},{10,4},{12,2},{14,0},{1,15},{3,13... | collective-permute-start | bytes 442376 | tf_op jit(solution)/shard_map/ppermute | solution.py:623
  33.8 7.1 %collective-permute-start.6 = (bf16[2,144,256]{2,1,0:T(8,128)(2,1)}, bf16[2,144,256]{2,1,0:T(8,128)(2,1)S(1)}, u32[]{:S(2)}, u32[]{:S(2)}) collective-permute-start(bf16[2,144,256]{2,1,0:T(8,128)(2,1)} %get-tuple-element.43), channel_id=1, source_target_pairs={{0,4},{2,6},{4,0},{6,2},{8,12},{10,14},{12,8},{14,10},{1,5},{3,7},... | collective-permute-start | bytes 442376 | tf_op jit(solution)/shard_map/ppermute | solution.py:623
  33.8 7.2 %collective-permute-start.7 = (bf16[2,144,256]{2,1,0:T(8,128)(2,1)}, bf16[2,144,256]{2,1,0:T(8,128)(2,1)S(1)}, u32[]{:S(2)}, u32[]{:S(2)}) collective-permute-start(bf16[2,144,256]{2,1,0:T(8,128)(2,1)} %get-tuple-element.44), channel_id=1, source_target_pairs={{0,2},{2,0},{4,6},{6,4},{8,10},{10,8},{12,14},{14,12},{1,3},{3,1},... | collective-permute-start | bytes 442376 | tf_op jit(solution)/shard_map/ppermute | solution.py:623
  34.4 3.2 %copy-start = (bf16[768,128]{1,0:T(8,128)(2,1)S(1)}, bf16[768,128]{1,0:T(8,128)(2,1)}, u32[]{:S(2)}) copy-start(bf16[768,128]{1,0:T(8,128)(2,1)} %get-tuple-element.37.mixed_ref) | copy-start | bytes 589828

commit v9 on v5

--- a/solution.py
+++ b/solution.py
@@ -41,25 +41,15 @@
     count, chunks, dest_ref, length_ref, hidden_ref, kv_ref, key_ref, value_ref, *refs
 ):
     block_refs = refs[: count - 1]
-    pick_ref, own_ref, other_ref, blocks, held, total = refs[count - 1 : count + 5]
-    in_sems, out_sems, weight_sems = refs[count + 5 :]
+    pick_ref, own_ref, other_ref, blocks, hidden_held, held, total = refs[count - 1 : count + 6]
+    in_sems, out_sems, hidden_sem, weight_sems = refs[count + 6 :]
     rows = dest_ref.shape[0]
     capacity, lanes = kv_ref.shape[2:]
     me = lax.axis_index("inst")
     shifts = range(1, count)
 
-    for peer in range(count):
-        pick_ref[peer] = 0
-    for row in range(rows):
-        pick_ref[quotient(dest_ref[row], rows, rows * count)] = row
-    fetches, stores = {}, {}
-    for shift in shifts:
-        row = pick_ref[peer_to(me, shift, count)]
-        fetches[shift] = pltpu.make_async_copy(
-            kv_ref.at[row], blocks.at[shift - 1], in_sems.at[shift - 1]
-        )
-        fetches[shift].start()
-
+    hidden_copy = pltpu.make_async_copy(hidden_ref, hidden_held, hidden_sem)
+    hidden_copy.start()
     steps, _, depth = hidden_ref.shape
     width = key_ref.shape[1]
     part = depth // chunks
@@ -73,6 +63,18 @@
                 )
             )
             weights[-1].start()
+
+    for peer in range(count):
+        pick_ref[peer] = 0
+    for row in range(rows):
+        pick_ref[quotient(dest_ref[row], rows, rows * count)] = row
+    fetches, stores = {}, {}
+    for shift in shifts:
+        row = pick_ref[peer_to(me, shift, count)]
+        fetches[shift] = pltpu.make_async_copy(
+            kv_ref.at[row], blocks.at[shift - 1], in_sems.at[shift - 1]
+        )
+        fetches[shift].start()
 
     tile = (TILE, lanes)
     last = lax.broadcasted_iota(jnp.int32, tile, 0) == TILE - 1
@@ -93,7 +95,8 @@
         )
         stores[shift].start()
 
-    hidden = hidden_ref[...].reshape(steps * rows, depth)
+    hidden_copy.wait()
+    hidden = hidden_held[...].reshape(steps * rows, depth)
     sums = [None, None]
     for chunk in range(chunks):
         for which in range(2):
@@ -129,14 +132,16 @@
         functools.partial(prepare_kernel, count, chunks),
         out_shape=[jax.ShapeDtypeStruct(shape, kv_cache.dtype)] * (count - 1)
         + [jax.ShapeDtypeStruct((count,), jnp.int32), part, part],
-        in_specs=[smem, smem, vmem, hbm, hbm, hbm],
+        in_specs=[smem, smem, hbm, hbm, hbm, hbm],
         out_specs=[hbm] * (count - 1) + [smem, vmem, vmem],
         scratch_shapes=[
             pltpu.VMEM((count - 1,) + shape, kv_cache.dtype),
+            pltpu.VMEM(hidden_new.shape, hidden_new.dtype),
             pltpu.VMEM((2, depth, width), key_weight.dtype),
             pltpu.VMEM((steps * rows, 2 * width), jnp.float32),
             pltpu.SemaphoreType.DMA((count - 1,)),
             pltpu.SemaphoreType.DMA((count - 1,)),
+            pltpu.SemaphoreType.DMA,
             pltpu.SemaphoreType.DMA((chunks, 2)),
         ],
         compiler_params=pltpu.CompilerParams(vmem_limit_bytes=VMEM_LIMIT),
@@ -148,16 +153,24 @@
 
 def rotation(length_ref, steps, rows):
     half = HD // 2
-    line = lax.broadcasted_iota(jnp.int32, (steps * rows, HD), 0)
+    line = lax.broadcasted_iota(jnp.int32, (rows, HD), 0)
     lane = lax.broadcasted_iota(jnp.int32, (steps * rows, HD), 1)
-    position = jnp.zeros((steps * rows, HD), jnp.int32)
-    for step in range(steps):
-        for row in range(rows):
-            position = jnp.where(line == step * rows + row, length_ref[row] + step, position)
+    length = jnp.zeros((rows, HD), jnp.int32)
+    for row in range(rows):
+        length = jnp.where(line == row, length_ref[row], length)
+    position = jnp.concatenate([length + step for step in range(steps)], axis=0)
     order = (lane % half).astype(jnp.float32)
     angle = position.astype(jnp.float32) * jnp.exp(-math.log(ROPE_BASE) * 2.0 * order / HD)
-    sine = jnp.sin(angle)
-    return jnp.cos(angle), jnp.where(lane < half, -sine, sine)
+    turns = jnp.floor(angle * (1.0 / math.pi) + 0.5)
+    rest = ((angle - turns * 3.140625) - turns * 9.67502593994140625e-4) - turns * 1.5099579909783e-7
+    sign = 1.0 - 2.0 * (turns - 2.0 * jnp.floor(turns * 0.5))
+    square = rest * rest
+    cosine, sine = jnp.ones_like(rest), jnp.ones_like(rest)
+    for power in range(6, 0, -1):
+        cosine = 1.0 - cosine * square * (1.0 / ((2 * power - 1) * (2 * power)))
+        sine = 1.0 - sine * square * (1.0 / ((2 * power) * (2 * power + 1)))
+    sine = sign * rest * sine
+    return sign * cosine, jnp.where(lane < half, -sine, sine)
 
 
 def attend_kernel(
@@ -315,7 +328,7 @@
         ],
         input_output_aliases={8 + i: 3 + i for i in range(len(late))},
         compiler_params=pltpu.CompilerParams(vmem_limit_bytes=ATTEND_LIMIT),
-        cost_estimate=LIGHT,
+        cost_estimate=HEAVY,
         name="attend",
     )(lengths, destination, pick, own, got, gain, queries, kv_cache, *late)
     return outs[0], outs[1], outs[2], outs[3:]
@@ -562,8 +575,9 @@
     steps = queries.shape[0]
     group = queries.shape[2] // kv_cache.shape[3]
     count = lax.axis_size("inst")
-    early = list(range(max(count // 2, 1), count - 1))
-    late = [count - 1] + list(range(1, max(count // 2, 1)))
+    half = max(count // 2, 1)
+    early = list(range(half, count - 1)) + [half - 1] * (half > 1)
+    late = [count - 1] + list(range(half - 2, 0, -1))
 
     def send(block, shift):
         pairs = [(i, peer_to(i, shift, count)) for i in range(count)]

time: 46.1 us -> 40.6 us (0.88)
  waiting for transfers between devices: 6.43 us -> 2.97 us
  starting transfers between devices: 20.5 us -> 18.6 us
    ppermute x7, waiting for transfers between devices: 4.91 us -> 1.15 us  [send(): return lax.ppermute(block, 'inst', pairs)]
    ppermute x7, starting transfers between devices: 17.1 us -> 13.9 us  [send(): return lax.ppermute(block, 'inst', pairs)]
    all_to_all x1, waiting for transfers between devices: 0.01 us -> 1.82 us  [local(): small_got = lax.all_to_all(small, 'inst', 0, 0, tiled=True)]
    ppermute x1, waiting for transfers between devices: 1.51 us -> 0.01 us  [local(): got = lax.ppermute(other, 'tp', [(0, 1), (1, 0)])]
    all_to_all x1, starting transfers between devices: 3.36 us -> 4.2 us  [local(): small_got = lax.all_to_all(small, 'inst', 0, 0, tiled=True)]
    ppermute x1, starting transfers between devices: 0.01 us -> 0.52 us  [local(): got = lax.ppermute(other, 'tp', [(0, 1), (1, 0)])]
  transfers between devices with their start and end apart: 9 -> 9, of which waited for: 3 -> 2; matrix products, arithmetic and copies ran while one was open for 0% -> 0% of each run, Pallas kernels for 23% -> 26%
where the time goes in v9:
time: 40.6 us; the launch traced here: 40.1 us
  starting transfers between devices  18.6 us (46%)
  Pallas kernels  17.2 us (42%)
  waiting for transfers between devices  2.97 us (7%)
  between operations  0.67 us (2%)
  local copies, waits for them, and re-layouts  0.64 us (2%)
    ppermute x7, starting transfers between devices, send(): return lax.ppermute(block, 'inst', pairs)  13.9 us
    pallas_call x1, Pallas kernels, attend(): pl.pallas_call(functools.partial(attend_kernel, count, block), grid=(rows...  6.74 us
    pallas_call x1, Pallas kernels, prepare(): pl.pallas_call(functools.partial(prepare_kernel, count, chunks), out_shap...  5.83 us
    all_to_all x1, starting transfers between devices, local(): small_got = lax.all_to_all(small, 'inst', 0, 0, tiled=True)  4.2 us
    pallas_call x1, Pallas kernels, settle(): pl.pallas_call(functools.partial(settle_kernel, count, early, group), out...  2.03 us
    all_to_all x1, waiting for transfers between devices, local(): small_got = lax.all_to_all(small, 'inst', 0, 0, tiled=True)  1.82 us
    pallas_call x1, Pallas kernels, land(): pl.pallas_call(functools.partial(land_kernel, pieces), out_shape=[jax.Sha...  1.62 us
    ppermute x7, waiting for transfers between devices, send(): return lax.ppermute(block, 'inst', pairs)  1.15 us
  transfers between devices with their start and end apart: 9, of which 2 were waited for; matrix products, arithmetic and copies ran while one was open for 0% of the time, Pallas kernels for 26%

profile of v9, /device:TPU:0, one launch (start us, length us, event | category | flops | bytes accessed | tf_op | source)
XLA Modules:
  0.0 40.1 jit_solution(16723178297014329225)
XLA Ops:
  0.6 5.8 %prepare.1 = (bf16[2,144,256]{2,1,0:T(8,128)(2,1)}, bf16[2,144,256]{2,1,0:T(8,128)(2,1)}, bf16[2,144,256]{2,1,0:T(8,128)(2,1)}, bf16[2,144,256]{2,1,0:T(8,128)(2...) custom-call(s32[24]{0:T(128)} %dest_ref.3, ...), custom_call_target="tpu_custom_call" | custom-call | flops 1 | bytes 1 | tf_op jit(solution)/shard_map/prepare/pallas_call | solution.py:131
  6.5 0.5 %collective-permute-start.4 = (f32[48,512]{1,0:T(8,128)}, f32[48,512]{1,0:T(8,128)S(1)}, u32[]{:S(2)}, u32[]{:S(2)}) collective-permute-start(f32[48,512]{1,0:T(8,128)} %get-tuple-element.30), channel_id=1, source_target_pairs={{0,1},{1,0},{2,3},{3,2},{4,5},{5,4},{6,7},{7,6},{8,9},{9,8},{10,11... | collective-permute-start | bytes 294920 | tf_op jit(solution)/shard_map/ppermute | solution.py:590
  7.0 3.7 %collective-permute-start = (bf16[2,144,256]{2,1,0:T(8,128)(2,1)}, bf16[2,144,256]{2,1,0:T(8,128)(2,1)S(1)}, u32[]{:S(2)}, u32[]{:S(2)}) collective-permute-start(bf16[2,144,256]{2,1,0:T(8,128)(2,1)} %get-tuple-element.24), channel_id=1, source_target_pairs={{0,8},{2,10},{4,12},{6,14},{8,0},{10,2},{12,4},{14,6},{1,9},{3,11}... | collective-permute-start | bytes 442376 | tf_op jit(solution)/shard_map/ppermute | solution.py:584
  10.6 1.3 %collective-permute-start.1 = (bf16[2,144,256]{2,1,0:T(8,128)(2,1)}, bf16[2,144,256]{2,1,0:T(8,128)(2,1)S(1)}, u32[]{:S(2)}, u32[]{:S(2)}) collective-permute-start(bf16[2,144,256]{2,1,0:T(8,128)(2,1)} %get-tuple-element.25), channel_id=1, source_target_pairs={{0,10},{2,8},{4,14},{6,12},{8,2},{10,0},{12,6},{14,4},{1,11},{3,9}... | collective-permute-start | bytes 442376 | tf_op jit(solution)/shard_map/ppermute | solution.py:584
  11.9 3.6 %collective-permute-start.2 = (bf16[2,144,256]{2,1,0:T(8,128)(2,1)}, bf16[2,144,256]{2,1,0:T(8,128)(2,1)S(1)}, u32[]{:S(2)}, u32[]{:S(2)}) collective-permute-start(bf16[2,144,256]{2,1,0:T(8,128)(2,1)} %get-tuple-element.26), channel_id=1, source_target_pairs={{0,12},{2,14},{4,8},{6,10},{8,4},{10,6},{12,0},{14,2},{1,13},{3,15... | collective-permute-start | bytes 442376 | tf_op jit(solution)/shard_map/ppermute | solution.py:584
  15.5 0.0 collective-permute-start.3
  15.5 0.0 collective-permute-done.4.got_ref
  15.5 0.6 %copy-done.1 = f32[48,512]{1,0:T(8,128)} copy-done((f32[48,512]{1,0:T(8,128)}, f32[48,512]{1,0:T(8,128)S(1)}, u32[]{:S(2)}) %copy-start.1) | copy-done | bytes 98328
  16.2 6.7 %attend.1 = (bf16[24,2,144,256]{3,2,1,0:T(8,128)(2,1)}, bf16[768,128]{1,0:T(8,128)(2,1)}, bf16[8,48,128]{2,1,0:T(8,128)(2,1)}, bf16[2,144,256]{2,1,0:T(8,128)(2,...) custom-call(s32[24]{0:T(128)} %length_ref.3, ...), custom_call_target="tpu_custom_call", output_to_operand_aliasing={{3}: (8, {}), {4}: (9, {}), {5}: (10, {})} | custom-call | flops 68719476736 | bytes 268435456 | tf_op jit(solution)/shard_map/attend/pallas_call | solution.py:312
  22.9 4.2 %all-to-all-start = ((bf16[8,48,128]{2,1,0:T(8,128)(2,1)}), bf16[8,48,128]{2,1,0:T(8,128)(2,1)S(1)}, u32[]{:S(2)}, u32[]{:S(2)}) async-start(bf16[8,48,128]{2,1,0:T(8,128)(2,1)} %get-tuple-element.38), calls=%async_computation | async-start | bytes 196608 | tf_op jit(solution)/shard_map/all_to_all | solution.py:604
  27.1 4.7 %collective-permute-start.5 = (bf16[2,144,256]{2,1,0:T(8,128)(2,1)}, bf16[2,144,256]{2,1,0:T(8,128)(2,1)S(1)}, u32[]{:S(2)}, u32[]{:S(2)}) collective-permute-start(bf16[2,144,256]{2,1,0:T(8,128)(2,1)} %get-tuple-element.42), channel_id=1, source_target_pairs={{0,14},{2,12},{4,10},{6,8},{8,6},{10,4},{12,2},{14,0},{1,15},{3,13... | collective-permute-start | bytes 442376 | tf_op jit(solution)/shard_map/ppermute | solution.py:584
  31.8 0.0 collective-permute-done.refs_0_
  31.8 0.0 collective-permute-start.6
  31.8 0.0 collective-permute-done.1.refs_1_
  31.9 0.6 %collective-permute-start.7 = (bf16[2,144,256]{2,1,0:T(8,128)(2,1)}, bf16[2,144,256]{2,1,0:T(8,128)(2,1)S(1)}, u32[]{:S(2)}, u32[]{:S(2)}) collective-permute-start(bf16[2,144,256]{2,1,0:T(8,128)(2,1)} %get-tuple-element.44), channel_id=1, source_target_pairs={{0,2},{2,0},{4,6},{6,4},{8,10},{10,8},{12,14},{14,12},{1,3},{3,1},... | collective-permute-start | bytes 442376 | tf_op jit(solution)/shard_map/ppermute | solution.py:584
  32.5 0.0 collective-permute-done.2.refs_2_
  32.5 0.0 collective-permute-done.3.refs_3_
  32.5 1.6 %land.1 = (bf16[24,2,144,256]{3,2,1,0:T(8,128)(2,1)}, s32[4]{0:T(128)S(1)}, s32[4]{0:T(128)S(1)}, bf16[4,2,32,256]{3,2,1,0:T(8,128)(2,1)S(1)}) custom-call(bf16[2,144,256]{2,1,0:T(8,128)(2,1)S(1)} %collective-permute-done.refs_0_, bf16[2,144,256]{2,1,0:T(8,128)(2,1)S(1)} %collective-permute-done.1.refs_1_, ...), custom_call_target="tpu_custom_call", output_to_operand_aliasing={{0}: (4, {})} | custom-call | flops 68719476736 | bytes 268435456 | tf_op jit(solution)/shard_map/land/pallas_call | solution.py:406
  34.1 1.8 %all-to-all-done.small_ref.refs_3_ = bf16[8,48,128]{2,1,0:T(8,128)(2,1)S(1)} async-done(((bf16[8,48,128]{2,1,0:T(8,128)(2,1)}), bf16[8,48,128]{2,1,0:T(8,128)(2,1)S(1)}, u32[]{:S(2)}, u32[]{:S(2)}) %all-to-all-start) | async-done | bytes 98336 | tf_op jit(solution)/shard_map/all_to_all | solution.py:604
  35.9 2.0 %settle.1 = (bf16[2,24,2048]{2,1,0:T(8,128)(2,1)}, bf16[24,2,144,256]{3,2,1,0:T(8,128)(2,1)}) custom-call(s32[4]{0:T(128)S(1)} %get-tuple-element.35.slot_ref, s32[4]{0:T(128)S(1)} %get-tuple-element.36.length_ref, bf16[768,128]{1,0:T(8,128)(2,1)S(1)} %copy-done, ...), custom_call_target="tpu_custom_call", output_to_operand_aliasing={{1}: (5, {})} | custom-call | flops 1 | bytes 1 | tf_op jit(solution)/shard_map/settle/pallas_call | solution.py:502
  38.0 0.0 collective-permute-done.5.refs_0_
  38.0 1.1 %collective-permute-done.6.refs_1_ = bf16[2,144,256]{2,1,0:T(8,128)(2,1)S(1)} collective-permute-done((bf16[2,144,256]{2,1,0:T(8,128)(2,1)}, bf16[2,144,256]{2,1,0:T(8,128)(2,1)S(1)}, u32[]{:S(2)}, u32[]{:S(2)}) %collective-permute-start.6) | collective-permute-done | bytes 147488 | tf_op jit(solution)/shard_map/ppermute | solution.py:584
  39.1 0.0 collective-permute-done.7.refs_2_
  39.1 1.0 %finish.1 = bf16[24,2,144,256]{3,2,1,0:T(8,128)(2,1)} custom-call(bf16[2,144,256]{2,1,0:T(8,128)(2,1)S(1)} %collective-permute-done.5.refs_0_, bf16[2,144,256]{2,1,0:T(8,128)(2,1)S(1)} %collective-permute-done.6.refs_1_, bf16[2,144,256]{2,1,0:T(8,128)(2,1)S(1)} %collective-permute-done.7.refs_2_, ...), custom_call_target="tpu_custom_call", output_to_operand_aliasing={{}: (4, {})} | custom-call | flops 1 | bytes 1 | tf_op jit(solution)/shard_map/finish/pallas_call | solution.py:557
  (3 shorter events, 0.0 us)
Async XLA Ops:
  6.5 9.1 %collective-permute-start.4 = (f32[48,512]{1,0:T(8,128)}, f32[48,512]{1,0:T(8,128)S(1)}, u32[]{:S(2)}, u32[]{:S(2)}) collective-permute-start(f32[48,512]{1,0:T(8,128)} %get-tuple-element.30), channel_id=1, source_target_pairs={{0,1},{1,0},{2,3},{3,2},{4,5},{5,4},{6,7},{7,6},{8,9},{9,8},{10,11... | collective-permute-start | bytes 294920 | tf_op jit(solution)/shard_map/ppermute | solution.py:590
  7.0 24.9 %collective-permute-start = (bf16[2,144,256]{2,1,0:T(8,128)(2,1)}, bf16[2,144,256]{2,1,0:T(8,128)(2,1)S(1)}, u32[]{:S(2)}, u32[]{:S(2)}) collective-permute-start(bf16[2,144,256]{2,1,0:T(8,128)(2,1)} %get-tuple-element.24), channel_id=1, source_target_pairs={{0,8},{2,10},{4,12},{6,14},{8,0},{10,2},{12,4},{14,6},{1,9},{3,11}... | collective-permute-start | bytes 442376 | tf_op jit(solution)/shard_map/ppermute | solution.py:584
  10.6 21.2 %collective-permute-start.1 = (bf16[2,144,256]{2,1,0:T(8,128)(2,1)}, bf16[2,144,256]{2,1,0:T(8,128)(2,1)S(1)}, u32[]{:S(2)}, u32[]{:S(2)}) collective-permute-start(bf16[2,144,256]{2,1,0:T(8,128)(2,1)} %get-tuple-element.25), channel_id=1, source_target_pairs={{0,10},{2,8},{4,14},{6,12},{8,2},{10,0},{12,6},{14,4},{1,11},{3,9}... | collective-permute-start | bytes 442376 | tf_op jit(solution)/shard_map/ppermute | solution.py:584
  11.9 20.5 %collective-permute-start.2 = (bf16[2,144,256]{2,1,0:T(8,128)(2,1)}, bf16[2,144,256]{2,1,0:T(8,128)(2,1)S(1)}, u32[]{:S(2)}, u32[]{:S(2)}) collective-permute-start(bf16[2,144,256]{2,1,0:T(8,128)(2,1)} %get-tuple-element.26), channel_id=1, source_target_pairs={{0,12},{2,14},{4,8},{6,10},{8,4},{10,6},{12,0},{14,2},{1,13},{3,15... | collective-permute-start | bytes 442376 | tf_op jit(solution)/shard_map/ppermute | solution.py:584
  15.5 16.9 %collective-permute-start.3 = (bf16[2,144,256]{2,1,0:T(8,128)(2,1)}, bf16[2,144,256]{2,1,0:T(8,128)(2,1)S(1)}, u32[]{:S(2)}, u32[]{:S(2)}) collective-permute-start(bf16[2,144,256]{2,1,0:T(8,128)(2,1)} %get-tuple-element.27), channel_id=1, source_target_pairs={{0,6},{2,4},{4,2},{6,0},{8,14},{10,12},{12,10},{14,8},{1,7},{3,5},... | collective-permute-start | bytes 442376 | tf_op jit(solution)/shard_map/ppermute | solution.py:584
  15.5 0.6 %copy-start.1 = (f32[48,512]{1,0:T(8,128)}, f32[48,512]{1,0:T(8,128)S(1)}, u32[]{:S(2)}) copy-start(f32[48,512]{1,0:T(8,128)S(1)} %collective-permute-done.4.got_ref) | copy-start | bytes 294916
  22.9 13.0 %all-to-all-start = ((bf16[8,48,128]{2,1,0:T(8,128)(2,1)}), bf16[8,48,128]{2,1,0:T(8,128)(2,1)S(1)}, u32[]{:S(2)}, u32[]{:S(2)}) async-start(bf16[8,48,128]{2,1,0:T(8,128)(2,1)} %get-tuple-element.38), calls=%async_computation | async-start | bytes 196608 | tf_op jit(solution)/shard_map/all_to_all | solution.py:604
  27.1 10.9 %collective-permute-start.5 = (bf16[2,144,256]{2,1,0:T(8,128)(2,1)}, bf16[2,144,256]{2,1,0:T(8,128)(2,1)S(1)}, u32[]{:S(2)}, u32[]{:S(2)}) collective-permute-start(bf16[2,144,256]{2,1,0:T(8,128)(2,1)} %get-tuple-element.42), channel_id=1, source_target_pairs={{0,14},{2,12},{4,10},{6,8},{8,6},{10,4},{12,2},{14,0},{1,15},{3,13... | collective-permute-start | bytes 442376 | tf_op jit(solution)/shard_map/ppermute | solution.py:584
  31.8 7.3 %collective-permute-start.6 = (bf16[2,144,256]{2,1,0:T(8,128)(2,1)}, bf16[2,144,256]{2,1,0:T(8,128)(2,1)S(1)}, u32[]{:S(2)}, u32[]{:S(2)}) collective-permute-start(bf16[2,144,256]{2,1,0:T(8,128)(2,1)} %get-tuple-element.43), channel_id=1, source_target_pairs={{0,4},{2,6},{4,0},{6,2},{8,12},{10,14},{12,8},{14,10},{1,5},{3,7},... | collective-permute-start | bytes 442376 | tf_op jit(solution)/shard_map/ppermute | solution.py:584
  31.9 7.3 %collective-permute-start.7 = (bf16[2,144,256]{2,1,0:T(8,128)(2,1)}, bf16[2,144,256]{2,1,0:T(8,128)(2,1)S(1)}, u32[]{:S(2)}, u32[]{:S(2)}) collective-permute-start(bf16[2,144,256]{2,1,0:T(8,128)(2,1)} %get-tuple-element.44), channel_id=1, source_target_pairs={{0,2},{2,0},{4,6},{6,4},{8,10},{10,8},{12,14},{14,12},{1,3},{3,1},... | collective-permute-start | bytes 442376 | tf_op jit(solution)/shard_map/ppermute | solution.py:584
  32.5 3.5 %copy-start = (bf16[768,128]{1,0:T(8,128)(2,1)S(1)}, bf16[768,128]{1,0:T(8,128)(2,1)}, u32[]{:S(2)}) copy-start(bf16[768,128]{1,0:T(8,128)(2,1)} %get-tuple-element.37.mixed_ref) | copy-start | bytes 589828

commit v10 on v9

--- a/solution.py
+++ b/solution.py
@@ -37,22 +37,84 @@
     return index ^ shift if count & (count - 1) == 0 else (index + count - shift) % count
 
 
-def prepare_kernel(
-    count, chunks, dest_ref, length_ref, hidden_ref, kv_ref, key_ref, value_ref, *refs
-):
-    block_refs = refs[: count - 1]
-    pick_ref, own_ref, other_ref, blocks, hidden_held, held, total = refs[count - 1 : count + 6]
-    in_sems, out_sems, hidden_sem, weight_sems = refs[count + 6 :]
+def pack_kernel(count, early, dest_ref, length_ref, kv_ref, *refs):
+    block_refs = refs[: len(early)]
+    pick_ref, blocks, in_sems, out_sems = refs[len(early) :]
     rows = dest_ref.shape[0]
     capacity, lanes = kv_ref.shape[2:]
     me = lax.axis_index("inst")
-    shifts = range(1, count)
-
+    for peer in range(count):
+        pick_ref[peer] = 0
+    for row in range(rows):
+        pick_ref[quotient(dest_ref[row], rows, rows * count)] = row
+    fetches, stores = [], []
+    for piece, shift in enumerate(early):
+        row = pick_ref[peer_to(me, shift, count)]
+        fetches.append(
+            pltpu.make_async_copy(kv_ref.at[row], blocks.at[piece], in_sems.at[piece])
+        )
+        fetches[-1].start()
+    tile = (TILE, lanes)
+    last = lax.broadcasted_iota(jnp.int32, tile, 0) == TILE - 1
+    first_lanes = lax.broadcasted_iota(jnp.int32, tile, 1) < HD
+    for piece, shift in enumerate(early):
+        peer = peer_to(me, shift, count)
+        row = pick_ref[peer]
+        slot = dest_ref[row] - peer * rows
+        slot = jnp.where((slot >= 0) & (slot < rows), slot, -1)
+        facts = jnp.where(first_lanes, slot, length_ref[row]).astype(jnp.float32)
+        fetches[piece].wait()
+        end = blocks[piece, 0, capacity - TILE :, :].astype(jnp.float32)
+        blocks[piece, 0, capacity - TILE :, :] = jnp.where(last, facts, end).astype(jnp.bfloat16)
+        stores.append(
+            pltpu.make_async_copy(blocks.at[piece], block_refs[piece], out_sems.at[piece])
+        )
+        stores[-1].start()
+    for copy in stores:
+        copy.wait()
+
+
+def pack(kv_cache, destination, lengths, count, early):
+    shape = kv_cache.shape[1:]
+    smem = pl.BlockSpec(memory_space=pltpu.SMEM)
+    hbm = pl.BlockSpec(memory_space=pl.ANY)
+    outs = pl.pallas_call(
+        functools.partial(pack_kernel, count, early),
+        out_shape=[jax.ShapeDtypeStruct(shape, kv_cache.dtype)] * len(early)
+        + [jax.ShapeDtypeStruct((count,), jnp.int32)],
+        in_specs=[smem, smem, hbm],
+        out_specs=[hbm] * len(early) + [smem],
+        scratch_shapes=[
+            pltpu.VMEM((len(early),) + shape, kv_cache.dtype),
+            pltpu.SemaphoreType.DMA((len(early),)),
+            pltpu.SemaphoreType.DMA((len(early),)),
+        ],
+        compiler_params=pltpu.CompilerParams(vmem_limit_bytes=VMEM_LIMIT),
+        cost_estimate=LIGHT,
+        name="pack",
+    )(destination, lengths, kv_cache)
+    return outs[:-1], outs[-1]
+
+
+def project_kernel(
+    chunks,
+    _,
+    hidden_ref,
+    key_ref,
+    value_ref,
+    own_ref,
+    other_ref,
+    hidden_held,
+    held,
+    total,
+    hidden_sem,
+    weight_sems,
+):
+    steps, rows, depth = hidden_ref.shape
+    width = key_ref.shape[1]
+    part = depth // chunks
     hidden_copy = pltpu.make_async_copy(hidden_ref, hidden_held, hidden_sem)
     hidden_copy.start()
-    steps, _, depth = hidden_ref.shape
-    width = key_ref.shape[1]
-    part = depth // chunks
     weights = []
     for chunk in range(chunks):
         span = pl.ds(chunk * part, part)
@@ -63,38 +125,6 @@
                 )
             )
             weights[-1].start()
-
-    for peer in range(count):
-        pick_ref[peer] = 0
-    for row in range(rows):
-        pick_ref[quotient(dest_ref[row], rows, rows * count)] = row
-    fetches, stores = {}, {}
-    for shift in shifts:
-        row = pick_ref[peer_to(me, shift, count)]
-        fetches[shift] = pltpu.make_async_copy(
-            kv_ref.at[row], blocks.at[shift - 1], in_sems.at[shift - 1]
-        )
-        fetches[shift].start()
-
-    tile = (TILE, lanes)
-    last = lax.broadcasted_iota(jnp.int32, tile, 0) == TILE - 1
-    first_lanes = lax.broadcasted_iota(jnp.int32, tile, 1) < HD
-    for shift in shifts:
-        peer = peer_to(me, shift, count)
-        row = pick_ref[peer]
-        slot = dest_ref[row] - peer * rows
-        slot = jnp.where((slot >= 0) & (slot < rows), slot, -1)
-        facts = jnp.where(first_lanes, slot, length_ref[row]).astype(jnp.float32)
-        fetches[shift].wait()
-        end = blocks[shift - 1, 0, capacity - TILE :, :].astype(jnp.float32)
-        blocks[shift - 1, 0, capacity - TILE :, :] = jnp.where(last, facts, end).astype(
-            jnp.bfloat16
-        )
-        stores[shift] = pltpu.make_async_copy(
-            blocks.at[shift - 1], block_refs[shift - 1], out_sems.at[shift - 1]
-        )
-        stores[shift].start()
-
     hidden_copy.wait()
     hidden = hidden_held[...].reshape(steps * rows, depth)
     sums = [None, None]
@@ -115,40 +145,31 @@
         at = pl.multiple_of(place * half, half)
         ref[:, :half] = total[:, pl.ds(at, half)]
         ref[:, half:] = total[:, pl.ds(pl.multiple_of(width + at, half), half)]
-    for shift in shifts:
-        stores[shift].wait()
-
-
-def prepare(destination, lengths, hidden_new, kv_cache, key_weight, value_weight, count):
+
+
+def project(hidden_new, key_weight, value_weight, pick):
     steps, rows, depth = hidden_new.shape
     width = key_weight.shape[1]
     chunks = 5
-    shape = kv_cache.shape[1:]
     part = jax.ShapeDtypeStruct((steps * rows, width), jnp.float32)
-    smem = pl.BlockSpec(memory_space=pltpu.SMEM)
     vmem = pl.BlockSpec(memory_space=pltpu.VMEM)
     hbm = pl.BlockSpec(memory_space=pl.ANY)
-    outs = pl.pallas_call(
-        functools.partial(prepare_kernel, count, chunks),
-        out_shape=[jax.ShapeDtypeStruct(shape, kv_cache.dtype)] * (count - 1)
-        + [jax.ShapeDtypeStruct((count,), jnp.int32), part, part],
-        in_specs=[smem, smem, hbm, hbm, hbm, hbm],
-        out_specs=[hbm] * (count - 1) + [smem, vmem, vmem],
+    return pl.pallas_call(
+        functools.partial(project_kernel, chunks),
+        out_shape=[part, part],
+        in_specs=[hbm, hbm, hbm, hbm],
+        out_specs=[vmem, vmem],
         scratch_shapes=[
-            pltpu.VMEM((count - 1,) + shape, kv_cache.dtype),
             pltpu.VMEM(hidden_new.shape, hidden_new.dtype),
             pltpu.VMEM((2, depth, width), key_weight.dtype),
             pltpu.VMEM((steps * rows, 2 * width), jnp.float32),
-            pltpu.SemaphoreType.DMA((count - 1,)),
-            pltpu.SemaphoreType.DMA((count - 1,)),
             pltpu.SemaphoreType.DMA,
             pltpu.SemaphoreType.DMA((chunks, 2)),
         ],
         compiler_params=pltpu.CompilerParams(vmem_limit_bytes=VMEM_LIMIT),
         cost_estimate=LIGHT,
-        name="prepare",
-    )(destination, lengths, hidden_new, kv_cache, key_weight, value_weight)
-    return outs[: count - 1], *outs[count - 1 :]
+        name="project",
+    )(pick, hidden_new, key_weight, value_weight)
 
 
 def rotation(length_ref, steps, rows):
@@ -175,6 +196,7 @@
 
 def attend_kernel(
     count,
+    late,
     block,
     length_ref,
     dest_ref,
@@ -186,8 +208,8 @@
     kv_ref,
     *refs,
 ):
-    late = (len(refs) - 7) // 2
-    moved_ref, mixed_ref, small_ref = refs[late : late + 3]
+    moved_ref, mixed_ref, small_ref = refs[:3]
+    late_refs = refs[3:-4]
     fresh, query_rows, query_columns, mixed = refs[-4:]
     part = pl.program_id(0)
     steps, rows, query_width = query_ref.shape
@@ -274,6 +296,14 @@
                     head * per_head : (head + 1) * per_head, head * HD : (head + 1) * HD
                 ]
 
+    me = lax.axis_index("inst")
+    for late_ref, shift in zip(late_refs, late):
+        item = pick_ref[peer_to(me, shift, count)] - part * block
+
+        @pl.when((item >= 0) & (item < block))
+        def _():
+            late_ref[...] = moved_ref[item]
+
     @pl.when(part == pl.num_programs(0) - 1)
     def _():
         mixed_ref[...] = mixed[...].astype(jnp.bfloat16)
@@ -289,49 +319,44 @@
                     news += [new[:, h * HD : (h + 1) * HD] for h in range(heads)]
             slot = dest_ref[row] - peer * rows
             slot = jnp.where((slot >= 0) & (slot < rows), slot, -1).astype(jnp.float32)
-            fill = small_ref.shape[1] - per_row - len(news)
-            news.append(jnp.full((fill, HD), slot))
+            news.append(jnp.full((1, HD), slot))
+            fill = small_ref.shape[1] - per_row - 2 * steps * heads - 1
+            news.append(jnp.full((fill, HD), length_ref[row].astype(jnp.float32)))
             small_ref[peer, per_row:, :] = jnp.concatenate(news, axis=0).astype(jnp.bfloat16)
 
 
-def attend(
-    kv_cache, queries, own, got, gain, lengths, destination, pick, late, count
-):
-    late_shapes = [jax.ShapeDtypeStruct(x.shape, x.dtype) for x in late]
+def attend(kv_cache, queries, own, got, gain, lengths, destination, pick, count, late):
     steps, rows, query_width = queries.shape
     capacity, lanes = kv_cache.shape[2:]
     heads = lanes // HD
     per_row = steps * query_width // HD
     block = 8
-    small_rows = per_row + -(-(2 * steps * heads + 1) // TILE) * TILE
+    small_rows = per_row + -(-(2 * steps * heads + 2) // TILE) * TILE
     small = jax.ShapeDtypeStruct((count, small_rows, HD), jnp.bfloat16)
     smem = pl.BlockSpec(memory_space=pltpu.SMEM)
     vmem = pl.BlockSpec(memory_space=pltpu.VMEM)
-    hbm = pl.BlockSpec(memory_space=pl.ANY)
     cache_block = pl.BlockSpec((block, 2, capacity, lanes), lambda i: (i, 0, 0, 0))
-    outs = pl.pallas_call(
-        functools.partial(attend_kernel, count, block),
+    return pl.pallas_call(
+        functools.partial(attend_kernel, count, late, block),
         grid=(rows // block,),
         out_shape=[
             jax.ShapeDtypeStruct(kv_cache.shape, kv_cache.dtype),
             jax.ShapeDtypeStruct((rows * per_row, HD), jnp.bfloat16),
             small,
         ]
-        + late_shapes,
-        in_specs=[smem, smem, smem, vmem, vmem, vmem, vmem, cache_block] + [hbm] * len(late),
-        out_specs=[cache_block, vmem, vmem] + [hbm] * len(late),
+        + [jax.ShapeDtypeStruct(kv_cache.shape[1:], kv_cache.dtype)] * len(late),
+        in_specs=[smem, smem, smem, vmem, vmem, vmem, vmem, cache_block],
+        out_specs=[cache_block, vmem, vmem] + [vmem] * len(late),
         scratch_shapes=[
             pltpu.VMEM((2, steps * rows, lanes), jnp.float32),
             pltpu.VMEM((rows * per_row, HD), jnp.float32),
             pltpu.VMEM((rows * per_row // HD, HD, HD), jnp.float32),
             pltpu.VMEM((rows * per_row, HD), jnp.float32),
         ],
-        input_output_aliases={8 + i: 3 + i for i in range(len(late))},
         compiler_params=pltpu.CompilerParams(vmem_limit_bytes=ATTEND_LIMIT),
-        cost_estimate=HEAVY,
+        cost_estimate=LIGHT,
         name="attend",
-    )(lengths, destination, pick, own, got, gain, queries, kv_cache, *late)
-    return outs[0], outs[1], outs[2], outs[3:]
+    )(lengths, destination, pick, own, got, gain, queries, kv_cache)
 
 
 def read_facts(block):
@@ -371,51 +396,47 @@
 
 def land_kernel(pieces, *refs):
     blocks = refs[:pieces]
-    _, out_ref, slot_ref, length_ref, window_ref, buffer, sems = refs[pieces:]
+    _, out_ref, window_ref, buffer, sems, slots = refs[pieces:]
     capacity = buffer.shape[2]
 
     def store(piece):
-        slot = jnp.maximum(slot_ref[piece], 0)
+        slot = jnp.maximum(slots[piece], 0)
         return pltpu.make_async_copy(buffer.at[piece], out_ref.at[slot], sems.at[piece])
 
-    for piece, block in enumerate(blocks):
-        slot_ref[piece], length_ref[piece] = read_facts(block)
-    for piece, block in enumerate(blocks):
-
-        @pl.when(slot_ref[piece] >= 0)
+    facts = [read_facts(block) for block in blocks]
+    for piece, (slot, length) in enumerate(facts):
+        slots[piece] = slot
+
+        @pl.when(slot >= 0)
         def _():
-            length = length_ref[piece]
-            clean(block, length, buffer.at[piece])
+            clean(blocks[piece], length, buffer.at[piece])
             store(piece).start()
             start = window_start(length, capacity)
             window_ref[piece] = buffer[piece, :, pl.ds(start, WINDOW), :]
 
     for piece in range(pieces):
 
-        @pl.when(slot_ref[piece] >= 0)
+        @pl.when(slots[piece] >= 0)
         def _():
             store(piece).wait()
 
 
 def land(got, moved):
     pieces = len(got)
-    smem = pl.BlockSpec(memory_space=pltpu.SMEM)
     vmem = pl.BlockSpec(memory_space=pltpu.VMEM)
     hbm = pl.BlockSpec(memory_space=pl.ANY)
-    scalars = jax.ShapeDtypeStruct((pieces,), jnp.int32)
     return pl.pallas_call(
         functools.partial(land_kernel, pieces),
         out_shape=[
             jax.ShapeDtypeStruct(moved.shape, moved.dtype),
-            scalars,
-            scalars,
             jax.ShapeDtypeStruct((pieces, 2, WINDOW, moved.shape[3]), moved.dtype),
         ],
         in_specs=[vmem] * pieces + [hbm],
-        out_specs=[hbm, smem, smem, vmem],
+        out_specs=[hbm, vmem],
         scratch_shapes=[
             pltpu.VMEM((pieces,) + moved.shape[1:], moved.dtype),
             pltpu.SemaphoreType.DMA((pieces,)),
+            pltpu.SMEM((pieces,), jnp.int32),
         ],
         input_output_aliases={pieces: 0},
         compiler_params=pltpu.CompilerParams(vmem_limit_bytes=SMALL_LIMIT),
@@ -424,12 +445,15 @@
     )(*got, moved)
 
 
+def read_small(small_ref, peer, per_row, line):
+    rows = small_ref[peer, per_row:, :].astype(jnp.float32)
+    return jnp.max(rows[line : line + 1]).astype(jnp.int32)
+
+
 def settle_kernel(
     count,
     early,
     group,
-    slot_ref,
-    length_ref,
     mixed_ref,
     small_ref,
     window_ref,
@@ -439,47 +463,46 @@
     mixed,
     windows,
     sems,
+    slots,
+    lengths,
 ):
     steps, rows, query_width = out_ref.shape
     per_row = steps * query_width // HD
     capacity, lanes = moved_ref.shape[2:]
-    heads = lanes // HD
+    line = 2 * steps * (lanes // HD)
     me = lax.axis_index("inst")
-    pieces = len(early)
 
     def store(piece):
-        slot = jnp.maximum(slot_ref[piece], 0)
-        start = window_start(length_ref[piece], capacity)
+        slot = jnp.maximum(slots[early[piece]], 0)
+        start = window_start(lengths[early[piece]], capacity)
         return pltpu.make_async_copy(
             windows.at[piece], moved_ref.at[slot, :, pl.ds(start, WINDOW), :], sems.at[piece]
         )
 
-    def take(slot, peer):
-        mixed[pl.ds(pl.multiple_of(slot * per_row, per_row), per_row), :] = small_ref[
-            peer, :per_row, :
-        ].astype(jnp.float32)
-
-    for piece in range(pieces):
-
-        @pl.when(slot_ref[piece] >= 0)
+    for shift in range(1, count):
+        peer = peer_from(me, shift, count)
+        slots[shift] = read_small(small_ref, peer, per_row, line)
+        lengths[shift] = read_small(small_ref, peer, per_row, line + 1)
+
+    for piece, shift in enumerate(early):
+
+        @pl.when(slots[shift] >= 0)
         def _():
-            length = length_ref[piece]
-            peer = peer_from(me, early[piece], count)
+            peer = peer_from(me, shift, count)
             news = small_ref[peer, per_row:, :].astype(jnp.float32)
-            ahead = length - window_start(length, capacity)
+            ahead = lengths[shift] - window_start(lengths[shift], capacity)
             insert(window_ref.at[piece], news, ahead, steps, windows.at[piece])
             store(piece).start()
 
     mixed[...] = mixed_ref[...].astype(jnp.float32)
     for shift in range(1, count):
-        peer = peer_from(me, shift, count)
-        if shift in early:
-            slot = slot_ref[early.index(shift)]
-        else:
-            line = 2 * steps * heads
-            facts = small_ref[peer, per_row:, :].astype(jnp.float32)[line : line + 1]
-            slot = jnp.max(facts).astype(jnp.int32)
-        pl.when(slot >= 0)(functools.partial(take, slot, peer))
+
+        @pl.when(slots[shift] >= 0)
+        def _():
+            mixed[pl.ds(pl.multiple_of(slots[shift] * per_row, per_row), per_row), :] = small_ref[
+                peer_from(me, shift, count), :per_row, :
+            ].astype(jnp.float32)
+
     for step in range(steps):
         for chunk in range(query_width // HD):
             head, member = chunk // group, chunk % group
@@ -488,15 +511,14 @@
                 pl.ds(at, rows, stride=per_row), :
             ].astype(jnp.bfloat16)
 
-    for piece in range(pieces):
-
-        @pl.when(slot_ref[piece] >= 0)
+    for piece, shift in enumerate(early):
+
+        @pl.when(slots[shift] >= 0)
         def _():
             store(piece).wait()
 
 
-def settle(slots, lengths, mixed, small, windows, moved, shape, group, count, early):
-    smem = pl.BlockSpec(memory_space=pltpu.SMEM)
+def settle(mixed, small, windows, moved, shape, group, count, early):
     vmem = pl.BlockSpec(memory_space=pltpu.VMEM)
     hbm = pl.BlockSpec(memory_space=pl.ANY)
     return pl.pallas_call(
@@ -505,50 +527,40 @@
             jax.ShapeDtypeStruct(shape, jnp.bfloat16),
             jax.ShapeDtypeStruct(moved.shape, moved.dtype),
         ],
-        in_specs=[smem, smem, vmem, vmem, vmem, hbm],
+        in_specs=[vmem, vmem, vmem, hbm],
         out_specs=[vmem, hbm],
         scratch_shapes=[
             pltpu.VMEM(mixed.shape, jnp.float32),
             pltpu.VMEM(windows.shape, windows.dtype),
-            pltpu.SemaphoreType.DMA((slots.shape[0],)),
-        ],
-        input_output_aliases={5: 1},
+            pltpu.SemaphoreType.DMA((len(early),)),
+            pltpu.SMEM((count,), jnp.int32),
+            pltpu.SMEM((count,), jnp.int32),
+        ],
+        input_output_aliases={3: 1},
         compiler_params=pltpu.CompilerParams(vmem_limit_bytes=SMALL_LIMIT),
         cost_estimate=LIGHT,
         name="settle",
-    )(slots, lengths, mixed, small, windows, moved)
+    )(mixed, small, windows, moved)
 
 
 def finish_kernel(count, late, steps, *refs):
     blocks = refs[: len(late)]
-    small_ref, _, out_ref, buffer, sems, slot_ref = refs[len(late) :]
-    capacity, lanes = buffer.shape[2:]
-    height = small_ref.shape[1]
-    tail = height - -(-(2 * steps * (lanes // HD) + 1) // TILE) * TILE
+    small_ref, _, out_ref, sems, slots = refs[len(late) :]
+    line = 2 * steps * (out_ref.shape[3] // HD)
+    facts = -(-(line + 2) // TILE) * TILE
     me = lax.axis_index("inst")
 
     def store(piece):
-        slot = jnp.maximum(slot_ref[piece], 0)
-        return pltpu.make_async_copy(buffer.at[piece], out_ref.at[slot], sems.at[piece])
-
-    facts = [read_facts(block) for block in blocks]
-    for piece, (slot, length) in enumerate(facts):
-        slot_ref[piece] = slot
-
-        @pl.when(slot >= 0)
-        def _():
-            clean(blocks[piece], length, buffer.at[piece])
-            start = window_start(length, capacity)
-            window = buffer.at[piece, :, pl.ds(start, WINDOW), :]
-            news = small_ref[peer_from(me, late[piece], count), tail:, :].astype(jnp.float32)
-            insert(window, news, length - start, steps, window)
-            store(piece).start()
-
+        slot = jnp.maximum(slots[piece], 0)
+        return pltpu.make_async_copy(blocks[piece], out_ref.at[slot], sems.at[piece])
+
+    for piece, shift in enumerate(late):
+        peer = peer_from(me, shift, count)
+        slots[piece] = read_small(small_ref, peer, small_ref.shape[1] - facts, line)
     for piece in range(len(late)):
-
-        @pl.when(slot_ref[piece] >= 0)
-        def _():
-            store(piece).wait()
+        pl.when(slots[piece] >= 0)(store(piece).start)
+    for piece in range(len(late)):
+        pl.when(slots[piece] >= 0)(store(piece).wait)
 
 
 def finish(got, small, moved, steps, count, late):
@@ -560,7 +572,6 @@
         in_specs=[vmem] * len(got) + [vmem, hbm],
         out_specs=hbm,
         scratch_shapes=[
-            pltpu.VMEM((len(got),) + moved.shape[1:], moved.dtype),
             pltpu.SemaphoreType.DMA((len(got),)),
             pltpu.SMEM((len(got),), jnp.int32),
         ],
@@ -583,29 +594,17 @@
         pairs = [(i, peer_to(i, shift, count)) for i in range(count)]
         return lax.ppermute(block, "inst", pairs)
 
-    blocks, pick, own, other = prepare(
-        destination, lengths, hidden_new, kv_cache, key_weight, value_weight, count
-    )
-    early_got = [send(blocks[shift - 1], shift) for shift in early]
+    blocks, pick = pack(kv_cache, destination, lengths, count, early)
+    early_got = [send(block, shift) for block, shift in zip(blocks, early)]
+    own, other = project(hidden_new, key_weight, value_weight, pick)
     got = lax.ppermute(other, "tp", [(0, 1), (1, 0)])
-    moved, mixed, small, late_blocks = attend(
-        kv_cache,
-        queries,
-        own,
-        got,
-        key_gain[None, :],
-        lengths,
-        destination,
-        pick,
-        [blocks[shift - 1] for shift in late],
-        count,
+    moved, mixed, small, *late_blocks = attend(
+        kv_cache, queries, own, got, key_gain[None, :], lengths, destination, pick, count, late
     )
     late_got = [send(block, shift) for block, shift in zip(late_blocks, late)]
     small_got = lax.all_to_all(small, "inst", 0, 0, tiled=True)
-    moved, slots, arrived, windows = land(early_got, moved)
-    attended, moved = settle(
-        slots, arrived, mixed, small_got, windows, moved, queries.shape, group, count, early
-    )
+    moved, windows = land(early_got, moved)
+    attended, moved = settle(mixed, small_got, windows, moved, queries.shape, group, count, early)
     return attended, finish(late_got, small_got, moved, steps, count, late)
 
 

time: 40.6 us -> 44.6 us (1.099)
  waiting for transfers between devices: 2.97 us -> 6.41 us
  Pallas kernels: 17.2 us -> 17.9 us
    pallas_call x2 -> x3, Pallas kernels: 12.6 us -> 14.4 us  [the longest x1 6.92 us: attend(): pl.pallas_call(functools.partial(attend_kernel, count, late, block), grid...]
    ppermute x1, waiting for transfers between devices: 0.01 us -> 1.5 us  [local(): got = lax.ppermute(other, 'tp', [(0, 1), (1, 0)])]
    all_to_all x1, waiting for transfers between devices: 1.82 us -> 3.16 us  [local(): small_got = lax.all_to_all(small, 'inst', 0, 0, tiled=True)]
    pallas_call x1, Pallas kernels: 1.62 us -> 1.02 us  [land(): pl.pallas_call(functools.partial(land_kernel, pieces), out_shape=[jax.Sha...]
    ppermute x7, waiting for transfers between devices: 1.15 us -> 1.75 us  [send(): return lax.ppermute(block, 'inst', pairs)]
    pallas_call x1, Pallas kernels: 2.03 us -> 1.57 us  [settle(): pl.pallas_call(functools.partial(settle_kernel, count, early, group), out...]
  transfers between devices with their start and end apart: 9 -> 9, of which waited for: 2 -> 5; matrix products, arithmetic and copies ran while one was open for 0% -> 0% of each run, Pallas kernels for 26% -> 31%
where the time goes in v10:
time: 44.6 us; the launch traced here: 44.3 us
  starting transfers between devices  18.6 us (42%)
  Pallas kernels  17.9 us (40%)
  waiting for transfers between devices  6.41 us (14%)
  between operations  0.69 us (2%)
  local copies, waits for them, and re-layouts  0.63 us (1%)
    ppermute x7, starting transfers between devices, send(): return lax.ppermute(block, 'inst', pairs)  14.3 us
    pallas_call x1, Pallas kernels, attend(): pl.pallas_call(functools.partial(attend_kernel, count, late, block), grid...  6.92 us
    pallas_call x1, Pallas kernels, project(): pl.pallas_call(functools.partial(project_kernel, chunks), out_shape=[part...  4.42 us
    all_to_all x1, starting transfers between devices, local(): small_got = lax.all_to_all(small, 'inst', 0, 0, tiled=True)  4.22 us
    all_to_all x1, waiting for transfers between devices, local(): small_got = lax.all_to_all(small, 'inst', 0, 0, tiled=True)  3.16 us
    pallas_call x1, Pallas kernels, pack(): pl.pallas_call(functools.partial(pack_kernel, count, early), out_shape=[j...  3.09 us
    ppermute x7, waiting for transfers between devices, send(): return lax.ppermute(block, 'inst', pairs)  1.75 us
    pallas_call x1, Pallas kernels, settle(): pl.pallas_call(functools.partial(settle_kernel, count, early, group), out...  1.57 us
  transfers between devices with their start and end apart: 9, of which 5 were waited for; matrix products, arithmetic and copies ran while one was open for 0% of the time, Pallas kernels for 31%

profile of v10, /device:TPU:0, one launch (start us, length us, event | category | flops | bytes accessed | tf_op | source)
XLA Modules:
  0.0 44.3 jit_solution(2984451730384201217)
XLA Ops:
  0.6 3.1 %pack.1 = (bf16[2,144,256]{2,1,0:T(8,128)(2,1)}, bf16[2,144,256]{2,1,0:T(8,128)(2,1)}, bf16[2,144,256]{2,1,0:T(8,128)(2,1)}, bf16[2,144,256]{2,1,0:T(8,128)(2,1)}, s32[8]{0:T(128)}) custom-call(s32[24]{0:T(128)} %dest_ref.3, s32[24]{0:T(128)} %length_ref.3, bf16[24,2,144,256]{3,2,1,0:T(8,128)(2,1)} %kv_ref.3), custom_call_target="tpu_custom_call" | custom-call | flops 1 | bytes 1 | tf_op jit(solution)/shard_map/pack/pallas_call | solution.py:81
  3.7 4.1 %collective-permute-start.1 = (bf16[2,144,256]{2,1,0:T(8,128)(2,1)}, bf16[2,144,256]{2,1,0:T(8,128)(2,1)S(1)}, u32[]{:S(2)}, u32[]{:S(2)}) collective-permute-start(bf16[2,144,256]{2,1,0:T(8,128)(2,1)} %get-tuple-element.24), channel_id=1, source_target_pairs={{0,8},{2,10},{4,12},{6,14},{8,0},{10,2},{12,4},{14,6},{1,9},{3,11}... | collective-permute-start | bytes 442376 | tf_op jit(solution)/shard_map/ppermute | solution.py:595
  7.8 1.3 %collective-permute-start.2 = (bf16[2,144,256]{2,1,0:T(8,128)(2,1)}, bf16[2,144,256]{2,1,0:T(8,128)(2,1)S(1)}, u32[]{:S(2)}, u32[]{:S(2)}) collective-permute-start(bf16[2,144,256]{2,1,0:T(8,128)(2,1)} %get-tuple-element.25), channel_id=1, source_target_pairs={{0,10},{2,8},{4,14},{6,12},{8,2},{10,0},{12,6},{14,4},{1,11},{3,9}... | collective-permute-start | bytes 442376 | tf_op jit(solution)/shard_map/ppermute | solution.py:595
  9.1 3.6 %collective-permute-start.3 = (bf16[2,144,256]{2,1,0:T(8,128)(2,1)}, bf16[2,144,256]{2,1,0:T(8,128)(2,1)S(1)}, u32[]{:S(2)}, u32[]{:S(2)}) collective-permute-start(bf16[2,144,256]{2,1,0:T(8,128)(2,1)} %get-tuple-element.26), channel_id=1, source_target_pairs={{0,12},{2,14},{4,8},{6,10},{8,4},{10,6},{12,0},{14,2},{1,13},{3,15... | collective-permute-start | bytes 442376 | tf_op jit(solution)/shard_map/ppermute | solution.py:595
  12.7 0.0 collective-permute-start.4
  12.7 4.4 %project.1 = (f32[48,512]{1,0:T(8,128)}, f32[48,512]{1,0:T(8,128)}) custom-call(s32[8]{0:T(128)} %get-tuple-element.19._.pick_ref, bf16[2,24,2560]{2,1,0:T(8,128)(2,1)} %hidden_ref.1, bf16[2560,512]{1,0:T(8,128)(2,1)} %key_ref.1, bf16[2560,512]{1,0:T(8,128)(2,1)} %value_ref.1), custom_call_target="tpu_custom_call" | custom-call | flops 1 | bytes 1 | tf_op jit(solution)/shard_map/project/pallas_call | solution.py:157
  17.2 0.1 collective-permute-start
  17.2 1.5 %collective-permute-done.got_ref = f32[48,512]{1,0:T(8,128)S(1)} collective-permute-done((f32[48,512]{1,0:T(8,128)}, f32[48,512]{1,0:T(8,128)S(1)}, u32[]{:S(2)}, u32[]{:S(2)}) %collective-permute-start) | collective-permute-done | bytes 98336 | tf_op jit(solution)/shard_map/ppermute | solution.py:600
  18.7 0.6 %copy-done.1 = f32[48,512]{1,0:T(8,128)} copy-done((f32[48,512]{1,0:T(8,128)}, f32[48,512]{1,0:T(8,128)S(1)}, u32[]{:S(2)}) %copy-start.1) | copy-done | bytes 98328
  19.4 6.9 %attend.1 = (bf16[24,2,144,256]{3,2,1,0:T(8,128)(2,1)}, bf16[768,128]{1,0:T(8,128)(2,1)}, bf16[8,48,128]{2,1,0:T(8,128)(2,1)}, bf16[2,144,256]{2,1,0:T(8,128)(2,...) custom-call(s32[24]{0:T(128)} %length_ref.3, s32[24]{0:T(128)} %dest_ref.3, ...), custom_call_target="tpu_custom_call" | custom-call | flops 1 | bytes 1 | tf_op jit(solution)/shard_map/attend/pallas_call | solution.py:339
  26.3 4.2 %all-to-all-start = ((bf16[8,48,128]{2,1,0:T(8,128)(2,1)}), bf16[8,48,128]{2,1,0:T(8,128)(2,1)S(1)}, u32[]{:S(2)}, u32[]{:S(2)}) async-start(bf16[8,48,128]{2,1,0:T(8,128)(2,1)} %get-tuple-element.23), calls=%async_computation | async-start | bytes 196608 | tf_op jit(solution)/shard_map/all_to_all | solution.py:605
  30.5 4.7 %collective-permute-start.5 = (bf16[2,144,256]{2,1,0:T(8,128)(2,1)}, bf16[2,144,256]{2,1,0:T(8,128)(2,1)S(1)}, u32[]{:S(2)}, u32[]{:S(2)}) collective-permute-start(bf16[2,144,256]{2,1,0:T(8,128)(2,1)} %get-tuple-element.32), channel_id=1, source_target_pairs={{0,14},{2,12},{4,10},{6,8},{8,6},{10,4},{12,2},{14,0},{1,15},{3,13... | collective-permute-start | bytes 442376 | tf_op jit(solution)/shard_map/ppermute | solution.py:595
  35.2 0.0 collective-permute-done.1.refs_0_
  35.2 0.0 collective-permute-start.6
  35.2 0.0 collective-permute-done.2.refs_1_
  35.2 0.6 %collective-permute-start.7 = (bf16[2,144,256]{2,1,0:T(8,128)(2,1)}, bf16[2,144,256]{2,1,0:T(8,128)(2,1)S(1)}, u32[]{:S(2)}, u32[]{:S(2)}) collective-permute-start(bf16[2,144,256]{2,1,0:T(8,128)(2,1)} %get-tuple-element.34), channel_id=1, source_target_pairs={{0,2},{2,0},{4,6},{6,4},{8,10},{10,8},{12,14},{14,12},{1,3},{3,1},... | collective-permute-start | bytes 442376 | tf_op jit(solution)/shard_map/ppermute | solution.py:595
  35.9 0.0 collective-permute-done.3.refs_2_
  35.9 1.0 %land.1 = (bf16[24,2,144,256]{3,2,1,0:T(8,128)(2,1)}, bf16[4,2,32,256]{3,2,1,0:T(8,128)(2,1)S(1)}) custom-call(bf16[2,144,256]{2,1,0:T(8,128)(2,1)S(1)} %collective-permute-done.1.refs_0_, bf16[2,144,256]{2,1,0:T(8,128)(2,1)S(1)} %collective-permute-done.2.refs_1_, ...), custom_call_target="tpu_custom_call", output_to_operand_aliasing={{0}: (4, {})} | custom-call | flops 68719476736 | bytes 268435456 | tf_op jit(solution)/shard_map/land/pallas_call | solution.py:428
  36.9 3.2 %all-to-all-done.small_ref.refs_3_ = bf16[8,48,128]{2,1,0:T(8,128)(2,1)S(1)} async-done(((bf16[8,48,128]{2,1,0:T(8,128)(2,1)}), bf16[8,48,128]{2,1,0:T(8,128)(2,1)S(1)}, u32[]{:S(2)}, u32[]{:S(2)}) %all-to-all-start) | async-done | bytes 98336 | tf_op jit(solution)/shard_map/all_to_all | solution.py:605
  40.1 1.6 %settle.1 = (bf16[2,24,2048]{2,1,0:T(8,128)(2,1)}, bf16[24,2,144,256]{3,2,1,0:T(8,128)(2,1)}) custom-call(bf16[768,128]{1,0:T(8,128)(2,1)S(1)} %copy-done, bf16[8,48,128]{2,1,0:T(8,128)(2,1)S(1)} %all-to-all-done.small_ref.refs_3_, bf16[4,2,32,256]{3,2,1,0:T(8,128)(2,1)S(1)} %get-tuple-element.29.window_ref, ...), custom_call_target="tpu_custom_call", output_to_operand_aliasing={{1}: (3, {})} | custom-call | flops 1 | bytes 1 | tf_op jit(solution)/shard_map/settle/pallas_call | solution.py:524
  41.6 0.1 collective-permute-done.5.refs_0_
  41.7 1.5 %collective-permute-done.6.refs_1_ = bf16[2,144,256]{2,1,0:T(8,128)(2,1)S(1)} collective-permute-done((bf16[2,144,256]{2,1,0:T(8,128)(2,1)}, bf16[2,144,256]{2,1,0:T(8,128)(2,1)S(1)}, u32[]{:S(2)}, u32[]{:S(2)}) %collective-permute-start.6) | collective-permute-done | bytes 147488 | tf_op jit(solution)/shard_map/ppermute | solution.py:595
  43.2 0.1 collective-permute-done.7.refs_2_
  43.4 0.9 %finish.1 = bf16[24,2,144,256]{3,2,1,0:T(8,128)(2,1)} custom-call(bf16[2,144,256]{2,1,0:T(8,128)(2,1)S(1)} %collective-permute-done.5.refs_0_, bf16[2,144,256]{2,1,0:T(8,128)(2,1)S(1)} %collective-permute-done.6.refs_1_, bf16[2,144,256]{2,1,0:T(8,128)(2,1)S(1)} %collective-permute-done.7.refs_2_, ...), custom_call_target="tpu_custom_call", output_to_operand_aliasing={{}: (4, {})} | custom-call | flops 1 | bytes 1 | tf_op jit(solution)/shard_map/finish/pallas_call | solution.py:569
  (4 shorter events, 0.0 us)
Async XLA Ops:
  3.7 31.5 %collective-permute-start.1 = (bf16[2,144,256]{2,1,0:T(8,128)(2,1)}, bf16[2,144,256]{2,1,0:T(8,128)(2,1)S(1)}, u32[]{:S(2)}, u32[]{:S(2)}) collective-permute-start(bf16[2,144,256]{2,1,0:T(8,128)(2,1)} %get-tuple-element.24), channel_id=1, source_target_pairs={{0,8},{2,10},{4,12},{6,14},{8,0},{10,2},{12,4},{14,6},{1,9},{3,11}... | collective-permute-start | bytes 442376 | tf_op jit(solution)/shard_map/ppermute | solution.py:595
  7.8 27.4 %collective-permute-start.2 = (bf16[2,144,256]{2,1,0:T(8,128)(2,1)}, bf16[2,144,256]{2,1,0:T(8,128)(2,1)S(1)}, u32[]{:S(2)}, u32[]{:S(2)}) collective-permute-start(bf16[2,144,256]{2,1,0:T(8,128)(2,1)} %get-tuple-element.25), channel_id=1, source_target_pairs={{0,10},{2,8},{4,14},{6,12},{8,2},{10,0},{12,6},{14,4},{1,11},{3,9}... | collective-permute-start | bytes 442376 | tf_op jit(solution)/shard_map/ppermute | solution.py:595
  9.1 26.7 %collective-permute-start.3 = (bf16[2,144,256]{2,1,0:T(8,128)(2,1)}, bf16[2,144,256]{2,1,0:T(8,128)(2,1)S(1)}, u32[]{:S(2)}, u32[]{:S(2)}) collective-permute-start(bf16[2,144,256]{2,1,0:T(8,128)(2,1)} %get-tuple-element.26), channel_id=1, source_target_pairs={{0,12},{2,14},{4,8},{6,10},{8,4},{10,6},{12,0},{14,2},{1,13},{3,15... | collective-permute-start | bytes 442376 | tf_op jit(solution)/shard_map/ppermute | solution.py:595
  12.7 23.1 %collective-permute-start.4 = (bf16[2,144,256]{2,1,0:T(8,128)(2,1)}, bf16[2,144,256]{2,1,0:T(8,128)(2,1)S(1)}, u32[]{:S(2)}, u32[]{:S(2)}) collective-permute-start(bf16[2,144,256]{2,1,0:T(8,128)(2,1)} %get-tuple-element.27), channel_id=1, source_target_pairs={{0,6},{2,4},{4,2},{6,0},{8,14},{10,12},{12,10},{14,8},{1,7},{3,5},... | collective-permute-start | bytes 442376 | tf_op jit(solution)/shard_map/ppermute | solution.py:595
  17.2 1.6 %collective-permute-start = (f32[48,512]{1,0:T(8,128)}, f32[48,512]{1,0:T(8,128)S(1)}, u32[]{:S(2)}, u32[]{:S(2)}) collective-permute-start(f32[48,512]{1,0:T(8,128)} %get-tuple-element.21), channel_id=1, source_target_pairs={{0,1},{1,0},{2,3},{3,2},{4,5},{5,4},{6,7},{7,6},{8,9},{9,8},{10,11... | collective-permute-start | bytes 294920 | tf_op jit(solution)/shard_map/ppermute | solution.py:600
  18.7 0.6 %copy-start.1 = (f32[48,512]{1,0:T(8,128)}, f32[48,512]{1,0:T(8,128)S(1)}, u32[]{:S(2)}) copy-start(f32[48,512]{1,0:T(8,128)S(1)} %collective-permute-done.got_ref) | copy-start | bytes 294916
  26.3 13.8 %all-to-all-start = ((bf16[8,48,128]{2,1,0:T(8,128)(2,1)}), bf16[8,48,128]{2,1,0:T(8,128)(2,1)S(1)}, u32[]{:S(2)}, u32[]{:S(2)}) async-start(bf16[8,48,128]{2,1,0:T(8,128)(2,1)} %get-tuple-element.23), calls=%async_computation | async-start | bytes 196608 | tf_op jit(solution)/shard_map/all_to_all | solution.py:605
  30.5 11.2 %collective-permute-start.5 = (bf16[2,144,256]{2,1,0:T(8,128)(2,1)}, bf16[2,144,256]{2,1,0:T(8,128)(2,1)S(1)}, u32[]{:S(2)}, u32[]{:S(2)}) collective-permute-start(bf16[2,144,256]{2,1,0:T(8,128)(2,1)} %get-tuple-element.32), channel_id=1, source_target_pairs={{0,14},{2,12},{4,10},{6,8},{8,6},{10,4},{12,2},{14,0},{1,15},{3,13... | collective-permute-start | bytes 442376 | tf_op jit(solution)/shard_map/ppermute | solution.py:595
  35.2 8.0 %collective-permute-start.6 = (bf16[2,144,256]{2,1,0:T(8,128)(2,1)}, bf16[2,144,256]{2,1,0:T(8,128)(2,1)S(1)}, u32[]{:S(2)}, u32[]{:S(2)}) collective-permute-start(bf16[2,144,256]{2,1,0:T(8,128)(2,1)} %get-tuple-element.33), channel_id=1, source_target_pairs={{0,4},{2,6},{4,0},{6,2},{8,12},{10,14},{12,8},{14,10},{1,5},{3,7},... | collective-permute-start | bytes 442376 | tf_op jit(solution)/shard_map/ppermute | solution.py:595
  35.2 8.1 %collective-permute-start.7 = (bf16[2,144,256]{2,1,0:T(8,128)(2,1)}, bf16[2,144,256]{2,1,0:T(8,128)(2,1)S(1)}, u32[]{:S(2)}, u32[]{:S(2)}) collective-permute-start(bf16[2,144,256]{2,1,0:T(8,128)(2,1)} %get-tuple-element.34), channel_id=1, source_target_pairs={{0,2},{2,0},{4,6},{6,4},{8,10},{10,8},{12,14},{14,12},{1,3},{3,1},... | collective-permute-start | bytes 442376 | tf_op jit(solution)/shard_map/ppermute | solution.py:595
  35.9 4.2 %copy-start = (bf16[768,128]{1,0:T(8,128)(2,1)S(1)}, bf16[768,128]{1,0:T(8,128)(2,1)}, u32[]{:S(2)}) copy-start(bf16[768,128]{1,0:T(8,128)(2,1)} %get-tuple-element.22.mixed_ref) | copy-start | bytes 589828

commit v11 on v10

--- a/solution.py
+++ b/solution.py
@@ -11,8 +11,8 @@
 HD = 128
 ROPE_BASE = 1000000.0
 NORM_EPS = 1e-06
-VMEM_LIMIT = 62 * 1024 * 1024
-ATTEND_LIMIT = 56 * 1024 * 1024
+VMEM_LIMIT = 54 * 1024 * 1024
+ATTEND_LIMIT = 50 * 1024 * 1024
 SMALL_LIMIT = 40 * 1024 * 1024
 LIGHT = pl.CostEstimate(flops=1, bytes_accessed=1, transcendentals=0)
 HEAVY = pl.CostEstimate(flops=1 << 36, bytes_accessed=1 << 28, transcendentals=0)
@@ -37,100 +37,51 @@
     return index ^ shift if count & (count - 1) == 0 else (index + count - shift) % count
 
 
-def pack_kernel(count, early, dest_ref, length_ref, kv_ref, *refs):
+def prepare_kernel(
+    count, early, chunks, dest_ref, length_ref, hidden_ref, kv_ref, key_ref, value_ref, *refs
+):
     block_refs = refs[: len(early)]
-    pick_ref, blocks, in_sems, out_sems = refs[len(early) :]
+    pick_ref, own_ref, other_ref, hidden_held, held, total = refs[len(early) : len(early) + 6]
+    block_sems, hidden_sem, weight_sems = refs[len(early) + 6 :]
     rows = dest_ref.shape[0]
     capacity, lanes = kv_ref.shape[2:]
+    steps, _, depth = hidden_ref.shape
+    width = key_ref.shape[1]
+    part = depth // chunks
     me = lax.axis_index("inst")
+
+    def weights(chunk):
+        span = pl.ds(chunk * part, part)
+        return [
+            pltpu.make_async_copy(ref.at[span], held.at[which, span], weight_sems.at[chunk, which])
+            for which, ref in enumerate((key_ref, value_ref))
+        ]
+
+    hidden_copy = pltpu.make_async_copy(hidden_ref, hidden_held, hidden_sem)
+    hidden_copy.start()
+    for copy in weights(0):
+        copy.start()
     for peer in range(count):
         pick_ref[peer] = 0
     for row in range(rows):
         pick_ref[quotient(dest_ref[row], rows, rows * count)] = row
-    fetches, stores = [], []
+    fetches = []
     for piece, shift in enumerate(early):
         row = pick_ref[peer_to(me, shift, count)]
         fetches.append(
-            pltpu.make_async_copy(kv_ref.at[row], blocks.at[piece], in_sems.at[piece])
+            pltpu.make_async_copy(kv_ref.at[row], block_refs[piece], block_sems.at[piece])
         )
         fetches[-1].start()
-    tile = (TILE, lanes)
-    last = lax.broadcasted_iota(jnp.int32, tile, 0) == TILE - 1
-    first_lanes = lax.broadcasted_iota(jnp.int32, tile, 1) < HD
-    for piece, shift in enumerate(early):
-        peer = peer_to(me, shift, count)
-        row = pick_ref[peer]
-        slot = dest_ref[row] - peer * rows
-        slot = jnp.where((slot >= 0) & (slot < rows), slot, -1)
-        facts = jnp.where(first_lanes, slot, length_ref[row]).astype(jnp.float32)
-        fetches[piece].wait()
-        end = blocks[piece, 0, capacity - TILE :, :].astype(jnp.float32)
-        blocks[piece, 0, capacity - TILE :, :] = jnp.where(last, facts, end).astype(jnp.bfloat16)
-        stores.append(
-            pltpu.make_async_copy(blocks.at[piece], block_refs[piece], out_sems.at[piece])
-        )
-        stores[-1].start()
-    for copy in stores:
-        copy.wait()
-
-
-def pack(kv_cache, destination, lengths, count, early):
-    shape = kv_cache.shape[1:]
-    smem = pl.BlockSpec(memory_space=pltpu.SMEM)
-    hbm = pl.BlockSpec(memory_space=pl.ANY)
-    outs = pl.pallas_call(
-        functools.partial(pack_kernel, count, early),
-        out_shape=[jax.ShapeDtypeStruct(shape, kv_cache.dtype)] * len(early)
-        + [jax.ShapeDtypeStruct((count,), jnp.int32)],
-        in_specs=[smem, smem, hbm],
-        out_specs=[hbm] * len(early) + [smem],
-        scratch_shapes=[
-            pltpu.VMEM((len(early),) + shape, kv_cache.dtype),
-            pltpu.SemaphoreType.DMA((len(early),)),
-            pltpu.SemaphoreType.DMA((len(early),)),
-        ],
-        compiler_params=pltpu.CompilerParams(vmem_limit_bytes=VMEM_LIMIT),
-        cost_estimate=LIGHT,
-        name="pack",
-    )(destination, lengths, kv_cache)
-    return outs[:-1], outs[-1]
-
-
-def project_kernel(
-    chunks,
-    _,
-    hidden_ref,
-    key_ref,
-    value_ref,
-    own_ref,
-    other_ref,
-    hidden_held,
-    held,
-    total,
-    hidden_sem,
-    weight_sems,
-):
-    steps, rows, depth = hidden_ref.shape
-    width = key_ref.shape[1]
-    part = depth // chunks
-    hidden_copy = pltpu.make_async_copy(hidden_ref, hidden_held, hidden_sem)
-    hidden_copy.start()
-    weights = []
-    for chunk in range(chunks):
-        span = pl.ds(chunk * part, part)
-        for which, ref in enumerate((key_ref, value_ref)):
-            weights.append(
-                pltpu.make_async_copy(
-                    ref.at[span], held.at[which, span], weight_sems.at[chunk, which]
-                )
-            )
-            weights[-1].start()
+    for chunk in range(1, chunks):
+        for copy in weights(chunk):
+            copy.start()
+
     hidden_copy.wait()
     hidden = hidden_held[...].reshape(steps * rows, depth)
     sums = [None, None]
     for chunk in range(chunks):
-        for which in range(2):
-            weights[2 * chunk + which].wait()
+        for which, copy in enumerate(weights(chunk)):
+            copy.wait()
             product = jnp.dot(
                 hidden[:, chunk * part : (chunk + 1) * part],
                 held[which, chunk * part : (chunk + 1) * part, :],
@@ -146,30 +97,48 @@
         ref[:, :half] = total[:, pl.ds(at, half)]
         ref[:, half:] = total[:, pl.ds(pl.multiple_of(width + at, half), half)]
 
-
-def project(hidden_new, key_weight, value_weight, pick):
+    tile = (TILE, lanes)
+    last = lax.broadcasted_iota(jnp.int32, tile, 0) == TILE - 1
+    first_lanes = lax.broadcasted_iota(jnp.int32, tile, 1) < HD
+    for piece, shift in enumerate(early):
+        peer = peer_to(me, shift, count)
+        row = pick_ref[peer]
+        slot = dest_ref[row] - peer * rows
+        slot = jnp.where((slot >= 0) & (slot < rows), slot, -1)
+        facts = jnp.where(first_lanes, slot, length_ref[row]).astype(jnp.float32)
+        fetches[piece].wait()
+        block = block_refs[piece]
+        end = block[0, capacity - TILE :, :].astype(jnp.float32)
+        block[0, capacity - TILE :, :] = jnp.where(last, facts, end).astype(jnp.bfloat16)
+
+
+def prepare(destination, lengths, hidden_new, kv_cache, key_weight, value_weight, count, early):
     steps, rows, depth = hidden_new.shape
     width = key_weight.shape[1]
     chunks = 5
     part = jax.ShapeDtypeStruct((steps * rows, width), jnp.float32)
+    smem = pl.BlockSpec(memory_space=pltpu.SMEM)
     vmem = pl.BlockSpec(memory_space=pltpu.VMEM)
     hbm = pl.BlockSpec(memory_space=pl.ANY)
-    return pl.pallas_call(
-        functools.partial(project_kernel, chunks),
-        out_shape=[part, part],
-        in_specs=[hbm, hbm, hbm, hbm],
-        out_specs=[vmem, vmem],
+    outs = pl.pallas_call(
+        functools.partial(prepare_kernel, count, early, chunks),
+        out_shape=[jax.ShapeDtypeStruct(kv_cache.shape[1:], kv_cache.dtype)] * len(early)
+        + [jax.ShapeDtypeStruct((count,), jnp.int32), part, part],
+        in_specs=[smem, smem, hbm, hbm, hbm, hbm],
+        out_specs=[vmem] * len(early) + [smem, vmem, vmem],
         scratch_shapes=[
             pltpu.VMEM(hidden_new.shape, hidden_new.dtype),
             pltpu.VMEM((2, depth, width), key_weight.dtype),
             pltpu.VMEM((steps * rows, 2 * width), jnp.float32),
+            pltpu.SemaphoreType.DMA((len(early),)),
             pltpu.SemaphoreType.DMA,
             pltpu.SemaphoreType.DMA((chunks, 2)),
         ],
         compiler_params=pltpu.CompilerParams(vmem_limit_bytes=VMEM_LIMIT),
         cost_estimate=LIGHT,
-        name="project",
-    )(pick, hidden_new, key_weight, value_weight)
+        name="prepare",
+    )(destination, lengths, hidden_new, kv_cache, key_weight, value_weight)
+    return outs[: len(early)], *outs[len(early) :]
 
 
 def rotation(length_ref, steps, rows):
@@ -354,7 +323,7 @@
             pltpu.VMEM((rows * per_row, HD), jnp.float32),
         ],
         compiler_params=pltpu.CompilerParams(vmem_limit_bytes=ATTEND_LIMIT),
-        cost_estimate=LIGHT,
+        cost_estimate=HEAVY,
         name="attend",
     )(lengths, destination, pick, own, got, gain, queries, kv_cache)
 
@@ -594,9 +563,10 @@
         pairs = [(i, peer_to(i, shift, count)) for i in range(count)]
         return lax.ppermute(block, "inst", pairs)
 
-    blocks, pick = pack(kv_cache, destination, lengths, count, early)
+    blocks, pick, own, other = prepare(
+        destination, lengths, hidden_new, kv_cache, key_weight, value_weight, count, early
+    )
     early_got = [send(block, shift) for block, shift in zip(blocks, early)]
-    own, other = project(hidden_new, key_weight, value_weight, pick)
     got = lax.ppermute(other, "tp", [(0, 1), (1, 0)])
     moved, mixed, small, *late_blocks = attend(
         kv_cache, queries, own, got, key_gain[None, :], lengths, destination, pick, count, late

time: 44.6 us -> 41 us (0.919)
  waiting for transfers between devices: 6.41 us -> 3.97 us
  Pallas kernels: 17.9 us -> 15.7 us
  local copies, waits for them, and re-layouts: 0.63 us -> 1.56 us
    pallas_call x2 -> x1, Pallas kernels: 7.52 us -> 5.65 us  [prepare(): pl.pallas_call(functools.partial(prepare_kernel, count, early, chunks), o...]
    ppermute x1, waiting for transfers between devices: 1.5 us -> 0.01 us  [local(): got = lax.ppermute(other, 'tp', [(0, 1), (1, 0)])]
    all_to_all x1, waiting for transfers between devices: 3.16 us -> 2.15 us  [local(): small_got = lax.all_to_all(small, 'inst', 0, 0, tiled=True)]
    unnamed x4 -> x12, local copies, waits for them, and re-layouts: 0.63 us -> 1.56 us
  transfers between devices with their start and end apart: 9 -> 9, of which waited for: 5 -> 4; matrix products, arithmetic and copies ran while one was open for 0% -> 0% of each run, Pallas kernels for 31% -> 23%
where the time goes in v11:
time: 41 us; the launch traced here: 40.6 us
  starting transfers between devices  18.6 us (45%)
  Pallas kernels  15.7 us (38%)
  waiting for transfers between devices  3.97 us (10%)
  local copies, waits for them, and re-layouts  1.56 us (4%)
  between operations  0.74 us (2%)
    ppermute x7, starting transfers between devices, send(): return lax.ppermute(block, 'inst', pairs)  13.9 us
    pallas_call x1, Pallas kernels, attend(): pl.pallas_call(functools.partial(attend_kernel, count, late, block), grid...  6.61 us
    pallas_call x1, Pallas kernels, prepare(): pl.pallas_call(functools.partial(prepare_kernel, count, early, chunks), o...  5.65 us
    all_to_all x1, starting transfers between devices, local(): small_got = lax.all_to_all(small, 'inst', 0, 0, tiled=True)  4.18 us
    all_to_all x1, waiting for transfers between devices, local(): small_got = lax.all_to_all(small, 'inst', 0, 0, tiled=True)  2.15 us
    ppermute x7, waiting for transfers between devices, send(): return lax.ppermute(block, 'inst', pairs)  1.82 us
    pallas_call x1, Pallas kernels, settle(): pl.pallas_call(functools.partial(settle_kernel, count, early, group), out...  1.56 us
    unnamed x12, local copies, waits for them, and re-layouts  1.56 us
  transfers between devices with their start and end apart: 9, of which 4 were waited for; matrix products, arithmetic and copies ran while one was open for 0% of the time, Pallas kernels for 23%

profile of v11, /device:TPU:0, one launch (start us, length us, event | category | flops | bytes accessed | tf_op | source)
XLA Modules:
  0.0 40.6 jit_solution(9559027389227341074)
XLA Ops:
  0.7 5.6 %prepare.1 = (bf16[2,144,256]{2,1,0:T(8,128)(2,1)}, bf16[2,144,256]{2,1,0:T(8,128)(2,1)}, bf16[2,144,256]{2,1,0:T(8,128)(2,1)}, bf16[2,144,256]{2,1,0:T(8,128)(2...) custom-call(s32[24]{0:T(128)} %dest_ref.3, s32[24]{0:T(128)} %length_ref.3, bf16[2,24,2560]{2,1,0:T(8,128)(2,1)} %hidden_ref.1, ...), custom_call_target="tpu_custom_call" | custom-call | flops 1 | bytes 1 | tf_op jit(solution)/shard_map/prepare/pallas_call | solution.py:123
  6.3 0.5 %collective-permute-start = (f32[48,512]{1,0:T(8,128)}, f32[48,512]{1,0:T(8,128)S(1)}, u32[]{:S(2)}, u32[]{:S(2)}) collective-permute-start(f32[48,512]{1,0:T(8,128)} %get-tuple-element.21), channel_id=1, source_target_pairs={{0,1},{1,0},{2,3},{3,2},{4,5},{5,4},{6,7},{7,6},{8,9},{9,8},{10,11... | collective-permute-start | bytes 294920 | tf_op jit(solution)/shard_map/ppermute | solution.py:570
  6.8 3.7 %collective-permute-start.1 = (bf16[2,144,256]{2,1,0:T(8,128)(2,1)}, bf16[2,144,256]{2,1,0:T(8,128)(2,1)S(1)}, u32[]{:S(2)}, u32[]{:S(2)}) collective-permute-start(bf16[2,144,256]{2,1,0:T(8,128)(2,1)} %get-tuple-element.24), channel_id=1, source_target_pairs={{0,8},{2,10},{4,12},{6,14},{8,0},{10,2},{12,4},{14,6},{1,9},{3,11}... | collective-permute-start | bytes 442376 | tf_op jit(solution)/shard_map/ppermute | solution.py:564
  10.5 1.3 %collective-permute-start.2 = (bf16[2,144,256]{2,1,0:T(8,128)(2,1)}, bf16[2,144,256]{2,1,0:T(8,128)(2,1)S(1)}, u32[]{:S(2)}, u32[]{:S(2)}) collective-permute-start(bf16[2,144,256]{2,1,0:T(8,128)(2,1)} %get-tuple-element.25), channel_id=1, source_target_pairs={{0,10},{2,8},{4,14},{6,12},{8,2},{10,0},{12,6},{14,4},{1,11},{3,9}... | collective-permute-start | bytes 442376 | tf_op jit(solution)/shard_map/ppermute | solution.py:564
  11.8 3.6 %collective-permute-start.3 = (bf16[2,144,256]{2,1,0:T(8,128)(2,1)}, bf16[2,144,256]{2,1,0:T(8,128)(2,1)S(1)}, u32[]{:S(2)}, u32[]{:S(2)}) collective-permute-start(bf16[2,144,256]{2,1,0:T(8,128)(2,1)} %get-tuple-element.26), channel_id=1, source_target_pairs={{0,12},{2,14},{4,8},{6,10},{8,4},{10,6},{12,0},{14,2},{1,13},{3,15... | collective-permute-start | bytes 442376 | tf_op jit(solution)/shard_map/ppermute | solution.py:564
  15.4 0.0 collective-permute-start.4
  15.4 0.0 copy-start.3
  15.5 0.9 %copy-done.3 = f32[48,512]{1,0:T(8,128)S(1)} copy-done((f32[48,512]{1,0:T(8,128)S(1)}, f32[48,512]{1,0:T(8,128)}, u32[]{:S(2)}) %copy-start.3) | copy-done | bytes 98328
  16.3 0.7 %copy-done.5 = s32[8]{0:T(128)S(1)} copy-done((s32[8]{0:T(128)S(1)}, s32[8]{0:T(128)}, u32[]{:S(2)}) %copy-start.5) | copy-done | bytes 56
  17.0 6.6 %attend.1 = (bf16[24,2,144,256]{3,2,1,0:T(8,128)(2,1)}, bf16[768,128]{1,0:T(8,128)(2,1)S(1)}, bf16[8,48,128]{2,1,0:T(8,128)(2,1)}, bf16[2,144,256]{2,1,0:T(8,128...) custom-call(s32[24]{0:T(128)S(1)} %copy-done, s32[24]{0:T(128)S(1)} %copy-done.1, ...), custom_call_target="tpu_custom_call" | custom-call | flops 68719476736 | bytes 268435456 | tf_op jit(solution)/shard_map/attend/pallas_call | solution.py:308
  23.6 4.2 %all-to-all-start = ((bf16[8,48,128]{2,1,0:T(8,128)(2,1)}), bf16[8,48,128]{2,1,0:T(8,128)(2,1)S(1)}, u32[]{:S(2)}, u32[]{:S(2)}) async-start(bf16[8,48,128]{2,1,0:T(8,128)(2,1)} %get-tuple-element.23), calls=%async_computation | async-start | bytes 196608 | tf_op jit(solution)/shard_map/all_to_all | solution.py:575
  27.8 4.7 %collective-permute-start.5 = (bf16[2,144,256]{2,1,0:T(8,128)(2,1)S(1)}, bf16[2,144,256]{2,1,0:T(8,128)(2,1)S(1)}, u32[]{:S(2)}, u32[]{:S(2)}) collective-permute-start(bf16[2,144,256]{2,1,0:T(8,128)(2,1)S(1)} %get-tuple-element.32), channel_id=1, source_target_pairs={{0,14},{2,12},{4,10},{6,8},{8,6},{10,4},{12,2},{14,0},{1,15},{3,13... | collective-permute-start | bytes 442376 | tf_op jit(solution)/shard_map/ppermute | solution.py:564
  32.5 0.0 collective-permute-done.1.refs_0_
  32.5 0.0 collective-permute-start.6
  32.5 0.0 collective-permute-done.2.refs_1_
  32.5 0.6 %collective-permute-start.7 = (bf16[2,144,256]{2,1,0:T(8,128)(2,1)S(1)}, bf16[2,144,256]{2,1,0:T(8,128)(2,1)S(1)}, u32[]{:S(2)}, u32[]{:S(2)}) collective-permute-start(bf16[2,144,256]{2,1,0:T(8,128)(2,1)S(1)} %get-tuple-element.34), channel_id=1, source_target_pairs={{0,2},{2,0},{4,6},{6,4},{8,10},{10,8},{12,14},{14,12},{1,3},{3,1},... | collective-permute-start | bytes 442376 | tf_op jit(solution)/shard_map/ppermute | solution.py:564
  33.2 0.0 collective-permute-done.3.refs_2_
  33.2 1.0 %land.1 = (bf16[24,2,144,256]{3,2,1,0:T(8,128)(2,1)}, bf16[4,2,32,256]{3,2,1,0:T(8,128)(2,1)S(1)}) custom-call(bf16[2,144,256]{2,1,0:T(8,128)(2,1)S(1)} %collective-permute-done.1.refs_0_, bf16[2,144,256]{2,1,0:T(8,128)(2,1)S(1)} %collective-permute-done.2.refs_1_, ...), custom_call_target="tpu_custom_call", output_to_operand_aliasing={{0}: (4, {})} | custom-call | flops 68719476736 | bytes 268435456 | tf_op jit(solution)/shard_map/land/pallas_call | solution.py:397
  34.2 2.1 %all-to-all-done.small_ref.refs_3_ = bf16[8,48,128]{2,1,0:T(8,128)(2,1)S(1)} async-done(((bf16[8,48,128]{2,1,0:T(8,128)(2,1)}), bf16[8,48,128]{2,1,0:T(8,128)(2,1)S(1)}, u32[]{:S(2)}, u32[]{:S(2)}) %all-to-all-start) | async-done | bytes 98336 | tf_op jit(solution)/shard_map/all_to_all | solution.py:575
  36.3 1.6 %settle.1 = (bf16[2,24,2048]{2,1,0:T(8,128)(2,1)}, bf16[24,2,144,256]{3,2,1,0:T(8,128)(2,1)}) custom-call(bf16[768,128]{1,0:T(8,128)(2,1)S(1)} %get-tuple-element.22.mixed_ref, bf16[8,48,128]{2,1,0:T(8,128)(2,1)S(1)} %all-to-all-done.small_ref.refs_3_, bf16[4,2,32,256]{3,2,1,0:T(8,128)(2,1)S(1)} %get-tuple-element.29.window_ref, ...), custom_call_target="tpu_custom_call", output_to_operand_aliasing={{1}: (3, {})} | custom-call | flops 1 | bytes 1 | tf_op jit(solution)/shard_map/settle/pallas_call | solution.py:493
  37.9 0.8 %collective-permute-done.5.refs_0_ = bf16[2,144,256]{2,1,0:T(8,128)(2,1)S(1)} collective-permute-done((bf16[2,144,256]{2,1,0:T(8,128)(2,1)S(1)}, bf16[2,144,256]{2,1,0:T(8,128)(2,1)S(1)}, u32[]{:S(2)}, u32[]{:S(2)}) %collective-permute-start.5) | collective-permute-done | bytes 147488 | tf_op jit(solution)/shard_map/ppermute | solution.py:564
  38.7 0.7 %collective-permute-done.6.refs_1_ = bf16[2,144,256]{2,1,0:T(8,128)(2,1)S(1)} collective-permute-done((bf16[2,144,256]{2,1,0:T(8,128)(2,1)S(1)}, bf16[2,144,256]{2,1,0:T(8,128)(2,1)S(1)}, u32[]{:S(2)}, u32[]{:S(2)}) %collective-permute-start.6) | collective-permute-done | bytes 147488 | tf_op jit(solution)/shard_map/ppermute | solution.py:564
  39.4 0.3 collective-permute-done.7.refs_2_
  39.7 0.9 %finish.1 = bf16[24,2,144,256]{3,2,1,0:T(8,128)(2,1)} custom-call(bf16[2,144,256]{2,1,0:T(8,128)(2,1)S(1)} %collective-permute-done.5.refs_0_, bf16[2,144,256]{2,1,0:T(8,128)(2,1)S(1)} %collective-permute-done.6.refs_1_, bf16[2,144,256]{2,1,0:T(8,128)(2,1)S(1)} %collective-permute-done.7.refs_2_, ...), custom_call_target="tpu_custom_call", output_to_operand_aliasing={{}: (4, {})} | custom-call | flops 1 | bytes 1 | tf_op jit(solution)/shard_map/finish/pallas_call | solution.py:538
  (11 shorter events, 0.0 us)
Async XLA Ops:
  0.6 14.8 %copy-start.1 = (s32[24]{0:T(128)S(1)}, s32[24]{0:T(128)}, u32[]{:S(2)}) copy-start(s32[24]{0:T(128)} %dest_ref.3) | copy-start | bytes 292
  0.6 14.8 %copy-start = (s32[24]{0:T(128)S(1)}, s32[24]{0:T(128)}, u32[]{:S(2)}) copy-start(s32[24]{0:T(128)} %length_ref.3) | copy-start | bytes 292
  0.7 14.8 %copy-start.4 = (bf16[128]{0:T(256)(128)(2,1)S(1)}, bf16[128]{0:T(256)(128)(2,1)}, u32[]{:S(2)}) copy-start(bf16[128]{0:T(256)(128)(2,1)} %param.15) | copy-start | bytes 772
  0.7 14.8 %copy-start.2 = (bf16[2,24,2048]{2,1,0:T(8,128)(2,1)S(1)}, bf16[2,24,2048]{2,1,0:T(8,128)(2,1)}, u32[]{:S(2)}) copy-start(bf16[2,24,2048]{2,1,0:T(8,128)(2,1)} %query_ref.1) | copy-start | bytes 589828
  6.3 9.1 %collective-permute-start = (f32[48,512]{1,0:T(8,128)}, f32[48,512]{1,0:T(8,128)S(1)}, u32[]{:S(2)}, u32[]{:S(2)}) collective-permute-start(f32[48,512]{1,0:T(8,128)} %get-tuple-element.21), channel_id=1, source_target_pairs={{0,1},{1,0},{2,3},{3,2},{4,5},{5,4},{6,7},{7,6},{8,9},{9,8},{10,11... | collective-permute-start | bytes 294920 | tf_op jit(solution)/shard_map/ppermute | solution.py:570
  6.8 25.7 %collective-permute-start.1 = (bf16[2,144,256]{2,1,0:T(8,128)(2,1)}, bf16[2,144,256]{2,1,0:T(8,128)(2,1)S(1)}, u32[]{:S(2)}, u32[]{:S(2)}) collective-permute-start(bf16[2,144,256]{2,1,0:T(8,128)(2,1)} %get-tuple-element.24), channel_id=1, source_target_pairs={{0,8},{2,10},{4,12},{6,14},{8,0},{10,2},{12,4},{14,6},{1,9},{3,11}... | collective-permute-start | bytes 442376 | tf_op jit(solution)/shard_map/ppermute | solution.py:564
  10.5 22.0 %collective-permute-start.2 = (bf16[2,144,256]{2,1,0:T(8,128)(2,1)}, bf16[2,144,256]{2,1,0:T(8,128)(2,1)S(1)}, u32[]{:S(2)}, u32[]{:S(2)}) collective-permute-start(bf16[2,144,256]{2,1,0:T(8,128)(2,1)} %get-tuple-element.25), channel_id=1, source_target_pairs={{0,10},{2,8},{4,14},{6,12},{8,2},{10,0},{12,6},{14,4},{1,11},{3,9}... | collective-permute-start | bytes 442376 | tf_op jit(solution)/shard_map/ppermute | solution.py:564
  11.8 21.4 %collective-permute-start.3 = (bf16[2,144,256]{2,1,0:T(8,128)(2,1)}, bf16[2,144,256]{2,1,0:T(8,128)(2,1)S(1)}, u32[]{:S(2)}, u32[]{:S(2)}) collective-permute-start(bf16[2,144,256]{2,1,0:T(8,128)(2,1)} %get-tuple-element.26), channel_id=1, source_target_pairs={{0,12},{2,14},{4,8},{6,10},{8,4},{10,6},{12,0},{14,2},{1,13},{3,15... | collective-permute-start | bytes 442376 | tf_op jit(solution)/shard_map/ppermute | solution.py:564
  15.4 17.8 %collective-permute-start.4 = (bf16[2,144,256]{2,1,0:T(8,128)(2,1)}, bf16[2,144,256]{2,1,0:T(8,128)(2,1)S(1)}, u32[]{:S(2)}, u32[]{:S(2)}) collective-permute-start(bf16[2,144,256]{2,1,0:T(8,128)(2,1)} %get-tuple-element.27), channel_id=1, source_target_pairs={{0,6},{2,4},{4,2},{6,0},{8,14},{10,12},{12,10},{14,8},{1,7},{3,5},... | collective-permute-start | bytes 442376 | tf_op jit(solution)/shard_map/ppermute | solution.py:564
  15.4 0.9 %copy-start.3 = (f32[48,512]{1,0:T(8,128)S(1)}, f32[48,512]{1,0:T(8,128)}, u32[]{:S(2)}) copy-start(f32[48,512]{1,0:T(8,128)} %get-tuple-element.20.own_ref) | copy-start | bytes 294916
  16.3 0.7 %copy-start.5 = (s32[8]{0:T(128)S(1)}, s32[8]{0:T(128)}, u32[]{:S(2)}) copy-start(s32[8]{0:T(128)} %get-tuple-element.19.pick_ref) | copy-start | bytes 100
  23.6 12.7 %all-to-all-start = ((bf16[8,48,128]{2,1,0:T(8,128)(2,1)}), bf16[8,48,128]{2,1,0:T(8,128)(2,1)S(1)}, u32[]{:S(2)}, u32[]{:S(2)}) async-start(bf16[8,48,128]{2,1,0:T(8,128)(2,1)} %get-tuple-element.23), calls=%async_computation | async-start | bytes 196608 | tf_op jit(solution)/shard_map/all_to_all | solution.py:575
  27.8 10.9 %collective-permute-start.5 = (bf16[2,144,256]{2,1,0:T(8,128)(2,1)S(1)}, bf16[2,144,256]{2,1,0:T(8,128)(2,1)S(1)}, u32[]{:S(2)}, u32[]{:S(2)}) collective-permute-start(bf16[2,144,256]{2,1,0:T(8,128)(2,1)S(1)} %get-tuple-element.32), channel_id=1, source_target_pairs={{0,14},{2,12},{4,10},{6,8},{8,6},{10,4},{12,2},{14,0},{1,15},{3,13... | collective-permute-start | bytes 442376 | tf_op jit(solution)/shard_map/ppermute | solution.py:564
  32.5 6.9 %collective-permute-start.6 = (bf16[2,144,256]{2,1,0:T(8,128)(2,1)S(1)}, bf16[2,144,256]{2,1,0:T(8,128)(2,1)S(1)}, u32[]{:S(2)}, u32[]{:S(2)}) collective-permute-start(bf16[2,144,256]{2,1,0:T(8,128)(2,1)S(1)} %get-tuple-element.33), channel_id=1, source_target_pairs={{0,4},{2,6},{4,0},{6,2},{8,12},{10,14},{12,8},{14,10},{1,5},{3,7},... | collective-permute-start | bytes 442376 | tf_op jit(solution)/shard_map/ppermute | solution.py:564
  32.5 7.2 %collective-permute-start.7 = (bf16[2,144,256]{2,1,0:T(8,128)(2,1)S(1)}, bf16[2,144,256]{2,1,0:T(8,128)(2,1)S(1)}, u32[]{:S(2)}, u32[]{:S(2)}) collective-permute-start(bf16[2,144,256]{2,1,0:T(8,128)(2,1)S(1)} %get-tuple-element.34), channel_id=1, source_target_pairs={{0,2},{2,0},{4,6},{6,4},{8,10},{10,8},{12,14},{14,12},{1,3},{3,1},... | collective-permute-start | bytes 442376 | tf_op jit(solution)/shard_map/ppermute | solution.py:564

commit v12 on v11

--- a/solution.py
+++ b/solution.py
@@ -11,8 +11,8 @@
 HD = 128
 ROPE_BASE = 1000000.0
 NORM_EPS = 1e-06
-VMEM_LIMIT = 54 * 1024 * 1024
-ATTEND_LIMIT = 50 * 1024 * 1024
+VMEM_LIMIT = 62 * 1024 * 1024
+ATTEND_LIMIT = 56 * 1024 * 1024
 SMALL_LIMIT = 40 * 1024 * 1024
 LIGHT = pl.CostEstimate(flops=1, bytes_accessed=1, transcendentals=0)
 HEAVY = pl.CostEstimate(flops=1 << 36, bytes_accessed=1 << 28, transcendentals=0)
@@ -37,15 +37,67 @@
     return index ^ shift if count & (count - 1) == 0 else (index + count - shift) % count
 
 
+def pick_rows(count, dest_ref, pick_ref):
+    rows = dest_ref.shape[0]
+    for peer in range(count):
+        pick_ref[peer] = 0
+    for row in range(rows):
+        pick_ref[quotient(dest_ref[row], rows, rows * count)] = row
+
+
+def add_facts(block, peer, row, dest_ref, length_ref):
+    capacity, lanes = block.shape[1:]
+    rows = dest_ref.shape[0]
+    slot = dest_ref[row] - peer * rows
+    slot = jnp.where((slot >= 0) & (slot < rows), slot, -1)
+    last = lax.broadcasted_iota(jnp.int32, (TILE, lanes), 0) == TILE - 1
+    first_lanes = lax.broadcasted_iota(jnp.int32, (TILE, lanes), 1) < HD
+    facts = jnp.where(first_lanes, slot, length_ref[row]).astype(jnp.float32)
+    end = block[0, capacity - TILE :, :].astype(jnp.float32)
+    block[0, capacity - TILE :, :] = jnp.where(last, facts, end).astype(jnp.bfloat16)
+
+
+def pack_kernel(count, shift, dest_ref, length_ref, kv_ref, block_ref, block, sem, pick):
+    pick_rows(count, dest_ref, pick)
+    peer = peer_to(lax.axis_index("inst"), shift, count)
+    row = pick[peer]
+    fetch = pltpu.make_async_copy(kv_ref.at[row], block, sem)
+    fetch.start()
+    fetch.wait()
+    add_facts(block, peer, row, dest_ref, length_ref)
+    store = pltpu.make_async_copy(block, block_ref, sem)
+    store.start()
+    store.wait()
+
+
+def pack(kv_cache, destination, lengths, count, shift):
+    smem = pl.BlockSpec(memory_space=pltpu.SMEM)
+    hbm = pl.BlockSpec(memory_space=pl.ANY)
+    return pl.pallas_call(
+        functools.partial(pack_kernel, count, shift),
+        out_shape=jax.ShapeDtypeStruct(kv_cache.shape[1:], kv_cache.dtype),
+        in_specs=[smem, smem, hbm],
+        out_specs=hbm,
+        scratch_shapes=[
+            pltpu.VMEM(kv_cache.shape[1:], kv_cache.dtype),
+            pltpu.SemaphoreType.DMA,
+            pltpu.SMEM((count,), jnp.int32),
+        ],
+        compiler_params=pltpu.CompilerParams(vmem_limit_bytes=VMEM_LIMIT),
+        cost_estimate=LIGHT,
+        name="pack",
+    )(destination, lengths, kv_cache)
+
+
 def prepare_kernel(
     count, early, chunks, dest_ref, length_ref, hidden_ref, kv_ref, key_ref, value_ref, *refs
 ):
-    block_refs = refs[: len(early)]
-    pick_ref, own_ref, other_ref, hidden_held, held, total = refs[len(early) : len(early) + 6]
-    block_sems, hidden_sem, weight_sems = refs[len(early) + 6 :]
-    rows = dest_ref.shape[0]
-    capacity, lanes = kv_ref.shape[2:]
-    steps, _, depth = hidden_ref.shape
+    block_refs = refs[1 : len(early) + 1]
+    pick_ref, own_ref, other_ref, blocks, hidden_held, held, total = refs[
+        len(early) + 1 : len(early) + 8
+    ]
+    in_sems, out_sems, hidden_sem, weight_sems = refs[len(early) + 8 :]
+    steps, rows, depth = hidden_ref.shape
     width = key_ref.shape[1]
     part = depth // chunks
     me = lax.axis_index("inst")
@@ -61,21 +113,26 @@
     hidden_copy.start()
     for copy in weights(0):
         copy.start()
-    for peer in range(count):
-        pick_ref[peer] = 0
-    for row in range(rows):
-        pick_ref[quotient(dest_ref[row], rows, rows * count)] = row
-    fetches = []
+    pick_rows(count, dest_ref, pick_ref)
+    fetches, stores = [], []
     for piece, shift in enumerate(early):
         row = pick_ref[peer_to(me, shift, count)]
         fetches.append(
-            pltpu.make_async_copy(kv_ref.at[row], block_refs[piece], block_sems.at[piece])
+            pltpu.make_async_copy(kv_ref.at[row], blocks.at[piece], in_sems.at[piece])
         )
         fetches[-1].start()
     for chunk in range(1, chunks):
         for copy in weights(chunk):
             copy.start()
 
+    for piece, shift in enumerate(early):
+        peer = peer_to(me, shift, count)
+        fetches[piece].wait()
+        add_facts(blocks.at[piece], peer, pick_ref[peer], dest_ref, length_ref)
+        stores.append(
+            pltpu.make_async_copy(blocks.at[piece], block_refs[piece], out_sems.at[piece])
+        )
+        stores[-1].start()
     hidden_copy.wait()
     hidden = hidden_held[...].reshape(steps * rows, depth)
     sums = [None, None]
@@ -97,22 +154,11 @@
         ref[:, :half] = total[:, pl.ds(at, half)]
         ref[:, half:] = total[:, pl.ds(pl.multiple_of(width + at, half), half)]
 
-    tile = (TILE, lanes)
-    last = lax.broadcasted_iota(jnp.int32, tile, 0) == TILE - 1
-    first_lanes = lax.broadcasted_iota(jnp.int32, tile, 1) < HD
-    for piece, shift in enumerate(early):
-        peer = peer_to(me, shift, count)
-        row = pick_ref[peer]
-        slot = dest_ref[row] - peer * rows
-        slot = jnp.where((slot >= 0) & (slot < rows), slot, -1)
-        facts = jnp.where(first_lanes, slot, length_ref[row]).astype(jnp.float32)
-        fetches[piece].wait()
-        block = block_refs[piece]
-        end = block[0, capacity - TILE :, :].astype(jnp.float32)
-        block[0, capacity - TILE :, :] = jnp.where(last, facts, end).astype(jnp.bfloat16)
-
-
-def prepare(destination, lengths, hidden_new, kv_cache, key_weight, value_weight, count, early):
+    for copy in stores:
+        copy.wait()
+
+
+def prepare(destination, lengths, hidden_new, kv_cache, key_weight, value_weight, count, early, first):
     steps, rows, depth = hidden_new.shape
     width = key_weight.shape[1]
     chunks = 5
@@ -124,20 +170,22 @@
         functools.partial(prepare_kernel, count, early, chunks),
         out_shape=[jax.ShapeDtypeStruct(kv_cache.shape[1:], kv_cache.dtype)] * len(early)
         + [jax.ShapeDtypeStruct((count,), jnp.int32), part, part],
-        in_specs=[smem, smem, hbm, hbm, hbm, hbm],
-        out_specs=[vmem] * len(early) + [smem, vmem, vmem],
+        in_specs=[smem, smem, hbm, hbm, hbm, hbm, hbm],
+        out_specs=[hbm] * len(early) + [smem, vmem, vmem],
         scratch_shapes=[
+            pltpu.VMEM((len(early),) + kv_cache.shape[1:], kv_cache.dtype),
             pltpu.VMEM(hidden_new.shape, hidden_new.dtype),
             pltpu.VMEM((2, depth, width), key_weight.dtype),
             pltpu.VMEM((steps * rows, 2 * width), jnp.float32),
             pltpu.SemaphoreType.DMA((len(early),)),
+            pltpu.SemaphoreType.DMA((len(early),)),
             pltpu.SemaphoreType.DMA,
             pltpu.SemaphoreType.DMA((chunks, 2)),
         ],
         compiler_params=pltpu.CompilerParams(vmem_limit_bytes=VMEM_LIMIT),
         cost_estimate=LIGHT,
         name="prepare",
-    )(destination, lengths, hidden_new, kv_cache, key_weight, value_weight)
+    )(destination, lengths, hidden_new, kv_cache, key_weight, value_weight, first)
     return outs[: len(early)], *outs[len(early) :]
 
 
@@ -177,8 +225,8 @@
     kv_ref,
     *refs,
 ):
-    moved_ref, mixed_ref, small_ref = refs[:3]
-    late_refs = refs[3:-4]
+    moved_ref, mixed_ref, small_ref = refs[1:4]
+    late_refs = refs[4:-4]
     fresh, query_rows, query_columns, mixed = refs[-4:]
     part = pl.program_id(0)
     steps, rows, query_width = query_ref.shape
@@ -294,7 +342,7 @@
             small_ref[peer, per_row:, :] = jnp.concatenate(news, axis=0).astype(jnp.bfloat16)
 
 
-def attend(kv_cache, queries, own, got, gain, lengths, destination, pick, count, late):
+def attend(kv_cache, queries, own, got, gain, lengths, destination, pick, count, late, arrived):
     steps, rows, query_width = queries.shape
     capacity, lanes = kv_cache.shape[2:]
     heads = lanes // HD
@@ -304,6 +352,7 @@
     small = jax.ShapeDtypeStruct((count, small_rows, HD), jnp.bfloat16)
     smem = pl.BlockSpec(memory_space=pltpu.SMEM)
     vmem = pl.BlockSpec(memory_space=pltpu.VMEM)
+    hbm = pl.BlockSpec(memory_space=pl.ANY)
     cache_block = pl.BlockSpec((block, 2, capacity, lanes), lambda i: (i, 0, 0, 0))
     return pl.pallas_call(
         functools.partial(attend_kernel, count, late, block),
@@ -314,7 +363,7 @@
             small,
         ]
         + [jax.ShapeDtypeStruct(kv_cache.shape[1:], kv_cache.dtype)] * len(late),
-        in_specs=[smem, smem, smem, vmem, vmem, vmem, vmem, cache_block],
+        in_specs=[smem, smem, smem, vmem, vmem, vmem, vmem, cache_block, hbm],
         out_specs=[cache_block, vmem, vmem] + [vmem] * len(late),
         scratch_shapes=[
             pltpu.VMEM((2, steps * rows, lanes), jnp.float32),
@@ -325,7 +374,7 @@
         compiler_params=pltpu.CompilerParams(vmem_limit_bytes=ATTEND_LIMIT),
         cost_estimate=HEAVY,
         name="attend",
-    )(lengths, destination, pick, own, got, gain, queries, kv_cache)
+    )(lengths, destination, pick, own, got, gain, queries, kv_cache, arrived)
 
 
 def read_facts(block):
@@ -563,13 +612,33 @@
         pairs = [(i, peer_to(i, shift, count)) for i in range(count)]
         return lax.ppermute(block, "inst", pairs)
 
+    first = pack(kv_cache, destination, lengths, count, early[0])
+    first_got = send(first, early[0])
     blocks, pick, own, other = prepare(
-        destination, lengths, hidden_new, kv_cache, key_weight, value_weight, count, early
+        destination,
+        lengths,
+        hidden_new,
+        kv_cache,
+        key_weight,
+        value_weight,
+        count,
+        early[1:],
+        first,
     )
-    early_got = [send(block, shift) for block, shift in zip(blocks, early)]
+    early_got = [first_got] + [send(block, shift) for block, shift in zip(blocks, early[1:])]
     got = lax.ppermute(other, "tp", [(0, 1), (1, 0)])
     moved, mixed, small, *late_blocks = attend(
-        kv_cache, queries, own, got, key_gain[None, :], lengths, destination, pick, count, late
+        kv_cache,
+        queries,
+        own,
+        got,
+        key_gain[None, :],
+        lengths,
+        destination,
+        pick,
+        count,
+        late,
+        first_got,
     )
     late_got = [send(block, shift) for block, shift in zip(late_blocks, late)]
     small_got = lax.all_to_all(small, "inst", 0, 0, tiled=True)

time: 41 us -> 42.9 us (1.046)
  Pallas kernels: 15.7 us -> 18.2 us
  waiting for transfers between devices: 3.97 us -> 3.41 us
    pallas_call x0 -> x1, Pallas kernels: none -> 2.31 us  [pack(): pl.pallas_call(functools.partial(pack_kernel, count, shift), out_shape=ja...]
    all_to_all x1, waiting for transfers between devices: 2.15 us -> 1.63 us  [local(): small_got = lax.all_to_all(small, 'inst', 0, 0, tiled=True)]
    ppermute x1, starting transfers between devices: 0.52 us -> 0.07 us  [local(): got = lax.ppermute(other, 'tp', [(0, 1), (1, 0)])]
    ppermute x7, starting transfers between devices: 13.9 us -> 14.4 us  [send(): return lax.ppermute(block, 'inst', pairs)]
    unnamed x12 -> x8, local copies, waits for them, and re-layouts: 1.56 us -> 1.59 us
  transfers between devices with their start and end apart: 9 -> 9, of which waited for: 4 -> 3; matrix products, arithmetic and copies ran while one was open for 0% -> 0% of each run, Pallas kernels for 23% -> 35%
where the time goes in v12:
time: 42.9 us; the launch traced here: 42.5 us
  starting transfers between devices  18.6 us (43%)
  Pallas kernels  18.2 us (42%)
  waiting for transfers between devices  3.41 us (8%)
  local copies, waits for them, and re-layouts  1.59 us (4%)
  between operations  0.7 us (2%)
    ppermute x7, starting transfers between devices, send(): return lax.ppermute(block, 'inst', pairs)  14.4 us
    pallas_call x1, Pallas kernels, attend(): pl.pallas_call(functools.partial(attend_kernel, count, late, block), grid...  6.94 us
    pallas_call x1, Pallas kernels, prepare(): pl.pallas_call(functools.partial(prepare_kernel, count, early, chunks), o...  5.47 us
    all_to_all x1, starting transfers between devices, local(): small_got = lax.all_to_all(small, 'inst', 0, 0, tiled=True)  4.2 us
    pallas_call x1, Pallas kernels, pack(): pl.pallas_call(functools.partial(pack_kernel, count, shift), out_shape=ja...  2.31 us
    ppermute x7, waiting for transfers between devices, send(): return lax.ppermute(block, 'inst', pairs)  1.77 us
    all_to_all x1, waiting for transfers between devices, local(): small_got = lax.all_to_all(small, 'inst', 0, 0, tiled=True)  1.63 us
    unnamed x8, local copies, waits for them, and re-layouts  1.59 us
  transfers between devices with their start and end apart: 9, of which 3 were waited for; matrix products, arithmetic and copies ran while one was open for 0% of the time, Pallas kernels for 35%

profile of v12, /device:TPU:0, one launch (start us, length us, event | category | flops | bytes accessed | tf_op | source)
XLA Modules:
  0.0 42.5 jit_solution(11653411420683300789)
XLA Ops:
  0.6 2.3 %pack.1.refs_0_ = bf16[2,144,256]{2,1,0:T(8,128)(2,1)} custom-call(s32[24]{0:T(128)} %dest_ref.5, s32[24]{0:T(128)} %length_ref.5, bf16[24,2,144,256]{3,2,1,0:T(8,128)(2,1)} %kv_ref.5), custom_call_target="tpu_custom_call" | custom-call | flops 1 | bytes 1 | tf_op jit(solution)/shard_map/pack/pallas_call | solution.py:76
  2.9 4.1 %collective-permute-start.1 = (bf16[2,144,256]{2,1,0:T(8,128)(2,1)}, bf16[2,144,256]{2,1,0:T(8,128)(2,1)S(1)}, u32[]{:S(2)}, u32[]{:S(2)}) collective-permute-start(bf16[2,144,256]{2,1,0:T(8,128)(2,1)} %pack.1.refs_0_), channel_id=1, source_target_pairs={{0,8},{2,10},{4,12},{6,14},{8,0},{10,2},{12,4},{14,6},{1,9},{3,11}... | collective-permute-start | bytes 442376 | tf_op jit(solution)/shard_map/ppermute | solution.py:613
  7.1 5.5 %prepare.1 = (bf16[2,144,256]{2,1,0:T(8,128)(2,1)}, bf16[2,144,256]{2,1,0:T(8,128)(2,1)}, bf16[2,144,256]{2,1,0:T(8,128)(2,1)}, s32[8]{0:T(128)}, f32[48,512]{1,0:T(8,128)}, /*index=5*/f32[48,512]{1,0:T(8,128)}) custom-call(s32[24]{0:T(128)} %dest_ref.5, s32[24]{0:T(128)} %length_ref.5, bf16[2,24,2560]{2,1,0:T(8,128)(2,1)} %hidden_ref.1, ...), custom_call_target="tpu_custom_call" | custom-call | flops 1 | bytes 1 | tf_op jit(solution)/shard_map/prepare/pallas_call | solution.py:169
  12.5 0.1 collective-permute-start
  12.6 1.4 %collective-permute-start.2 = (bf16[2,144,256]{2,1,0:T(8,128)(2,1)}, bf16[2,144,256]{2,1,0:T(8,128)(2,1)S(1)}, u32[]{:S(2)}, u32[]{:S(2)}) collective-permute-start(bf16[2,144,256]{2,1,0:T(8,128)(2,1)} %get-tuple-element.23), channel_id=1, source_target_pairs={{0,10},{2,8},{4,14},{6,12},{8,2},{10,0},{12,6},{14,4},{1,11},{3,9}... | collective-permute-start | bytes 442376 | tf_op jit(solution)/shard_map/ppermute | solution.py:613
  14.0 3.6 %collective-permute-start.3 = (bf16[2,144,256]{2,1,0:T(8,128)(2,1)}, bf16[2,144,256]{2,1,0:T(8,128)(2,1)S(1)}, u32[]{:S(2)}, u32[]{:S(2)}) collective-permute-start(bf16[2,144,256]{2,1,0:T(8,128)(2,1)} %get-tuple-element.24), channel_id=1, source_target_pairs={{0,12},{2,14},{4,8},{6,10},{8,4},{10,6},{12,0},{14,2},{1,13},{3,15... | collective-permute-start | bytes 442376 | tf_op jit(solution)/shard_map/ppermute | solution.py:613
  17.6 0.0 collective-permute-start.4
  17.6 0.0 collective-permute-done.got_ref
  17.6 0.0 collective-permute-done.1.refs_0_
  17.6 0.6 %copy-done.3 = f32[48,512]{1,0:T(8,128)} copy-done((f32[48,512]{1,0:T(8,128)}, f32[48,512]{1,0:T(8,128)S(1)}, u32[]{:S(2)}) %copy-start.3) | copy-done | bytes 98328
  18.2 0.1 copy-done.1
  18.3 6.9 %attend.1 = (bf16[24,2,144,256]{3,2,1,0:T(8,128)(2,1)}, bf16[768,128]{1,0:T(8,128)(2,1)}, bf16[8,48,128]{2,1,0:T(8,128)(2,1)}, bf16[2,144,256]{2,1,0:T(8,128)(2,...) custom-call(s32[24]{0:T(128)} %length_ref.5, s32[24]{0:T(128)} %dest_ref.5, s32[8]{0:T(128)} %get-tuple-element.18.pick_ref, ...), custom_call_target="tpu_custom_call" | custom-call | flops 68719476736 | bytes 268435456 | tf_op jit(solution)/shard_map/attend/pallas_call | solution.py:357
  25.2 4.2 %all-to-all-start = ((bf16[8,48,128]{2,1,0:T(8,128)(2,1)}), bf16[8,48,128]{2,1,0:T(8,128)(2,1)S(1)}, u32[]{:S(2)}, u32[]{:S(2)}) async-start(bf16[8,48,128]{2,1,0:T(8,128)(2,1)} %get-tuple-element.22), calls=%async_computation | async-start | bytes 196608 | tf_op jit(solution)/shard_map/all_to_all | solution.py:644
  29.4 4.7 %collective-permute-start.5 = (bf16[2,144,256]{2,1,0:T(8,128)(2,1)}, bf16[2,144,256]{2,1,0:T(8,128)(2,1)S(1)}, u32[]{:S(2)}, u32[]{:S(2)}) collective-permute-start(bf16[2,144,256]{2,1,0:T(8,128)(2,1)} %get-tuple-element.30), channel_id=1, source_target_pairs={{0,14},{2,12},{4,10},{6,8},{8,6},{10,4},{12,2},{14,0},{1,15},{3,13... | collective-permute-start | bytes 442376 | tf_op jit(solution)/shard_map/ppermute | solution.py:613
  34.1 0.0 collective-permute-start.6
  34.1 0.0 collective-permute-done.2.refs_1_
  34.1 0.6 %collective-permute-start.7 = (bf16[2,144,256]{2,1,0:T(8,128)(2,1)}, bf16[2,144,256]{2,1,0:T(8,128)(2,1)S(1)}, u32[]{:S(2)}, u32[]{:S(2)}) collective-permute-start(bf16[2,144,256]{2,1,0:T(8,128)(2,1)} %get-tuple-element.32), channel_id=1, source_target_pairs={{0,2},{2,0},{4,6},{6,4},{8,10},{10,8},{12,14},{14,12},{1,3},{3,1},... | collective-permute-start | bytes 442376 | tf_op jit(solution)/shard_map/ppermute | solution.py:613
  34.7 0.9 %copy-done.2 = bf16[2,144,256]{2,1,0:T(8,128)(2,1)S(1)} copy-done((bf16[2,144,256]{2,1,0:T(8,128)(2,1)S(1)}, bf16[2,144,256]{2,1,0:T(8,128)(2,1)}, u32[]{:S(2)}) %copy-start.2) | copy-done | bytes 147480
  35.6 1.0 %land.1 = (bf16[24,2,144,256]{3,2,1,0:T(8,128)(2,1)}, bf16[4,2,32,256]{3,2,1,0:T(8,128)(2,1)S(1)}) custom-call(bf16[2,144,256]{2,1,0:T(8,128)(2,1)S(1)} %copy-done.2, bf16[2,144,256]{2,1,0:T(8,128)(2,1)S(1)} %collective-permute-done.2.refs_1_, bf16[2,144,256]{2,1,0:T(8,128)(2,1)S(1)} %collective-permute-done.3.refs_2_, ...), custom_call_target="tpu_custom_call", output_to_operand_aliasing={{0}: (4, {})} | custom-call | flops 68719476736 | bytes 268435456 | tf_op jit(solution)/shard_map/land/pallas_call | solution.py:446
  36.6 1.6 %all-to-all-done.small_ref.refs_3_ = bf16[8,48,128]{2,1,0:T(8,128)(2,1)S(1)} async-done(((bf16[8,48,128]{2,1,0:T(8,128)(2,1)}), bf16[8,48,128]{2,1,0:T(8,128)(2,1)S(1)}, u32[]{:S(2)}, u32[]{:S(2)}) %all-to-all-start) | async-done | bytes 98336 | tf_op jit(solution)/shard_map/all_to_all | solution.py:644
  38.3 1.6 %settle.1 = (bf16[2,24,2048]{2,1,0:T(8,128)(2,1)}, bf16[24,2,144,256]{3,2,1,0:T(8,128)(2,1)}) custom-call(bf16[768,128]{1,0:T(8,128)(2,1)S(1)} %copy-done, bf16[8,48,128]{2,1,0:T(8,128)(2,1)S(1)} %all-to-all-done.small_ref.refs_3_, bf16[4,2,32,256]{3,2,1,0:T(8,128)(2,1)S(1)} %get-tuple-element.27.window_ref, ...), custom_call_target="tpu_custom_call", output_to_operand_aliasing={{1}: (3, {})} | custom-call | flops 1 | bytes 1 | tf_op jit(solution)/shard_map/settle/pallas_call | solution.py:542
  39.9 0.7 %collective-permute-done.5.refs_0_ = bf16[2,144,256]{2,1,0:T(8,128)(2,1)S(1)} collective-permute-done((bf16[2,144,256]{2,1,0:T(8,128)(2,1)}, bf16[2,144,256]{2,1,0:T(8,128)(2,1)S(1)}, u32[]{:S(2)}, u32[]{:S(2)}) %collective-permute-start.5) | collective-permute-done | bytes 147488 | tf_op jit(solution)/shard_map/ppermute | solution.py:613
  40.6 1.0 %collective-permute-done.6.refs_1_ = bf16[2,144,256]{2,1,0:T(8,128)(2,1)S(1)} collective-permute-done((bf16[2,144,256]{2,1,0:T(8,128)(2,1)}, bf16[2,144,256]{2,1,0:T(8,128)(2,1)S(1)}, u32[]{:S(2)}, u32[]{:S(2)}) %collective-permute-start.6) | collective-permute-done | bytes 147488 | tf_op jit(solution)/shard_map/ppermute | solution.py:613
  41.6 0.9 %finish.1 = bf16[24,2,144,256]{3,2,1,0:T(8,128)(2,1)} custom-call(bf16[2,144,256]{2,1,0:T(8,128)(2,1)S(1)} %collective-permute-done.5.refs_0_, bf16[2,144,256]{2,1,0:T(8,128)(2,1)S(1)} %collective-permute-done.6.refs_1_, bf16[2,144,256]{2,1,0:T(8,128)(2,1)S(1)} %collective-permute-done.7.refs_2_, ...), custom_call_target="tpu_custom_call", output_to_operand_aliasing={{}: (4, {})} | custom-call | flops 1 | bytes 1 | tf_op jit(solution)/shard_map/finish/pallas_call | solution.py:587
  (8 shorter events, 0.0 us)
Async XLA Ops:
  2.9 14.6 %collective-permute-start.1 = (bf16[2,144,256]{2,1,0:T(8,128)(2,1)}, bf16[2,144,256]{2,1,0:T(8,128)(2,1)S(1)}, u32[]{:S(2)}, u32[]{:S(2)}) collective-permute-start(bf16[2,144,256]{2,1,0:T(8,128)(2,1)} %pack.1.refs_0_), channel_id=1, source_target_pairs={{0,8},{2,10},{4,12},{6,14},{8,0},{10,2},{12,4},{14,6},{1,9},{3,11}... | collective-permute-start | bytes 442376 | tf_op jit(solution)/shard_map/ppermute | solution.py:613
  12.5 5.0 %collective-permute-start = (f32[48,512]{1,0:T(8,128)}, f32[48,512]{1,0:T(8,128)S(1)}, u32[]{:S(2)}, u32[]{:S(2)}) collective-permute-start(f32[48,512]{1,0:T(8,128)} %get-tuple-element.20), channel_id=1, source_target_pairs={{0,1},{1,0},{2,3},{3,2},{4,5},{5,4},{6,7},{7,6},{8,9},{9,8},{10,11... | collective-permute-start | bytes 294920 | tf_op jit(solution)/shard_map/ppermute | solution.py:629
  12.6 21.5 %collective-permute-start.2 = (bf16[2,144,256]{2,1,0:T(8,128)(2,1)}, bf16[2,144,256]{2,1,0:T(8,128)(2,1)S(1)}, u32[]{:S(2)}, u32[]{:S(2)}) collective-permute-start(bf16[2,144,256]{2,1,0:T(8,128)(2,1)} %get-tuple-element.23), channel_id=1, source_target_pairs={{0,10},{2,8},{4,14},{6,12},{8,2},{10,0},{12,6},{14,4},{1,11},{3,9}... | collective-permute-start | bytes 442376 | tf_op jit(solution)/shard_map/ppermute | solution.py:613
  14.0 20.7 %collective-permute-start.3 = (bf16[2,144,256]{2,1,0:T(8,128)(2,1)}, bf16[2,144,256]{2,1,0:T(8,128)(2,1)S(1)}, u32[]{:S(2)}, u32[]{:S(2)}) collective-permute-start(bf16[2,144,256]{2,1,0:T(8,128)(2,1)} %get-tuple-element.24), channel_id=1, source_target_pairs={{0,12},{2,14},{4,8},{6,10},{8,4},{10,6},{12,0},{14,2},{1,13},{3,15... | collective-permute-start | bytes 442376 | tf_op jit(solution)/shard_map/ppermute | solution.py:613
  17.6 17.1 %collective-permute-start.4 = (bf16[2,144,256]{2,1,0:T(8,128)(2,1)}, bf16[2,144,256]{2,1,0:T(8,128)(2,1)S(1)}, u32[]{:S(2)}, u32[]{:S(2)}) collective-permute-start(bf16[2,144,256]{2,1,0:T(8,128)(2,1)} %get-tuple-element.25), channel_id=1, source_target_pairs={{0,6},{2,4},{4,2},{6,0},{8,14},{10,12},{12,10},{14,8},{1,7},{3,5},... | collective-permute-start | bytes 442376 | tf_op jit(solution)/shard_map/ppermute | solution.py:613
  17.6 0.6 %copy-start.3 = (f32[48,512]{1,0:T(8,128)}, f32[48,512]{1,0:T(8,128)S(1)}, u32[]{:S(2)}) copy-start(f32[48,512]{1,0:T(8,128)S(1)} %collective-permute-done.got_ref) | copy-start | bytes 294916
  17.6 0.7 %copy-start.1 = (bf16[2,144,256]{2,1,0:T(8,128)(2,1)}, bf16[2,144,256]{2,1,0:T(8,128)(2,1)S(1)}, u32[]{:S(2)}) copy-start(bf16[2,144,256]{2,1,0:T(8,128)(2,1)S(1)} %collective-permute-done.1.refs_0_) | copy-start | bytes 442372
  25.2 13.1 %all-to-all-start = ((bf16[8,48,128]{2,1,0:T(8,128)(2,1)}), bf16[8,48,128]{2,1,0:T(8,128)(2,1)S(1)}, u32[]{:S(2)}, u32[]{:S(2)}) async-start(bf16[8,48,128]{2,1,0:T(8,128)(2,1)} %get-tuple-element.22), calls=%async_computation | async-start | bytes 196608 | tf_op jit(solution)/shard_map/all_to_all | solution.py:644
  29.4 11.2 %collective-permute-start.5 = (bf16[2,144,256]{2,1,0:T(8,128)(2,1)}, bf16[2,144,256]{2,1,0:T(8,128)(2,1)S(1)}, u32[]{:S(2)}, u32[]{:S(2)}) collective-permute-start(bf16[2,144,256]{2,1,0:T(8,128)(2,1)} %get-tuple-element.30), channel_id=1, source_target_pairs={{0,14},{2,12},{4,10},{6,8},{8,6},{10,4},{12,2},{14,0},{1,15},{3,13... | collective-permute-start | bytes 442376 | tf_op jit(solution)/shard_map/ppermute | solution.py:613
  34.1 7.5 %collective-permute-start.6 = (bf16[2,144,256]{2,1,0:T(8,128)(2,1)}, bf16[2,144,256]{2,1,0:T(8,128)(2,1)S(1)}, u32[]{:S(2)}, u32[]{:S(2)}) collective-permute-start(bf16[2,144,256]{2,1,0:T(8,128)(2,1)} %get-tuple-element.31), channel_id=1, source_target_pairs={{0,4},{2,6},{4,0},{6,2},{8,12},{10,14},{12,8},{14,10},{1,5},{3,7},... | collective-permute-start | bytes 442376 | tf_op jit(solution)/shard_map/ppermute | solution.py:613
  34.1 7.5 %collective-permute-start.7 = (bf16[2,144,256]{2,1,0:T(8,128)(2,1)}, bf16[2,144,256]{2,1,0:T(8,128)(2,1)S(1)}, u32[]{:S(2)}, u32[]{:S(2)}) collective-permute-start(bf16[2,144,256]{2,1,0:T(8,128)(2,1)} %get-tuple-element.32), channel_id=1, source_target_pairs={{0,2},{2,0},{4,6},{6,4},{8,10},{10,8},{12,14},{14,12},{1,3},{3,1},... | collective-permute-start | bytes 442376 | tf_op jit(solution)/shard_map/ppermute | solution.py:613
  34.7 0.9 %copy-start.2 = (bf16[2,144,256]{2,1,0:T(8,128)(2,1)S(1)}, bf16[2,144,256]{2,1,0:T(8,128)(2,1)}, u32[]{:S(2)}) copy-start(bf16[2,144,256]{2,1,0:T(8,128)(2,1)} %copy-done.1) | copy-start | bytes 442372
  35.6 2.7 %copy-start = (bf16[768,128]{1,0:T(8,128)(2,1)S(1)}, bf16[768,128]{1,0:T(8,128)(2,1)}, u32[]{:S(2)}) copy-start(bf16[768,128]{1,0:T(8,128)(2,1)} %get-tuple-element.21.mixed_ref) | copy-start | bytes 589828

commit v13 on v12

--- a/solution.py
+++ b/solution.py
@@ -14,6 +14,7 @@
 VMEM_LIMIT = 62 * 1024 * 1024
 ATTEND_LIMIT = 56 * 1024 * 1024
 SMALL_LIMIT = 40 * 1024 * 1024
+LAND_LIMIT = 52 * 1024 * 1024
 LIGHT = pl.CostEstimate(flops=1, bytes_accessed=1, transcendentals=0)
 HEAVY = pl.CostEstimate(flops=1 << 36, bytes_accessed=1 << 28, transcendentals=0)
 TILE = 16
@@ -27,6 +28,10 @@
     ):
         return (value * factor) >> 16
     return value // divisor
+
+
+def near_size(count):
+    return 4 if count >= 8 and count & (count - 1) == 0 else 1
 
 
 def peer_to(index, shift, count):
@@ -57,46 +62,14 @@
     block[0, capacity - TILE :, :] = jnp.where(last, facts, end).astype(jnp.bfloat16)
 
 
-def pack_kernel(count, shift, dest_ref, length_ref, kv_ref, block_ref, block, sem, pick):
-    pick_rows(count, dest_ref, pick)
-    peer = peer_to(lax.axis_index("inst"), shift, count)
-    row = pick[peer]
-    fetch = pltpu.make_async_copy(kv_ref.at[row], block, sem)
-    fetch.start()
-    fetch.wait()
-    add_facts(block, peer, row, dest_ref, length_ref)
-    store = pltpu.make_async_copy(block, block_ref, sem)
-    store.start()
-    store.wait()
-
-
-def pack(kv_cache, destination, lengths, count, shift):
-    smem = pl.BlockSpec(memory_space=pltpu.SMEM)
-    hbm = pl.BlockSpec(memory_space=pl.ANY)
-    return pl.pallas_call(
-        functools.partial(pack_kernel, count, shift),
-        out_shape=jax.ShapeDtypeStruct(kv_cache.shape[1:], kv_cache.dtype),
-        in_specs=[smem, smem, hbm],
-        out_specs=hbm,
-        scratch_shapes=[
-            pltpu.VMEM(kv_cache.shape[1:], kv_cache.dtype),
-            pltpu.SemaphoreType.DMA,
-            pltpu.SMEM((count,), jnp.int32),
-        ],
-        compiler_params=pltpu.CompilerParams(vmem_limit_bytes=VMEM_LIMIT),
-        cost_estimate=LIGHT,
-        name="pack",
-    )(destination, lengths, kv_cache)
-
-
 def prepare_kernel(
-    count, early, chunks, dest_ref, length_ref, hidden_ref, kv_ref, key_ref, value_ref, *refs
+    count, early, near, chunks, dest_ref, length_ref, hidden_ref, kv_ref, key_ref, value_ref, *refs
 ):
-    block_refs = refs[1 : len(early) + 1]
-    pick_ref, own_ref, other_ref, blocks, hidden_held, held, total = refs[
-        len(early) + 1 : len(early) + 8
-    ]
-    in_sems, out_sems, hidden_sem, weight_sems = refs[len(early) + 8 :]
+    outs = len(early) + (near > 1)
+    block_refs = list(refs[: len(early)]) + [refs[len(early)].at[i] for i in range(near - 1)]
+    early = list(early) + list(range(1, near))
+    pick_ref, own_ref, other_ref, blocks, hidden_held, held, total = refs[outs : outs + 7]
+    in_sems, out_sems, hidden_sem, weight_sems = refs[outs + 7 :]
     steps, rows, depth = hidden_ref.shape
     width = key_ref.shape[1]
     part = depth // chunks
@@ -158,7 +131,7 @@
         copy.wait()
 
 
-def prepare(destination, lengths, hidden_new, kv_cache, key_weight, value_weight, count, early, first):
+def prepare(destination, lengths, hidden_new, kv_cache, key_weight, value_weight, count, early, near):
     steps, rows, depth = hidden_new.shape
     width = key_weight.shape[1]
     chunks = 5
@@ -166,27 +139,32 @@
     smem = pl.BlockSpec(memory_space=pltpu.SMEM)
     vmem = pl.BlockSpec(memory_space=pltpu.VMEM)
     hbm = pl.BlockSpec(memory_space=pl.ANY)
+    block = kv_cache.shape[1:]
+    shapes = [jax.ShapeDtypeStruct(block, kv_cache.dtype)] * len(early)
+    if near > 1:
+        shapes.append(jax.ShapeDtypeStruct((near - 1,) + block, kv_cache.dtype))
+    pieces = len(early) + near - 1
     outs = pl.pallas_call(
-        functools.partial(prepare_kernel, count, early, chunks),
-        out_shape=[jax.ShapeDtypeStruct(kv_cache.shape[1:], kv_cache.dtype)] * len(early)
+        functools.partial(prepare_kernel, count, early, near, chunks),
+        out_shape=shapes
         + [jax.ShapeDtypeStruct((count,), jnp.int32), part, part],
-        in_specs=[smem, smem, hbm, hbm, hbm, hbm, hbm],
-        out_specs=[hbm] * len(early) + [smem, vmem, vmem],
+        in_specs=[smem, smem, hbm, hbm, hbm, hbm],
+        out_specs=[hbm] * len(shapes) + [smem, vmem, vmem],
         scratch_shapes=[
-            pltpu.VMEM((len(early),) + kv_cache.shape[1:], kv_cache.dtype),
+            pltpu.VMEM((pieces,) + block, kv_cache.dtype),
             pltpu.VMEM(hidden_new.shape, hidden_new.dtype),
             pltpu.VMEM((2, depth, width), key_weight.dtype),
             pltpu.VMEM((steps * rows, 2 * width), jnp.float32),
-            pltpu.SemaphoreType.DMA((len(early),)),
-            pltpu.SemaphoreType.DMA((len(early),)),
+            pltpu.SemaphoreType.DMA((pieces,)),
+            pltpu.SemaphoreType.DMA((pieces,)),
             pltpu.SemaphoreType.DMA,
             pltpu.SemaphoreType.DMA((chunks, 2)),
         ],
         compiler_params=pltpu.CompilerParams(vmem_limit_bytes=VMEM_LIMIT),
         cost_estimate=LIGHT,
         name="prepare",
-    )(destination, lengths, hidden_new, kv_cache, key_weight, value_weight, first)
-    return outs[: len(early)], *outs[len(early) :]
+    )(destination, lengths, hidden_new, kv_cache, key_weight, value_weight)
+    return outs[: len(shapes)], *outs[len(shapes) :]
 
 
 def rotation(length_ref, steps, rows):
@@ -225,8 +203,8 @@
     kv_ref,
     *refs,
 ):
-    moved_ref, mixed_ref, small_ref = refs[1:4]
-    late_refs = refs[4:-4]
+    moved_ref, mixed_ref, small_ref = refs[:3]
+    late_refs = refs[3:-4]
     fresh, query_rows, query_columns, mixed = refs[-4:]
     part = pl.program_id(0)
     steps, rows, query_width = query_ref.shape
@@ -342,7 +320,7 @@
             small_ref[peer, per_row:, :] = jnp.concatenate(news, axis=0).astype(jnp.bfloat16)
 
 
-def attend(kv_cache, queries, own, got, gain, lengths, destination, pick, count, late, arrived):
+def attend(kv_cache, queries, own, got, gain, lengths, destination, pick, count, late):
     steps, rows, query_width = queries.shape
     capacity, lanes = kv_cache.shape[2:]
     heads = lanes // HD
@@ -352,7 +330,6 @@
     small = jax.ShapeDtypeStruct((count, small_rows, HD), jnp.bfloat16)
     smem = pl.BlockSpec(memory_space=pltpu.SMEM)
     vmem = pl.BlockSpec(memory_space=pltpu.VMEM)
-    hbm = pl.BlockSpec(memory_space=pl.ANY)
     cache_block = pl.BlockSpec((block, 2, capacity, lanes), lambda i: (i, 0, 0, 0))
     return pl.pallas_call(
         functools.partial(attend_kernel, count, late, block),
@@ -363,7 +340,7 @@
             small,
         ]
         + [jax.ShapeDtypeStruct(kv_cache.shape[1:], kv_cache.dtype)] * len(late),
-        in_specs=[smem, smem, smem, vmem, vmem, vmem, vmem, cache_block, hbm],
+        in_specs=[smem, smem, smem, vmem, vmem, vmem, vmem, cache_block],
         out_specs=[cache_block, vmem, vmem] + [vmem] * len(late),
         scratch_shapes=[
             pltpu.VMEM((2, steps * rows, lanes), jnp.float32),
@@ -374,7 +351,7 @@
         compiler_params=pltpu.CompilerParams(vmem_limit_bytes=ATTEND_LIMIT),
         cost_estimate=HEAVY,
         name="attend",
-    )(lengths, destination, pick, own, got, gain, queries, kv_cache, arrived)
+    )(lengths, destination, pick, own, got, gain, queries, kv_cache)
 
 
 def read_facts(block):
@@ -412,17 +389,30 @@
         out[which] = stored.astype(jnp.bfloat16)
 
 
-def land_kernel(pieces, *refs):
-    blocks = refs[:pieces]
-    _, out_ref, window_ref, buffer, sems, slots = refs[pieces:]
+def land_kernel(early, near, *refs):
+    blocks = list(refs[:early])
+    if near > 1:
+        gathered_ref = refs[early]
+        held, held_sems = refs[-2:]
+        me = lax.axis_index("inst") % near
+        fetches = [
+            pltpu.make_async_copy(
+                gathered_ref.at[me ^ shift, shift - 1], held.at[shift - 1], held_sems.at[shift - 1]
+            )
+            for shift in range(1, near)
+        ]
+        for copy in fetches:
+            copy.start()
+        blocks += [held.at[i] for i in range(near - 1)]
+    _, out_ref, window_ref, buffer, sems, slots = refs[early + (near > 1) :][:6]
     capacity = buffer.shape[2]
 
     def store(piece):
         slot = jnp.maximum(slots[piece], 0)
         return pltpu.make_async_copy(buffer.at[piece], out_ref.at[slot], sems.at[piece])
 
-    facts = [read_facts(block) for block in blocks]
-    for piece, (slot, length) in enumerate(facts):
+    def take(piece):
+        slot, length = read_facts(blocks[piece])
         slots[piece] = slot
 
         @pl.when(slot >= 0)
@@ -432,35 +422,47 @@
             start = window_start(length, capacity)
             window_ref[piece] = buffer[piece, :, pl.ds(start, WINDOW), :]
 
-    for piece in range(pieces):
+    for piece in range(len(blocks)):
+        if piece >= early:
+            fetches[piece - early].wait()
+        take(piece)
+    for piece in range(len(blocks)):
 
         @pl.when(slots[piece] >= 0)
         def _():
             store(piece).wait()
 
 
-def land(got, moved):
-    pieces = len(got)
+def land(got, gathered, moved):
+    near = gathered[0].shape[0] if gathered else 1
+    pieces = len(got) + near - 1
     vmem = pl.BlockSpec(memory_space=pltpu.VMEM)
     hbm = pl.BlockSpec(memory_space=pl.ANY)
+    extra = []
+    if near > 1:
+        extra = [
+            pltpu.VMEM((near - 1,) + moved.shape[1:], moved.dtype),
+            pltpu.SemaphoreType.DMA((near - 1,)),
+        ]
     return pl.pallas_call(
-        functools.partial(land_kernel, pieces),
+        functools.partial(land_kernel, len(got), near),
         out_shape=[
             jax.ShapeDtypeStruct(moved.shape, moved.dtype),
             jax.ShapeDtypeStruct((pieces, 2, WINDOW, moved.shape[3]), moved.dtype),
         ],
-        in_specs=[vmem] * pieces + [hbm],
+        in_specs=[vmem] * len(got) + [hbm] * len(gathered) + [hbm],
         out_specs=[hbm, vmem],
         scratch_shapes=[
             pltpu.VMEM((pieces,) + moved.shape[1:], moved.dtype),
             pltpu.SemaphoreType.DMA((pieces,)),
             pltpu.SMEM((pieces,), jnp.int32),
-        ],
-        input_output_aliases={pieces: 0},
-        compiler_params=pltpu.CompilerParams(vmem_limit_bytes=SMALL_LIMIT),
+        ]
+        + extra,
+        input_output_aliases={len(got) + len(gathered): 0},
+        compiler_params=pltpu.CompilerParams(vmem_limit_bytes=LAND_LIMIT),
         cost_estimate=HEAVY,
         name="land",
-    )(*got, moved)
+    )(*got, *gathered, moved)
 
 
 def read_small(small_ref, peer, per_row, line):
@@ -604,28 +606,22 @@
     steps = queries.shape[0]
     group = queries.shape[2] // kv_cache.shape[3]
     count = lax.axis_size("inst")
-    half = max(count // 2, 1)
-    early = list(range(half, count - 1)) + [half - 1] * (half > 1)
-    late = [count - 1] + list(range(half - 2, 0, -1))
+    near = near_size(count)
+    early = list(range(near, count - 1))
+    late = [count - 1]
 
     def send(block, shift):
         pairs = [(i, peer_to(i, shift, count)) for i in range(count)]
         return lax.ppermute(block, "inst", pairs)
 
-    first = pack(kv_cache, destination, lengths, count, early[0])
-    first_got = send(first, early[0])
     blocks, pick, own, other = prepare(
-        destination,
-        lengths,
-        hidden_new,
-        kv_cache,
-        key_weight,
-        value_weight,
-        count,
-        early[1:],
-        first,
+        destination, lengths, hidden_new, kv_cache, key_weight, value_weight, count, early, near
     )
-    early_got = [first_got] + [send(block, shift) for block, shift in zip(blocks, early[1:])]
+    early_got = [send(block, shift) for block, shift in zip(blocks, early)]
+    gathered = []
+    if near > 1:
+        teams = [list(range(i, i + near)) for i in range(0, count, near)]
+        gathered = [lax.all_gather(blocks[-1], "inst", axis_index_groups=teams)]
     got = lax.ppermute(other, "tp", [(0, 1), (1, 0)])
     moved, mixed, small, *late_blocks = attend(
         kv_cache,
@@ -638,12 +634,12 @@
         pick,
         count,
         late,
-        first_got,
     )
     late_got = [send(block, shift) for block, shift in zip(late_blocks, late)]
     small_got = lax.all_to_all(small, "inst", 0, 0, tiled=True)
-    moved, windows = land(early_got, moved)
-    attended, moved = settle(mixed, small_got, windows, moved, queries.shape, group, count, early)
+    moved, windows = land(early_got, gathered, moved)
+    landed = early + list(range(1, near))
+    attended, moved = settle(mixed, small_got, windows, moved, queries.shape, group, count, landed)
     return attended, finish(late_got, small_got, moved, steps, count, late)
 
 

time: 42.9 us -> 75.3 us (1.76)
  waiting for transfers between devices: 3.41 us -> 25.9 us
  between operations: 0.7 us -> 14.1 us
  starting transfers between devices: 18.6 us -> 17.1 us
  Pallas kernels: 18.2 us -> 17.2 us
  local copies, waits for them, and re-layouts: 1.59 us -> 0.65 us
    all_gather x0 -> x1, waiting for transfers between devices: none -> 25.8 us  [local(): gathered = [lax.all_gather(blocks[-1], 'inst', axis_index_groups=teams)]]
    ppermute x7 -> x4, waiting for transfers between devices: 1.77 us -> 0.01 us  [send(): return lax.ppermute(block, 'inst', pairs)]
    all_to_all x1, waiting for transfers between devices: 1.63 us -> 0.01 us  [local(): small_got = lax.all_to_all(small, 'inst', 0, 0, tiled=True)]
    ppermute x7 -> x4, starting transfers between devices: 14.4 us -> 13.2 us  [send(): return lax.ppermute(block, 'inst', pairs)]
    unnamed x8 -> x4, local copies, waits for them, and re-layouts: 1.59 us -> 0.65 us
    pallas_call x3 -> x2, Pallas kernels: 8.79 us -> 7.94 us  [the longest x1 5.76 us: prepare(): pl.pallas_call(functools.partial(prepare_kernel, count, early, near, chun...]
    all_to_all x1, starting transfers between devices: 4.2 us -> 3.36 us  [local(): small_got = lax.all_to_all(small, 'inst', 0, 0, tiled=True)]
  transfers between devices with their start and end apart: 9 -> 7, of which waited for: 3 -> 1; matrix products, arithmetic and copies ran while one was open for 0% -> 0% of each run, Pallas kernels for 35% -> 14%
where the time goes in v13:
time: 75.3 us; the launch traced here: 75 us
  waiting for transfers between devices  25.9 us (34%)
  Pallas kernels  17.2 us (23%)
  starting transfers between devices  17.1 us (23%)
  between operations  14.1 us (19%)
    all_gather x1, waiting for transfers between devices, local(): gathered = [lax.all_gather(blocks[-1], 'inst', axis_index_groups=teams)]  25.8 us
    ppermute x4, starting transfers between devices, send(): return lax.ppermute(block, 'inst', pairs)  13.2 us
    pallas_call x1, Pallas kernels, attend(): pl.pallas_call(functools.partial(attend_kernel, count, late, block), grid...  6.83 us
    pallas_call x1, Pallas kernels, prepare(): pl.pallas_call(functools.partial(prepare_kernel, count, early, near, chun...  5.76 us
    all_to_all x1, starting transfers between devices, local(): small_got = lax.all_to_all(small, 'inst', 0, 0, tiled=True)  3.36 us
    pallas_call x1, Pallas kernels, land(): pl.pallas_call(functools.partial(land_kernel, len(got), near), out_shape=...  2.18 us
    pallas_call x1, Pallas kernels, settle(): pl.pallas_call(functools.partial(settle_kernel, count, early, group), out...  1.65 us
  transfers between devices with their start and end apart: 7, of which 1 were waited for; matrix products, arithmetic and copies ran while one was open for 0% of the time, Pallas kernels for 14%

profile of v13, /device:TPU:0, one launch (start us, length us, event | category | flops | bytes accessed | tf_op | source)
XLA Modules:
  0.0 75.0 jit_solution(13396011651874164426)
XLA Ops:
  7.2 0.0 all-gather.3.cloned.1.call-start
  7.2 5.8 %prepare.1 = (bf16[2,144,256]{2,1,0:T(8,128)(2,1)}, bf16[2,144,256]{2,1,0:T(8,128)(2,1)}, bf16[2,144,256]{2,1,0:T(8,128)(2,1)}, bf16[3,2,144,256]{3,2,1,0:T(8,12...) custom-call(s32[24]{0:T(128)} %dest_ref.3, s32[24]{0:T(128)} %length_ref.3, ...), custom_call_target="tpu_custom_call" | custom-call | flops 1 | bytes 1 | tf_op jit(solution)/shard_map/prepare/pallas_call | solution.py:147
  13.0 0.5 collective-permute-start
  13.5 0.0 all-gather.3.cloned.1.call-update
  13.5 3.7 %collective-permute-start.1 = (bf16[2,144,256]{2,1,0:T(8,128)(2,1)}, bf16[2,144,256]{2,1,0:T(8,128)(2,1)S(1)}, u32[]{:S(2)}, u32[]{:S(2)}) collective-permute-start(bf16[2,144,256]{2,1,0:T(8,128)(2,1)} %get-tuple-element.22), channel_id=1, source_target_pairs={{0,8},{2,10},{4,12},{6,14},{8,0},{10,2},{12,4},{14,6},{1,9},{3,11}... | collective-permute-start | bytes 442376 | tf_op jit(solution)/shard_map/ppermute | solution.py:615
  17.2 1.3 %collective-permute-start.2 = (bf16[2,144,256]{2,1,0:T(8,128)(2,1)}, bf16[2,144,256]{2,1,0:T(8,128)(2,1)S(1)}, u32[]{:S(2)}, u32[]{:S(2)}) collective-permute-start(bf16[2,144,256]{2,1,0:T(8,128)(2,1)} %get-tuple-element.23), channel_id=1, source_target_pairs={{0,10},{2,8},{4,14},{6,12},{8,2},{10,0},{12,6},{14,4},{1,11},{3,9}... | collective-permute-start | bytes 442376 | tf_op jit(solution)/shard_map/ppermute | solution.py:615
  18.5 3.6 %collective-permute-start.3 = (bf16[2,144,256]{2,1,0:T(8,128)(2,1)}, bf16[2,144,256]{2,1,0:T(8,128)(2,1)S(1)}, u32[]{:S(2)}, u32[]{:S(2)}) collective-permute-start(bf16[2,144,256]{2,1,0:T(8,128)(2,1)} %get-tuple-element.24), channel_id=1, source_target_pairs={{0,12},{2,14},{4,8},{6,10},{8,4},{10,6},{12,0},{14,2},{1,13},{3,15... | collective-permute-start | bytes 442376 | tf_op jit(solution)/shard_map/ppermute | solution.py:615
  22.1 0.0 collective-permute-done.got_ref
  22.1 0.0 copy-start.1
  22.1 0.6 copy-done.1
  22.7 6.8 %attend.1 = (bf16[24,2,144,256]{3,2,1,0:T(8,128)(2,1)}, bf16[768,128]{1,0:T(8,128)(2,1)}, bf16[8,48,128]{2,1,0:T(8,128)(2,1)}, bf16[2,144,256]{2,1,0:T(8,128)(2,1)}) custom-call(s32[24]{0:T(128)} %length_ref.3, s32[24]{0:T(128)} %dest_ref.3, s32[8]{0:T(128)} %get-tuple-element.17.pick_ref, f32[48,512]{1,0:T(8,128)} %get-tuple-element.18.own_ref, ...), custom_call_target="tpu_custom_call" | custom-call | flops 68719476736 | bytes 268435456 | tf_op jit(solution)/shard_map/attend/pallas_call | solution.py:334
  29.6 3.4 %all-to-all-start = ((bf16[8,48,128]{2,1,0:T(8,128)(2,1)}), bf16[8,48,128]{2,1,0:T(8,128)(2,1)S(1)}, u32[]{:S(2)}, u32[]{:S(2)}) async-start(bf16[8,48,128]{2,1,0:T(8,128)(2,1)} %get-tuple-element.21), calls=%async_computation | async-start | bytes 196608 | tf_op jit(solution)/shard_map/all_to_all | solution.py:639
  32.9 4.7 %collective-permute-start.4 = (bf16[2,144,256]{2,1,0:T(8,128)(2,1)}, bf16[2,144,256]{2,1,0:T(8,128)(2,1)S(1)}, u32[]{:S(2)}, u32[]{:S(2)}) collective-permute-start(bf16[2,144,256]{2,1,0:T(8,128)(2,1)} %get-tuple-element.30), channel_id=1, source_target_pairs={{0,14},{2,12},{4,10},{6,8},{8,6},{10,4},{12,2},{14,0},{1,15},{3,13... | collective-permute-start | bytes 442376 | tf_op jit(solution)/shard_map/ppermute | solution.py:615
  37.6 0.0 collective-permute-done.1.refs_0_
  37.6 0.0 collective-permute-done.2.refs_1_
  37.6 0.0 collective-permute-done.3.refs_2_
  37.6 25.8 %all-gather.3.cloned.1.call-done = bf16[12,2,144,256]{3,2,1,0:T(8,128)(2,1)} async-done(((bf16[3,2,144,256]{3,2,1,0:T(8,128)(2,1)}), bf16[12,2,144,256]{3,2,1,0:T(8,128)(2,1)}) %all-gather.3.cloned.1.call-update) | async-done | bytes 1769488 | tf_op jit(solution)/shard_map/all_gather | solution.py:624
  63.4 0.0 copy-start
  63.4 2.2 %land.1 = (bf16[24,2,144,256]{3,2,1,0:T(8,128)(2,1)}, bf16[6,2,32,256]{3,2,1,0:T(8,128)(2,1)S(1)}) custom-call(bf16[2,144,256]{2,1,0:T(8,128)(2,1)S(1)} %collective-permute-done.1.refs_0_, bf16[2,144,256]{2,1,0:T(8,128)(2,1)S(1)} %collective-permute-done.2.refs_1_, ...), custom_call_target="tpu_custom_call", output_to_operand_aliasing={{0}: (4, {})} | custom-call | flops 68719476736 | bytes 268435456 | tf_op jit(solution)/shard_map/land/pallas_call | solution.py:447
  65.6 0.0 all-to-all-done.small_ref.refs_1_
  65.6 0.0 copy-done
  65.6 1.6 %settle.1 = (bf16[2,24,2048]{2,1,0:T(8,128)(2,1)}, bf16[24,2,144,256]{3,2,1,0:T(8,128)(2,1)}) custom-call(bf16[768,128]{1,0:T(8,128)(2,1)S(1)} %copy-done, bf16[8,48,128]{2,1,0:T(8,128)(2,1)S(1)} %all-to-all-done.small_ref.refs_1_, bf16[6,2,32,256]{3,2,1,0:T(8,128)(2,1)S(1)} %get-tuple-element.27.window_ref, ...), custom_call_target="tpu_custom_call", output_to_operand_aliasing={{1}: (3, {})} | custom-call | flops 1 | bytes 1 | tf_op jit(solution)/shard_map/settle/pallas_call | solution.py:544
  67.3 0.0 collective-permute-done.4.refs_0_
  67.3 0.8 %finish.1 = bf16[24,2,144,256]{3,2,1,0:T(8,128)(2,1)} custom-call(bf16[2,144,256]{2,1,0:T(8,128)(2,1)S(1)} %collective-permute-done.4.refs_0_, bf16[8,48,128]{2,1,0:T(8,128)(2,1)S(1)} %all-to-all-done.small_ref.refs_1_, bf16[24,2,144,256]{3,2,1,0:T(8,128)(2,1)} %get-tuple-element.31.refs_2_), custom_call_target="tpu_custom_call", output_to_operand_aliasing={{}: (2, {})} | custom-call | flops 1 | bytes 1 | tf_op jit(solution)/shard_map/finish/pallas_call | solution.py:589
Async XLA Ops:
  7.2 56.3 %all-gather.3.cloned.1.call-start = ((), (), s32[]{:S(2)}) async-start(), calls=%async_computation.1 | async-start | bytes 2211840 | tf_op jit(solution)/shard_map/all_gather | solution.py:624
  13.0 9.1 %collective-permute-start = (f32[48,512]{1,0:T(8,128)}, f32[48,512]{1,0:T(8,128)S(1)}, u32[]{:S(2)}, u32[]{:S(2)}) collective-permute-start(f32[48,512]{1,0:T(8,128)} %get-tuple-element.19), channel_id=1, source_target_pairs={{0,1},{1,0},{2,3},{3,2},{4,5},{5,4},{6,7},{7,6},{8,9},{9,8},{10,11... | collective-permute-start | bytes 294920 | tf_op jit(solution)/shard_map/ppermute | solution.py:625
  13.5 24.1 %collective-permute-start.1 = (bf16[2,144,256]{2,1,0:T(8,128)(2,1)}, bf16[2,144,256]{2,1,0:T(8,128)(2,1)S(1)}, u32[]{:S(2)}, u32[]{:S(2)}) collective-permute-start(bf16[2,144,256]{2,1,0:T(8,128)(2,1)} %get-tuple-element.22), channel_id=1, source_target_pairs={{0,8},{2,10},{4,12},{6,14},{8,0},{10,2},{12,4},{14,6},{1,9},{3,11}... | collective-permute-start | bytes 442376 | tf_op jit(solution)/shard_map/ppermute | solution.py:615
  17.2 20.4 %collective-permute-start.2 = (bf16[2,144,256]{2,1,0:T(8,128)(2,1)}, bf16[2,144,256]{2,1,0:T(8,128)(2,1)S(1)}, u32[]{:S(2)}, u32[]{:S(2)}) collective-permute-start(bf16[2,144,256]{2,1,0:T(8,128)(2,1)} %get-tuple-element.23), channel_id=1, source_target_pairs={{0,10},{2,8},{4,14},{6,12},{8,2},{10,0},{12,6},{14,4},{1,11},{3,9}... | collective-permute-start | bytes 442376 | tf_op jit(solution)/shard_map/ppermute | solution.py:615
  18.5 19.1 %collective-permute-start.3 = (bf16[2,144,256]{2,1,0:T(8,128)(2,1)}, bf16[2,144,256]{2,1,0:T(8,128)(2,1)S(1)}, u32[]{:S(2)}, u32[]{:S(2)}) collective-permute-start(bf16[2,144,256]{2,1,0:T(8,128)(2,1)} %get-tuple-element.24), channel_id=1, source_target_pairs={{0,12},{2,14},{4,8},{6,10},{8,4},{10,6},{12,0},{14,2},{1,13},{3,15... | collective-permute-start | bytes 442376 | tf_op jit(solution)/shard_map/ppermute | solution.py:615
  22.1 0.6 copy-start.1
  29.6 36.1 %all-to-all-start = ((bf16[8,48,128]{2,1,0:T(8,128)(2,1)}), bf16[8,48,128]{2,1,0:T(8,128)(2,1)S(1)}, u32[]{:S(2)}, u32[]{:S(2)}) async-start(bf16[8,48,128]{2,1,0:T(8,128)(2,1)} %get-tuple-element.21), calls=%async_computation | async-start | bytes 196608 | tf_op jit(solution)/shard_map/all_to_all | solution.py:639
  32.9 34.4 %collective-permute-start.4 = (bf16[2,144,256]{2,1,0:T(8,128)(2,1)}, bf16[2,144,256]{2,1,0:T(8,128)(2,1)S(1)}, u32[]{:S(2)}, u32[]{:S(2)}) collective-permute-start(bf16[2,144,256]{2,1,0:T(8,128)(2,1)} %get-tuple-element.30), channel_id=1, source_target_pairs={{0,14},{2,12},{4,10},{6,8},{8,6},{10,4},{12,2},{14,0},{1,15},{3,13... | collective-permute-start | bytes 442376 | tf_op jit(solution)/shard_map/ppermute | solution.py:615
  63.4 2.2 %copy-start = (bf16[768,128]{1,0:T(8,128)(2,1)S(1)}, bf16[768,128]{1,0:T(8,128)(2,1)}, u32[]{:S(2)}) copy-start(bf16[768,128]{1,0:T(8,128)(2,1)} %get-tuple-element.20.mixed_ref) | copy-start | bytes 589828
Sparse Core Ops, SparseCore 0:
  13.6 49.7 all-gather.2

commit v14 on v12

--- a/solution.py
+++ b/solution.py
@@ -12,7 +12,8 @@
 ROPE_BASE = 1000000.0
 NORM_EPS = 1e-06
 VMEM_LIMIT = 62 * 1024 * 1024
-ATTEND_LIMIT = 56 * 1024 * 1024
+ATTEND_LIMIT = 50 * 1024 * 1024
+PREPARE_LIMIT = 53 * 1024 * 1024
 SMALL_LIMIT = 40 * 1024 * 1024
 LIGHT = pl.CostEstimate(flops=1, bytes_accessed=1, transcendentals=0)
 HEAVY = pl.CostEstimate(flops=1 << 36, bytes_accessed=1 << 28, transcendentals=0)
@@ -92,11 +93,9 @@
 def prepare_kernel(
     count, early, chunks, dest_ref, length_ref, hidden_ref, kv_ref, key_ref, value_ref, *refs
 ):
-    block_refs = refs[1 : len(early) + 1]
-    pick_ref, own_ref, other_ref, blocks, hidden_held, held, total = refs[
-        len(early) + 1 : len(early) + 8
-    ]
-    in_sems, out_sems, hidden_sem, weight_sems = refs[len(early) + 8 :]
+    block_refs = refs[: len(early)]
+    own_ref, other_ref, blocks, hidden_held, held, total = refs[len(early) : len(early) + 6]
+    in_sems, out_sems, hidden_sem, weight_sems, pick_ref = refs[len(early) + 6 :]
     steps, rows, depth = hidden_ref.shape
     width = key_ref.shape[1]
     part = depth // chunks
@@ -158,7 +157,7 @@
         copy.wait()
 
 
-def prepare(destination, lengths, hidden_new, kv_cache, key_weight, value_weight, count, early, first):
+def prepare(destination, lengths, hidden_new, kv_cache, key_weight, value_weight, count, early):
     steps, rows, depth = hidden_new.shape
     width = key_weight.shape[1]
     chunks = 5
@@ -169,9 +168,9 @@
     outs = pl.pallas_call(
         functools.partial(prepare_kernel, count, early, chunks),
         out_shape=[jax.ShapeDtypeStruct(kv_cache.shape[1:], kv_cache.dtype)] * len(early)
-        + [jax.ShapeDtypeStruct((count,), jnp.int32), part, part],
-        in_specs=[smem, smem, hbm, hbm, hbm, hbm, hbm],
-        out_specs=[hbm] * len(early) + [smem, vmem, vmem],
+        + [part, part],
+        in_specs=[smem, smem, hbm, hbm, hbm, hbm],
+        out_specs=[hbm] * len(early) + [vmem, vmem],
         scratch_shapes=[
             pltpu.VMEM((len(early),) + kv_cache.shape[1:], kv_cache.dtype),
             pltpu.VMEM(hidden_new.shape, hidden_new.dtype),
@@ -181,11 +180,12 @@
             pltpu.SemaphoreType.DMA((len(early),)),
             pltpu.SemaphoreType.DMA,
             pltpu.SemaphoreType.DMA((chunks, 2)),
-        ],
-        compiler_params=pltpu.CompilerParams(vmem_limit_bytes=VMEM_LIMIT),
+            pltpu.SMEM((count,), jnp.int32),
+        ],
+        compiler_params=pltpu.CompilerParams(vmem_limit_bytes=PREPARE_LIMIT),
         cost_estimate=LIGHT,
         name="prepare",
-    )(destination, lengths, hidden_new, kv_cache, key_weight, value_weight, first)
+    )(destination, lengths, hidden_new, kv_cache, key_weight, value_weight)
     return outs[: len(early)], *outs[len(early) :]
 
 
@@ -217,7 +217,6 @@
     block,
     length_ref,
     dest_ref,
-    pick_ref,
     own_ref,
     got_ref,
     gain_ref,
@@ -226,8 +225,8 @@
     *refs,
 ):
     moved_ref, mixed_ref, small_ref = refs[1:4]
-    late_refs = refs[4:-4]
-    fresh, query_rows, query_columns, mixed = refs[-4:]
+    late_refs = refs[4:-5]
+    fresh, query_rows, query_columns, mixed, pick_ref = refs[-5:]
     part = pl.program_id(0)
     steps, rows, query_width = query_ref.shape
     capacity, lanes = kv_ref.shape[2:]
@@ -239,6 +238,7 @@
 
     @pl.when(part == 0)
     def _():
+        pick_rows(count, dest_ref, pick_ref)
         raw = own_ref[...] + got_ref[...]
         cosine, sine = rotation(length_ref, steps, rows)
         gain = gain_ref[...].astype(jnp.float32)
@@ -342,7 +342,7 @@
             small_ref[peer, per_row:, :] = jnp.concatenate(news, axis=0).astype(jnp.bfloat16)
 
 
-def attend(kv_cache, queries, own, got, gain, lengths, destination, pick, count, late, arrived):
+def attend(kv_cache, queries, own, got, gain, lengths, destination, count, late, arrived):
     steps, rows, query_width = queries.shape
     capacity, lanes = kv_cache.shape[2:]
     heads = lanes // HD
@@ -363,18 +363,19 @@
             small,
         ]
         + [jax.ShapeDtypeStruct(kv_cache.shape[1:], kv_cache.dtype)] * len(late),
-        in_specs=[smem, smem, smem, vmem, vmem, vmem, vmem, cache_block, hbm],
+        in_specs=[smem, smem, vmem, vmem, vmem, vmem, cache_block, hbm],
         out_specs=[cache_block, vmem, vmem] + [vmem] * len(late),
         scratch_shapes=[
             pltpu.VMEM((2, steps * rows, lanes), jnp.float32),
             pltpu.VMEM((rows * per_row, HD), jnp.float32),
             pltpu.VMEM((rows * per_row // HD, HD, HD), jnp.float32),
             pltpu.VMEM((rows * per_row, HD), jnp.float32),
+            pltpu.SMEM((count,), jnp.int32),
         ],
         compiler_params=pltpu.CompilerParams(vmem_limit_bytes=ATTEND_LIMIT),
         cost_estimate=HEAVY,
         name="attend",
-    )(lengths, destination, pick, own, got, gain, queries, kv_cache, arrived)
+    )(lengths, destination, own, got, gain, queries, kv_cache, arrived)
 
 
 def read_facts(block):
@@ -605,8 +606,8 @@
     group = queries.shape[2] // kv_cache.shape[3]
     count = lax.axis_size("inst")
     half = max(count // 2, 1)
-    early = list(range(half, count - 1)) + [half - 1] * (half > 1)
-    late = [count - 1] + list(range(half - 2, 0, -1))
+    early = list(range(half, count))
+    late = list(range(half - 1, 0, -1))
 
     def send(block, shift):
         pairs = [(i, peer_to(i, shift, count)) for i in range(count)]
@@ -614,7 +615,7 @@
 
     first = pack(kv_cache, destination, lengths, count, early[0])
     first_got = send(first, early[0])
-    blocks, pick, own, other = prepare(
+    blocks, own, other = prepare(
         destination,
         lengths,
         hidden_new,
@@ -623,7 +624,6 @@
         value_weight,
         count,
         early[1:],
-        first,
     )
     early_got = [first_got] + [send(block, shift) for block, shift in zip(blocks, early[1:])]
     got = lax.ppermute(other, "tp", [(0, 1), (1, 0)])
@@ -635,7 +635,6 @@
         key_gain[None, :],
         lengths,
         destination,
-        pick,
         count,
         late,
         first_got,

time: 42.9 us -> 48.7 us (1.14)
  starting transfers between devices: 18.6 us -> 25 us
  local copies, waits for them, and re-layouts: 1.59 us -> 0.03 us
  waiting for transfers between devices: 3.41 us -> 4.94 us
  Pallas kernels: 18.2 us -> 17.6 us
    all_to_all x1, starting transfers between devices: 4.2 us -> 12.4 us  [local(): small_got = lax.all_to_all(small, 'inst', 0, 0, tiled=True)]
    ppermute x7, starting transfers between devices: 14.4 us -> 12.6 us  [send(): return lax.ppermute(block, 'inst', pairs)]
    all_to_all x1, waiting for transfers between devices: 1.63 us -> 3.28 us  [local(): small_got = lax.all_to_all(small, 'inst', 0, 0, tiled=True)]
    unnamed x8 -> x10, local copies, waits for them, and re-layouts: 1.59 us -> 0.03 us
  transfers between devices with their start and end apart: 9 -> 9, of which waited for: 3 -> 2; matrix products, arithmetic and copies ran while one was open for 0% -> 0% of each run, Pallas kernels for 35% -> 30%
where the time goes in v14:
time: 48.7 us; the launch traced here: 48.4 us
  starting transfers between devices  25 us (51%)
  Pallas kernels  17.6 us (36%)
  waiting for transfers between devices  4.94 us (10%)
  between operations  0.75 us (2%)
    ppermute x7, starting transfers between devices, send(): return lax.ppermute(block, 'inst', pairs)  12.6 us
    all_to_all x1, starting transfers between devices, local(): small_got = lax.all_to_all(small, 'inst', 0, 0, tiled=True)  12.4 us
    pallas_call x1, Pallas kernels, attend(): pl.pallas_call(functools.partial(attend_kernel, count, late, block), grid...  6.62 us
    pallas_call x1, Pallas kernels, prepare(): pl.pallas_call(functools.partial(prepare_kernel, count, early, chunks), o...  5.08 us
    all_to_all x1, waiting for transfers between devices, local(): small_got = lax.all_to_all(small, 'inst', 0, 0, tiled=True)  3.28 us
    pallas_call x1, Pallas kernels, pack(): pl.pallas_call(functools.partial(pack_kernel, count, shift), out_shape=ja...  2.44 us
    ppermute x7, waiting for transfers between devices, send(): return lax.ppermute(block, 'inst', pairs)  1.66 us
    pallas_call x1, Pallas kernels, settle(): pl.pallas_call(functools.partial(settle_kernel, count, early, group), out...  1.56 us
  transfers between devices with their start and end apart: 9, of which 2 were waited for; matrix products, arithmetic and copies ran while one was open for 0% of the time, Pallas kernels for 30%

profile of v14, /device:TPU:0, one launch (start us, length us, event | category | flops | bytes accessed | tf_op | source)
XLA Modules:
  0.0 48.4 jit_solution(17405947127889660238)
XLA Ops:
  0.7 2.4 %pack.1 = bf16[2,144,256]{2,1,0:T(8,128)(2,1)} custom-call(s32[24]{0:T(128)} %dest_ref.5, s32[24]{0:T(128)} %length_ref.5, bf16[24,2,144,256]{3,2,1,0:T(8,128)(2,1)} %kv_ref.5), custom_call_target="tpu_custom_call" | custom-call | flops 1 | bytes 1 | tf_op jit(solution)/shard_map/pack/pallas_call | solution.py:77
  3.1 0.0 copy-start.3
  3.1 0.0 copy-start.4
  3.1 4.1 %collective-permute-start.1 = (bf16[2,144,256]{2,1,0:T(8,128)(2,1)}, bf16[2,144,256]{2,1,0:T(8,128)(2,1)S(1)}, u32[]{:S(2)}, u32[]{:S(2)}) collective-permute-start(bf16[2,144,256]{2,1,0:T(8,128)(2,1)} %pack.1), channel_id=1, source_target_pairs={{0,8},{2,10},{4,12},{6,14},{8,0},{10,2},{12,4},{14,6},{1,9},{3,11}... | collective-permute-start | bytes 442376 | tf_op jit(solution)/shard_map/ppermute | solution.py:614
  7.2 5.1 %prepare.1 = (bf16[2,144,256]{2,1,0:T(8,128)(2,1)S(1)}, bf16[2,144,256]{2,1,0:T(8,128)(2,1)S(1)}, bf16[2,144,256]{2,1,0:T(8,128)(2,1)S(1)}, f32[48,512]{1,0:T(8,128)S(1)}, f32[48,512]{1,0:T(8,128)S(1)}) custom-call(s32[24]{0:T(128)S(1)} %copy-done.2, s32[24]{0:T(128)S(1)} %copy-done.1, bf16[2,24,2560]{2,1,0:T(8,128)(2,1)S(1)} %copy-done, ...), custom_call_target="tpu_custom_call" | custom-call | flops 1 | bytes 1 | tf_op jit(solution)/shard_map/prepare/pallas_call | solution.py:168
  12.3 0.1 collective-permute-start
  12.4 1.4 %collective-permute-start.2 = (bf16[2,144,256]{2,1,0:T(8,128)(2,1)S(1)}, bf16[2,144,256]{2,1,0:T(8,128)(2,1)S(1)}, u32[]{:S(2)}, u32[]{:S(2)}) collective-permute-start(bf16[2,144,256]{2,1,0:T(8,128)(2,1)S(1)} %get-tuple-element.21), channel_id=1, source_target_pairs={{0,10},{2,8},{4,14},{6,12},{8,2},{10,0},{12,6},{14,4},{1,11},{3,9}... | collective-permute-start | bytes 442376 | tf_op jit(solution)/shard_map/ppermute | solution.py:614
  13.8 3.6 %collective-permute-start.3 = (bf16[2,144,256]{2,1,0:T(8,128)(2,1)S(1)}, bf16[2,144,256]{2,1,0:T(8,128)(2,1)S(1)}, u32[]{:S(2)}, u32[]{:S(2)}) collective-permute-start(bf16[2,144,256]{2,1,0:T(8,128)(2,1)S(1)} %get-tuple-element.22), channel_id=1, source_target_pairs={{0,12},{2,14},{4,8},{6,10},{8,4},{10,6},{12,0},{14,2},{1,13},{3,15... | collective-permute-start | bytes 442376 | tf_op jit(solution)/shard_map/ppermute | solution.py:614
  17.4 0.0 collective-permute-start.4
  17.4 0.0 collective-permute-done.got_ref
  17.4 0.0 collective-permute-done.1.refs_0_
  17.4 6.6 %attend.1 = (bf16[24,2,144,256]{3,2,1,0:T(8,128)(2,1)}, bf16[768,128]{1,0:T(8,128)(2,1)S(1)}, bf16[8,48,128]{2,1,0:T(8,128)(2,1)}, bf16[2,144,256]{2,1,0:T(8,128...) custom-call(s32[24]{0:T(128)S(1)} %copy-done.1, s32[24]{0:T(128)S(1)} %copy-done.2, ...), custom_call_target="tpu_custom_call" | custom-call | flops 68719476736 | bytes 268435456 | tf_op jit(solution)/shard_map/attend/pallas_call | solution.py:357
  24.0 12.4 %all-to-all-start = ((bf16[8,48,128]{2,1,0:T(8,128)(2,1)}), bf16[8,48,128]{2,1,0:T(8,128)(2,1)S(1)}, u32[]{:S(2)}, u32[]{:S(2)}) async-start(bf16[8,48,128]{2,1,0:T(8,128)(2,1)} %get-tuple-element.20), calls=%async_computation | async-start | bytes 196608 | tf_op jit(solution)/shard_map/all_to_all | solution.py:643
  36.4 2.9 %collective-permute-start.5 = (bf16[2,144,256]{2,1,0:T(8,128)(2,1)S(1)}, bf16[2,144,256]{2,1,0:T(8,128)(2,1)S(1)}, u32[]{:S(2)}, u32[]{:S(2)}) collective-permute-start(bf16[2,144,256]{2,1,0:T(8,128)(2,1)S(1)} %get-tuple-element.28), channel_id=1, source_target_pairs={{0,6},{2,4},{4,2},{6,0},{8,14},{10,12},{12,10},{14,8},{1,7},{3,5},... | collective-permute-start | bytes 442376 | tf_op jit(solution)/shard_map/ppermute | solution.py:614
  39.3 0.6 %collective-permute-start.6 = (bf16[2,144,256]{2,1,0:T(8,128)(2,1)S(1)}, bf16[2,144,256]{2,1,0:T(8,128)(2,1)S(1)}, u32[]{:S(2)}, u32[]{:S(2)}) collective-permute-start(bf16[2,144,256]{2,1,0:T(8,128)(2,1)S(1)} %get-tuple-element.29), channel_id=1, source_target_pairs={{0,4},{2,6},{4,0},{6,2},{8,12},{10,14},{12,8},{14,10},{1,5},{3,7},... | collective-permute-start | bytes 442376 | tf_op jit(solution)/shard_map/ppermute | solution.py:614
  39.9 0.0 collective-permute-done.2.refs_1_
  39.9 0.0 collective-permute-start.7
  39.9 0.0 collective-permute-done.3.refs_2_
  39.9 0.0 collective-permute-done.4.refs_3_
  39.9 1.0 %land.1 = (bf16[24,2,144,256]{3,2,1,0:T(8,128)(2,1)}, bf16[4,2,32,256]{3,2,1,0:T(8,128)(2,1)S(1)}) custom-call(bf16[2,144,256]{2,1,0:T(8,128)(2,1)S(1)} %collective-permute-done.1.refs_0_, bf16[2,144,256]{2,1,0:T(8,128)(2,1)S(1)} %collective-permute-done.2.refs_1_, ...), custom_call_target="tpu_custom_call", output_to_operand_aliasing={{0}: (4, {})} | custom-call | flops 68719476736 | bytes 268435456 | tf_op jit(solution)/shard_map/land/pallas_call | solution.py:447
  41.0 3.3 %all-to-all-done.small_ref.refs_3_ = bf16[8,48,128]{2,1,0:T(8,128)(2,1)S(1)} async-done(((bf16[8,48,128]{2,1,0:T(8,128)(2,1)}), bf16[8,48,128]{2,1,0:T(8,128)(2,1)S(1)}, u32[]{:S(2)}, u32[]{:S(2)}) %all-to-all-start) | async-done | bytes 98336 | tf_op jit(solution)/shard_map/all_to_all | solution.py:643
  44.2 1.6 %settle.1 = (bf16[2,24,2048]{2,1,0:T(8,128)(2,1)}, bf16[24,2,144,256]{3,2,1,0:T(8,128)(2,1)}) custom-call(bf16[768,128]{1,0:T(8,128)(2,1)S(1)} %get-tuple-element.19.mixed_ref, bf16[8,48,128]{2,1,0:T(8,128)(2,1)S(1)} %all-to-all-done.small_ref.refs_3_, bf16[4,2,32,256]{3,2,1,0:T(8,128)(2,1)S(1)} %get-tuple-element.25.window_ref, ...), custom_call_target="tpu_custom_call", output_to_operand_aliasing={{1}: (3, {})} | custom-call | flops 1 | bytes 1 | tf_op jit(solution)/shard_map/settle/pallas_call | solution.py:543
  45.8 1.6 %collective-permute-done.6.refs_1_ = bf16[2,144,256]{2,1,0:T(8,128)(2,1)S(1)} collective-permute-done((bf16[2,144,256]{2,1,0:T(8,128)(2,1)S(1)}, bf16[2,144,256]{2,1,0:T(8,128)(2,1)S(1)}, u32[]{:S(2)}, u32[]{:S(2)}) %collective-permute-start.6) | collective-permute-done | bytes 147488 | tf_op jit(solution)/shard_map/ppermute | solution.py:614
  47.5 0.9 %finish.1 = bf16[24,2,144,256]{3,2,1,0:T(8,128)(2,1)} custom-call(bf16[2,144,256]{2,1,0:T(8,128)(2,1)S(1)} %collective-permute-done.5.refs_0_, bf16[2,144,256]{2,1,0:T(8,128)(2,1)S(1)} %collective-permute-done.6.refs_1_, bf16[2,144,256]{2,1,0:T(8,128)(2,1)S(1)} %collective-permute-done.7.refs_2_, ...), custom_call_target="tpu_custom_call", output_to_operand_aliasing={{}: (4, {})} | custom-call | flops 1 | bytes 1 | tf_op jit(solution)/shard_map/finish/pallas_call | solution.py:588
  (10 shorter events, 0.0 us)
Async XLA Ops:
  0.6 6.6 %copy-start.2 = (s32[24]{0:T(128)S(1)}, s32[24]{0:T(128)}, u32[]{:S(2)}) copy-start(s32[24]{0:T(128)} %dest_ref.5) | copy-start | bytes 292
  0.6 6.6 %copy-start.1 = (s32[24]{0:T(128)S(1)}, s32[24]{0:T(128)}, u32[]{:S(2)}) copy-start(s32[24]{0:T(128)} %length_ref.5) | copy-start | bytes 292
  0.6 6.6 %copy-start = (bf16[2,24,2560]{2,1,0:T(8,128)(2,1)S(1)}, bf16[2,24,2560]{2,1,0:T(8,128)(2,1)}, u32[]{:S(2)}) copy-start(bf16[2,24,2560]{2,1,0:T(8,128)(2,1)} %hidden_ref.1) | copy-start | bytes 737284
  3.1 14.3 %copy-start.3 = (bf16[2,24,2048]{2,1,0:T(8,128)(2,1)S(1)}, bf16[2,24,2048]{2,1,0:T(8,128)(2,1)}, u32[]{:S(2)}) copy-start(bf16[2,24,2048]{2,1,0:T(8,128)(2,1)} %query_ref.1) | copy-start | bytes 589828
  3.1 14.3 %copy-start.4 = (bf16[128]{0:T(256)(128)(2,1)S(1)}, bf16[128]{0:T(256)(128)(2,1)}, u32[]{:S(2)}) copy-start(bf16[128]{0:T(256)(128)(2,1)} %param.15) | copy-start | bytes 772
  3.1 14.2 %collective-permute-start.1 = (bf16[2,144,256]{2,1,0:T(8,128)(2,1)}, bf16[2,144,256]{2,1,0:T(8,128)(2,1)S(1)}, u32[]{:S(2)}, u32[]{:S(2)}) collective-permute-start(bf16[2,144,256]{2,1,0:T(8,128)(2,1)} %pack.1), channel_id=1, source_target_pairs={{0,8},{2,10},{4,12},{6,14},{8,0},{10,2},{12,4},{14,6},{1,9},{3,11}... | collective-permute-start | bytes 442376 | tf_op jit(solution)/shard_map/ppermute | solution.py:614
  12.3 5.0 %collective-permute-start = (f32[48,512]{1,0:T(8,128)S(1)}, f32[48,512]{1,0:T(8,128)S(1)}, u32[]{:S(2)}, u32[]{:S(2)}) collective-permute-start(f32[48,512]{1,0:T(8,128)S(1)} %get-tuple-element.18), channel_id=1, source_target_pairs={{0,1},{1,0},{2,3},{3,2},{4,5},{5,4},{6,7},{7,6},{8,9},{9,8},{10,11... | collective-permute-start | bytes 294920 | tf_op jit(solution)/shard_map/ppermute | solution.py:629
  12.4 27.5 %collective-permute-start.2 = (bf16[2,144,256]{2,1,0:T(8,128)(2,1)S(1)}, bf16[2,144,256]{2,1,0:T(8,128)(2,1)S(1)}, u32[]{:S(2)}, u32[]{:S(2)}) collective-permute-start(bf16[2,144,256]{2,1,0:T(8,128)(2,1)S(1)} %get-tuple-element.21), channel_id=1, source_target_pairs={{0,10},{2,8},{4,14},{6,12},{8,2},{10,0},{12,6},{14,4},{1,11},{3,9}... | collective-permute-start | bytes 442376 | tf_op jit(solution)/shard_map/ppermute | solution.py:614
  13.8 26.2 %collective-permute-start.3 = (bf16[2,144,256]{2,1,0:T(8,128)(2,1)S(1)}, bf16[2,144,256]{2,1,0:T(8,128)(2,1)S(1)}, u32[]{:S(2)}, u32[]{:S(2)}) collective-permute-start(bf16[2,144,256]{2,1,0:T(8,128)(2,1)S(1)} %get-tuple-element.22), channel_id=1, source_target_pairs={{0,12},{2,14},{4,8},{6,10},{8,4},{10,6},{12,0},{14,2},{1,13},{3,15... | collective-permute-start | bytes 442376 | tf_op jit(solution)/shard_map/ppermute | solution.py:614
  17.4 22.6 %collective-permute-start.4 = (bf16[2,144,256]{2,1,0:T(8,128)(2,1)S(1)}, bf16[2,144,256]{2,1,0:T(8,128)(2,1)S(1)}, u32[]{:S(2)}, u32[]{:S(2)}) collective-permute-start(bf16[2,144,256]{2,1,0:T(8,128)(2,1)S(1)} %get-tuple-element.23), channel_id=1, source_target_pairs={{0,14},{2,12},{4,10},{6,8},{8,6},{10,4},{12,2},{14,0},{1,15},{3,13... | collective-permute-start | bytes 442376 | tf_op jit(solution)/shard_map/ppermute | solution.py:614
  24.0 20.2 %all-to-all-start = ((bf16[8,48,128]{2,1,0:T(8,128)(2,1)}), bf16[8,48,128]{2,1,0:T(8,128)(2,1)S(1)}, u32[]{:S(2)}, u32[]{:S(2)}) async-start(bf16[8,48,128]{2,1,0:T(8,128)(2,1)} %get-tuple-element.20), calls=%async_computation | async-start | bytes 196608 | tf_op jit(solution)/shard_map/all_to_all | solution.py:643
  36.4 9.4 %collective-permute-start.5 = (bf16[2,144,256]{2,1,0:T(8,128)(2,1)S(1)}, bf16[2,144,256]{2,1,0:T(8,128)(2,1)S(1)}, u32[]{:S(2)}, u32[]{:S(2)}) collective-permute-start(bf16[2,144,256]{2,1,0:T(8,128)(2,1)S(1)} %get-tuple-element.28), channel_id=1, source_target_pairs={{0,6},{2,4},{4,2},{6,0},{8,14},{10,12},{12,10},{14,8},{1,7},{3,5},... | collective-permute-start | bytes 442376 | tf_op jit(solution)/shard_map/ppermute | solution.py:614
  39.3 8.1 %collective-permute-start.6 = (bf16[2,144,256]{2,1,0:T(8,128)(2,1)S(1)}, bf16[2,144,256]{2,1,0:T(8,128)(2,1)S(1)}, u32[]{:S(2)}, u32[]{:S(2)}) collective-permute-start(bf16[2,144,256]{2,1,0:T(8,128)(2,1)S(1)} %get-tuple-element.29), channel_id=1, source_target_pairs={{0,4},{2,6},{4,0},{6,2},{8,12},{10,14},{12,8},{14,10},{1,5},{3,7},... | collective-permute-start | bytes 442376 | tf_op jit(solution)/shard_map/ppermute | solution.py:614
  39.9 7.6 %collective-permute-start.7 = (bf16[2,144,256]{2,1,0:T(8,128)(2,1)S(1)}, bf16[2,144,256]{2,1,0:T(8,128)(2,1)S(1)}, u32[]{:S(2)}, u32[]{:S(2)}) collective-permute-start(bf16[2,144,256]{2,1,0:T(8,128)(2,1)S(1)} %get-tuple-element.30), channel_id=1, source_target_pairs={{0,2},{2,0},{4,6},{6,4},{8,10},{10,8},{12,14},{14,12},{1,3},{3,1},... | collective-permute-start | bytes 442376 | tf_op jit(solution)/shard_map/ppermute | solution.py:614

commit v15 on v14

--- a/solution.py
+++ b/solution.py
@@ -13,7 +13,7 @@
 NORM_EPS = 1e-06
 VMEM_LIMIT = 62 * 1024 * 1024
 ATTEND_LIMIT = 50 * 1024 * 1024
-PREPARE_LIMIT = 53 * 1024 * 1024
+PREPARE_LIMIT = 62 * 1024 * 1024
 SMALL_LIMIT = 40 * 1024 * 1024
 LIGHT = pl.CostEstimate(flops=1, bytes_accessed=1, transcendentals=0)
 HEAVY = pl.CostEstimate(flops=1 << 36, bytes_accessed=1 << 28, transcendentals=0)
@@ -56,38 +56,6 @@
     facts = jnp.where(first_lanes, slot, length_ref[row]).astype(jnp.float32)
     end = block[0, capacity - TILE :, :].astype(jnp.float32)
     block[0, capacity - TILE :, :] = jnp.where(last, facts, end).astype(jnp.bfloat16)
-
-
-def pack_kernel(count, shift, dest_ref, length_ref, kv_ref, block_ref, block, sem, pick):
-    pick_rows(count, dest_ref, pick)
-    peer = peer_to(lax.axis_index("inst"), shift, count)
-    row = pick[peer]
-    fetch = pltpu.make_async_copy(kv_ref.at[row], block, sem)
-    fetch.start()
-    fetch.wait()
-    add_facts(block, peer, row, dest_ref, length_ref)
-    store = pltpu.make_async_copy(block, block_ref, sem)
-    store.start()
-    store.wait()
-
-
-def pack(kv_cache, destination, lengths, count, shift):
-    smem = pl.BlockSpec(memory_space=pltpu.SMEM)
-    hbm = pl.BlockSpec(memory_space=pl.ANY)
-    return pl.pallas_call(
-        functools.partial(pack_kernel, count, shift),
-        out_shape=jax.ShapeDtypeStruct(kv_cache.shape[1:], kv_cache.dtype),
-        in_specs=[smem, smem, hbm],
-        out_specs=hbm,
-        scratch_shapes=[
-            pltpu.VMEM(kv_cache.shape[1:], kv_cache.dtype),
-            pltpu.SemaphoreType.DMA,
-            pltpu.SMEM((count,), jnp.int32),
-        ],
-        compiler_params=pltpu.CompilerParams(vmem_limit_bytes=VMEM_LIMIT),
-        cost_estimate=LIGHT,
-        name="pack",
-    )(destination, lengths, kv_cache)
 
 
 def prepare_kernel(
@@ -224,8 +192,8 @@
     kv_ref,
     *refs,
 ):
-    moved_ref, mixed_ref, small_ref = refs[1:4]
-    late_refs = refs[4:-5]
+    moved_ref, mixed_ref, small_ref = refs[:3]
+    late_refs = refs[3:-5]
     fresh, query_rows, query_columns, mixed, pick_ref = refs[-5:]
     part = pl.program_id(0)
     steps, rows, query_width = query_ref.shape
@@ -342,7 +310,7 @@
             small_ref[peer, per_row:, :] = jnp.concatenate(news, axis=0).astype(jnp.bfloat16)
 
 
-def attend(kv_cache, queries, own, got, gain, lengths, destination, count, late, arrived):
+def attend(kv_cache, queries, own, got, gain, lengths, destination, count, late):
     steps, rows, query_width = queries.shape
     capacity, lanes = kv_cache.shape[2:]
     heads = lanes // HD
@@ -352,7 +320,6 @@
     small = jax.ShapeDtypeStruct((count, small_rows, HD), jnp.bfloat16)
     smem = pl.BlockSpec(memory_space=pltpu.SMEM)
     vmem = pl.BlockSpec(memory_space=pltpu.VMEM)
-    hbm = pl.BlockSpec(memory_space=pl.ANY)
     cache_block = pl.BlockSpec((block, 2, capacity, lanes), lambda i: (i, 0, 0, 0))
     return pl.pallas_call(
         functools.partial(attend_kernel, count, late, block),
@@ -363,7 +330,7 @@
             small,
         ]
         + [jax.ShapeDtypeStruct(kv_cache.shape[1:], kv_cache.dtype)] * len(late),
-        in_specs=[smem, smem, vmem, vmem, vmem, vmem, cache_block, hbm],
+        in_specs=[smem, smem, vmem, vmem, vmem, vmem, cache_block],
         out_specs=[cache_block, vmem, vmem] + [vmem] * len(late),
         scratch_shapes=[
             pltpu.VMEM((2, steps * rows, lanes), jnp.float32),
@@ -375,7 +342,7 @@
         compiler_params=pltpu.CompilerParams(vmem_limit_bytes=ATTEND_LIMIT),
         cost_estimate=HEAVY,
         name="attend",
-    )(lengths, destination, own, got, gain, queries, kv_cache, arrived)
+    )(lengths, destination, own, got, gain, queries, kv_cache)
 
 
 def read_facts(block):
@@ -606,26 +573,17 @@
     group = queries.shape[2] // kv_cache.shape[3]
     count = lax.axis_size("inst")
     half = max(count // 2, 1)
-    early = list(range(half, count))
-    late = list(range(half - 1, 0, -1))
+    early = list(range(half, count - 1)) + [half - 1] * (half > 1)
+    late = [count - 1] + list(range(half - 2, 0, -1))
 
     def send(block, shift):
         pairs = [(i, peer_to(i, shift, count)) for i in range(count)]
         return lax.ppermute(block, "inst", pairs)
 
-    first = pack(kv_cache, destination, lengths, count, early[0])
-    first_got = send(first, early[0])
     blocks, own, other = prepare(
-        destination,
-        lengths,
-        hidden_new,
-        kv_cache,
-        key_weight,
-        value_weight,
-        count,
-        early[1:],
+        destination, lengths, hidden_new, kv_cache, key_weight, value_weight, count, early
     )
-    early_got = [first_got] + [send(block, shift) for block, shift in zip(blocks, early[1:])]
+    early_got = [send(block, shift) for block, shift in zip(blocks, early)]
     got = lax.ppermute(other, "tp", [(0, 1), (1, 0)])
     moved, mixed, small, *late_blocks = attend(
         kv_cache,
@@ -637,7 +595,6 @@
         destination,
         count,
         late,
-        first_got,
     )
     late_got = [send(block, shift) for block, shift in zip(late_blocks, late)]
     small_got = lax.all_to_all(small, "inst", 0, 0, tiled=True)

time: 48.7 us -> 40.4 us (0.83)
  starting transfers between devices: 25 us -> 18.6 us
  Pallas kernels: 17.6 us -> 15.8 us
  waiting for transfers between devices: 4.94 us -> 4.02 us
  local copies, waits for them, and re-layouts: 0.03 us -> 0.9 us
    all_to_all x1, starting transfers between devices: 12.4 us -> 4.19 us  [local(): small_got = lax.all_to_all(small, 'inst', 0, 0, tiled=True)]
    pallas_call x1 -> x0, Pallas kernels: 2.44 us -> none  [pack(): pl.pallas_call(functools.partial(pack_kernel, count, shift), out_shape=ja...]
    ppermute x7, starting transfers between devices: 12.6 us -> 13.9 us  [send(): return lax.ppermute(block, 'inst', pairs)]
    all_to_all x1, waiting for transfers between devices: 3.28 us -> 2.06 us  [local(): small_got = lax.all_to_all(small, 'inst', 0, 0, tiled=True)]
    unnamed x10, local copies, waits for them, and re-layouts: 0.03 us -> 0.9 us
    pallas_call x1, Pallas kernels: 5.08 us -> 5.64 us  [prepare(): pl.pallas_call(functools.partial(prepare_kernel, count, early, chunks), o...]
  transfers between devices with their start and end apart: 9 -> 9, of which waited for: 2 -> 4; matrix products, arithmetic and copies ran while one was open for 0% -> 0% of each run, Pallas kernels for 30% -> 23%
where the time goes in v15:
time: 40.4 us; the launch traced here: 40 us
  starting transfers between devices  18.6 us (46%)
  Pallas kernels  15.8 us (39%)
  waiting for transfers between devices  4.02 us (10%)
  local copies, waits for them, and re-layouts  0.9 us (2%)
  between operations  0.74 us (2%)
    ppermute x7, starting transfers between devices, send(): return lax.ppermute(block, 'inst', pairs)  13.9 us
    pallas_call x1, Pallas kernels, attend(): pl.pallas_call(functools.partial(attend_kernel, count, late, block), grid...  6.62 us
    pallas_call x1, Pallas kernels, prepare(): pl.pallas_call(functools.partial(prepare_kernel, count, early, chunks), o...  5.64 us
    all_to_all x1, starting transfers between devices, local(): small_got = lax.all_to_all(small, 'inst', 0, 0, tiled=True)  4.19 us
    all_to_all x1, waiting for transfers between devices, local(): small_got = lax.all_to_all(small, 'inst', 0, 0, tiled=True)  2.06 us
    ppermute x7, waiting for transfers between devices, send(): return lax.ppermute(block, 'inst', pairs)  1.96 us
    pallas_call x1, Pallas kernels, settle(): pl.pallas_call(functools.partial(settle_kernel, count, early, group), out...  1.56 us
    pallas_call x1, Pallas kernels, land(): pl.pallas_call(functools.partial(land_kernel, pieces), out_shape=[jax.Sha...  1.01 us
  transfers between devices with their start and end apart: 9, of which 4 were waited for; matrix products, arithmetic and copies ran while one was open for 0% of the time, Pallas kernels for 23%

profile of v15, /device:TPU:0, one launch (start us, length us, event | category | flops | bytes accessed | tf_op | source)
XLA Modules:
  0.0 40.0 jit_solution(2794650111881934209)
XLA Ops:
  0.7 5.6 %prepare.1 = (bf16[2,144,256]{2,1,0:T(8,128)(2,1)}, bf16[2,144,256]{2,1,0:T(8,128)(2,1)}, bf16[2,144,256]{2,1,0:T(8,128)(2,1)}, bf16[2,144,256]{2,1,0:T(8,128)(2...) custom-call(s32[24]{0:T(128)} %dest_ref.3, s32[24]{0:T(128)} %length_ref.3, bf16[2,24,2560]{2,1,0:T(8,128)(2,1)} %hidden_ref.1, ...), custom_call_target="tpu_custom_call" | custom-call | flops 1 | bytes 1 | tf_op jit(solution)/shard_map/prepare/pallas_call | solution.py:136
  6.3 0.5 %collective-permute-start = (f32[48,512]{1,0:T(8,128)}, f32[48,512]{1,0:T(8,128)S(1)}, u32[]{:S(2)}, u32[]{:S(2)}) collective-permute-start(f32[48,512]{1,0:T(8,128)} %get-tuple-element.19), channel_id=1, source_target_pairs={{0,1},{1,0},{2,3},{3,2},{4,5},{5,4},{6,7},{7,6},{8,9},{9,8},{10,11... | collective-permute-start | bytes 294920 | tf_op jit(solution)/shard_map/ppermute | solution.py:587
  6.8 3.7 %collective-permute-start.1 = (bf16[2,144,256]{2,1,0:T(8,128)(2,1)}, bf16[2,144,256]{2,1,0:T(8,128)(2,1)S(1)}, u32[]{:S(2)}, u32[]{:S(2)}) collective-permute-start(bf16[2,144,256]{2,1,0:T(8,128)(2,1)} %get-tuple-element.22), channel_id=1, source_target_pairs={{0,8},{2,10},{4,12},{6,14},{8,0},{10,2},{12,4},{14,6},{1,9},{3,11}... | collective-permute-start | bytes 442376 | tf_op jit(solution)/shard_map/ppermute | solution.py:581
  10.5 1.3 %collective-permute-start.2 = (bf16[2,144,256]{2,1,0:T(8,128)(2,1)}, bf16[2,144,256]{2,1,0:T(8,128)(2,1)S(1)}, u32[]{:S(2)}, u32[]{:S(2)}) collective-permute-start(bf16[2,144,256]{2,1,0:T(8,128)(2,1)} %get-tuple-element.23), channel_id=1, source_target_pairs={{0,10},{2,8},{4,14},{6,12},{8,2},{10,0},{12,6},{14,4},{1,11},{3,9}... | collective-permute-start | bytes 442376 | tf_op jit(solution)/shard_map/ppermute | solution.py:581
  11.8 3.6 %collective-permute-start.3 = (bf16[2,144,256]{2,1,0:T(8,128)(2,1)}, bf16[2,144,256]{2,1,0:T(8,128)(2,1)S(1)}, u32[]{:S(2)}, u32[]{:S(2)}) collective-permute-start(bf16[2,144,256]{2,1,0:T(8,128)(2,1)} %get-tuple-element.24), channel_id=1, source_target_pairs={{0,12},{2,14},{4,8},{6,10},{8,4},{10,6},{12,0},{14,2},{1,13},{3,15... | collective-permute-start | bytes 442376 | tf_op jit(solution)/shard_map/ppermute | solution.py:581
  15.4 0.0 collective-permute-start.4
  15.4 0.0 collective-permute-done.got_ref
  15.4 0.0 copy-start.3
  15.5 0.9 %copy-done.3 = f32[48,512]{1,0:T(8,128)S(1)} copy-done((f32[48,512]{1,0:T(8,128)S(1)}, f32[48,512]{1,0:T(8,128)}, u32[]{:S(2)}) %copy-start.3) | copy-done | bytes 98328
  16.3 6.6 %attend.1 = (bf16[24,2,144,256]{3,2,1,0:T(8,128)(2,1)}, bf16[768,128]{1,0:T(8,128)(2,1)S(1)}, bf16[8,48,128]{2,1,0:T(8,128)(2,1)}, bf16[2,144,256]{2,1,0:T(8,128...) custom-call(s32[24]{0:T(128)S(1)} %copy-done, s32[24]{0:T(128)S(1)} %copy-done.1, ...), custom_call_target="tpu_custom_call" | custom-call | flops 68719476736 | bytes 268435456 | tf_op jit(solution)/shard_map/attend/pallas_call | solution.py:324
  23.0 4.2 %all-to-all-start = ((bf16[8,48,128]{2,1,0:T(8,128)(2,1)}), bf16[8,48,128]{2,1,0:T(8,128)(2,1)S(1)}, u32[]{:S(2)}, u32[]{:S(2)}) async-start(bf16[8,48,128]{2,1,0:T(8,128)(2,1)} %get-tuple-element.21), calls=%async_computation | async-start | bytes 196608 | tf_op jit(solution)/shard_map/all_to_all | solution.py:600
  27.2 4.7 %collective-permute-start.5 = (bf16[2,144,256]{2,1,0:T(8,128)(2,1)S(1)}, bf16[2,144,256]{2,1,0:T(8,128)(2,1)S(1)}, u32[]{:S(2)}, u32[]{:S(2)}) collective-permute-start(bf16[2,144,256]{2,1,0:T(8,128)(2,1)S(1)} %get-tuple-element.30), channel_id=1, source_target_pairs={{0,14},{2,12},{4,10},{6,8},{8,6},{10,4},{12,2},{14,0},{1,15},{3,13... | collective-permute-start | bytes 442376 | tf_op jit(solution)/shard_map/ppermute | solution.py:581
  31.9 0.0 collective-permute-done.1.refs_0_
  31.9 0.0 collective-permute-done.2.refs_1_
  31.9 0.6 %collective-permute-start.7 = (bf16[2,144,256]{2,1,0:T(8,128)(2,1)S(1)}, bf16[2,144,256]{2,1,0:T(8,128)(2,1)S(1)}, u32[]{:S(2)}, u32[]{:S(2)}) collective-permute-start(bf16[2,144,256]{2,1,0:T(8,128)(2,1)S(1)} %get-tuple-element.32), channel_id=1, source_target_pairs={{0,2},{2,0},{4,6},{6,4},{8,10},{10,8},{12,14},{14,12},{1,3},{3,1},... | collective-permute-start | bytes 442376 | tf_op jit(solution)/shard_map/ppermute | solution.py:581
  32.5 0.0 collective-permute-done.3.refs_2_
  32.5 0.0 collective-permute-done.4.refs_3_
  32.5 1.0 %land.1 = (bf16[24,2,144,256]{3,2,1,0:T(8,128)(2,1)}, bf16[4,2,32,256]{3,2,1,0:T(8,128)(2,1)S(1)}) custom-call(bf16[2,144,256]{2,1,0:T(8,128)(2,1)S(1)} %collective-permute-done.1.refs_0_, bf16[2,144,256]{2,1,0:T(8,128)(2,1)S(1)} %collective-permute-done.2.refs_1_, ...), custom_call_target="tpu_custom_call", output_to_operand_aliasing={{0}: (4, {})} | custom-call | flops 68719476736 | bytes 268435456 | tf_op jit(solution)/shard_map/land/pallas_call | solution.py:414
  33.5 2.1 %all-to-all-done.small_ref.refs_3_ = bf16[8,48,128]{2,1,0:T(8,128)(2,1)S(1)} async-done(((bf16[8,48,128]{2,1,0:T(8,128)(2,1)}), bf16[8,48,128]{2,1,0:T(8,128)(2,1)S(1)}, u32[]{:S(2)}, u32[]{:S(2)}) %all-to-all-start) | async-done | bytes 98336 | tf_op jit(solution)/shard_map/all_to_all | solution.py:600
  35.6 1.6 %settle.1 = (bf16[2,24,2048]{2,1,0:T(8,128)(2,1)}, bf16[24,2,144,256]{3,2,1,0:T(8,128)(2,1)}) custom-call(bf16[768,128]{1,0:T(8,128)(2,1)S(1)} %get-tuple-element.20.mixed_ref, bf16[8,48,128]{2,1,0:T(8,128)(2,1)S(1)} %all-to-all-done.small_ref.refs_3_, bf16[4,2,32,256]{3,2,1,0:T(8,128)(2,1)S(1)} %get-tuple-element.27.window_ref, ...), custom_call_target="tpu_custom_call", output_to_operand_aliasing={{1}: (3, {})} | custom-call | flops 1 | bytes 1 | tf_op jit(solution)/shard_map/settle/pallas_call | solution.py:510
  37.2 0.9 %collective-permute-done.5.refs_0_ = bf16[2,144,256]{2,1,0:T(8,128)(2,1)S(1)} collective-permute-done((bf16[2,144,256]{2,1,0:T(8,128)(2,1)S(1)}, bf16[2,144,256]{2,1,0:T(8,128)(2,1)S(1)}, u32[]{:S(2)}, u32[]{:S(2)}) %collective-permute-start.5) | collective-permute-done | bytes 147488 | tf_op jit(solution)/shard_map/ppermute | solution.py:581
  38.1 0.9 %collective-permute-done.6.refs_1_ = bf16[2,144,256]{2,1,0:T(8,128)(2,1)S(1)} collective-permute-done((bf16[2,144,256]{2,1,0:T(8,128)(2,1)S(1)}, bf16[2,144,256]{2,1,0:T(8,128)(2,1)S(1)}, u32[]{:S(2)}, u32[]{:S(2)}) %collective-permute-start.6) | collective-permute-done | bytes 147488 | tf_op jit(solution)/shard_map/ppermute | solution.py:581
  39.0 0.2 collective-permute-done.7.refs_2_
  39.1 0.9 %finish.1 = bf16[24,2,144,256]{3,2,1,0:T(8,128)(2,1)} custom-call(bf16[2,144,256]{2,1,0:T(8,128)(2,1)S(1)} %collective-permute-done.5.refs_0_, bf16[2,144,256]{2,1,0:T(8,128)(2,1)S(1)} %collective-permute-done.6.refs_1_, bf16[2,144,256]{2,1,0:T(8,128)(2,1)S(1)} %collective-permute-done.7.refs_2_, ...), custom_call_target="tpu_custom_call", output_to_operand_aliasing={{}: (4, {})} | custom-call | flops 1 | bytes 1 | tf_op jit(solution)/shard_map/finish/pallas_call | solution.py:555
  (9 shorter events, 0.0 us)
Async XLA Ops:
  0.6 14.8 %copy-start.1 = (s32[24]{0:T(128)S(1)}, s32[24]{0:T(128)}, u32[]{:S(2)}) copy-start(s32[24]{0:T(128)} %dest_ref.3) | copy-start | bytes 292
  0.6 14.8 %copy-start = (s32[24]{0:T(128)S(1)}, s32[24]{0:T(128)}, u32[]{:S(2)}) copy-start(s32[24]{0:T(128)} %length_ref.3) | copy-start | bytes 292
  0.7 14.8 %copy-start.4 = (bf16[128]{0:T(256)(128)(2,1)S(1)}, bf16[128]{0:T(256)(128)(2,1)}, u32[]{:S(2)}) copy-start(bf16[128]{0:T(256)(128)(2,1)} %param.15) | copy-start | bytes 772
  0.7 14.8 %copy-start.2 = (bf16[2,24,2048]{2,1,0:T(8,128)(2,1)S(1)}, bf16[2,24,2048]{2,1,0:T(8,128)(2,1)}, u32[]{:S(2)}) copy-start(bf16[2,24,2048]{2,1,0:T(8,128)(2,1)} %query_ref.1) | copy-start | bytes 589828
  6.3 9.1 %collective-permute-start = (f32[48,512]{1,0:T(8,128)}, f32[48,512]{1,0:T(8,128)S(1)}, u32[]{:S(2)}, u32[]{:S(2)}) collective-permute-start(f32[48,512]{1,0:T(8,128)} %get-tuple-element.19), channel_id=1, source_target_pairs={{0,1},{1,0},{2,3},{3,2},{4,5},{5,4},{6,7},{7,6},{8,9},{9,8},{10,11... | collective-permute-start | bytes 294920 | tf_op jit(solution)/shard_map/ppermute | solution.py:587
  6.8 25.0 %collective-permute-start.1 = (bf16[2,144,256]{2,1,0:T(8,128)(2,1)}, bf16[2,144,256]{2,1,0:T(8,128)(2,1)S(1)}, u32[]{:S(2)}, u32[]{:S(2)}) collective-permute-start(bf16[2,144,256]{2,1,0:T(8,128)(2,1)} %get-tuple-element.22), channel_id=1, source_target_pairs={{0,8},{2,10},{4,12},{6,14},{8,0},{10,2},{12,4},{14,6},{1,9},{3,11}... | collective-permute-start | bytes 442376 | tf_op jit(solution)/shard_map/ppermute | solution.py:581
  10.5 21.4 %collective-permute-start.2 = (bf16[2,144,256]{2,1,0:T(8,128)(2,1)}, bf16[2,144,256]{2,1,0:T(8,128)(2,1)S(1)}, u32[]{:S(2)}, u32[]{:S(2)}) collective-permute-start(bf16[2,144,256]{2,1,0:T(8,128)(2,1)} %get-tuple-element.23), channel_id=1, source_target_pairs={{0,10},{2,8},{4,14},{6,12},{8,2},{10,0},{12,6},{14,4},{1,11},{3,9}... | collective-permute-start | bytes 442376 | tf_op jit(solution)/shard_map/ppermute | solution.py:581
  11.8 20.7 %collective-permute-start.3 = (bf16[2,144,256]{2,1,0:T(8,128)(2,1)}, bf16[2,144,256]{2,1,0:T(8,128)(2,1)S(1)}, u32[]{:S(2)}, u32[]{:S(2)}) collective-permute-start(bf16[2,144,256]{2,1,0:T(8,128)(2,1)} %get-tuple-element.24), channel_id=1, source_target_pairs={{0,12},{2,14},{4,8},{6,10},{8,4},{10,6},{12,0},{14,2},{1,13},{3,15... | collective-permute-start | bytes 442376 | tf_op jit(solution)/shard_map/ppermute | solution.py:581
  15.4 17.1 %collective-permute-start.4 = (bf16[2,144,256]{2,1,0:T(8,128)(2,1)}, bf16[2,144,256]{2,1,0:T(8,128)(2,1)S(1)}, u32[]{:S(2)}, u32[]{:S(2)}) collective-permute-start(bf16[2,144,256]{2,1,0:T(8,128)(2,1)} %get-tuple-element.25), channel_id=1, source_target_pairs={{0,6},{2,4},{4,2},{6,0},{8,14},{10,12},{12,10},{14,8},{1,7},{3,5},... | collective-permute-start | bytes 442376 | tf_op jit(solution)/shard_map/ppermute | solution.py:581
  15.4 0.9 %copy-start.3 = (f32[48,512]{1,0:T(8,128)S(1)}, f32[48,512]{1,0:T(8,128)}, u32[]{:S(2)}) copy-start(f32[48,512]{1,0:T(8,128)} %get-tuple-element.18.own_ref) | copy-start | bytes 294916
  23.0 12.6 %all-to-all-start = ((bf16[8,48,128]{2,1,0:T(8,128)(2,1)}), bf16[8,48,128]{2,1,0:T(8,128)(2,1)S(1)}, u32[]{:S(2)}, u32[]{:S(2)}) async-start(bf16[8,48,128]{2,1,0:T(8,128)(2,1)} %get-tuple-element.21), calls=%async_computation | async-start | bytes 196608 | tf_op jit(solution)/shard_map/all_to_all | solution.py:600
  27.2 10.9 %collective-permute-start.5 = (bf16[2,144,256]{2,1,0:T(8,128)(2,1)S(1)}, bf16[2,144,256]{2,1,0:T(8,128)(2,1)S(1)}, u32[]{:S(2)}, u32[]{:S(2)}) collective-permute-start(bf16[2,144,256]{2,1,0:T(8,128)(2,1)S(1)} %get-tuple-element.30), channel_id=1, source_target_pairs={{0,14},{2,12},{4,10},{6,8},{8,6},{10,4},{12,2},{14,0},{1,15},{3,13... | collective-permute-start | bytes 442376 | tf_op jit(solution)/shard_map/ppermute | solution.py:581
  31.9 7.1 %collective-permute-start.6 = (bf16[2,144,256]{2,1,0:T(8,128)(2,1)S(1)}, bf16[2,144,256]{2,1,0:T(8,128)(2,1)S(1)}, u32[]{:S(2)}, u32[]{:S(2)}) collective-permute-start(bf16[2,144,256]{2,1,0:T(8,128)(2,1)S(1)} %get-tuple-element.31), channel_id=1, source_target_pairs={{0,4},{2,6},{4,0},{6,2},{8,12},{10,14},{12,8},{14,10},{1,5},{3,7},... | collective-permute-start | bytes 442376 | tf_op jit(solution)/shard_map/ppermute | solution.py:581
  31.9 7.2 %collective-permute-start.7 = (bf16[2,144,256]{2,1,0:T(8,128)(2,1)S(1)}, bf16[2,144,256]{2,1,0:T(8,128)(2,1)S(1)}, u32[]{:S(2)}, u32[]{:S(2)}) collective-permute-start(bf16[2,144,256]{2,1,0:T(8,128)(2,1)S(1)} %get-tuple-element.32), channel_id=1, source_target_pairs={{0,2},{2,0},{4,6},{6,4},{8,10},{10,8},{12,14},{14,12},{1,3},{3,1},... | collective-permute-start | bytes 442376 | tf_op jit(solution)/shard_map/ppermute | solution.py:581

commit v16 on v15

--- a/solution.py
+++ b/solution.py
@@ -573,8 +573,8 @@
     group = queries.shape[2] // kv_cache.shape[3]
     count = lax.axis_size("inst")
     half = max(count // 2, 1)
-    early = list(range(half, count - 1)) + [half - 1] * (half > 1)
-    late = [count - 1] + list(range(half - 2, 0, -1))
+    early = list(range(count - 1, half, -1)) + [half - 1] * (half > 1)
+    late = [half] + list(range(half - 2, 0, -1))
 
     def send(block, shift):
         pairs = [(i, peer_to(i, shift, count)) for i in range(count)]

time: 40.4 us -> 41.8 us (1.035)
  starting transfers between devices: 18.6 us -> 20.6 us
  waiting for transfers between devices: 4.02 us -> 3.47 us
    ppermute x7, starting transfers between devices: 13.9 us -> 16.7 us  [send(): return lax.ppermute(block, 'inst', pairs)]
    all_to_all x1, starting transfers between devices: 4.19 us -> 3.36 us  [local(): small_got = lax.all_to_all(small, 'inst', 0, 0, tiled=True)]
  transfers between devices with their start and end apart: 9 -> 9, of which waited for: 4 -> 2; matrix products, arithmetic and copies ran while one was open for 0% -> 0% of each run, Pallas kernels for 23% -> 22%
where the time goes in v16:
time: 41.8 us; the launch traced here: 41.4 us
  starting transfers between devices  20.6 us (49%)
  Pallas kernels  15.8 us (38%)
  waiting for transfers between devices  3.47 us (8%)
  local copies, waits for them, and re-layouts  0.9 us (2%)
  between operations  0.73 us (2%)
    ppermute x7, starting transfers between devices, send(): return lax.ppermute(block, 'inst', pairs)  16.7 us
    pallas_call x1, Pallas kernels, attend(): pl.pallas_call(functools.partial(attend_kernel, count, late, block), grid...  6.61 us
    pallas_call x1, Pallas kernels, prepare(): pl.pallas_call(functools.partial(prepare_kernel, count, early, chunks), o...  5.64 us
    all_to_all x1, starting transfers between devices, local(): small_got = lax.all_to_all(small, 'inst', 0, 0, tiled=True)  3.36 us
    all_to_all x1, waiting for transfers between devices, local(): small_got = lax.all_to_all(small, 'inst', 0, 0, tiled=True)  1.77 us
    ppermute x7, waiting for transfers between devices, send(): return lax.ppermute(block, 'inst', pairs)  1.7 us
    pallas_call x1, Pallas kernels, settle(): pl.pallas_call(functools.partial(settle_kernel, count, early, group), out...  1.57 us
    pallas_call x1, Pallas kernels, land(): pl.pallas_call(functools.partial(land_kernel, pieces), out_shape=[jax.Sha...  1.01 us
  transfers between devices with their start and end apart: 9, of which 2 were waited for; matrix products, arithmetic and copies ran while one was open for 0% of the time, Pallas kernels for 22%

profile of v16, /device:TPU:0, one launch (start us, length us, event | category | flops | bytes accessed | tf_op | source)
XLA Modules:
  0.0 41.4 jit_solution(16078640663218684158)
XLA Ops:
  0.7 5.6 %prepare.1 = (bf16[2,144,256]{2,1,0:T(8,128)(2,1)}, bf16[2,144,256]{2,1,0:T(8,128)(2,1)}, bf16[2,144,256]{2,1,0:T(8,128)(2,1)}, bf16[2,144,256]{2,1,0:T(8,128)(2...) custom-call(s32[24]{0:T(128)} %dest_ref.3, s32[24]{0:T(128)} %length_ref.3, bf16[2,24,2560]{2,1,0:T(8,128)(2,1)} %hidden_ref.1, ...), custom_call_target="tpu_custom_call" | custom-call | flops 1 | bytes 1 | tf_op jit(solution)/shard_map/prepare/pallas_call | solution.py:136
  6.3 0.5 %collective-permute-start = (f32[48,512]{1,0:T(8,128)}, f32[48,512]{1,0:T(8,128)S(1)}, u32[]{:S(2)}, u32[]{:S(2)}) collective-permute-start(f32[48,512]{1,0:T(8,128)} %get-tuple-element.19), channel_id=1, source_target_pairs={{0,1},{1,0},{2,3},{3,2},{4,5},{5,4},{6,7},{7,6},{8,9},{9,8},{10,11... | collective-permute-start | bytes 294920 | tf_op jit(solution)/shard_map/ppermute | solution.py:587
  6.8 5.6 %collective-permute-start.1 = (bf16[2,144,256]{2,1,0:T(8,128)(2,1)}, bf16[2,144,256]{2,1,0:T(8,128)(2,1)S(1)}, u32[]{:S(2)}, u32[]{:S(2)}) collective-permute-start(bf16[2,144,256]{2,1,0:T(8,128)(2,1)} %get-tuple-element.22), channel_id=1, source_target_pairs={{0,14},{2,12},{4,10},{6,8},{8,6},{10,4},{12,2},{14,0},{1,15},{3,13... | collective-permute-start | bytes 442376 | tf_op jit(solution)/shard_map/ppermute | solution.py:581
  12.5 0.2 collective-permute-start.2
  12.7 0.7 %collective-permute-start.3 = (bf16[2,144,256]{2,1,0:T(8,128)(2,1)}, bf16[2,144,256]{2,1,0:T(8,128)(2,1)S(1)}, u32[]{:S(2)}, u32[]{:S(2)}) collective-permute-start(bf16[2,144,256]{2,1,0:T(8,128)(2,1)} %get-tuple-element.24), channel_id=1, source_target_pairs={{0,10},{2,8},{4,14},{6,12},{8,2},{10,0},{12,6},{14,4},{1,11},{3,9}... | collective-permute-start | bytes 442376 | tf_op jit(solution)/shard_map/ppermute | solution.py:581
  13.4 4.3 %collective-permute-start.4 = (bf16[2,144,256]{2,1,0:T(8,128)(2,1)}, bf16[2,144,256]{2,1,0:T(8,128)(2,1)S(1)}, u32[]{:S(2)}, u32[]{:S(2)}) collective-permute-start(bf16[2,144,256]{2,1,0:T(8,128)(2,1)} %get-tuple-element.25), channel_id=1, source_target_pairs={{0,6},{2,4},{4,2},{6,0},{8,14},{10,12},{12,10},{14,8},{1,7},{3,5},... | collective-permute-start | bytes 442376 | tf_op jit(solution)/shard_map/ppermute | solution.py:581
  17.8 0.0 collective-permute-done.got_ref
  17.8 0.0 copy-start.3
  17.8 0.9 %copy-done.3 = f32[48,512]{1,0:T(8,128)S(1)} copy-done((f32[48,512]{1,0:T(8,128)S(1)}, f32[48,512]{1,0:T(8,128)}, u32[]{:S(2)}) %copy-start.3) | copy-done | bytes 98328
  18.7 6.6 %attend.1 = (bf16[24,2,144,256]{3,2,1,0:T(8,128)(2,1)}, bf16[768,128]{1,0:T(8,128)(2,1)S(1)}, bf16[8,48,128]{2,1,0:T(8,128)(2,1)}, bf16[2,144,256]{2,1,0:T(8,128...) custom-call(s32[24]{0:T(128)S(1)} %copy-done, s32[24]{0:T(128)S(1)} %copy-done.1, ...), custom_call_target="tpu_custom_call" | custom-call | flops 68719476736 | bytes 268435456 | tf_op jit(solution)/shard_map/attend/pallas_call | solution.py:324
  25.3 3.4 %all-to-all-start = ((bf16[8,48,128]{2,1,0:T(8,128)(2,1)}), bf16[8,48,128]{2,1,0:T(8,128)(2,1)S(1)}, u32[]{:S(2)}, u32[]{:S(2)}) async-start(bf16[8,48,128]{2,1,0:T(8,128)(2,1)} %get-tuple-element.21), calls=%async_computation | async-start | bytes 196608 | tf_op jit(solution)/shard_map/all_to_all | solution.py:600
  28.7 2.8 %collective-permute-start.5 = (bf16[2,144,256]{2,1,0:T(8,128)(2,1)S(1)}, bf16[2,144,256]{2,1,0:T(8,128)(2,1)S(1)}, u32[]{:S(2)}, u32[]{:S(2)}) collective-permute-start(bf16[2,144,256]{2,1,0:T(8,128)(2,1)S(1)} %get-tuple-element.30), channel_id=1, source_target_pairs={{0,8},{2,10},{4,12},{6,14},{8,0},{10,2},{12,4},{14,6},{1,9},{3,11}... | collective-permute-start | bytes 442376 | tf_op jit(solution)/shard_map/ppermute | solution.py:581
  31.5 0.0 collective-permute-done.1.refs_0_
  31.5 1.5 %collective-permute-start.6 = (bf16[2,144,256]{2,1,0:T(8,128)(2,1)S(1)}, bf16[2,144,256]{2,1,0:T(8,128)(2,1)S(1)}, u32[]{:S(2)}, u32[]{:S(2)}) collective-permute-start(bf16[2,144,256]{2,1,0:T(8,128)(2,1)S(1)} %get-tuple-element.31), channel_id=1, source_target_pairs={{0,4},{2,6},{4,0},{6,2},{8,12},{10,14},{12,8},{14,10},{1,5},{3,7},... | collective-permute-start | bytes 442376 | tf_op jit(solution)/shard_map/ppermute | solution.py:581
  33.0 0.0 collective-permute-done.2.refs_1_
  33.0 1.5 %collective-permute-start.7 = (bf16[2,144,256]{2,1,0:T(8,128)(2,1)S(1)}, bf16[2,144,256]{2,1,0:T(8,128)(2,1)S(1)}, u32[]{:S(2)}, u32[]{:S(2)}) collective-permute-start(bf16[2,144,256]{2,1,0:T(8,128)(2,1)S(1)} %get-tuple-element.32), channel_id=1, source_target_pairs={{0,2},{2,0},{4,6},{6,4},{8,10},{10,8},{12,14},{14,12},{1,3},{3,1},... | collective-permute-start | bytes 442376 | tf_op jit(solution)/shard_map/ppermute | solution.py:581
  34.5 0.0 collective-permute-done.3.refs_2_
  34.5 0.0 collective-permute-done.4.refs_3_
  34.5 1.0 %land.1 = (bf16[24,2,144,256]{3,2,1,0:T(8,128)(2,1)}, bf16[4,2,32,256]{3,2,1,0:T(8,128)(2,1)S(1)}) custom-call(bf16[2,144,256]{2,1,0:T(8,128)(2,1)S(1)} %collective-permute-done.1.refs_0_, bf16[2,144,256]{2,1,0:T(8,128)(2,1)S(1)} %collective-permute-done.2.refs_1_, ...), custom_call_target="tpu_custom_call", output_to_operand_aliasing={{0}: (4, {})} | custom-call | flops 68719476736 | bytes 268435456 | tf_op jit(solution)/shard_map/land/pallas_call | solution.py:414
  35.5 1.8 %all-to-all-done.small_ref.refs_3_ = bf16[8,48,128]{2,1,0:T(8,128)(2,1)S(1)} async-done(((bf16[8,48,128]{2,1,0:T(8,128)(2,1)}), bf16[8,48,128]{2,1,0:T(8,128)(2,1)S(1)}, u32[]{:S(2)}, u32[]{:S(2)}) %all-to-all-start) | async-done | bytes 98336 | tf_op jit(solution)/shard_map/all_to_all | solution.py:600
  37.3 1.6 %settle.1 = (bf16[2,24,2048]{2,1,0:T(8,128)(2,1)}, bf16[24,2,144,256]{3,2,1,0:T(8,128)(2,1)}) custom-call(bf16[768,128]{1,0:T(8,128)(2,1)S(1)} %get-tuple-element.20.mixed_ref, bf16[8,48,128]{2,1,0:T(8,128)(2,1)S(1)} %all-to-all-done.small_ref.refs_3_, bf16[4,2,32,256]{3,2,1,0:T(8,128)(2,1)S(1)} %get-tuple-element.27.window_ref, ...), custom_call_target="tpu_custom_call", output_to_operand_aliasing={{1}: (3, {})} | custom-call | flops 1 | bytes 1 | tf_op jit(solution)/shard_map/settle/pallas_call | solution.py:510
  38.8 1.7 %collective-permute-done.5.refs_0_ = bf16[2,144,256]{2,1,0:T(8,128)(2,1)S(1)} collective-permute-done((bf16[2,144,256]{2,1,0:T(8,128)(2,1)S(1)}, bf16[2,144,256]{2,1,0:T(8,128)(2,1)S(1)}, u32[]{:S(2)}, u32[]{:S(2)}) %collective-permute-start.5) | collective-permute-done | bytes 147488 | tf_op jit(solution)/shard_map/ppermute | solution.py:581
  40.5 0.0 collective-permute-done.7.refs_2_
  40.5 0.9 %finish.1 = bf16[24,2,144,256]{3,2,1,0:T(8,128)(2,1)} custom-call(bf16[2,144,256]{2,1,0:T(8,128)(2,1)S(1)} %collective-permute-done.5.refs_0_, bf16[2,144,256]{2,1,0:T(8,128)(2,1)S(1)} %collective-permute-done.6.refs_1_, bf16[2,144,256]{2,1,0:T(8,128)(2,1)S(1)} %collective-permute-done.7.refs_2_, ...), custom_call_target="tpu_custom_call", output_to_operand_aliasing={{}: (4, {})} | custom-call | flops 1 | bytes 1 | tf_op jit(solution)/shard_map/finish/pallas_call | solution.py:555
  (9 shorter events, 0.0 us)
Async XLA Ops:
  0.6 17.1 %copy-start.1 = (s32[24]{0:T(128)S(1)}, s32[24]{0:T(128)}, u32[]{:S(2)}) copy-start(s32[24]{0:T(128)} %dest_ref.3) | copy-start | bytes 292
  0.6 17.1 %copy-start = (s32[24]{0:T(128)S(1)}, s32[24]{0:T(128)}, u32[]{:S(2)}) copy-start(s32[24]{0:T(128)} %length_ref.3) | copy-start | bytes 292
  0.7 17.1 %copy-start.4 = (bf16[128]{0:T(256)(128)(2,1)S(1)}, bf16[128]{0:T(256)(128)(2,1)}, u32[]{:S(2)}) copy-start(bf16[128]{0:T(256)(128)(2,1)} %param.15) | copy-start | bytes 772
  0.7 17.1 %copy-start.2 = (bf16[2,24,2048]{2,1,0:T(8,128)(2,1)S(1)}, bf16[2,24,2048]{2,1,0:T(8,128)(2,1)}, u32[]{:S(2)}) copy-start(bf16[2,24,2048]{2,1,0:T(8,128)(2,1)} %query_ref.1) | copy-start | bytes 589828
  6.3 11.4 %collective-permute-start = (f32[48,512]{1,0:T(8,128)}, f32[48,512]{1,0:T(8,128)S(1)}, u32[]{:S(2)}, u32[]{:S(2)}) collective-permute-start(f32[48,512]{1,0:T(8,128)} %get-tuple-element.19), channel_id=1, source_target_pairs={{0,1},{1,0},{2,3},{3,2},{4,5},{5,4},{6,7},{7,6},{8,9},{9,8},{10,11... | collective-permute-start | bytes 294920 | tf_op jit(solution)/shard_map/ppermute | solution.py:587
  6.8 24.7 %collective-permute-start.1 = (bf16[2,144,256]{2,1,0:T(8,128)(2,1)}, bf16[2,144,256]{2,1,0:T(8,128)(2,1)S(1)}, u32[]{:S(2)}, u32[]{:S(2)}) collective-permute-start(bf16[2,144,256]{2,1,0:T(8,128)(2,1)} %get-tuple-element.22), channel_id=1, source_target_pairs={{0,14},{2,12},{4,10},{6,8},{8,6},{10,4},{12,2},{14,0},{1,15},{3,13... | collective-permute-start | bytes 442376 | tf_op jit(solution)/shard_map/ppermute | solution.py:581
  12.5 20.5 %collective-permute-start.2 = (bf16[2,144,256]{2,1,0:T(8,128)(2,1)}, bf16[2,144,256]{2,1,0:T(8,128)(2,1)S(1)}, u32[]{:S(2)}, u32[]{:S(2)}) collective-permute-start(bf16[2,144,256]{2,1,0:T(8,128)(2,1)} %get-tuple-element.23), channel_id=1, source_target_pairs={{0,12},{2,14},{4,8},{6,10},{8,4},{10,6},{12,0},{14,2},{1,13},{3,15... | collective-permute-start | bytes 442376 | tf_op jit(solution)/shard_map/ppermute | solution.py:581
  12.7 21.8 %collective-permute-start.3 = (bf16[2,144,256]{2,1,0:T(8,128)(2,1)}, bf16[2,144,256]{2,1,0:T(8,128)(2,1)S(1)}, u32[]{:S(2)}, u32[]{:S(2)}) collective-permute-start(bf16[2,144,256]{2,1,0:T(8,128)(2,1)} %get-tuple-element.24), channel_id=1, source_target_pairs={{0,10},{2,8},{4,14},{6,12},{8,2},{10,0},{12,6},{14,4},{1,11},{3,9}... | collective-permute-start | bytes 442376 | tf_op jit(solution)/shard_map/ppermute | solution.py:581
  13.4 21.0 %collective-permute-start.4 = (bf16[2,144,256]{2,1,0:T(8,128)(2,1)}, bf16[2,144,256]{2,1,0:T(8,128)(2,1)S(1)}, u32[]{:S(2)}, u32[]{:S(2)}) collective-permute-start(bf16[2,144,256]{2,1,0:T(8,128)(2,1)} %get-tuple-element.25), channel_id=1, source_target_pairs={{0,6},{2,4},{4,2},{6,0},{8,14},{10,12},{12,10},{14,8},{1,7},{3,5},... | collective-permute-start | bytes 442376 | tf_op jit(solution)/shard_map/ppermute | solution.py:581
  17.8 0.9 %copy-start.3 = (f32[48,512]{1,0:T(8,128)S(1)}, f32[48,512]{1,0:T(8,128)}, u32[]{:S(2)}) copy-start(f32[48,512]{1,0:T(8,128)} %get-tuple-element.18.own_ref) | copy-start | bytes 294916
  25.3 12.0 %all-to-all-start = ((bf16[8,48,128]{2,1,0:T(8,128)(2,1)}), bf16[8,48,128]{2,1,0:T(8,128)(2,1)S(1)}, u32[]{:S(2)}, u32[]{:S(2)}) async-start(bf16[8,48,128]{2,1,0:T(8,128)(2,1)} %get-tuple-element.21), calls=%async_computation | async-start | bytes 196608 | tf_op jit(solution)/shard_map/all_to_all | solution.py:600
  28.7 11.8 %collective-permute-start.5 = (bf16[2,144,256]{2,1,0:T(8,128)(2,1)S(1)}, bf16[2,144,256]{2,1,0:T(8,128)(2,1)S(1)}, u32[]{:S(2)}, u32[]{:S(2)}) collective-permute-start(bf16[2,144,256]{2,1,0:T(8,128)(2,1)S(1)} %get-tuple-element.30), channel_id=1, source_target_pairs={{0,8},{2,10},{4,12},{6,14},{8,0},{10,2},{12,4},{14,6},{1,9},{3,11}... | collective-permute-start | bytes 442376 | tf_op jit(solution)/shard_map/ppermute | solution.py:581
  31.5 9.0 %collective-permute-start.6 = (bf16[2,144,256]{2,1,0:T(8,128)(2,1)S(1)}, bf16[2,144,256]{2,1,0:T(8,128)(2,1)S(1)}, u32[]{:S(2)}, u32[]{:S(2)}) collective-permute-start(bf16[2,144,256]{2,1,0:T(8,128)(2,1)S(1)} %get-tuple-element.31), channel_id=1, source_target_pairs={{0,4},{2,6},{4,0},{6,2},{8,12},{10,14},{12,8},{14,10},{1,5},{3,7},... | collective-permute-start | bytes 442376 | tf_op jit(solution)/shard_map/ppermute | solution.py:581
  33.0 7.5 %collective-permute-start.7 = (bf16[2,144,256]{2,1,0:T(8,128)(2,1)S(1)}, bf16[2,144,256]{2,1,0:T(8,128)(2,1)S(1)}, u32[]{:S(2)}, u32[]{:S(2)}) collective-permute-start(bf16[2,144,256]{2,1,0:T(8,128)(2,1)S(1)} %get-tuple-element.32), channel_id=1, source_target_pairs={{0,2},{2,0},{4,6},{6,4},{8,10},{10,8},{12,14},{14,12},{1,3},{3,1},... | collective-permute-start | bytes 442376 | tf_op jit(solution)/shard_map/ppermute | solution.py:581

commit v17 on v16

--- a/solution.py
+++ b/solution.py
@@ -573,8 +573,9 @@
     group = queries.shape[2] // kv_cache.shape[3]
     count = lax.axis_size("inst")
     half = max(count // 2, 1)
-    early = list(range(count - 1, half, -1)) + [half - 1] * (half > 1)
-    late = [half] + list(range(half - 2, 0, -1))
+    inner = list(range(half - 1, 0, -1))
+    early = list(range(half, count - 1)) + inner[:2]
+    late = [count - 1] + inner[2:]
 
     def send(block, shift):
         pairs = [(i, peer_to(i, shift, count)) for i in range(count)]

time: 41.8 us -> 41.5 us (level)
  starting transfers between devices: 20.6 us -> 19.6 us
  waiting for transfers between devices: 3.47 us -> 4.12 us
    ppermute x7, starting transfers between devices: 16.7 us -> 15.7 us  [send(): return lax.ppermute(block, 'inst', pairs)]
    ppermute x7, waiting for transfers between devices: 1.7 us -> 2.17 us  [send(): return lax.ppermute(block, 'inst', pairs)]
  transfers between devices with their start and end apart: 9 -> 9, of which waited for: 2 -> 3; matrix products, arithmetic and copies ran while one was open for 0% -> 0% of each run, Pallas kernels for 22% -> 22%
where the time goes in v17:
time: 41.5 us; the launch traced here: 41.2 us
  starting transfers between devices  19.6 us (47%)
  Pallas kernels  15.8 us (38%)
  waiting for transfers between devices  4.12 us (10%)
  local copies, waits for them, and re-layouts  0.9 us (2%)
  between operations  0.73 us (2%)
    ppermute x7, starting transfers between devices, send(): return lax.ppermute(block, 'inst', pairs)  15.7 us
    pallas_call x1, Pallas kernels, attend(): pl.pallas_call(functools.partial(attend_kernel, count, late, block), grid...  6.6 us
    pallas_call x1, Pallas kernels, prepare(): pl.pallas_call(functools.partial(prepare_kernel, count, early, chunks), o...  5.72 us
    all_to_all x1, starting transfers between devices, local(): small_got = lax.all_to_all(small, 'inst', 0, 0, tiled=True)  3.36 us
    ppermute x7, waiting for transfers between devices, send(): return lax.ppermute(block, 'inst', pairs)  2.17 us
    all_to_all x1, waiting for transfers between devices, local(): small_got = lax.all_to_all(small, 'inst', 0, 0, tiled=True)  1.94 us
    pallas_call x1, Pallas kernels, settle(): pl.pallas_call(functools.partial(settle_kernel, count, early, group), out...  1.6 us
    pallas_call x1, Pallas kernels, land(): pl.pallas_call(functools.partial(land_kernel, pieces), out_shape=[jax.Sha...  1.07 us
  transfers between devices with their start and end apart: 9, of which 3 were waited for; matrix products, arithmetic and copies ran while one was open for 0% of the time, Pallas kernels for 22%

profile of v17, /device:TPU:0, one launch (start us, length us, event | category | flops | bytes accessed | tf_op | source)
XLA Modules:
  0.0 41.2 jit_solution(13376849612515523810)
XLA Ops:
  0.7 5.7 %prepare.1 = (bf16[2,144,256]{2,1,0:T(8,128)(2,1)}, bf16[2,144,256]{2,1,0:T(8,128)(2,1)}, bf16[2,144,256]{2,1,0:T(8,128)(2,1)}, bf16[2,144,256]{2,1,0:T(8,128)(2...) custom-call(s32[24]{0:T(128)} %dest_ref.3, s32[24]{0:T(128)} %length_ref.3, ...), custom_call_target="tpu_custom_call" | custom-call | flops 1 | bytes 1 | tf_op jit(solution)/shard_map/prepare/pallas_call | solution.py:136
  6.4 0.5 %collective-permute-start = (f32[48,512]{1,0:T(8,128)}, f32[48,512]{1,0:T(8,128)S(1)}, u32[]{:S(2)}, u32[]{:S(2)}) collective-permute-start(f32[48,512]{1,0:T(8,128)} %get-tuple-element.19), channel_id=1, source_target_pairs={{0,1},{1,0},{2,3},{3,2},{4,5},{5,4},{6,7},{7,6},{8,9},{9,8},{10,11... | collective-permute-start | bytes 294920 | tf_op jit(solution)/shard_map/ppermute | solution.py:588
  6.9 3.7 %collective-permute-start.1 = (bf16[2,144,256]{2,1,0:T(8,128)(2,1)}, bf16[2,144,256]{2,1,0:T(8,128)(2,1)S(1)}, u32[]{:S(2)}, u32[]{:S(2)}) collective-permute-start(bf16[2,144,256]{2,1,0:T(8,128)(2,1)} %get-tuple-element.22), channel_id=1, source_target_pairs={{0,8},{2,10},{4,12},{6,14},{8,0},{10,2},{12,4},{14,6},{1,9},{3,11}... | collective-permute-start | bytes 442376 | tf_op jit(solution)/shard_map/ppermute | solution.py:582
  10.6 1.3 %collective-permute-start.2 = (bf16[2,144,256]{2,1,0:T(8,128)(2,1)}, bf16[2,144,256]{2,1,0:T(8,128)(2,1)S(1)}, u32[]{:S(2)}, u32[]{:S(2)}) collective-permute-start(bf16[2,144,256]{2,1,0:T(8,128)(2,1)} %get-tuple-element.23), channel_id=1, source_target_pairs={{0,10},{2,8},{4,14},{6,12},{8,2},{10,0},{12,6},{14,4},{1,11},{3,9}... | collective-permute-start | bytes 442376 | tf_op jit(solution)/shard_map/ppermute | solution.py:582
  11.9 3.6 %collective-permute-start.3 = (bf16[2,144,256]{2,1,0:T(8,128)(2,1)}, bf16[2,144,256]{2,1,0:T(8,128)(2,1)S(1)}, u32[]{:S(2)}, u32[]{:S(2)}) collective-permute-start(bf16[2,144,256]{2,1,0:T(8,128)(2,1)} %get-tuple-element.24), channel_id=1, source_target_pairs={{0,12},{2,14},{4,8},{6,10},{8,4},{10,6},{12,0},{14,2},{1,13},{3,15... | collective-permute-start | bytes 442376 | tf_op jit(solution)/shard_map/ppermute | solution.py:582
  15.5 0.0 collective-permute-start.4
  15.5 0.0 collective-permute-done.got_ref
  15.5 2.0 %collective-permute-start.5 = (bf16[2,144,256]{2,1,0:T(8,128)(2,1)}, bf16[2,144,256]{2,1,0:T(8,128)(2,1)S(1)}, u32[]{:S(2)}, u32[]{:S(2)}) collective-permute-start(bf16[2,144,256]{2,1,0:T(8,128)(2,1)} %get-tuple-element.26), channel_id=1, source_target_pairs={{0,4},{2,6},{4,0},{6,2},{8,12},{10,14},{12,8},{14,10},{1,5},{3,7},... | collective-permute-start | bytes 442376 | tf_op jit(solution)/shard_map/ppermute | solution.py:582
  17.5 0.0 copy-start.3
  17.5 0.9 %copy-done.3 = f32[48,512]{1,0:T(8,128)S(1)} copy-done((f32[48,512]{1,0:T(8,128)S(1)}, f32[48,512]{1,0:T(8,128)}, u32[]{:S(2)}) %copy-start.3) | copy-done | bytes 98328
  18.4 6.6 %attend.1 = (bf16[24,2,144,256]{3,2,1,0:T(8,128)(2,1)}, bf16[768,128]{1,0:T(8,128)(2,1)S(1)}, bf16[8,48,128]{2,1,0:T(8,128)(2,1)}, bf16[2,144,256]{2,1,0:T(8,128)(2,1)S(1)}, bf16[2,144,256]{2,1,0:T(8,128)(2,1)S(1)}) custom-call(s32[24]{0:T(128)S(1)} %copy-done, s32[24]{0:T(128)S(1)} %copy-done.1, f32[48,512]{1,0:T(8,128)S(1)} %copy-done.3, ...), custom_call_target="tpu_custom_call" | custom-call | flops 68719476736 | bytes 268435456 | tf_op jit(solution)/shard_map/attend/pallas_call | solution.py:324
  25.0 3.4 %all-to-all-start = ((bf16[8,48,128]{2,1,0:T(8,128)(2,1)}), bf16[8,48,128]{2,1,0:T(8,128)(2,1)S(1)}, u32[]{:S(2)}, u32[]{:S(2)}) async-start(bf16[8,48,128]{2,1,0:T(8,128)(2,1)} %get-tuple-element.21), calls=%async_computation | async-start | bytes 196608 | tf_op jit(solution)/shard_map/all_to_all | solution.py:601
  28.3 0.0 collective-permute-done.1.refs_0_
  28.3 4.7 %collective-permute-start.6 = (bf16[2,144,256]{2,1,0:T(8,128)(2,1)S(1)}, bf16[2,144,256]{2,1,0:T(8,128)(2,1)S(1)}, u32[]{:S(2)}, u32[]{:S(2)}) collective-permute-start(bf16[2,144,256]{2,1,0:T(8,128)(2,1)S(1)} %get-tuple-element.31), channel_id=1, source_target_pairs={{0,14},{2,12},{4,10},{6,8},{8,6},{10,4},{12,2},{14,0},{1,15},{3,13... | collective-permute-start | bytes 442376 | tf_op jit(solution)/shard_map/ppermute | solution.py:582
  33.0 0.6 %collective-permute-start.7 = (bf16[2,144,256]{2,1,0:T(8,128)(2,1)S(1)}, bf16[2,144,256]{2,1,0:T(8,128)(2,1)S(1)}, u32[]{:S(2)}, u32[]{:S(2)}) collective-permute-start(bf16[2,144,256]{2,1,0:T(8,128)(2,1)S(1)} %get-tuple-element.32), channel_id=1, source_target_pairs={{0,2},{2,0},{4,6},{6,4},{8,10},{10,8},{12,14},{14,12},{1,3},{3,1},... | collective-permute-start | bytes 442376 | tf_op jit(solution)/shard_map/ppermute | solution.py:582
  33.5 0.0 collective-permute-done.3.refs_2_
  33.5 0.0 collective-permute-done.4.refs_3_
  33.5 1.5 %collective-permute-done.5.refs_4_ = bf16[2,144,256]{2,1,0:T(8,128)(2,1)S(1)} collective-permute-done((bf16[2,144,256]{2,1,0:T(8,128)(2,1)}, bf16[2,144,256]{2,1,0:T(8,128)(2,1)S(1)}, u32[]{:S(2)}, u32[]{:S(2)}) %collective-permute-start.5) | collective-permute-done | bytes 147488 | tf_op jit(solution)/shard_map/ppermute | solution.py:582
  35.1 1.1 %land.1 = (bf16[24,2,144,256]{3,2,1,0:T(8,128)(2,1)}, bf16[5,2,32,256]{3,2,1,0:T(8,128)(2,1)S(1)}) custom-call(bf16[2,144,256]{2,1,0:T(8,128)(2,1)S(1)} %collective-permute-done.1.refs_0_, bf16[2,144,256]{2,1,0:T(8,128)(2,1)S(1)} %collective-permute-done.2.refs_1_, ...), custom_call_target="tpu_custom_call", output_to_operand_aliasing={{0}: (5, {})} | custom-call | flops 68719476736 | bytes 268435456 | tf_op jit(solution)/shard_map/land/pallas_call | solution.py:414
  36.1 1.9 %all-to-all-done.small_ref.refs_2_ = bf16[8,48,128]{2,1,0:T(8,128)(2,1)S(1)} async-done(((bf16[8,48,128]{2,1,0:T(8,128)(2,1)}), bf16[8,48,128]{2,1,0:T(8,128)(2,1)S(1)}, u32[]{:S(2)}, u32[]{:S(2)}) %all-to-all-start) | async-done | bytes 98336 | tf_op jit(solution)/shard_map/all_to_all | solution.py:601
  38.1 1.6 %settle.1 = (bf16[2,24,2048]{2,1,0:T(8,128)(2,1)}, bf16[24,2,144,256]{3,2,1,0:T(8,128)(2,1)}) custom-call(bf16[768,128]{1,0:T(8,128)(2,1)S(1)} %get-tuple-element.20.mixed_ref, bf16[8,48,128]{2,1,0:T(8,128)(2,1)S(1)} %all-to-all-done.small_ref.refs_2_, bf16[5,2,32,256]{3,2,1,0:T(8,128)(2,1)S(1)} %get-tuple-element.28.window_ref, ...), custom_call_target="tpu_custom_call", output_to_operand_aliasing={{1}: (3, {})} | custom-call | flops 1 | bytes 1 | tf_op jit(solution)/shard_map/settle/pallas_call | solution.py:510
  39.7 0.0 collective-permute-done.6.refs_0_
  39.7 0.6 %collective-permute-done.7.refs_1_ = bf16[2,144,256]{2,1,0:T(8,128)(2,1)S(1)} collective-permute-done((bf16[2,144,256]{2,1,0:T(8,128)(2,1)S(1)}, bf16[2,144,256]{2,1,0:T(8,128)(2,1)S(1)}, u32[]{:S(2)}, u32[]{:S(2)}) %collective-permute-start.7) | collective-permute-done | bytes 147488 | tf_op jit(solution)/shard_map/ppermute | solution.py:582
  40.4 0.8 %finish.1 = bf16[24,2,144,256]{3,2,1,0:T(8,128)(2,1)} custom-call(bf16[2,144,256]{2,1,0:T(8,128)(2,1)S(1)} %collective-permute-done.6.refs_0_, bf16[2,144,256]{2,1,0:T(8,128)(2,1)S(1)} %collective-permute-done.7.refs_1_, bf16[8,48,128]{2,1,0:T(8,128)(2,1)S(1)} %all-to-all-done.small_ref.refs_2_, ...), custom_call_target="tpu_custom_call", output_to_operand_aliasing={{}: (3, {})} | custom-call | flops 1 | bytes 1 | tf_op jit(solution)/shard_map/finish/pallas_call | solution.py:555
  (9 shorter events, 0.0 us)
Async XLA Ops:
  0.6 16.8 %copy-start.1 = (s32[24]{0:T(128)S(1)}, s32[24]{0:T(128)}, u32[]{:S(2)}) copy-start(s32[24]{0:T(128)} %dest_ref.3) | copy-start | bytes 292
  0.6 16.8 %copy-start = (s32[24]{0:T(128)S(1)}, s32[24]{0:T(128)}, u32[]{:S(2)}) copy-start(s32[24]{0:T(128)} %length_ref.3) | copy-start | bytes 292
  0.7 16.8 %copy-start.4 = (bf16[128]{0:T(256)(128)(2,1)S(1)}, bf16[128]{0:T(256)(128)(2,1)}, u32[]{:S(2)}) copy-start(bf16[128]{0:T(256)(128)(2,1)} %param.15) | copy-start | bytes 772
  0.7 16.8 %copy-start.2 = (bf16[2,24,2048]{2,1,0:T(8,128)(2,1)S(1)}, bf16[2,24,2048]{2,1,0:T(8,128)(2,1)}, u32[]{:S(2)}) copy-start(bf16[2,24,2048]{2,1,0:T(8,128)(2,1)} %query_ref.1) | copy-start | bytes 589828
  6.4 9.1 %collective-permute-start = (f32[48,512]{1,0:T(8,128)}, f32[48,512]{1,0:T(8,128)S(1)}, u32[]{:S(2)}, u32[]{:S(2)}) collective-permute-start(f32[48,512]{1,0:T(8,128)} %get-tuple-element.19), channel_id=1, source_target_pairs={{0,1},{1,0},{2,3},{3,2},{4,5},{5,4},{6,7},{7,6},{8,9},{9,8},{10,11... | collective-permute-start | bytes 294920 | tf_op jit(solution)/shard_map/ppermute | solution.py:588
  6.9 21.4 %collective-permute-start.1 = (bf16[2,144,256]{2,1,0:T(8,128)(2,1)}, bf16[2,144,256]{2,1,0:T(8,128)(2,1)S(1)}, u32[]{:S(2)}, u32[]{:S(2)}) collective-permute-start(bf16[2,144,256]{2,1,0:T(8,128)(2,1)} %get-tuple-element.22), channel_id=1, source_target_pairs={{0,8},{2,10},{4,12},{6,14},{8,0},{10,2},{12,4},{14,6},{1,9},{3,11}... | collective-permute-start | bytes 442376 | tf_op jit(solution)/shard_map/ppermute | solution.py:582
  10.6 22.4 %collective-permute-start.2 = (bf16[2,144,256]{2,1,0:T(8,128)(2,1)}, bf16[2,144,256]{2,1,0:T(8,128)(2,1)S(1)}, u32[]{:S(2)}, u32[]{:S(2)}) collective-permute-start(bf16[2,144,256]{2,1,0:T(8,128)(2,1)} %get-tuple-element.23), channel_id=1, source_target_pairs={{0,10},{2,8},{4,14},{6,12},{8,2},{10,0},{12,6},{14,4},{1,11},{3,9}... | collective-permute-start | bytes 442376 | tf_op jit(solution)/shard_map/ppermute | solution.py:582
  11.9 21.7 %collective-permute-start.3 = (bf16[2,144,256]{2,1,0:T(8,128)(2,1)}, bf16[2,144,256]{2,1,0:T(8,128)(2,1)S(1)}, u32[]{:S(2)}, u32[]{:S(2)}) collective-permute-start(bf16[2,144,256]{2,1,0:T(8,128)(2,1)} %get-tuple-element.24), channel_id=1, source_target_pairs={{0,12},{2,14},{4,8},{6,10},{8,4},{10,6},{12,0},{14,2},{1,13},{3,15... | collective-permute-start | bytes 442376 | tf_op jit(solution)/shard_map/ppermute | solution.py:582
  15.5 18.1 %collective-permute-start.4 = (bf16[2,144,256]{2,1,0:T(8,128)(2,1)}, bf16[2,144,256]{2,1,0:T(8,128)(2,1)S(1)}, u32[]{:S(2)}, u32[]{:S(2)}) collective-permute-start(bf16[2,144,256]{2,1,0:T(8,128)(2,1)} %get-tuple-element.25), channel_id=1, source_target_pairs={{0,6},{2,4},{4,2},{6,0},{8,14},{10,12},{12,10},{14,8},{1,7},{3,5},... | collective-permute-start | bytes 442376 | tf_op jit(solution)/shard_map/ppermute | solution.py:582
  15.5 19.6 %collective-permute-start.5 = (bf16[2,144,256]{2,1,0:T(8,128)(2,1)}, bf16[2,144,256]{2,1,0:T(8,128)(2,1)S(1)}, u32[]{:S(2)}, u32[]{:S(2)}) collective-permute-start(bf16[2,144,256]{2,1,0:T(8,128)(2,1)} %get-tuple-element.26), channel_id=1, source_target_pairs={{0,4},{2,6},{4,0},{6,2},{8,12},{10,14},{12,8},{14,10},{1,5},{3,7},... | collective-permute-start | bytes 442376 | tf_op jit(solution)/shard_map/ppermute | solution.py:582
  17.5 0.9 %copy-start.3 = (f32[48,512]{1,0:T(8,128)S(1)}, f32[48,512]{1,0:T(8,128)}, u32[]{:S(2)}) copy-start(f32[48,512]{1,0:T(8,128)} %get-tuple-element.18.own_ref) | copy-start | bytes 294916
  25.0 13.1 %all-to-all-start = ((bf16[8,48,128]{2,1,0:T(8,128)(2,1)}), bf16[8,48,128]{2,1,0:T(8,128)(2,1)S(1)}, u32[]{:S(2)}, u32[]{:S(2)}) async-start(bf16[8,48,128]{2,1,0:T(8,128)(2,1)} %get-tuple-element.21), calls=%async_computation | async-start | bytes 196608 | tf_op jit(solution)/shard_map/all_to_all | solution.py:601
  28.3 11.4 %collective-permute-start.6 = (bf16[2,144,256]{2,1,0:T(8,128)(2,1)S(1)}, bf16[2,144,256]{2,1,0:T(8,128)(2,1)S(1)}, u32[]{:S(2)}, u32[]{:S(2)}) collective-permute-start(bf16[2,144,256]{2,1,0:T(8,128)(2,1)S(1)} %get-tuple-element.31), channel_id=1, source_target_pairs={{0,14},{2,12},{4,10},{6,8},{8,6},{10,4},{12,2},{14,0},{1,15},{3,13... | collective-permute-start | bytes 442376 | tf_op jit(solution)/shard_map/ppermute | solution.py:582
  33.0 7.4 %collective-permute-start.7 = (bf16[2,144,256]{2,1,0:T(8,128)(2,1)S(1)}, bf16[2,144,256]{2,1,0:T(8,128)(2,1)S(1)}, u32[]{:S(2)}, u32[]{:S(2)}) collective-permute-start(bf16[2,144,256]{2,1,0:T(8,128)(2,1)S(1)} %get-tuple-element.32), channel_id=1, source_target_pairs={{0,2},{2,0},{4,6},{6,4},{8,10},{10,8},{12,14},{14,12},{1,3},{3,1},... | collective-permute-start | bytes 442376 | tf_op jit(solution)/shard_map/ppermute | solution.py:582

commit v18 on v15

--- a/solution.py
+++ b/solution.py
@@ -574,7 +574,8 @@
     count = lax.axis_size("inst")
     half = max(count // 2, 1)
     early = list(range(half, count - 1)) + [half - 1] * (half > 1)
-    late = [count - 1] + list(range(half - 2, 0, -1))
+    inner = list(range(half - 2, 0, -1))
+    late = inner[:1] + [count - 1] + inner[1:]
 
     def send(block, shift):
         pairs = [(i, peer_to(i, shift, count)) for i in range(count)]

time: 40.4 us -> 41.2 us (1.020)
  starting transfers between devices: 18.6 us -> 19.1 us
    ppermute x7, waiting for transfers between devices: 1.96 us -> 3.31 us  [send(): return lax.ppermute(block, 'inst', pairs)]
    all_to_all x1, waiting for transfers between devices: 2.06 us -> 1.05 us  [local(): small_got = lax.all_to_all(small, 'inst', 0, 0, tiled=True)]
    ppermute x7, starting transfers between devices: 13.9 us -> 14.4 us  [send(): return lax.ppermute(block, 'inst', pairs)]
  transfers between devices with their start and end apart: 9 -> 9, of which waited for: 4 -> 3; matrix products, arithmetic and copies ran while one was open for 0% -> 0% of each run, Pallas kernels for 23% -> 22%
where the time goes in v18:
time: 41.2 us; the launch traced here: 40.8 us
  starting transfers between devices  19.1 us (46%)
  Pallas kernels  15.7 us (38%)
  waiting for transfers between devices  4.36 us (11%)
  local copies, waits for them, and re-layouts  0.9 us (2%)
  between operations  0.74 us (2%)
    ppermute x7, starting transfers between devices, send(): return lax.ppermute(block, 'inst', pairs)  14.4 us
    pallas_call x1, Pallas kernels, attend(): pl.pallas_call(functools.partial(attend_kernel, count, late, block), grid...  6.6 us
    pallas_call x1, Pallas kernels, prepare(): pl.pallas_call(functools.partial(prepare_kernel, count, early, chunks), o...  5.64 us
    all_to_all x1, starting transfers between devices, local(): small_got = lax.all_to_all(small, 'inst', 0, 0, tiled=True)  4.18 us
    ppermute x7, waiting for transfers between devices, send(): return lax.ppermute(block, 'inst', pairs)  3.31 us
    pallas_call x1, Pallas kernels, settle(): pl.pallas_call(functools.partial(settle_kernel, count, early, group), out...  1.56 us
    all_to_all x1, waiting for transfers between devices, local(): small_got = lax.all_to_all(small, 'inst', 0, 0, tiled=True)  1.05 us
    pallas_call x1, Pallas kernels, land(): pl.pallas_call(functools.partial(land_kernel, pieces), out_shape=[jax.Sha...  1.01 us
  transfers between devices with their start and end apart: 9, of which 3 were waited for; matrix products, arithmetic and copies ran while one was open for 0% of the time, Pallas kernels for 22%

profile of v18, /device:TPU:0, one launch (start us, length us, event | category | flops | bytes accessed | tf_op | source)
XLA Modules:
  0.0 40.8 jit_solution(1931439576678913733)
XLA Ops:
  0.7 5.6 %prepare.1 = (bf16[2,144,256]{2,1,0:T(8,128)(2,1)}, bf16[2,144,256]{2,1,0:T(8,128)(2,1)}, bf16[2,144,256]{2,1,0:T(8,128)(2,1)}, bf16[2,144,256]{2,1,0:T(8,128)(2...) custom-call(s32[24]{0:T(128)} %dest_ref.3, s32[24]{0:T(128)} %length_ref.3, bf16[2,24,2560]{2,1,0:T(8,128)(2,1)} %hidden_ref.1, ...), custom_call_target="tpu_custom_call" | custom-call | flops 1 | bytes 1 | tf_op jit(solution)/shard_map/prepare/pallas_call | solution.py:136
  6.3 0.5 %collective-permute-start = (f32[48,512]{1,0:T(8,128)}, f32[48,512]{1,0:T(8,128)S(1)}, u32[]{:S(2)}, u32[]{:S(2)}) collective-permute-start(f32[48,512]{1,0:T(8,128)} %get-tuple-element.19), channel_id=1, source_target_pairs={{0,1},{1,0},{2,3},{3,2},{4,5},{5,4},{6,7},{7,6},{8,9},{9,8},{10,11... | collective-permute-start | bytes 294920 | tf_op jit(solution)/shard_map/ppermute | solution.py:588
  6.8 3.7 %collective-permute-start.1 = (bf16[2,144,256]{2,1,0:T(8,128)(2,1)}, bf16[2,144,256]{2,1,0:T(8,128)(2,1)S(1)}, u32[]{:S(2)}, u32[]{:S(2)}) collective-permute-start(bf16[2,144,256]{2,1,0:T(8,128)(2,1)} %get-tuple-element.22), channel_id=1, source_target_pairs={{0,8},{2,10},{4,12},{6,14},{8,0},{10,2},{12,4},{14,6},{1,9},{3,11}... | collective-permute-start | bytes 442376 | tf_op jit(solution)/shard_map/ppermute | solution.py:582
  10.5 1.3 %collective-permute-start.2 = (bf16[2,144,256]{2,1,0:T(8,128)(2,1)}, bf16[2,144,256]{2,1,0:T(8,128)(2,1)S(1)}, u32[]{:S(2)}, u32[]{:S(2)}) collective-permute-start(bf16[2,144,256]{2,1,0:T(8,128)(2,1)} %get-tuple-element.23), channel_id=1, source_target_pairs={{0,10},{2,8},{4,14},{6,12},{8,2},{10,0},{12,6},{14,4},{1,11},{3,9}... | collective-permute-start | bytes 442376 | tf_op jit(solution)/shard_map/ppermute | solution.py:582
  11.8 3.6 %collective-permute-start.3 = (bf16[2,144,256]{2,1,0:T(8,128)(2,1)}, bf16[2,144,256]{2,1,0:T(8,128)(2,1)S(1)}, u32[]{:S(2)}, u32[]{:S(2)}) collective-permute-start(bf16[2,144,256]{2,1,0:T(8,128)(2,1)} %get-tuple-element.24), channel_id=1, source_target_pairs={{0,12},{2,14},{4,8},{6,10},{8,4},{10,6},{12,0},{14,2},{1,13},{3,15... | collective-permute-start | bytes 442376 | tf_op jit(solution)/shard_map/ppermute | solution.py:582
  15.4 0.0 collective-permute-start.4
  15.4 0.0 collective-permute-done.got_ref
  15.4 0.0 copy-start.3
  15.5 0.9 %copy-done.3 = f32[48,512]{1,0:T(8,128)S(1)} copy-done((f32[48,512]{1,0:T(8,128)S(1)}, f32[48,512]{1,0:T(8,128)}, u32[]{:S(2)}) %copy-start.3) | copy-done | bytes 98328
  16.3 6.6 %attend.1 = (bf16[24,2,144,256]{3,2,1,0:T(8,128)(2,1)}, bf16[768,128]{1,0:T(8,128)(2,1)S(1)}, bf16[8,48,128]{2,1,0:T(8,128)(2,1)}, bf16[2,144,256]{2,1,0:T(8,128...) custom-call(s32[24]{0:T(128)S(1)} %copy-done, s32[24]{0:T(128)S(1)} %copy-done.1, ...), custom_call_target="tpu_custom_call" | custom-call | flops 68719476736 | bytes 268435456 | tf_op jit(solution)/shard_map/attend/pallas_call | solution.py:324
  22.9 4.2 %all-to-all-start = ((bf16[8,48,128]{2,1,0:T(8,128)(2,1)}), bf16[8,48,128]{2,1,0:T(8,128)(2,1)S(1)}, u32[]{:S(2)}, u32[]{:S(2)}) async-start(bf16[8,48,128]{2,1,0:T(8,128)(2,1)} %get-tuple-element.21), calls=%async_computation | async-start | bytes 196608 | tf_op jit(solution)/shard_map/all_to_all | solution.py:601
  27.1 2.0 %collective-permute-start.5 = (bf16[2,144,256]{2,1,0:T(8,128)(2,1)S(1)}, bf16[2,144,256]{2,1,0:T(8,128)(2,1)S(1)}, u32[]{:S(2)}, u32[]{:S(2)}) collective-permute-start(bf16[2,144,256]{2,1,0:T(8,128)(2,1)S(1)} %get-tuple-element.30), channel_id=1, source_target_pairs={{0,4},{2,6},{4,0},{6,2},{8,12},{10,14},{12,8},{14,10},{1,5},{3,7},... | collective-permute-start | bytes 442376 | tf_op jit(solution)/shard_map/ppermute | solution.py:582
  29.1 0.0 collective-permute-done.1.refs_0_
  29.1 3.3 %collective-permute-start.6 = (bf16[2,144,256]{2,1,0:T(8,128)(2,1)S(1)}, bf16[2,144,256]{2,1,0:T(8,128)(2,1)S(1)}, u32[]{:S(2)}, u32[]{:S(2)}) collective-permute-start(bf16[2,144,256]{2,1,0:T(8,128)(2,1)S(1)} %get-tuple-element.31), channel_id=1, source_target_pairs={{0,14},{2,12},{4,10},{6,8},{8,6},{10,4},{12,2},{14,0},{1,15},{3,13... | collective-permute-start | bytes 442376 | tf_op jit(solution)/shard_map/ppermute | solution.py:582
  32.4 0.0 collective-permute-done.2.refs_1_
  32.4 0.6 %collective-permute-start.7 = (bf16[2,144,256]{2,1,0:T(8,128)(2,1)S(1)}, bf16[2,144,256]{2,1,0:T(8,128)(2,1)S(1)}, u32[]{:S(2)}, u32[]{:S(2)}) collective-permute-start(bf16[2,144,256]{2,1,0:T(8,128)(2,1)S(1)} %get-tuple-element.32), channel_id=1, source_target_pairs={{0,2},{2,0},{4,6},{6,4},{8,10},{10,8},{12,14},{14,12},{1,3},{3,1},... | collective-permute-start | bytes 442376 | tf_op jit(solution)/shard_map/ppermute | solution.py:582
  33.0 0.0 collective-permute-done.3.refs_2_
  33.0 0.0 collective-permute-done.4.refs_3_
  33.0 1.0 %land.1 = (bf16[24,2,144,256]{3,2,1,0:T(8,128)(2,1)}, bf16[4,2,32,256]{3,2,1,0:T(8,128)(2,1)S(1)}) custom-call(bf16[2,144,256]{2,1,0:T(8,128)(2,1)S(1)} %collective-permute-done.1.refs_0_, bf16[2,144,256]{2,1,0:T(8,128)(2,1)S(1)} %collective-permute-done.2.refs_1_, ...), custom_call_target="tpu_custom_call", output_to_operand_aliasing={{0}: (4, {})} | custom-call | flops 68719476736 | bytes 268435456 | tf_op jit(solution)/shard_map/land/pallas_call | solution.py:414
  34.0 1.0 %all-to-all-done.small_ref.refs_3_ = bf16[8,48,128]{2,1,0:T(8,128)(2,1)S(1)} async-done(((bf16[8,48,128]{2,1,0:T(8,128)(2,1)}), bf16[8,48,128]{2,1,0:T(8,128)(2,1)S(1)}, u32[]{:S(2)}, u32[]{:S(2)}) %all-to-all-start) | async-done | bytes 98336 | tf_op jit(solution)/shard_map/all_to_all | solution.py:601
  35.0 1.6 %settle.1 = (bf16[2,24,2048]{2,1,0:T(8,128)(2,1)}, bf16[24,2,144,256]{3,2,1,0:T(8,128)(2,1)}) custom-call(bf16[768,128]{1,0:T(8,128)(2,1)S(1)} %get-tuple-element.20.mixed_ref, bf16[8,48,128]{2,1,0:T(8,128)(2,1)S(1)} %all-to-all-done.small_ref.refs_3_, bf16[4,2,32,256]{3,2,1,0:T(8,128)(2,1)S(1)} %get-tuple-element.27.window_ref, ...), custom_call_target="tpu_custom_call", output_to_operand_aliasing={{1}: (3, {})} | custom-call | flops 1 | bytes 1 | tf_op jit(solution)/shard_map/settle/pallas_call | solution.py:510
  36.6 3.0 %collective-permute-done.6.refs_1_ = bf16[2,144,256]{2,1,0:T(8,128)(2,1)S(1)} collective-permute-done((bf16[2,144,256]{2,1,0:T(8,128)(2,1)S(1)}, bf16[2,144,256]{2,1,0:T(8,128)(2,1)S(1)}, u32[]{:S(2)}, u32[]{:S(2)}) %collective-permute-start.6) | collective-permute-done | bytes 147488 | tf_op jit(solution)/shard_map/ppermute | solution.py:582
  39.6 0.3 collective-permute-done.7.refs_2_
  39.9 0.9 %finish.1 = bf16[24,2,144,256]{3,2,1,0:T(8,128)(2,1)} custom-call(bf16[2,144,256]{2,1,0:T(8,128)(2,1)S(1)} %collective-permute-done.5.refs_0_, bf16[2,144,256]{2,1,0:T(8,128)(2,1)S(1)} %collective-permute-done.6.refs_1_, bf16[2,144,256]{2,1,0:T(8,128)(2,1)S(1)} %collective-permute-done.7.refs_2_, ...), custom_call_target="tpu_custom_call", output_to_operand_aliasing={{}: (4, {})} | custom-call | flops 1 | bytes 1 | tf_op jit(solution)/shard_map/finish/pallas_call | solution.py:555
  (9 shorter events, 0.0 us)
Async XLA Ops:
  0.6 14.8 %copy-start.1 = (s32[24]{0:T(128)S(1)}, s32[24]{0:T(128)}, u32[]{:S(2)}) copy-start(s32[24]{0:T(128)} %dest_ref.3) | copy-start | bytes 292
  0.6 14.8 %copy-start = (s32[24]{0:T(128)S(1)}, s32[24]{0:T(128)}, u32[]{:S(2)}) copy-start(s32[24]{0:T(128)} %length_ref.3) | copy-start | bytes 292
  0.7 14.8 %copy-start.4 = (bf16[128]{0:T(256)(128)(2,1)S(1)}, bf16[128]{0:T(256)(128)(2,1)}, u32[]{:S(2)}) copy-start(bf16[128]{0:T(256)(128)(2,1)} %param.15) | copy-start | bytes 772
  0.7 14.8 %copy-start.2 = (bf16[2,24,2048]{2,1,0:T(8,128)(2,1)S(1)}, bf16[2,24,2048]{2,1,0:T(8,128)(2,1)}, u32[]{:S(2)}) copy-start(bf16[2,24,2048]{2,1,0:T(8,128)(2,1)} %query_ref.1) | copy-start | bytes 589828
  6.3 9.1 %collective-permute-start = (f32[48,512]{1,0:T(8,128)}, f32[48,512]{1,0:T(8,128)S(1)}, u32[]{:S(2)}, u32[]{:S(2)}) collective-permute-start(f32[48,512]{1,0:T(8,128)} %get-tuple-element.19), channel_id=1, source_target_pairs={{0,1},{1,0},{2,3},{3,2},{4,5},{5,4},{6,7},{7,6},{8,9},{9,8},{10,11... | collective-permute-start | bytes 294920 | tf_op jit(solution)/shard_map/ppermute | solution.py:588
  6.8 22.3 %collective-permute-start.1 = (bf16[2,144,256]{2,1,0:T(8,128)(2,1)}, bf16[2,144,256]{2,1,0:T(8,128)(2,1)S(1)}, u32[]{:S(2)}, u32[]{:S(2)}) collective-permute-start(bf16[2,144,256]{2,1,0:T(8,128)(2,1)} %get-tuple-element.22), channel_id=1, source_target_pairs={{0,8},{2,10},{4,12},{6,14},{8,0},{10,2},{12,4},{14,6},{1,9},{3,11}... | collective-permute-start | bytes 442376 | tf_op jit(solution)/shard_map/ppermute | solution.py:582
  10.5 21.9 %collective-permute-start.2 = (bf16[2,144,256]{2,1,0:T(8,128)(2,1)}, bf16[2,144,256]{2,1,0:T(8,128)(2,1)S(1)}, u32[]{:S(2)}, u32[]{:S(2)}) collective-permute-start(bf16[2,144,256]{2,1,0:T(8,128)(2,1)} %get-tuple-element.23), channel_id=1, source_target_pairs={{0,10},{2,8},{4,14},{6,12},{8,2},{10,0},{12,6},{14,4},{1,11},{3,9}... | collective-permute-start | bytes 442376 | tf_op jit(solution)/shard_map/ppermute | solution.py:582
  11.8 21.2 %collective-permute-start.3 = (bf16[2,144,256]{2,1,0:T(8,128)(2,1)}, bf16[2,144,256]{2,1,0:T(8,128)(2,1)S(1)}, u32[]{:S(2)}, u32[]{:S(2)}) collective-permute-start(bf16[2,144,256]{2,1,0:T(8,128)(2,1)} %get-tuple-element.24), channel_id=1, source_target_pairs={{0,12},{2,14},{4,8},{6,10},{8,4},{10,6},{12,0},{14,2},{1,13},{3,15... | collective-permute-start | bytes 442376 | tf_op jit(solution)/shard_map/ppermute | solution.py:582
  15.4 17.6 %collective-permute-start.4 = (bf16[2,144,256]{2,1,0:T(8,128)(2,1)}, bf16[2,144,256]{2,1,0:T(8,128)(2,1)S(1)}, u32[]{:S(2)}, u32[]{:S(2)}) collective-permute-start(bf16[2,144,256]{2,1,0:T(8,128)(2,1)} %get-tuple-element.25), channel_id=1, source_target_pairs={{0,6},{2,4},{4,2},{6,0},{8,14},{10,12},{12,10},{14,8},{1,7},{3,5},... | collective-permute-start | bytes 442376 | tf_op jit(solution)/shard_map/ppermute | solution.py:582
  15.4 0.9 %copy-start.3 = (f32[48,512]{1,0:T(8,128)S(1)}, f32[48,512]{1,0:T(8,128)}, u32[]{:S(2)}) copy-start(f32[48,512]{1,0:T(8,128)} %get-tuple-element.18.own_ref) | copy-start | bytes 294916
  22.9 12.1 %all-to-all-start = ((bf16[8,48,128]{2,1,0:T(8,128)(2,1)}), bf16[8,48,128]{2,1,0:T(8,128)(2,1)S(1)}, u32[]{:S(2)}, u32[]{:S(2)}) async-start(bf16[8,48,128]{2,1,0:T(8,128)(2,1)} %get-tuple-element.21), calls=%async_computation | async-start | bytes 196608 | tf_op jit(solution)/shard_map/all_to_all | solution.py:601
  27.1 9.5 %collective-permute-start.5 = (bf16[2,144,256]{2,1,0:T(8,128)(2,1)S(1)}, bf16[2,144,256]{2,1,0:T(8,128)(2,1)S(1)}, u32[]{:S(2)}, u32[]{:S(2)}) collective-permute-start(bf16[2,144,256]{2,1,0:T(8,128)(2,1)S(1)} %get-tuple-element.30), channel_id=1, source_target_pairs={{0,4},{2,6},{4,0},{6,2},{8,12},{10,14},{12,8},{14,10},{1,5},{3,7},... | collective-permute-start | bytes 442376 | tf_op jit(solution)/shard_map/ppermute | solution.py:582
  29.1 10.5 %collective-permute-start.6 = (bf16[2,144,256]{2,1,0:T(8,128)(2,1)S(1)}, bf16[2,144,256]{2,1,0:T(8,128)(2,1)S(1)}, u32[]{:S(2)}, u32[]{:S(2)}) collective-permute-start(bf16[2,144,256]{2,1,0:T(8,128)(2,1)S(1)} %get-tuple-element.31), channel_id=1, source_target_pairs={{0,14},{2,12},{4,10},{6,8},{8,6},{10,4},{12,2},{14,0},{1,15},{3,13... | collective-permute-start | bytes 442376 | tf_op jit(solution)/shard_map/ppermute | solution.py:582
  32.4 7.5 %collective-permute-start.7 = (bf16[2,144,256]{2,1,0:T(8,128)(2,1)S(1)}, bf16[2,144,256]{2,1,0:T(8,128)(2,1)S(1)}, u32[]{:S(2)}, u32[]{:S(2)}) collective-permute-start(bf16[2,144,256]{2,1,0:T(8,128)(2,1)S(1)} %get-tuple-element.32), channel_id=1, source_target_pairs={{0,2},{2,0},{4,6},{6,4},{8,10},{10,8},{12,14},{14,12},{1,3},{3,1},... | collective-permute-start | bytes 442376 | tf_op jit(solution)/shard_map/ppermute | solution.py:582

commit v19 on v15

--- a/solution.py
+++ b/solution.py
@@ -128,7 +128,7 @@
 def prepare(destination, lengths, hidden_new, kv_cache, key_weight, value_weight, count, early):
     steps, rows, depth = hidden_new.shape
     width = key_weight.shape[1]
-    chunks = 5
+    chunks = 10
     part = jax.ShapeDtypeStruct((steps * rows, width), jnp.float32)
     smem = pl.BlockSpec(memory_space=pltpu.SMEM)
     vmem = pl.BlockSpec(memory_space=pltpu.VMEM)

time: 40.4 us -> 40.6 us (level)
  no operation moved by 1% of the time
where the time goes in v19:
time: 40.6 us; the launch traced here: 40.2 us
  starting transfers between devices  18.7 us (46%)
  Pallas kernels  15.9 us (39%)
  waiting for transfers between devices  4.02 us (10%)
  local copies, waits for them, and re-layouts  0.9 us (2%)
  between operations  0.74 us (2%)
    ppermute x7, starting transfers between devices, send(): return lax.ppermute(block, 'inst', pairs)  13.9 us
    pallas_call x1, Pallas kernels, attend(): pl.pallas_call(functools.partial(attend_kernel, count, late, block), grid...  6.59 us
    pallas_call x1, Pallas kernels, prepare(): pl.pallas_call(functools.partial(prepare_kernel, count, early, chunks), o...  5.82 us
    all_to_all x1, starting transfers between devices, local(): small_got = lax.all_to_all(small, 'inst', 0, 0, tiled=True)  4.23 us
    all_to_all x1, waiting for transfers between devices, local(): small_got = lax.all_to_all(small, 'inst', 0, 0, tiled=True)  2.06 us
    ppermute x7, waiting for transfers between devices, send(): return lax.ppermute(block, 'inst', pairs)  1.96 us
    pallas_call x1, Pallas kernels, settle(): pl.pallas_call(functools.partial(settle_kernel, count, early, group), out...  1.56 us
    pallas_call x1, Pallas kernels, land(): pl.pallas_call(functools.partial(land_kernel, pieces), out_shape=[jax.Sha...  1.01 us
  transfers between devices with their start and end apart: 9, of which 4 were waited for; matrix products, arithmetic and copies ran while one was open for 0% of the time, Pallas kernels for 23%

profile of v19, /device:TPU:0, one launch (start us, length us, event | category | flops | bytes accessed | tf_op | source)
XLA Modules:
  0.0 40.2 jit_solution(6919676057574361525)
XLA Ops:
  0.7 5.8 %prepare.1 = (bf16[2,144,256]{2,1,0:T(8,128)(2,1)}, bf16[2,144,256]{2,1,0:T(8,128)(2,1)}, bf16[2,144,256]{2,1,0:T(8,128)(2,1)}, bf16[2,144,256]{2,1,0:T(8,128)(2...) custom-call(s32[24]{0:T(128)} %dest_ref.3, s32[24]{0:T(128)} %length_ref.3, bf16[2,24,2560]{2,1,0:T(8,128)(2,1)} %hidden_ref.1, ...), custom_call_target="tpu_custom_call" | custom-call | flops 1 | bytes 1 | tf_op jit(solution)/shard_map/prepare/pallas_call | solution.py:136
  6.5 0.5 %collective-permute-start = (f32[48,512]{1,0:T(8,128)}, f32[48,512]{1,0:T(8,128)S(1)}, u32[]{:S(2)}, u32[]{:S(2)}) collective-permute-start(f32[48,512]{1,0:T(8,128)} %get-tuple-element.19), channel_id=1, source_target_pairs={{0,1},{1,0},{2,3},{3,2},{4,5},{5,4},{6,7},{7,6},{8,9},{9,8},{10,11... | collective-permute-start | bytes 294920 | tf_op jit(solution)/shard_map/ppermute | solution.py:587
  7.0 3.7 %collective-permute-start.1 = (bf16[2,144,256]{2,1,0:T(8,128)(2,1)}, bf16[2,144,256]{2,1,0:T(8,128)(2,1)S(1)}, u32[]{:S(2)}, u32[]{:S(2)}) collective-permute-start(bf16[2,144,256]{2,1,0:T(8,128)(2,1)} %get-tuple-element.22), channel_id=1, source_target_pairs={{0,8},{2,10},{4,12},{6,14},{8,0},{10,2},{12,4},{14,6},{1,9},{3,11}... | collective-permute-start | bytes 442376 | tf_op jit(solution)/shard_map/ppermute | solution.py:581
  10.7 1.3 %collective-permute-start.2 = (bf16[2,144,256]{2,1,0:T(8,128)(2,1)}, bf16[2,144,256]{2,1,0:T(8,128)(2,1)S(1)}, u32[]{:S(2)}, u32[]{:S(2)}) collective-permute-start(bf16[2,144,256]{2,1,0:T(8,128)(2,1)} %get-tuple-element.23), channel_id=1, source_target_pairs={{0,10},{2,8},{4,14},{6,12},{8,2},{10,0},{12,6},{14,4},{1,11},{3,9}... | collective-permute-start | bytes 442376 | tf_op jit(solution)/shard_map/ppermute | solution.py:581
  12.0 3.6 %collective-permute-start.3 = (bf16[2,144,256]{2,1,0:T(8,128)(2,1)}, bf16[2,144,256]{2,1,0:T(8,128)(2,1)S(1)}, u32[]{:S(2)}, u32[]{:S(2)}) collective-permute-start(bf16[2,144,256]{2,1,0:T(8,128)(2,1)} %get-tuple-element.24), channel_id=1, source_target_pairs={{0,12},{2,14},{4,8},{6,10},{8,4},{10,6},{12,0},{14,2},{1,13},{3,15... | collective-permute-start | bytes 442376 | tf_op jit(solution)/shard_map/ppermute | solution.py:581
  15.6 0.0 collective-permute-start.4
  15.6 0.0 collective-permute-done.got_ref
  15.6 0.0 copy-start.3
  15.6 0.9 %copy-done.3 = f32[48,512]{1,0:T(8,128)S(1)} copy-done((f32[48,512]{1,0:T(8,128)S(1)}, f32[48,512]{1,0:T(8,128)}, u32[]{:S(2)}) %copy-start.3) | copy-done | bytes 98328
  16.5 6.6 %attend.1 = (bf16[24,2,144,256]{3,2,1,0:T(8,128)(2,1)}, bf16[768,128]{1,0:T(8,128)(2,1)S(1)}, bf16[8,48,128]{2,1,0:T(8,128)(2,1)}, bf16[2,144,256]{2,1,0:T(8,128...) custom-call(s32[24]{0:T(128)S(1)} %copy-done, s32[24]{0:T(128)S(1)} %copy-done.1, ...), custom_call_target="tpu_custom_call" | custom-call | flops 68719476736 | bytes 268435456 | tf_op jit(solution)/shard_map/attend/pallas_call | solution.py:324
  23.1 4.2 %all-to-all-start = ((bf16[8,48,128]{2,1,0:T(8,128)(2,1)}), bf16[8,48,128]{2,1,0:T(8,128)(2,1)S(1)}, u32[]{:S(2)}, u32[]{:S(2)}) async-start(bf16[8,48,128]{2,1,0:T(8,128)(2,1)} %get-tuple-element.21), calls=%async_computation | async-start | bytes 196608 | tf_op jit(solution)/shard_map/all_to_all | solution.py:600
  27.3 4.7 %collective-permute-start.5 = (bf16[2,144,256]{2,1,0:T(8,128)(2,1)S(1)}, bf16[2,144,256]{2,1,0:T(8,128)(2,1)S(1)}, u32[]{:S(2)}, u32[]{:S(2)}) collective-permute-start(bf16[2,144,256]{2,1,0:T(8,128)(2,1)S(1)} %get-tuple-element.30), channel_id=1, source_target_pairs={{0,14},{2,12},{4,10},{6,8},{8,6},{10,4},{12,2},{14,0},{1,15},{3,13... | collective-permute-start | bytes 442376 | tf_op jit(solution)/shard_map/ppermute | solution.py:581
  32.1 0.0 collective-permute-done.1.refs_0_
  32.1 0.0 collective-permute-start.6
  32.1 0.0 collective-permute-done.2.refs_1_
  32.1 0.6 %collective-permute-start.7 = (bf16[2,144,256]{2,1,0:T(8,128)(2,1)S(1)}, bf16[2,144,256]{2,1,0:T(8,128)(2,1)S(1)}, u32[]{:S(2)}, u32[]{:S(2)}) collective-permute-start(bf16[2,144,256]{2,1,0:T(8,128)(2,1)S(1)} %get-tuple-element.32), channel_id=1, source_target_pairs={{0,2},{2,0},{4,6},{6,4},{8,10},{10,8},{12,14},{14,12},{1,3},{3,1},... | collective-permute-start | bytes 442376 | tf_op jit(solution)/shard_map/ppermute | solution.py:581
  32.7 0.0 collective-permute-done.3.refs_2_
  32.7 1.0 %land.1 = (bf16[24,2,144,256]{3,2,1,0:T(8,128)(2,1)}, bf16[4,2,32,256]{3,2,1,0:T(8,128)(2,1)S(1)}) custom-call(bf16[2,144,256]{2,1,0:T(8,128)(2,1)S(1)} %collective-permute-done.1.refs_0_, bf16[2,144,256]{2,1,0:T(8,128)(2,1)S(1)} %collective-permute-done.2.refs_1_, ...), custom_call_target="tpu_custom_call", output_to_operand_aliasing={{0}: (4, {})} | custom-call | flops 68719476736 | bytes 268435456 | tf_op jit(solution)/shard_map/land/pallas_call | solution.py:414
  33.7 2.1 %all-to-all-done.small_ref.refs_3_ = bf16[8,48,128]{2,1,0:T(8,128)(2,1)S(1)} async-done(((bf16[8,48,128]{2,1,0:T(8,128)(2,1)}), bf16[8,48,128]{2,1,0:T(8,128)(2,1)S(1)}, u32[]{:S(2)}, u32[]{:S(2)}) %all-to-all-start) | async-done | bytes 98336 | tf_op jit(solution)/shard_map/all_to_all | solution.py:600
  35.8 1.6 %settle.1 = (bf16[2,24,2048]{2,1,0:T(8,128)(2,1)}, bf16[24,2,144,256]{3,2,1,0:T(8,128)(2,1)}) custom-call(bf16[768,128]{1,0:T(8,128)(2,1)S(1)} %get-tuple-element.20.mixed_ref, bf16[8,48,128]{2,1,0:T(8,128)(2,1)S(1)} %all-to-all-done.small_ref.refs_3_, bf16[4,2,32,256]{3,2,1,0:T(8,128)(2,1)S(1)} %get-tuple-element.27.window_ref, ...), custom_call_target="tpu_custom_call", output_to_operand_aliasing={{1}: (3, {})} | custom-call | flops 1 | bytes 1 | tf_op jit(solution)/shard_map/settle/pallas_call | solution.py:510
  37.4 0.9 %collective-permute-done.5.refs_0_ = bf16[2,144,256]{2,1,0:T(8,128)(2,1)S(1)} collective-permute-done((bf16[2,144,256]{2,1,0:T(8,128)(2,1)S(1)}, bf16[2,144,256]{2,1,0:T(8,128)(2,1)S(1)}, u32[]{:S(2)}, u32[]{:S(2)}) %collective-permute-start.5) | collective-permute-done | bytes 147488 | tf_op jit(solution)/shard_map/ppermute | solution.py:581
  38.2 0.9 %collective-permute-done.6.refs_1_ = bf16[2,144,256]{2,1,0:T(8,128)(2,1)S(1)} collective-permute-done((bf16[2,144,256]{2,1,0:T(8,128)(2,1)S(1)}, bf16[2,144,256]{2,1,0:T(8,128)(2,1)S(1)}, u32[]{:S(2)}, u32[]{:S(2)}) %collective-permute-start.6) | collective-permute-done | bytes 147488 | tf_op jit(solution)/shard_map/ppermute | solution.py:581
  39.1 0.2 collective-permute-done.7.refs_2_
  39.3 0.9 %finish.1 = bf16[24,2,144,256]{3,2,1,0:T(8,128)(2,1)} custom-call(bf16[2,144,256]{2,1,0:T(8,128)(2,1)S(1)} %collective-permute-done.5.refs_0_, bf16[2,144,256]{2,1,0:T(8,128)(2,1)S(1)} %collective-permute-done.6.refs_1_, bf16[2,144,256]{2,1,0:T(8,128)(2,1)S(1)} %collective-permute-done.7.refs_2_, ...), custom_call_target="tpu_custom_call", output_to_operand_aliasing={{}: (4, {})} | custom-call | flops 1 | bytes 1 | tf_op jit(solution)/shard_map/finish/pallas_call | solution.py:555
  (9 shorter events, 0.0 us)
Async XLA Ops:
  0.6 15.0 %copy-start.1 = (s32[24]{0:T(128)S(1)}, s32[24]{0:T(128)}, u32[]{:S(2)}) copy-start(s32[24]{0:T(128)} %dest_ref.3) | copy-start | bytes 292
  0.6 14.9 %copy-start = (s32[24]{0:T(128)S(1)}, s32[24]{0:T(128)}, u32[]{:S(2)}) copy-start(s32[24]{0:T(128)} %length_ref.3) | copy-start | bytes 292
  0.7 14.9 %copy-start.4 = (bf16[128]{0:T(256)(128)(2,1)S(1)}, bf16[128]{0:T(256)(128)(2,1)}, u32[]{:S(2)}) copy-start(bf16[128]{0:T(256)(128)(2,1)} %param.15) | copy-start | bytes 772
  0.7 14.9 %copy-start.2 = (bf16[2,24,2048]{2,1,0:T(8,128)(2,1)S(1)}, bf16[2,24,2048]{2,1,0:T(8,128)(2,1)}, u32[]{:S(2)}) copy-start(bf16[2,24,2048]{2,1,0:T(8,128)(2,1)} %query_ref.1) | copy-start | bytes 589828
  6.5 9.1 %collective-permute-start = (f32[48,512]{1,0:T(8,128)}, f32[48,512]{1,0:T(8,128)S(1)}, u32[]{:S(2)}, u32[]{:S(2)}) collective-permute-start(f32[48,512]{1,0:T(8,128)} %get-tuple-element.19), channel_id=1, source_target_pairs={{0,1},{1,0},{2,3},{3,2},{4,5},{5,4},{6,7},{7,6},{8,9},{9,8},{10,11... | collective-permute-start | bytes 294920 | tf_op jit(solution)/shard_map/ppermute | solution.py:587
  7.0 25.0 %collective-permute-start.1 = (bf16[2,144,256]{2,1,0:T(8,128)(2,1)}, bf16[2,144,256]{2,1,0:T(8,128)(2,1)S(1)}, u32[]{:S(2)}, u32[]{:S(2)}) collective-permute-start(bf16[2,144,256]{2,1,0:T(8,128)(2,1)} %get-tuple-element.22), channel_id=1, source_target_pairs={{0,8},{2,10},{4,12},{6,14},{8,0},{10,2},{12,4},{14,6},{1,9},{3,11}... | collective-permute-start | bytes 442376 | tf_op jit(solution)/shard_map/ppermute | solution.py:581
  10.7 21.4 %collective-permute-start.2 = (bf16[2,144,256]{2,1,0:T(8,128)(2,1)}, bf16[2,144,256]{2,1,0:T(8,128)(2,1)S(1)}, u32[]{:S(2)}, u32[]{:S(2)}) collective-permute-start(bf16[2,144,256]{2,1,0:T(8,128)(2,1)} %get-tuple-element.23), channel_id=1, source_target_pairs={{0,10},{2,8},{4,14},{6,12},{8,2},{10,0},{12,6},{14,4},{1,11},{3,9}... | collective-permute-start | bytes 442376 | tf_op jit(solution)/shard_map/ppermute | solution.py:581
  12.0 20.7 %collective-permute-start.3 = (bf16[2,144,256]{2,1,0:T(8,128)(2,1)}, bf16[2,144,256]{2,1,0:T(8,128)(2,1)S(1)}, u32[]{:S(2)}, u32[]{:S(2)}) collective-permute-start(bf16[2,144,256]{2,1,0:T(8,128)(2,1)} %get-tuple-element.24), channel_id=1, source_target_pairs={{0,12},{2,14},{4,8},{6,10},{8,4},{10,6},{12,0},{14,2},{1,13},{3,15... | collective-permute-start | bytes 442376 | tf_op jit(solution)/shard_map/ppermute | solution.py:581
  15.6 17.1 %collective-permute-start.4 = (bf16[2,144,256]{2,1,0:T(8,128)(2,1)}, bf16[2,144,256]{2,1,0:T(8,128)(2,1)S(1)}, u32[]{:S(2)}, u32[]{:S(2)}) collective-permute-start(bf16[2,144,256]{2,1,0:T(8,128)(2,1)} %get-tuple-element.25), channel_id=1, source_target_pairs={{0,6},{2,4},{4,2},{6,0},{8,14},{10,12},{12,10},{14,8},{1,7},{3,5},... | collective-permute-start | bytes 442376 | tf_op jit(solution)/shard_map/ppermute | solution.py:581
  15.6 0.9 %copy-start.3 = (f32[48,512]{1,0:T(8,128)S(1)}, f32[48,512]{1,0:T(8,128)}, u32[]{:S(2)}) copy-start(f32[48,512]{1,0:T(8,128)} %get-tuple-element.18.own_ref) | copy-start | bytes 294916
  23.1 12.7 %all-to-all-start = ((bf16[8,48,128]{2,1,0:T(8,128)(2,1)}), bf16[8,48,128]{2,1,0:T(8,128)(2,1)S(1)}, u32[]{:S(2)}, u32[]{:S(2)}) async-start(bf16[8,48,128]{2,1,0:T(8,128)(2,1)} %get-tuple-element.21), calls=%async_computation | async-start | bytes 196608 | tf_op jit(solution)/shard_map/all_to_all | solution.py:600
  27.3 10.9 %collective-permute-start.5 = (bf16[2,144,256]{2,1,0:T(8,128)(2,1)S(1)}, bf16[2,144,256]{2,1,0:T(8,128)(2,1)S(1)}, u32[]{:S(2)}, u32[]{:S(2)}) collective-permute-start(bf16[2,144,256]{2,1,0:T(8,128)(2,1)S(1)} %get-tuple-element.30), channel_id=1, source_target_pairs={{0,14},{2,12},{4,10},{6,8},{8,6},{10,4},{12,2},{14,0},{1,15},{3,13... | collective-permute-start | bytes 442376 | tf_op jit(solution)/shard_map/ppermute | solution.py:581
  32.1 7.1 %collective-permute-start.6 = (bf16[2,144,256]{2,1,0:T(8,128)(2,1)S(1)}, bf16[2,144,256]{2,1,0:T(8,128)(2,1)S(1)}, u32[]{:S(2)}, u32[]{:S(2)}) collective-permute-start(bf16[2,144,256]{2,1,0:T(8,128)(2,1)S(1)} %get-tuple-element.31), channel_id=1, source_target_pairs={{0,4},{2,6},{4,0},{6,2},{8,12},{10,14},{12,8},{14,10},{1,5},{3,7},... | collective-permute-start | bytes 442376 | tf_op jit(solution)/shard_map/ppermute | solution.py:581
  32.1 7.2 %collective-permute-start.7 = (bf16[2,144,256]{2,1,0:T(8,128)(2,1)S(1)}, bf16[2,144,256]{2,1,0:T(8,128)(2,1)S(1)}, u32[]{:S(2)}, u32[]{:S(2)}) collective-permute-start(bf16[2,144,256]{2,1,0:T(8,128)(2,1)S(1)} %get-tuple-element.32), channel_id=1, source_target_pairs={{0,2},{2,0},{4,6},{6,4},{8,10},{10,8},{12,14},{14,12},{1,3},{3,1},... | collective-permute-start | bytes 442376 | tf_op jit(solution)/shard_map/ppermute | solution.py:581

commit v20 on v15

--- a/solution.py
+++ b/solution.py
@@ -78,8 +78,9 @@
 
     hidden_copy = pltpu.make_async_copy(hidden_ref, hidden_held, hidden_sem)
     hidden_copy.start()
-    for copy in weights(0):
-        copy.start()
+    for chunk in range(chunks):
+        for copy in weights(chunk):
+            copy.start()
     pick_rows(count, dest_ref, pick_ref)
     fetches, stores = [], []
     for piece, shift in enumerate(early):
@@ -88,9 +89,6 @@
             pltpu.make_async_copy(kv_ref.at[row], blocks.at[piece], in_sems.at[piece])
         )
         fetches[-1].start()
-    for chunk in range(1, chunks):
-        for copy in weights(chunk):
-            copy.start()
 
     for piece, shift in enumerate(early):
         peer = peer_to(me, shift, count)

time: 40.4 us -> 40.4 us (level)
  no operation moved by 1% of the time
where the time goes in v20:
time: 40.4 us; the launch traced here: 40 us
  starting transfers between devices  18.6 us (46%)
  Pallas kernels  15.7 us (39%)
  waiting for transfers between devices  4.02 us (10%)
  local copies, waits for them, and re-layouts  0.9 us (2%)
  between operations  0.74 us (2%)
    ppermute x7, starting transfers between devices, send(): return lax.ppermute(block, 'inst', pairs)  13.9 us
    pallas_call x1, Pallas kernels, attend(): pl.pallas_call(functools.partial(attend_kernel, count, late, block), grid...  6.62 us
    pallas_call x1, Pallas kernels, prepare(): pl.pallas_call(functools.partial(prepare_kernel, count, early, chunks), o...  5.65 us
    all_to_all x1, starting transfers between devices, local(): small_got = lax.all_to_all(small, 'inst', 0, 0, tiled=True)  4.2 us
    all_to_all x1, waiting for transfers between devices, local(): small_got = lax.all_to_all(small, 'inst', 0, 0, tiled=True)  2.06 us
    ppermute x7, waiting for transfers between devices, send(): return lax.ppermute(block, 'inst', pairs)  1.96 us
    pallas_call x1, Pallas kernels, settle(): pl.pallas_call(functools.partial(settle_kernel, count, early, group), out...  1.56 us
    pallas_call x1, Pallas kernels, land(): pl.pallas_call(functools.partial(land_kernel, pieces), out_shape=[jax.Sha...  1.01 us
  transfers between devices with their start and end apart: 9, of which 4 were waited for; matrix products, arithmetic and copies ran while one was open for 0% of the time, Pallas kernels for 23%

profile of v20, /device:TPU:0, one launch (start us, length us, event | category | flops | bytes accessed | tf_op | source)
XLA Modules:
  0.0 40.0 jit_solution(5788479319372066765)
XLA Ops:
  0.7 5.6 %prepare.1 = (bf16[2,144,256]{2,1,0:T(8,128)(2,1)}, bf16[2,144,256]{2,1,0:T(8,128)(2,1)}, bf16[2,144,256]{2,1,0:T(8,128)(2,1)}, bf16[2,144,256]{2,1,0:T(8,128)(2...) custom-call(s32[24]{0:T(128)} %dest_ref.3, s32[24]{0:T(128)} %length_ref.3, bf16[2,24,2560]{2,1,0:T(8,128)(2,1)} %hidden_ref.1, ...), custom_call_target="tpu_custom_call" | custom-call | flops 1 | bytes 1 | tf_op jit(solution)/shard_map/prepare/pallas_call | solution.py:134
  6.3 0.5 %collective-permute-start = (f32[48,512]{1,0:T(8,128)}, f32[48,512]{1,0:T(8,128)S(1)}, u32[]{:S(2)}, u32[]{:S(2)}) collective-permute-start(f32[48,512]{1,0:T(8,128)} %get-tuple-element.19), channel_id=1, source_target_pairs={{0,1},{1,0},{2,3},{3,2},{4,5},{5,4},{6,7},{7,6},{8,9},{9,8},{10,11... | collective-permute-start | bytes 294920 | tf_op jit(solution)/shard_map/ppermute | solution.py:585
  6.8 3.7 %collective-permute-start.1 = (bf16[2,144,256]{2,1,0:T(8,128)(2,1)}, bf16[2,144,256]{2,1,0:T(8,128)(2,1)S(1)}, u32[]{:S(2)}, u32[]{:S(2)}) collective-permute-start(bf16[2,144,256]{2,1,0:T(8,128)(2,1)} %get-tuple-element.22), channel_id=1, source_target_pairs={{0,8},{2,10},{4,12},{6,14},{8,0},{10,2},{12,4},{14,6},{1,9},{3,11}... | collective-permute-start | bytes 442376 | tf_op jit(solution)/shard_map/ppermute | solution.py:579
  10.5 1.3 %collective-permute-start.2 = (bf16[2,144,256]{2,1,0:T(8,128)(2,1)}, bf16[2,144,256]{2,1,0:T(8,128)(2,1)S(1)}, u32[]{:S(2)}, u32[]{:S(2)}) collective-permute-start(bf16[2,144,256]{2,1,0:T(8,128)(2,1)} %get-tuple-element.23), channel_id=1, source_target_pairs={{0,10},{2,8},{4,14},{6,12},{8,2},{10,0},{12,6},{14,4},{1,11},{3,9}... | collective-permute-start | bytes 442376 | tf_op jit(solution)/shard_map/ppermute | solution.py:579
  11.8 3.6 %collective-permute-start.3 = (bf16[2,144,256]{2,1,0:T(8,128)(2,1)}, bf16[2,144,256]{2,1,0:T(8,128)(2,1)S(1)}, u32[]{:S(2)}, u32[]{:S(2)}) collective-permute-start(bf16[2,144,256]{2,1,0:T(8,128)(2,1)} %get-tuple-element.24), channel_id=1, source_target_pairs={{0,12},{2,14},{4,8},{6,10},{8,4},{10,6},{12,0},{14,2},{1,13},{3,15... | collective-permute-start | bytes 442376 | tf_op jit(solution)/shard_map/ppermute | solution.py:579
  15.4 0.0 collective-permute-start.4
  15.4 0.0 collective-permute-done.got_ref
  15.4 0.0 copy-start.3
  15.5 0.9 %copy-done.3 = f32[48,512]{1,0:T(8,128)S(1)} copy-done((f32[48,512]{1,0:T(8,128)S(1)}, f32[48,512]{1,0:T(8,128)}, u32[]{:S(2)}) %copy-start.3) | copy-done | bytes 98328
  16.3 6.6 %attend.1 = (bf16[24,2,144,256]{3,2,1,0:T(8,128)(2,1)}, bf16[768,128]{1,0:T(8,128)(2,1)S(1)}, bf16[8,48,128]{2,1,0:T(8,128)(2,1)}, bf16[2,144,256]{2,1,0:T(8,128...) custom-call(s32[24]{0:T(128)S(1)} %copy-done, s32[24]{0:T(128)S(1)} %copy-done.1, ...), custom_call_target="tpu_custom_call" | custom-call | flops 68719476736 | bytes 268435456 | tf_op jit(solution)/shard_map/attend/pallas_call | solution.py:322
  23.0 4.2 %all-to-all-start = ((bf16[8,48,128]{2,1,0:T(8,128)(2,1)}), bf16[8,48,128]{2,1,0:T(8,128)(2,1)S(1)}, u32[]{:S(2)}, u32[]{:S(2)}) async-start(bf16[8,48,128]{2,1,0:T(8,128)(2,1)} %get-tuple-element.21), calls=%async_computation | async-start | bytes 196608 | tf_op jit(solution)/shard_map/all_to_all | solution.py:598
  27.2 4.7 %collective-permute-start.5 = (bf16[2,144,256]{2,1,0:T(8,128)(2,1)S(1)}, bf16[2,144,256]{2,1,0:T(8,128)(2,1)S(1)}, u32[]{:S(2)}, u32[]{:S(2)}) collective-permute-start(bf16[2,144,256]{2,1,0:T(8,128)(2,1)S(1)} %get-tuple-element.30), channel_id=1, source_target_pairs={{0,14},{2,12},{4,10},{6,8},{8,6},{10,4},{12,2},{14,0},{1,15},{3,13... | collective-permute-start | bytes 442376 | tf_op jit(solution)/shard_map/ppermute | solution.py:579
  31.9 0.0 collective-permute-done.1.refs_0_
  31.9 0.0 collective-permute-done.2.refs_1_
  31.9 0.6 %collective-permute-start.7 = (bf16[2,144,256]{2,1,0:T(8,128)(2,1)S(1)}, bf16[2,144,256]{2,1,0:T(8,128)(2,1)S(1)}, u32[]{:S(2)}, u32[]{:S(2)}) collective-permute-start(bf16[2,144,256]{2,1,0:T(8,128)(2,1)S(1)} %get-tuple-element.32), channel_id=1, source_target_pairs={{0,2},{2,0},{4,6},{6,4},{8,10},{10,8},{12,14},{14,12},{1,3},{3,1},... | collective-permute-start | bytes 442376 | tf_op jit(solution)/shard_map/ppermute | solution.py:579
  32.5 0.0 collective-permute-done.3.refs_2_
  32.5 0.0 collective-permute-done.4.refs_3_
  32.5 1.0 %land.1 = (bf16[24,2,144,256]{3,2,1,0:T(8,128)(2,1)}, bf16[4,2,32,256]{3,2,1,0:T(8,128)(2,1)S(1)}) custom-call(bf16[2,144,256]{2,1,0:T(8,128)(2,1)S(1)} %collective-permute-done.1.refs_0_, bf16[2,144,256]{2,1,0:T(8,128)(2,1)S(1)} %collective-permute-done.2.refs_1_, ...), custom_call_target="tpu_custom_call", output_to_operand_aliasing={{0}: (4, {})} | custom-call | flops 68719476736 | bytes 268435456 | tf_op jit(solution)/shard_map/land/pallas_call | solution.py:412
  33.5 2.1 %all-to-all-done.small_ref.refs_3_ = bf16[8,48,128]{2,1,0:T(8,128)(2,1)S(1)} async-done(((bf16[8,48,128]{2,1,0:T(8,128)(2,1)}), bf16[8,48,128]{2,1,0:T(8,128)(2,1)S(1)}, u32[]{:S(2)}, u32[]{:S(2)}) %all-to-all-start) | async-done | bytes 98336 | tf_op jit(solution)/shard_map/all_to_all | solution.py:598
  35.6 1.6 %settle.1 = (bf16[2,24,2048]{2,1,0:T(8,128)(2,1)}, bf16[24,2,144,256]{3,2,1,0:T(8,128)(2,1)}) custom-call(bf16[768,128]{1,0:T(8,128)(2,1)S(1)} %get-tuple-element.20.mixed_ref, bf16[8,48,128]{2,1,0:T(8,128)(2,1)S(1)} %all-to-all-done.small_ref.refs_3_, bf16[4,2,32,256]{3,2,1,0:T(8,128)(2,1)S(1)} %get-tuple-element.27.window_ref, ...), custom_call_target="tpu_custom_call", output_to_operand_aliasing={{1}: (3, {})} | custom-call | flops 1 | bytes 1 | tf_op jit(solution)/shard_map/settle/pallas_call | solution.py:508
  37.2 0.9 %collective-permute-done.5.refs_0_ = bf16[2,144,256]{2,1,0:T(8,128)(2,1)S(1)} collective-permute-done((bf16[2,144,256]{2,1,0:T(8,128)(2,1)S(1)}, bf16[2,144,256]{2,1,0:T(8,128)(2,1)S(1)}, u32[]{:S(2)}, u32[]{:S(2)}) %collective-permute-start.5) | collective-permute-done | bytes 147488 | tf_op jit(solution)/shard_map/ppermute | solution.py:579
  38.1 0.9 %collective-permute-done.6.refs_1_ = bf16[2,144,256]{2,1,0:T(8,128)(2,1)S(1)} collective-permute-done((bf16[2,144,256]{2,1,0:T(8,128)(2,1)S(1)}, bf16[2,144,256]{2,1,0:T(8,128)(2,1)S(1)}, u32[]{:S(2)}, u32[]{:S(2)}) %collective-permute-start.6) | collective-permute-done | bytes 147488 | tf_op jit(solution)/shard_map/ppermute | solution.py:579
  39.0 0.2 collective-permute-done.7.refs_2_
  39.1 0.9 %finish.1 = bf16[24,2,144,256]{3,2,1,0:T(8,128)(2,1)} custom-call(bf16[2,144,256]{2,1,0:T(8,128)(2,1)S(1)} %collective-permute-done.5.refs_0_, bf16[2,144,256]{2,1,0:T(8,128)(2,1)S(1)} %collective-permute-done.6.refs_1_, bf16[2,144,256]{2,1,0:T(8,128)(2,1)S(1)} %collective-permute-done.7.refs_2_, ...), custom_call_target="tpu_custom_call", output_to_operand_aliasing={{}: (4, {})} | custom-call | flops 1 | bytes 1 | tf_op jit(solution)/shard_map/finish/pallas_call | solution.py:553
  (9 shorter events, 0.0 us)
Async XLA Ops:
  0.6 14.8 %copy-start.1 = (s32[24]{0:T(128)S(1)}, s32[24]{0:T(128)}, u32[]{:S(2)}) copy-start(s32[24]{0:T(128)} %dest_ref.3) | copy-start | bytes 292
  0.6 14.8 %copy-start = (s32[24]{0:T(128)S(1)}, s32[24]{0:T(128)}, u32[]{:S(2)}) copy-start(s32[24]{0:T(128)} %length_ref.3) | copy-start | bytes 292
  0.7 14.8 %copy-start.4 = (bf16[128]{0:T(256)(128)(2,1)S(1)}, bf16[128]{0:T(256)(128)(2,1)}, u32[]{:S(2)}) copy-start(bf16[128]{0:T(256)(128)(2,1)} %param.15) | copy-start | bytes 772
  0.7 14.8 %copy-start.2 = (bf16[2,24,2048]{2,1,0:T(8,128)(2,1)S(1)}, bf16[2,24,2048]{2,1,0:T(8,128)(2,1)}, u32[]{:S(2)}) copy-start(bf16[2,24,2048]{2,1,0:T(8,128)(2,1)} %query_ref.1) | copy-start | bytes 589828
  6.3 9.1 %collective-permute-start = (f32[48,512]{1,0:T(8,128)}, f32[48,512]{1,0:T(8,128)S(1)}, u32[]{:S(2)}, u32[]{:S(2)}) collective-permute-start(f32[48,512]{1,0:T(8,128)} %get-tuple-element.19), channel_id=1, source_target_pairs={{0,1},{1,0},{2,3},{3,2},{4,5},{5,4},{6,7},{7,6},{8,9},{9,8},{10,11... | collective-permute-start | bytes 294920 | tf_op jit(solution)/shard_map/ppermute | solution.py:585
  6.8 25.0 %collective-permute-start.1 = (bf16[2,144,256]{2,1,0:T(8,128)(2,1)}, bf16[2,144,256]{2,1,0:T(8,128)(2,1)S(1)}, u32[]{:S(2)}, u32[]{:S(2)}) collective-permute-start(bf16[2,144,256]{2,1,0:T(8,128)(2,1)} %get-tuple-element.22), channel_id=1, source_target_pairs={{0,8},{2,10},{4,12},{6,14},{8,0},{10,2},{12,4},{14,6},{1,9},{3,11}... | collective-permute-start | bytes 442376 | tf_op jit(solution)/shard_map/ppermute | solution.py:579
  10.5 21.4 %collective-permute-start.2 = (bf16[2,144,256]{2,1,0:T(8,128)(2,1)}, bf16[2,144,256]{2,1,0:T(8,128)(2,1)S(1)}, u32[]{:S(2)}, u32[]{:S(2)}) collective-permute-start(bf16[2,144,256]{2,1,0:T(8,128)(2,1)} %get-tuple-element.23), channel_id=1, source_target_pairs={{0,10},{2,8},{4,14},{6,12},{8,2},{10,0},{12,6},{14,4},{1,11},{3,9}... | collective-permute-start | bytes 442376 | tf_op jit(solution)/shard_map/ppermute | solution.py:579
  11.8 20.7 %collective-permute-start.3 = (bf16[2,144,256]{2,1,0:T(8,128)(2,1)}, bf16[2,144,256]{2,1,0:T(8,128)(2,1)S(1)}, u32[]{:S(2)}, u32[]{:S(2)}) collective-permute-start(bf16[2,144,256]{2,1,0:T(8,128)(2,1)} %get-tuple-element.24), channel_id=1, source_target_pairs={{0,12},{2,14},{4,8},{6,10},{8,4},{10,6},{12,0},{14,2},{1,13},{3,15... | collective-permute-start | bytes 442376 | tf_op jit(solution)/shard_map/ppermute | solution.py:579
  15.4 17.1 %collective-permute-start.4 = (bf16[2,144,256]{2,1,0:T(8,128)(2,1)}, bf16[2,144,256]{2,1,0:T(8,128)(2,1)S(1)}, u32[]{:S(2)}, u32[]{:S(2)}) collective-permute-start(bf16[2,144,256]{2,1,0:T(8,128)(2,1)} %get-tuple-element.25), channel_id=1, source_target_pairs={{0,6},{2,4},{4,2},{6,0},{8,14},{10,12},{12,10},{14,8},{1,7},{3,5},... | collective-permute-start | bytes 442376 | tf_op jit(solution)/shard_map/ppermute | solution.py:579
  15.4 0.9 %copy-start.3 = (f32[48,512]{1,0:T(8,128)S(1)}, f32[48,512]{1,0:T(8,128)}, u32[]{:S(2)}) copy-start(f32[48,512]{1,0:T(8,128)} %get-tuple-element.18.own_ref) | copy-start | bytes 294916
  23.0 12.7 %all-to-all-start = ((bf16[8,48,128]{2,1,0:T(8,128)(2,1)}), bf16[8,48,128]{2,1,0:T(8,128)(2,1)S(1)}, u32[]{:S(2)}, u32[]{:S(2)}) async-start(bf16[8,48,128]{2,1,0:T(8,128)(2,1)} %get-tuple-element.21), calls=%async_computation | async-start | bytes 196608 | tf_op jit(solution)/shard_map/all_to_all | solution.py:598
  27.2 10.9 %collective-permute-start.5 = (bf16[2,144,256]{2,1,0:T(8,128)(2,1)S(1)}, bf16[2,144,256]{2,1,0:T(8,128)(2,1)S(1)}, u32[]{:S(2)}, u32[]{:S(2)}) collective-permute-start(bf16[2,144,256]{2,1,0:T(8,128)(2,1)S(1)} %get-tuple-element.30), channel_id=1, source_target_pairs={{0,14},{2,12},{4,10},{6,8},{8,6},{10,4},{12,2},{14,0},{1,15},{3,13... | collective-permute-start | bytes 442376 | tf_op jit(solution)/shard_map/ppermute | solution.py:579
  31.9 7.1 %collective-permute-start.6 = (bf16[2,144,256]{2,1,0:T(8,128)(2,1)S(1)}, bf16[2,144,256]{2,1,0:T(8,128)(2,1)S(1)}, u32[]{:S(2)}, u32[]{:S(2)}) collective-permute-start(bf16[2,144,256]{2,1,0:T(8,128)(2,1)S(1)} %get-tuple-element.31), channel_id=1, source_target_pairs={{0,4},{2,6},{4,0},{6,2},{8,12},{10,14},{12,8},{14,10},{1,5},{3,7},... | collective-permute-start | bytes 442376 | tf_op jit(solution)/shard_map/ppermute | solution.py:579
  31.9 7.2 %collective-permute-start.7 = (bf16[2,144,256]{2,1,0:T(8,128)(2,1)S(1)}, bf16[2,144,256]{2,1,0:T(8,128)(2,1)S(1)}, u32[]{:S(2)}, u32[]{:S(2)}) collective-permute-start(bf16[2,144,256]{2,1,0:T(8,128)(2,1)S(1)} %get-tuple-element.32), channel_id=1, source_target_pairs={{0,2},{2,0},{4,6},{6,4},{8,10},{10,8},{12,14},{14,12},{1,3},{3,1},... | collective-permute-start | bytes 442376 | tf_op jit(solution)/shard_map/ppermute | solution.py:579
